TPU v7x, 128 devices: a whole 4x4x4 slice. The times are simulated.
128 devices in a mesh: dp: 4 (over y_hi, core), ctx: 2 (over y_lo), tp: 16 (over x, z).
Axes of the slice: x: 4, y: 4 (y_hi: 2, y_lo: 2; y = y_hi * 2 + y_lo), z: 4, core: 2. Of those that a mesh axis runs over, the one named last changes fastest.
Arguments:
- queries: bfloat16 [16384, 4096], P(('dp', 'ctx'), 'tp'), may hold values from -16 to 16
- key_rows: bfloat16 [16384, 512], P(('dp', 'ctx', 'tp')), may hold values from -4 to 4
- value_rows: bfloat16 [16384, 512], P(('dp', 'ctx', 'tp')), may hold values from -6 to 6
- span_order: int32 [4], replicated, may hold values from 0 to 3, each once
- out_proj: bfloat16 [4096, 4096], P('tp'), may hold values from -0.09375 to 0.09375
- residual: bfloat16 [16384, 4096], P(('dp', 'ctx', 'tp')), may hold values from -6 to 6
- norm_gain: float32 [4096], replicated, may hold values from 0.1 to 1.9
- expert_ids: int32 [16384, 8], P(('dp', 'ctx', 'tp')), may hold values from 0 to 127, all different within a row; in each aligned block of 128 rows (0 to 127, 128 to 255, ...) at most 9 rows name the same one
- route_weights: float32 [16384, 8], P(('dp', 'ctx', 'tp')), may hold values from 0.1 to 0.4
- w_up: bfloat16 [128, 4096, 768], P(('dp', 'ctx', 'tp')), may hold values from -0.09375 to 0.09375
- w_down: bfloat16 [128, 768, 4096], P(('dp', 'ctx', 'tp')), may hold values from -0.21875 to 0.21875
Outputs:
- layer_out: bfloat16 [16384, 4096], P(('dp', 'ctx', 'tp'))
Inputs may be any that keep to these rules, and one draw needn't show every extreme that they name: `expert_ids`: in the 128 rows of one device no expert is named by more than 9 entries, a bound that some block reaches; a row names 8 different experts. `span_order`: each span appears once.
All inputs are finite; a program needn't handle non-finite values.
Results may differ from a plain program's by a relative error of at most 0.01.
Values may be sent and summed in bfloat16 or wider, within the bound.
No kernel may reach another device: no remote copies, remote signals or barrier semaphores. Data moves between devices by JAX's collectives and lax.ppermute only.
A program may use at most 256 MiB of HBM per device.

v0:
```python
import math

import jax
import jax.numpy as jnp
from jax import lax
from jax.sharding import PartitionSpec as P

HD = 128
KVH = 4


NEGATIVE = -1e30


def place_of(row_ids, span_order, span_len):
    slot_ids = row_ids // span_len
    owners = jnp.sum(
        jnp.where(
            slot_ids[:, None] == jnp.arange(span_order.shape[0], dtype=jnp.int32)[None, :],
            span_order[None, :],
            0,
        ),
        axis=1,
    )
    return owners * span_len + row_ids % span_len


def attend_piece(carry, piece, query_heads, query_places, span_order, span_len):
    key_piece, value_piece = piece
    length = key_piece.shape[0]
    key_places = place_of(jnp.arange(length, dtype=jnp.int32), span_order, span_len)
    visible = key_places[None, :] <= query_places[:, None]
    maxima, totals, sums = carry
    factor = 1.0 / math.sqrt(key_piece.shape[1])
    new_maxima = []
    new_totals = []
    new_sums = []
    for head in range(len(query_heads)):
        scores = (
            lax.dot_general(
                query_heads[head],
                key_piece,
                (((1,), (1,)), ((), ())),
                preferred_element_type=jnp.float32,
            )
            * factor
        )
        scores = jnp.where(visible, scores, NEGATIVE)
        peak = jnp.maximum(maxima[head], jnp.max(scores, axis=1))
        weights = jnp.where(visible, jnp.exp(scores - peak[:, None]), 0.0)
        fading = jnp.exp(maxima[head] - peak)
        new_totals.append(totals[head] * fading + jnp.sum(weights, axis=1))
        new_sums.append(
            sums[head] * fading[:, None]
            + jnp.dot(weights.astype(jnp.bfloat16), value_piece, preferred_element_type=jnp.float32)
        )
        new_maxima.append(peak)
    return (jnp.stack(new_maxima), jnp.stack(new_totals), jnp.stack(new_sums))


def local(
    queries,
    key_rows,
    value_rows,
    span_order,
    out_proj,
    residual,
    norm_gain,
    expert_ids,
    route_weights,
    w_up,
    w_down,
):
    rows_ctx = queries.shape[0]
    heads_dev = queries.shape[1] // HD
    span_len = rows_ctx // 2
    ctx_index = lax.axis_index("ctx")
    heads_all = heads_dev * lax.axis_size("tp")
    kv_head = lax.axis_index("tp") * heads_dev // (heads_all // KVH)
    keys_ctx, values_ctx = (
        lax.all_gather(key_rows, "tp", axis=0, tiled=True),
        lax.all_gather(value_rows, "tp", axis=0, tiled=True),
    )
    own_keys = lax.dynamic_slice_in_dim(keys_ctx, kv_head * HD, HD, 1)
    own_values = lax.dynamic_slice_in_dim(values_ctx, kv_head * HD, HD, 1)
    my_start = ctx_index * rows_ctx
    query_places = place_of(my_start + jnp.arange(rows_ctx, dtype=jnp.int32), span_order, span_len)
    query_heads = [queries[:, head * HD : (head + 1) * HD] for head in range(heads_dev)]
    initial = (
        jnp.full((heads_dev, rows_ctx), NEGATIVE, jnp.float32),
        jnp.zeros((heads_dev, rows_ctx), jnp.float32),
        jnp.zeros((heads_dev, rows_ctx, HD), jnp.float32),
    )
    carry = attend_piece(
        initial,
        (
            lax.all_gather(own_keys, "ctx", axis=0, tiled=True),
            lax.all_gather(own_values, "ctx", axis=0, tiled=True),
        ),
        query_heads,
        query_places,
        span_order,
        span_len,
    )
    maxima, totals, sums = carry
    context = (sums / totals[:, :, None]).astype(jnp.bfloat16)
    context = jnp.transpose(context, (1, 0, 2)).reshape(rows_ctx, heads_dev * HD)
    attn_proj = lax.psum_scatter(
        jnp.dot(context, out_proj, preferred_element_type=jnp.float32).astype(jnp.bfloat16),
        "tp",
        scatter_dimension=0,
        tiled=True,
    ).astype(jnp.float32)
    state = residual.astype(jnp.float32) + attn_proj
    normed = (
        state * lax.rsqrt(jnp.mean(state * state, axis=1, keepdims=True) + 1e-06) * norm_gain
    ).astype(jnp.bfloat16)
    n_devices = lax.axis_size("dp") * lax.axis_size("ctx") * lax.axis_size("tp")
    token_count, top_count = expert_ids.shape
    mean_load = token_count * top_count // n_devices
    capacity = mean_load + max(1, mean_load // 8)
    flat_ids = expert_ids.reshape(-1)
    one_hot = (flat_ids[:, None] == jnp.arange(n_devices, dtype=jnp.int32)[None, :]).astype(
        jnp.int32
    )
    slot_ids = jnp.sum(jnp.cumsum(one_hot, axis=0) * one_hot, axis=1) - 1
    targets = flat_ids * capacity + slot_ids
    sources = jnp.arange(token_count * top_count, dtype=jnp.int32) // top_count
    outgoing = (
        jnp.zeros((n_devices * capacity, normed.shape[1]), jnp.bfloat16)
        .at[targets]
        .set(normed[sources])
    )
    up_local = w_up[0]
    down_local = w_down[0]
    arrived = lax.all_to_all(
        outgoing.reshape(n_devices, capacity, outgoing.shape[1]),
        ("dp", "ctx", "tp"),
        split_axis=0,
        concat_axis=0,
        tiled=True,
    )
    flat_rows = arrived.reshape(-1, arrived.shape[-1])
    inner = jax.nn.silu(jnp.dot(flat_rows, up_local, preferred_element_type=jnp.float32)).astype(
        jnp.bfloat16
    )
    output = jnp.dot(inner, down_local, preferred_element_type=jnp.float32).astype(jnp.bfloat16)
    returned = lax.all_to_all(
        output.reshape(arrived.shape), ("dp", "ctx", "tp"), split_axis=0, concat_axis=0, tiled=True
    )
    returned = returned.reshape(n_devices * capacity, outgoing.shape[1])
    picked = returned[targets].reshape(token_count, top_count, outgoing.shape[1])
    mixture = jnp.einsum("tk,tkd->td", route_weights, picked.astype(jnp.float32))
    return (state + mixture).astype(jnp.bfloat16)


def solution(mesh):
    return jax.shard_map(
        local,
        mesh=mesh,
        in_specs=(
            P(("dp", "ctx"), "tp"),
            P(("dp", "ctx", "tp"), None),
            P(("dp", "ctx", "tp"), None),
            P(),
            P("tp", None),
            P(("dp", "ctx", "tp"), None),
            P(),
            P(("dp", "ctx", "tp"), None),
            P(("dp", "ctx", "tp"), None),
            P(("dp", "ctx", "tp"), None, None),
            P(("dp", "ctx", "tp"), None, None),
        ),
        out_specs=P(("dp", "ctx", "tp"), None),
        check_vma=False,
    )
```

profile of v0, /device:TPU:114, one launch (start us, length us, event | category | flops | bytes accessed | tf_op | source)
XLA Modules:
  0.0 950.6 jit_solution(15852638928801916286)
XLA Ops:
  6.5 0.7 all-gather.5.cloned.1.call-update
  7.3 0.0 all-gather.9.cloned.1.call-start
  7.3 0.7 all-gather.9.cloned.1.call-update
  8.0 0.0 all-gather.7.cloned.1.call-start
  8.1 46.0 %all-gather.5.cloned.1.call-done = bf16[2048,512]{1,0:T(8,128)(2,1)} async-done(((bf16[128,512]{1,0:T(8,128)(2,1)}), bf16[2048,512]{1,0:T(8,128)(2,1)}) %all-gather.5.cloned.1.call-update) | async-done | bytes 2097168 | tf_op jit(solution)/shard_map/all_gather | solution.py:81
  54.1 1.9 constant_dynamic-slice_fusion.1
  56.0 0.0 all-gather.11.cloned.1.call-start
  56.1 0.7 select_reduce_fusion.1
  56.8 0.8 select_reduce_fusion
  57.6 43.2 %all-gather.9.cloned.1.call-done = bf16[2048,512]{1,0:T(8,128)(2,1)} async-done(((bf16[128,512]{1,0:T(8,128)(2,1)}), bf16[2048,512]{1,0:T(8,128)(2,1)}) %all-gather.9.cloned.1.call-update) | async-done | bytes 2097168 | tf_op jit(solution)/shard_map/all_gather | solution.py:82
  100.8 1.9 constant_dynamic-slice_fusion
  102.7 0.0 reduce-scatter.2.cloned.1.call-start
  102.8 24.3 %all-gather.7.cloned.1.call-done = bf16[4096,128]{1,0:T(8,128)(2,1)} async-done(((bf16[2048,128]{1,0:T(8,128)(2,1)}), bf16[4096,128]{1,0:T(8,128)(2,1)}) %all-gather.7.cloned.1.call-update) | async-done | bytes 1048592 | tf_op jit(solution)/shard_map/all_gather | solution.py:97
  127.1 15.2 %fusion = (f32[2048]{0:T(1024)S(1)}, f32[4096,2048]{1,0:T(8,128)}) fusion(s32[2048]{0:T(1024)S(1)} %fusion.49, s32[4096]{0:T(1024)S(1)} %fusion.47, bf16[4096,128]{1,0:T(8,128)(2,1)} %all-gather.7.cloned.1.call-done, bf16[2048,256]{1,0:T(8,128)(2,1)} %param.11), kind=kOutput, calls=%fused_computation.7 | convolution fusion | flops 2181036032 | bytes 35160064 | tf_op jit(solution)/shard_map/dot_general | solution.py:40
  142.3 25.8 %fusion.2 = (f32[2048]{0:T(1024)S(1)}, f32[2048]{0:T(1024)S(1)}, f32[4096,2048]{1,0:T(8,128)}) fusion(f32[4096,2048]{1,0:T(8,128)} %get-tuple-element.12, f32[2048]{0:T(1024)S(1)} %broadcast_maximum_fusion.1, s32[2048]{0:T(1024)S(1)} %fusion.49, s32[4096]{0:T(1024)S(1)} %fusion.47, bf16[4096,128]{1,0:T(8,128)(2,1)S(1)} %copy-done.8, ...), kind=kOutput, calls=%fused_computation.9 | convolution fusion | flops 2222977024 | bytes 68730880 | tf_op jit(solution)/shard_map/dot_general | solution.py:40
  168.1 15.7 %fusion.4 = f32[2048]{0:T(1024)S(1)} fusion(f32[4096,2048]{1,0:T(8,128)} %get-tuple-element.13, f32[2048]{0:T(1024)S(1)} %get-tuple-element.14, s32[2048]{0:T(1024)S(1)} %fusion.49, s32[4096]{0:T(1024)S(1)} %fusion.47), kind=kLoop, calls=%fused_computation.11 | loop fusion | flops 50329600 | bytes 33595392 | tf_op jit(solution)/shard_map/reduce_sum | solution.py:52
  183.9 17.5 %fusion.28 = f32[1,2048,128]{1,2,0:T(8,128)S(1)} fusion(bf16[4096,128]{1,0:T(8,128)(2,1)} %all-gather.11.cloned.1.call-done, f32[4096,2048]{1,0:T(8,128)} %get-tuple-element.12, f32[2048]{0:T(1024)S(1)} %broadcast_maximum_fusion.1, s32[2048]{0:T(1024)S(1)} %fusion.49, s32[4096]{0:T(1024)S(1)} %fusion.47, f32[2048]{0:T(1024)S(1)} %get-tuple-element.8), kind=kOutput, calls=%fused_computation.28 | convolution fusion | flops 2198077440 | bytes 35692544 | tf_op jit(solution)/shard_map/dot_general | solution.py:55
  201.4 14.2 %fusion.25 = f32[1,2048,128]{1,2,0:T(8,128)S(1)} fusion(bf16[4096,128]{1,0:T(8,128)(2,1)S(1)} %copy-done.7, f32[4096,2048]{1,0:T(8,128)} %get-tuple-element.13, f32[2048]{0:T(1024)S(1)} %get-tuple-element.14, s32[2048]{0:T(1024)S(1)} %fusion.49, s32[4096]{0:T(1024)S(1)} %fusion.47, f32[2048]{0:T(1024)S(1)} %get-tuple-element.10), kind=kOutput, calls=%fused_computation.27 | convolution fusion | flops 2198077440 | bytes 35692544 | tf_op jit(solution)/shard_map/dot_general | solution.py:55
  215.6 0.2 fusion.31
  215.8 8.1 convolution_convert_fusion.1
  223.9 0.7 copy-done.4
  224.6 0.1 copy.18
  224.7 0.1 eq.65
  224.8 0.1 eq.61
  224.9 0.1 copy.17
  225.0 0.1 mul.103
  225.1 0.1 copy.20
  225.2 0.2 fusion.34
  225.5 0.1 copy.21
  225.6 0.4 fusion.33
  226.0 108.4 %reduce-scatter.2.cloned.1.call-done = bf16[128,4096]{1,0:T(8,128)(2,1)} async-done(((bf16[2048,4096]{1,0:T(8,128)(2,1)}), bf16[128,4096]{1,0:T(8,128)(2,1)}) %reduce-scatter.2.cloned.1.call-update) | async-done | bytes 1048592 | tf_op jit(solution)/shard_map/reduce_scatter | solution.py:108
  334.4 1.6 multiply_reduce_fusion
  336.0 1.6 multiply_convert_fusion.1
  337.7 7.7 gather_fusion
  345.4 18.4 %scatter_custom_fusion = bf16[1152,4096]{1,0:T(8,128)(2,1)} fusion(s32[1024]{0:T(1024)S(1)} %bitcast.79, bf16[1024,4096]{1,0:T(8,128)(2,1)} %gather_fusion, bf16[]{:T(256)} %constant.119.clone.1), kind=kCustom, calls=%fused_computation.22 | custom fusion | bytes 9437696 | tf_op jit(solution)/shard_map/scatter | solution.py:132
  363.9 15.1 %reshape.261 = bf16[128,9,4096]{2,1,0:T(8,128)(2,1)} reshape(bf16[1152,4096]{1,0:T(8,128)(2,1)} %scatter_custom_fusion) | data formatting | bytes 18874368 | tf_op jit(solution)/shard_map/reshape | solution.py:137
  379.0 192.6 %all_to_all.10 = bf16[128,9,4096]{2,1,0:T(8,128)(2,1)} all-to-all(bf16[128,9,4096]{2,1,0:T(8,128)(2,1)} %reshape.261), channel_id=1, replica_groups=mesh['dp'=4,'ctx'=2,'tp'=16] {'dp','ctx','tp'}, dimensions={0} | all-to-all | bytes 18874368 | tf_op jit(solution)/shard_map/all_to_all | solution.py:136
  571.6 15.8 %reshape.262 = bf16[1152,4096]{1,0:T(8,128)(2,1)} reshape(bf16[128,9,4096]{2,1,0:T(8,128)(2,1)} %all_to_all.10) | data formatting | bytes 18874368 | tf_op jit(solution)/shard_map/reshape | solution.py:143
  587.4 12.2 %multiply_convert_fusion = bf16[1152,768]{1,0:T(8,128)(2,1)S(1)} fusion(bf16[1152,4096]{1,0:T(8,128)(2,1)} %reshape.262, bf16[1,4096,768]{2,1,0:T(8,128)(2,1)} %param.20), kind=kOutput, calls=%fused_computation.24 | convolution fusion | flops 7252180992 | bytes 17498112 | tf_op jit(solution)/shard_map/dot_general | solution.py:144
  599.6 12.5 %convolution_convert_fusion = bf16[1152,4096]{1,0:T(8,128)(2,1)} fusion(bf16[1152,768]{1,0:T(8,128)(2,1)S(1)} %multiply_convert_fusion, bf16[1,768,4096]{2,1,0:T(8,128)(2,1)} %param.21), kind=kOutput, calls=%fused_computation.15 | convolution fusion | flops 7252475904 | bytes 17498112 | tf_op jit(solution)/shard_map/dot_general | solution.py:147
  612.2 15.1 %reshape.263 = bf16[128,9,4096]{2,1,0:T(8,128)(2,1)} reshape(bf16[1152,4096]{1,0:T(8,128)(2,1)} %convolution_convert_fusion) | data formatting | bytes 18874368 | tf_op jit(solution)/shard_map/reshape | solution.py:149
  627.3 17.0 %all-to-all-start.1 = ((bf16[128,9,4096]{2,1,0:T(8,128)(2,1)}), bf16[128,9,4096]{2,1,0:T(8,128)(2,1)}, u32[]{:S(2)}, u32[]{:S(2)}) async-start(bf16[128,9,4096]{2,1,0:T(8,128)(2,1)} %reshape.263), calls=%async_computation.2 | async-start | bytes 33554432 | tf_op jit(solution)/shard_map/all_to_all | solution.py:148
  644.3 0.1 copy.22
  644.5 251.8 %all-to-all-done.1 = bf16[128,9,4096]{2,1,0:T(8,128)(2,1)} async-done(((bf16[128,9,4096]{2,1,0:T(8,128)(2,1)}), bf16[128,9,4096]{2,1,0:T(8,128)(2,1)}, u32[]{:S(2)}, u32[]{:S(2)}) %all-to-all-start.1) | async-done | bytes 9437216 | tf_op jit(solution)/shard_map/all_to_all | solution.py:148
  896.3 15.8 %reshape.264 = bf16[1152,4096]{1,0:T(8,128)(2,1)} reshape(bf16[128,9,4096]{2,1,0:T(8,128)(2,1)} %all-to-all-done.1) | data formatting | bytes 18874368 | tf_op jit(solution)/shard_map/reshape | solution.py:151
  912.1 20.1 %gather_fusion.1 = bf16[1024,4096]{1,0:T(8,128)(2,1)} fusion(bf16[1152,4096]{1,0:T(8,128)(2,1)} %reshape.264, s32[1024]{0:T(1024)S(1)} %broadcast_clamp_fusion), kind=kCustom, calls=%fused_computation.1 | custom fusion | bytes 16781312 | tf_op jit(solution)/shard_map/gather | solution.py:152
  932.2 7.1 fusion.10
  939.3 4.3 fusion.32
  (41 shorter events, 0.3 us)
Async XLA Ops:
  6.5 209.3 %copy-start = (bf16[256,4096]{1,0:T(8,128)(2,1)S(1)}, bf16[256,4096]{1,0:T(8,128)(2,1)}, u32[]{:S(2)}) copy-start(bf16[256,4096]{1,0:T(8,128)(2,1)} %param.15) | copy-start | bytes 6291460
  6.5 47.6 %all-gather.5.cloned.1.call-start = ((), (), s32[]{:S(2)}) async-start(), calls=%async_computation.3 | async-start | bytes 2228224 | tf_op jit(solution)/shard_map/all_gather | solution.py:81
  7.3 93.6 %all-gather.9.cloned.1.call-start = ((), (), s32[]{:S(2)}) async-start(), calls=%async_computation.5 | async-start | bytes 2228224 | tf_op jit(solution)/shard_map/all_gather | solution.py:82
  8.0 119.1 %all-gather.7.cloned.1.call-start = ((), (), s32[]{:S(2)}) async-start(), calls=%async_computation.4 | async-start | bytes 1572864 | tf_op jit(solution)/shard_map/all_gather | solution.py:97
  56.0 127.8 %all-gather.11.cloned.1.call-start = ((), (), s32[]{:S(2)}) async-start(), calls=%async_computation.6 | async-start | bytes 1572864 | tf_op jit(solution)/shard_map/all_gather | solution.py:98
  102.7 39.6 %copy-start.6 = (bf16[2048,256]{1,0:T(8,128)(2,1)S(1)}, bf16[2048,256]{1,0:T(8,128)(2,1)}, u32[]{:S(2)}) copy-start(bf16[2048,256]{1,0:T(8,128)(2,1)} %param.11) | copy-start | bytes 3145732
  102.7 231.6 %reduce-scatter.2.cloned.1.call-start = ((), (), s32[]{:S(2)}) async-start(), calls=%async_computation.7 | async-start | bytes 17825792 | tf_op jit(solution)/shard_map/reduce_scatter | solution.py:108
  127.1 15.2 %copy-start.8 = (bf16[4096,128]{1,0:T(8,128)(2,1)S(1)}, bf16[4096,128]{1,0:T(8,128)(2,1)}, u32[]{:S(2)}) copy-start(bf16[4096,128]{1,0:T(8,128)(2,1)} %all-gather.7.cloned.1.call-done) | copy-start | bytes 3145732
  183.9 17.6 %copy-start.7 = (bf16[4096,128]{1,0:T(8,128)(2,1)S(1)}, bf16[4096,128]{1,0:T(8,128)(2,1)}, u32[]{:S(2)}) copy-start(bf16[4096,128]{1,0:T(8,128)(2,1)} %all-gather.11.cloned.1.call-done) | copy-start | bytes 3145732
  223.9 0.7 copy-start.4
  223.9 110.5 %copy-start.2 = (bf16[128,4096]{1,0:T(8,128)(2,1)S(1)}, bf16[128,4096]{1,0:T(8,128)(2,1)}, u32[]{:S(2)}) copy-start(bf16[128,4096]{1,0:T(8,128)(2,1)} %param.16) | copy-start | bytes 3145732
  223.9 112.1 %copy-start.3 = (f32[4096]{0:T(1024)S(1)}, f32[4096]{0:T(1024)}, u32[]{:S(2)}) copy-start(f32[4096]{0:T(1024)} %param.17) | copy-start | bytes 49156
  627.3 17.1 %copy-start.5 = (f32[128,8]{0,1:T(8,128)S(1)}, f32[128,8]{0,1:T(8,128)}, u32[]{:S(2)}) copy-start(f32[128,8]{0,1:T(8,128)} %param.19) | copy-start | bytes 12292
  627.3 269.0 %all-to-all-start.1 = ((bf16[128,9,4096]{2,1,0:T(8,128)(2,1)}), bf16[128,9,4096]{2,1,0:T(8,128)(2,1)}, u32[]{:S(2)}, u32[]{:S(2)}) async-start(bf16[128,9,4096]{2,1,0:T(8,128)(2,1)} %reshape.263), calls=%async_computation.2 | async-start | bytes 33554432 | tf_op jit(solution)/shard_map/all_to_all | solution.py:148
  912.1 31.5 %copy-start.1 = (bf16[256,4096]{1,0:T(8,128)(2,1)S(1)}, bf16[256,4096]{1,0:T(8,128)(2,1)}, u32[]{:S(2)}) copy-start(bf16[256,4096]{1,0:T(8,128)(2,1)} %param.15) | copy-start | bytes 6291460
Sparse Core Ops, SparseCore 0:
  9.5 44.5 all-gather.4
  56.2 44.5 all-gather.8
  102.5 24.5 all-gather.6
  128.6 24.7 all-gather.10
  224.1 110.2 reduce-scatter.1
where the time goes:
time: 961 us; the launch traced here: 951 us
  waiting for transfers between devices  475 us (49%)
  blocking collectives  193 us (20%)
  local copies, waits for them, and re-layouts  113 us (12%)
  matrix products  113 us (12%)
  other arithmetic  25.7 us (3%)
  starting transfers between devices  17.2 us (2%)
  between operations  13.9 us (1%)
    all_to_all x1, waiting for transfers between devices, local(): lax.all_to_all(output.reshape(arrived.shape), ('dp', 'ctx', 'tp'), split_...  252 us
    all_to_all x1, blocking collectives, local(): lax.all_to_all(outgoing.reshape(n_devices, capacity, outgoing.shape[1]),...  193 us
    reduce_scatter x1, waiting for transfers between devices, local(): lax.psum_scatter(jnp.dot(context, out_proj, preferred_element_type=jnp.fl...  108 us
    all_gather x1, waiting for transfers between devices, local(): lax.all_gather(key_rows, 'tp', axis=0, tiled=True)  46 us
    all_gather x1, waiting for transfers between devices, local(): lax.all_gather(value_rows, 'tp', axis=0, tiled=True)  43.2 us
    dot_general x2, matrix products, attend_piece(): lax.dot_general(query_heads[head], key_piece, (((1,), (1,)), ((), ())), p...  40.9 us
    dot_general x2, matrix products, attend_piece(): jnp.dot(weights.astype(jnp.bfloat16), value_piece, preferred_element_type...  31.7 us
    all_gather x1, waiting for transfers between devices, local(): lax.all_gather(own_keys, 'ctx', axis=0, tiled=True)  24.3 us
  transfers between devices with their start and end apart: 6, of which 5 were waited for; matrix products, arithmetic and copies ran while one was open for 7% of the time, Pallas kernels for 0%

commit v1 on v0

v1 whole, which is shorter than its diff:
```python
import functools
import math

import jax
import jax.numpy as jnp
from jax import lax
from jax.experimental import pallas as pl
from jax.experimental.pallas import tpu as pltpu
from jax.sharding import PartitionSpec as P

HD = 128
KVH = 4
SIDE = 4
TOKENS = 128
SLOTS = 8
SEG = 512
BLOCK = 512
NEGATIVE = -1e30
MIB = 1 << 20
F32 = jnp.float32
BF16 = jnp.bfloat16


def shift_x(value, step):
    return lax.ppermute(
        value,
        "tp",
        [(x * SIDE + z, (x + step) % SIDE * SIDE + z) for x in range(SIDE) for z in range(SIDE)],
    )


def shift_z(value, step):
    return lax.ppermute(
        value,
        "tp",
        [(x * SIDE + z, x * SIDE + (z + step) % SIDE) for x in range(SIDE) for z in range(SIDE)],
    )


def swap_ctx(value):
    return lax.ppermute(value, "ctx", [(0, 1), (1, 0)])


def swap_core(value):
    return lax.ppermute(value, "dp", [(0, 1), (1, 0), (2, 3), (3, 2)])


def gather_ring(shift, rows):
    half = rows.shape[0] // 2
    before, after = shift(rows, 1), shift(rows, -1)
    far_low, far_high = shift(before[:half], 1), shift(after[half:], -1)
    return jnp.concatenate([rows, before, far_low, far_high, after], axis=0)


def exchange(shift, blocks):
    return [blocks[0], shift(blocks[1], 1), shift(blocks[2], 2), shift(blocks[3], -1)]


def call(kernel, name, out_shape, in_specs, out_specs, grid=(), scratch=(), limit=32, cost=None):
    return pl.pallas_call(
        kernel,
        name=name,
        out_shape=out_shape,
        grid=grid,
        in_specs=in_specs,
        out_specs=out_specs,
        scratch_shapes=list(scratch),
        compiler_params=pltpu.CompilerParams(vmem_limit_bytes=limit * MIB),
        cost_estimate=cost,
    )


def smem():
    return pl.BlockSpec(memory_space=pltpu.SMEM)


def vmem():
    return pl.BlockSpec(memory_space=pltpu.VMEM)


def dot(left, right):
    return jnp.dot(left, right, preferred_element_type=F32)


def dot_nt(left, right):
    return lax.dot_general(left, right, (((1,), (1,)), ((), ())), preferred_element_type=F32)


def attention_kernel(meta, q_ref, *refs):
    pieces, refs = refs[:8], refs[8:]
    outs_x, outs_z, (keys, values, sums, context) = refs[:4], refs[4:8], refs[8:]
    ctx, x, z = meta[4], meta[5], meta[6]
    factor = math.log2(math.e) / math.sqrt(HD)

    for number, piece in enumerate(pieces):
        part = lax.rem(ctx + number % 2, 2)
        back = (0, 1, 3, 2)[number // 2]
        z_of = lax.rem(z + SIDE - back, SIDE)
        for block in range(SIDE):
            x_of = lax.rem(x + SIDE - block, SIDE)
            place = meta[part * 2 + x_of // 2] * 8 + lax.rem(x_of, 2) * SIDE + z_of
            rows = pl.ds(pl.multiple_of(place * HD, HD), HD)
            keys[rows, :] = piece[block, :, :HD]
            values[:, rows] = piece[block, :, HD:].T

    def step(chunk, state, heads, masked):
        rows = pl.ds(pl.multiple_of(chunk * BLOCK, BLOCK), BLOCK)
        key_block = keys[rows, :]
        value_block = values[:, rows]
        scores = [dot_nt(key_block, head) for head in heads]
        if masked:
            seen = lax.broadcasted_iota(jnp.int32, (BLOCK, BLOCK), 0) <= lax.broadcasted_iota(
                jnp.int32, (BLOCK, BLOCK), 1
            )
            scores = [jnp.where(seen, score, NEGATIVE) for score in scores]
        later = []
        for head, (peak, total) in enumerate(state):
            new_peak = jnp.maximum(peak, jnp.max(scores[head], axis=0, keepdims=True))
            weights = jnp.exp2(scores[head] * factor - new_peak * factor)
            fading = jnp.exp2((peak - new_peak) * factor)
            new_total = total * fading + jnp.sum(weights, axis=0, keepdims=True)
            sums[head] = sums[head] * fading + dot(value_block, weights.astype(BF16))
            later.append((new_peak, new_total))
        return tuple(later)

    for chunk in range(4):
        mine = meta[ctx * 2 + chunk // 2] * 2 + chunk % 2
        heads = [
            q_ref[chunk * BLOCK : (chunk + 1) * BLOCK, head * HD : (head + 1) * HD]
            for head in range(2)
        ]
        sums[...] = jnp.zeros_like(sums)
        first = (jnp.full((1, BLOCK), NEGATIVE, F32), jnp.zeros((1, BLOCK), F32))
        state = lax.fori_loop(
            0, mine, lambda i, s: step(i, s, heads, False), (first, first)
        )
        state = step(mine, state, heads, True)
        for head, (_, total) in enumerate(state):
            mixed = (sums[head] / total).T.astype(BF16)
            context[chunk * BLOCK : (chunk + 1) * BLOCK, head * HD : (head + 1) * HD] = mixed

    for step_of in range(SIDE):
        to_x = lax.rem(x + step_of, SIDE)
        to_z = lax.rem(z + step_of, SIDE)
        outs_x[step_of][...] = context[pl.ds(pl.multiple_of(to_x * BLOCK, BLOCK), BLOCK), :]
        for block in range(SIDE):
            rows = pl.ds(pl.multiple_of(block * BLOCK + to_z * TOKENS, TOKENS), TOKENS)
            outs_z[step_of][block * TOKENS : (block + 1) * TOKENS, :] = context[rows, :]


def attention(meta, queries, pieces):
    rows, width = queries.shape
    return call(
        attention_kernel,
        "attention",
        [jax.ShapeDtypeStruct((BLOCK, width), BF16)] * 8,
        [smem()] + [vmem()] * 9,
        [vmem()] * 8,
        scratch=[
            pltpu.VMEM((2 * rows, HD), BF16),
            pltpu.VMEM((HD, 2 * rows), BF16),
            pltpu.VMEM((2, HD, BLOCK), F32),
            pltpu.VMEM((rows, width), BF16),
        ],
        cost=pl.CostEstimate(
            flops=7 * 10**9, bytes_accessed=5 * 10**6, transcendentals=14 * 10**6
        ),
    )(meta, queries, *pieces)


def projection_kernel(axis, meta, *refs):
    context, weights, outs, held = refs[:4], refs[4:6], refs[6:10], refs[10]
    me = meta[axis]
    width = context[0].shape[1]
    columns = 256
    for side, weight in enumerate(weights):
        for start in range(0, weight.shape[1], columns):
            total = None
            for number, rows in enumerate(context):
                term = dot(
                    rows[...],
                    weight[number * width : (number + 1) * width, start : start + columns],
                )
                total = term if total is None else total + term
            held[:, side * weight.shape[1] + start : side * weight.shape[1] + start + columns] = (
                total.astype(BF16)
            )
    for number, out in enumerate(outs):
        to = lax.rem(me + number, SIDE)
        out[...] = held[pl.ds(pl.multiple_of(to * TOKENS, TOKENS), TOKENS), :]


def projection(axis, meta, context, weights):
    columns = 2 * weights[0].shape[1]
    return call(
        functools.partial(projection_kernel, axis),
        "projection",
        [jax.ShapeDtypeStruct((TOKENS, columns), BF16)] * 4,
        [smem()] + [vmem()] * 6,
        [vmem()] * 4,
        scratch=[pltpu.VMEM((SIDE * TOKENS, columns), BF16)],
        cost=pl.CostEstimate(
            flops=2 * 512 * 1024 * columns, bytes_accessed=7 * 10**6, transcendentals=0
        ),
    )(meta, *context, *weights)


def dispatch_kernel(meta, *refs):
    terms_z, terms_x, refs = refs[:4], refs[4:8], refs[8:]
    residual, gain, main, over, outgoing, state, normed = refs
    step = pl.program_id(0)
    half = terms_z[0].shape[1]
    quarter = half // 2
    core = meta[7]

    @pl.when(step == 0)
    def _():
        for base, terms in ((0, terms_z), (half, terms_x)):
            for side in range(2):
                place = base + quarter * lax.rem(core + side, 2)
                columns = pl.ds(pl.multiple_of(place, quarter), quarter)
                part = slice(side * quarter, (side + 1) * quarter)
                total = terms[0][:, part].astype(F32)
                for term in terms[1:]:
                    total = total + term[:, part].astype(F32)
                state[:, columns] = residual[:, columns].astype(F32) + total
        value = state[...]
        scale = lax.rsqrt(jnp.mean(value * value, axis=1, keepdims=True) + 1e-06)
        for segment in range(SLOTS):
            columns = slice(segment * SEG, (segment + 1) * SEG)
            normed[segment] = (state[:, columns] * scale * gain[:, columns]).astype(BF16)

    @pl.when(step < SLOTS)
    def _():
        outgoing[...] = dot(main[...], normed[step]).astype(BF16)

    @pl.when(step == SLOTS)
    def _():
        slot = lax.rem(lax.broadcasted_iota(jnp.int32, over.shape, 0), SLOTS)
        total = None
        for segment in range(SLOTS):
            picked = jnp.where(slot == segment, over[...], 0.0).astype(BF16)
            term = dot(picked, normed[segment])
            total = term if total is None else total + term
        outgoing[...] = total.astype(BF16)


def dispatch(meta, terms_z, terms_x, residual, gain, main, over):
    rows, width = main.shape[0], residual.shape[1]
    return call(
        dispatch_kernel,
        "dispatch",
        [
            jax.ShapeDtypeStruct((rows, width + SEG), BF16),
            jax.ShapeDtypeStruct((TOKENS, width), F32),
        ],
        [smem()] + [vmem()] * 12,
        [
            pl.BlockSpec((rows, SEG), lambda i: (0, i)),
            pl.BlockSpec((TOKENS, width), lambda i: (0, 0)),
        ],
        grid=(SLOTS + 1,),
        scratch=[pltpu.VMEM((SLOTS, TOKENS, SEG), BF16)],
        cost=pl.CostEstimate(flops=3 * 10**9, bytes_accessed=16 * 10**6, transcendentals=0),
    )(meta, *terms_z, *terms_x, residual, gain, main, over)


EXPERT_ROWS = 256


def expert_kernel(rows_ref, over_ref, up_ref, down_ref, out_ref, spread):
    step = pl.program_id(0)
    width = down_ref.shape[1]

    def act(value):
        return (value / (1.0 + jnp.exp(-value))).astype(BF16)

    @pl.when(step == 0)
    def _():
        shape = (TOKENS, TOKENS * SLOTS)
        row = lax.broadcasted_iota(jnp.int32, shape, 0)
        column = lax.broadcasted_iota(jnp.int32, shape, 1)
        total = None
        for segment in range(SLOTS):
            pick = (column == row * SLOTS + segment).astype(BF16)
            part = dot(pick, over_ref[...]).astype(BF16)
            term = dot(part, up_ref[0, segment * SEG : (segment + 1) * SEG, :])
            total = term if total is None else total + term
        inner = act(total)
        shape = (TOKENS * SLOTS, TOKENS)
        row = lax.broadcasted_iota(jnp.int32, shape, 0)
        column = lax.broadcasted_iota(jnp.int32, shape, 1)
        total = None
        for segment in range(SLOTS):
            put = (row == column * SLOTS + segment).astype(BF16)
            part = dot(inner, down_ref[0, :, segment * SEG : (segment + 1) * SEG]).astype(BF16)
            term = dot(put, part)
            total = term if total is None else total + term
        spread[...] = total.astype(BF16)

    width = down_ref.shape[2]
    inner = act(dot(rows_ref[:, :width], up_ref[0]))
    for segment in range(SLOTS):
        columns = slice(segment * SEG, (segment + 1) * SEG)
        out_ref[:, columns] = dot(inner, down_ref[0, :, columns]).astype(BF16)
    mine = pl.ds(pl.multiple_of(step * EXPERT_ROWS, EXPERT_ROWS), EXPERT_ROWS)
    out_ref[:, width:] = spread[mine, :]


def experts(arrived, up, down):
    rows, columns = arrived.shape
    inner = up.shape[2]
    return call(
        expert_kernel,
        "experts",
        jax.ShapeDtypeStruct((rows, columns), BF16),
        [
            pl.BlockSpec((EXPERT_ROWS, columns), lambda i: (i, 0)),
            pl.BlockSpec((rows, SEG), lambda i: (0, SLOTS)),
            pl.BlockSpec(up.shape, lambda i: (0, 0, 0), pipeline_mode=pl.Buffered(1)),
            pl.BlockSpec(down.shape, lambda i: (0, 0, 0), pipeline_mode=pl.Buffered(1)),
        ],
        pl.BlockSpec((EXPERT_ROWS, columns), lambda i: (i, 0)),
        grid=(rows // EXPERT_ROWS,),
        scratch=[pltpu.VMEM((rows, SEG), BF16)],
        limit=48,
        cost=pl.CostEstimate(
            flops=4 * rows * columns * inner,
            bytes_accessed=32 * 10**6,
            transcendentals=rows * inner,
        ),
    )(arrived, arrived, up, down)


def combine_kernel(main, over, rows_ref, over_ref, state, out):
    step = pl.program_id(0)
    slot = lax.rem(lax.broadcasted_iota(jnp.int32, over.shape, 1), SLOTS)
    picked = jnp.where(slot == step, over[...], 0.0).astype(BF16)
    total = dot(main[...], rows_ref[...]) + dot(picked, over_ref[...])
    out[...] = (state[...] + (total[:TOKENS] + total[TOKENS:])).astype(BF16)


def combine(main, over, returned, state):
    rows, width = returned.shape[0], state.shape[1]
    return call(
        combine_kernel,
        "combine",
        jax.ShapeDtypeStruct(state.shape, BF16),
        [
            vmem(),
            vmem(),
            pl.BlockSpec((rows, SEG), lambda i: (0, i)),
            pl.BlockSpec((rows, SEG), lambda i: (0, SLOTS)),
            pl.BlockSpec((TOKENS, SEG), lambda i: (0, i)),
        ],
        pl.BlockSpec((TOKENS, SEG), lambda i: (0, i)),
        grid=(width // SEG,),
        cost=pl.CostEstimate(flops=4 * 10**9, bytes_accessed=13 * 10**6, transcendentals=0),
    )(main, over, returned, returned, state)


def routes(expert_ids, route_weights, n_experts):
    tokens = expert_ids.shape[0]
    chosen = expert_ids.T[:, None, :] == jnp.arange(n_experts, dtype=jnp.int32)[None, :, None]
    named = jnp.sum(chosen.astype(F32), axis=0)
    weight = jnp.sum(jnp.where(chosen, route_weights.T[:, None, :], 0.0), axis=0)
    order = jnp.arange(tokens, dtype=jnp.int32)
    earlier = (order[:, None] < order[None, :]).astype(BF16)
    rank = dot(named.astype(BF16), earlier)
    rank = jnp.where(named > 0, rank, -1.0)
    slots = jnp.arange(SLOTS, dtype=jnp.int32).astype(F32)
    hit = rank[:, None, :] == slots[None, :, None]
    late = jnp.broadcast_to((rank == SLOTS)[:, None, :], hit.shape)
    high = lax.reduce_precision(weight, 8, 7)
    low = weight - high

    def rows(mask, value):
        spread = jnp.where(mask, value, 0.0)
        return spread.astype(BF16).reshape(n_experts * SLOTS, tokens)

    def both(mask):
        high_rows = rows(mask, high[:, None, :])
        low_rows = rows(mask, low[:, None, :])
        return jnp.concatenate([high_rows.T, low_rows.T], axis=0)

    return rows(hit, 1.0), rows(late, 1.0), both(hit), both(late)


def local(
    queries,
    key_rows,
    value_rows,
    span_order,
    out_proj,
    residual,
    norm_gain,
    expert_ids,
    route_weights,
    w_up,
    w_down,
):
    n_devices = lax.axis_size("dp") * lax.axis_size("ctx") * lax.axis_size("tp")
    core = lax.axis_index("dp") % 2
    ctx = lax.axis_index("ctx")
    x, z = lax.axis_index("tp") // SIDE, lax.axis_index("tp") % SIDE
    meta = jnp.concatenate([span_order, jnp.stack([ctx, x, z, core]).astype(jnp.int32)])

    def head_block(step):
        start = (x + step) % SIDE * HD
        return jnp.concatenate(
            [
                lax.dynamic_slice_in_dim(key_rows, start, HD, 1),
                lax.dynamic_slice_in_dim(value_rows, start, HD, 1),
            ],
            axis=1,
        )

    own = jnp.stack(exchange(shift_x, [head_block(step) for step in range(SIDE)]))
    other = swap_ctx(own)
    before_own, after_own = shift_z(own, 1), shift_z(own, -1)
    before_other, after_other = shift_z(other, 1), shift_z(other, -1)
    far_own = shift_z(before_own, 1)
    far_other = shift_z(after_other, -1)
    pieces = [
        own,
        other,
        before_own,
        before_other,
        after_own,
        after_other,
        far_own,
        far_other,
    ]

    width = out_proj.shape[1]
    quarter = width // 4

    def weights_of(shift, base):
        part = lax.dynamic_slice_in_dim(out_proj, base + core * quarter, quarter, 1)
        mine = gather_ring(shift, part)
        return [mine, swap_core(mine)]

    weights_x = weights_of(shift_x, 0)
    weights_z = weights_of(shift_z, width // 2)
    main, over, back_main, back_over = routes(expert_ids, route_weights, n_devices)

    parts = attention(meta, queries, pieces)
    terms_z = projection(6, meta, exchange(shift_x, parts[:4]), weights_x)
    terms_x = projection(5, meta, exchange(shift_z, parts[4:]), weights_z)
    terms_z = exchange(shift_z, terms_z)
    terms_x = exchange(shift_x, terms_x)

    outgoing, state = dispatch(
        meta, terms_z, terms_x, residual, norm_gain[None, :], main, over
    )

    def all_to_all(rows):
        blocks = rows.reshape(n_devices, SLOTS, rows.shape[1])
        return lax.all_to_all(
            blocks, ("dp", "ctx", "tp"), split_axis=0, concat_axis=0, tiled=True
        ).reshape(rows.shape)

    arrived = all_to_all(outgoing)
    returned = all_to_all(experts(arrived, w_up, w_down))
    return combine(back_main, back_over, returned, state)


def solution(mesh):
    return jax.shard_map(
        local,
        mesh=mesh,
        in_specs=(
            P(("dp", "ctx"), "tp"),
            P(("dp", "ctx", "tp"), None),
            P(("dp", "ctx", "tp"), None),
            P(),
            P("tp", None),
            P(("dp", "ctx", "tp"), None),
            P(),
            P(("dp", "ctx", "tp"), None),
            P(("dp", "ctx", "tp"), None),
            P(("dp", "ctx", "tp"), None, None),
            P(("dp", "ctx", "tp"), None, None),
        ),
        out_specs=P(("dp", "ctx", "tp"), None),
        check_vma=False,
    )
```

time: 961 us -> 473 us (0.49)
  the two profiles are of different devices: /device:TPU:114 before, /device:TPU:0 now
where the time goes in v1:
time: 473 us; the launch traced here: 466 us
  waiting for transfers between devices  168 us (36%)
  blocking collectives  118 us (25%)
  Pallas kernels  90.9 us (19%)
  starting transfers between devices  62.4 us (13%)
  local copies, waits for them, and re-layouts  24.1 us (5%)
    all_to_all x1, blocking collectives, all_to_all(): lax.all_to_all(blocks, ('dp', 'ctx', 'tp'), split_axis=0, concat_axis=0,...  118 us
    all_to_all x1, waiting for transfers between devices, all_to_all(): lax.all_to_all(blocks, ('dp', 'ctx', 'tp'), split_axis=0, concat_axis=0,...  117 us
    ppermute x16, waiting for transfers between devices, shift_z(): lax.ppermute(value, 'tp', [(x * SIDE + z, x * SIDE + (z + step) % SIDE) f...  36.7 us
    pallas_call x1, Pallas kernels, experts(): call(expert_kernel, 'experts', jax.ShapeDtypeStruct((rows, columns), BF16...  32.6 us
    ppermute x16, starting transfers between devices, shift_z(): lax.ppermute(value, 'tp', [(x * SIDE + z, x * SIDE + (z + step) % SIDE) f...  32.3 us
    pallas_call x1, Pallas kernels, attention(): call(attention_kernel, 'attention', [jax.ShapeDtypeStruct((BLOCK, width),...  28.5 us
    ppermute x13, starting transfers between devices, shift_x(): lax.ppermute(value, 'tp', [(x * SIDE + z, (x + step) % SIDE * SIDE + z) f...  21.5 us
    unnamed x49, local copies, waits for them, and re-layouts  18.1 us
  transfers between devices with their start and end apart: 33, of which 14 were waited for; matrix products, arithmetic and copies ran while one was open for 3% of the time, Pallas kernels for 8%

profile of v1, /device:TPU:0, one launch (start us, length us, event | category | flops | bytes accessed | tf_op | source)
XLA Modules:
  0.0 465.9 jit_solution(9204964567230428841)
XLA Ops:
  0.0 2.5 constant_dynamic-update-slice_fusion.9
  2.5 2.0 collective-permute-start.24
  4.5 2.1 collective-permute-start.26
  6.7 1.5 collective-permute-start.13
  8.2 1.7 collective-permute-start.15
  10.3 8.6 %collective-permute-done.24 = bf16[256,1024]{1,0:T(8,128)(2,1)} collective-permute-done((bf16[256,1024]{1,0:T(8,128)(2,1)}, bf16[256,1024]{1,0:T(8,128)(2,1)}, u32[]{:S(2)}, u32[]{:S(2)}) %collective-permute-start.24) | collective-permute-done | bytes 524320 | tf_op jit(solution)/shard_map/ppermute | solution.py:33
  20.0 3.3 collective-permute-start.27
  23.3 1.9 constant_dynamic-update-slice_fusion.8
  25.2 3.5 collective-permute-done.25
  28.6 3.0 collective-permute-start.1
  32.4 1.1 collective-permute-start.2
  35.1 1.6 collective-permute-done.2
  36.7 1.7 collective-permute-start.3
  38.4 1.0 slice.16
  40.8 2.6 collective-permute-start.16
  43.5 1.1 constant_dynamic-update-slice_fusion.3
  44.6 3.2 collective-permute-start.6
  48.7 2.4 collective-permute-done.4.refs_2_
  51.0 3.2 collective-permute-done.6.refs_4_
  54.2 2.8 collective-permute-done.7.refs_5_
  57.0 3.7 collective-permute-start.9
  61.5 2.8 collective-permute-done.8.refs_6_
  64.6 1.2 copy-done
  65.8 28.5 %attention.1 = (bf16[512,256]{1,0:T(8,128)(2,1)S(1)}, bf16[512,256]{1,0:T(8,128)(2,1)S(1)}, bf16[512,256]{1,0:T(8,128)(2,1)S(1)}, bf16[512,256]{1,0:T(8,128)(2,1...) custom-call(s32[8]{0:T(128)S(1)} %concatenate.29.meta, ...), custom_call_target="tpu_custom_call" | custom-call | flops 7000000000 | bytes 5000000 | tf_op jit(solution)/shard_map/attention/pallas_call | solution.py:153
  94.4 5.2 %collective-permute-start.22 = (bf16[512,256]{1,0:T(8,128)(2,1)S(1)}, bf16[512,256]{1,0:T(8,128)(2,1)S(1)}, u32[]{:S(2)}, u32[]{:S(2)}) collective-permute-start(bf16[512,256]{1,0:T(8,128)(2,1)S(1)} %get-tuple-element.33), channel_id=1, source_target_pairs={{0,2},{1,3},{2,0},{3,1},{4,6},{5,7},{6,4},{7,5},{8,10},{9,11},{10,... | collective-permute-start | bytes 786440 | tf_op jit(solution)/shard_map/ppermute | solution.py:33
  99.8 4.6 collective-permute-done.21.refs_1_
  104.4 2.8 collective-permute-done.22.refs_2_
  107.2 5.0 %collective-permute-start.11 = (bf16[512,256]{1,0:T(8,128)(2,1)S(1)}, bf16[512,256]{1,0:T(8,128)(2,1)S(1)}, u32[]{:S(2)}, u32[]{:S(2)}) collective-permute-start(bf16[512,256]{1,0:T(8,128)(2,1)S(1)} %get-tuple-element.25), channel_id=1, source_target_pairs={{0,8},{1,9},{2,10},{3,11},{4,12},{5,13},{6,14},{7,15},{8,0},{9,1},... | collective-permute-start | bytes 786440 | tf_op jit(solution)/shard_map/ppermute | solution.py:25
  112.3 5.8 %projection.3 = (bf16[128,2048]{1,0:T(8,128)(2,1)S(1)}, bf16[128,2048]{1,0:T(8,128)(2,1)S(1)}, bf16[128,2048]{1,0:T(8,128)(2,1)}, bf16[128,2048]{1,0:T(8,128)(2,1)}) custom-call(s32[8]{0:T(128)S(1)} %concatenate.29.meta, bf16[512,256]{1,0:T(8,128)(2,1)S(1)} %get-tuple-element.31.refs_0_, bf16[512,256]{1,0:T(8,128)(2,1)S(1)} %collective-permute-done.21.refs_1_, ...), custom_call_target="tpu_custom_call" | custom-call | flops 2147483648 | bytes 7000000 | tf_op jit(solution)/shard_map/projection/pallas_call | solution.py:195
  118.1 2.0 collective-permute-start.29
  121.1 3.2 collective-permute-start.30
  124.4 5.3 %projection.2 = (bf16[128,2048]{1,0:T(8,128)(2,1)S(1)}, bf16[128,2048]{1,0:T(8,128)(2,1)}, bf16[128,2048]{1,0:T(8,128)(2,1)}, bf16[128,2048]{1,0:T(8,128)(2,1)}) custom-call(s32[8]{0:T(128)S(1)} %concatenate.29.meta, bf16[512,256]{1,0:T(8,128)(2,1)S(1)} %get-tuple-element.23.refs_0_, bf16[512,256]{1,0:T(8,128)(2,1)S(1)} %collective-permute-done.10.refs_1_, ...), custom_call_target="tpu_custom_call" | custom-call | flops 2147483648 | bytes 7000000 | tf_op jit(solution)/shard_map/projection/pallas_call | solution.py:195
  131.5 12.6 %collective-permute-done.29.refs_5_ = bf16[128,2048]{1,0:T(8,128)(2,1)S(1)} collective-permute-done((bf16[128,2048]{1,0:T(8,128)(2,1)S(1)}, bf16[128,2048]{1,0:T(8,128)(2,1)S(1)}, u32[]{:S(2)}, u32[]{:S(2)}) %collective-permute-start.29) | collective-permute-done | bytes 524320 | tf_op jit(solution)/shard_map/ppermute | solution.py:25
  144.1 11.1 %collective-permute-start.20 = (bf16[128,2048]{1,0:T(8,128)(2,1)}, bf16[128,2048]{1,0:T(8,128)(2,1)S(1)}, u32[]{:S(2)}, u32[]{:S(2)}) collective-permute-start(bf16[128,2048]{1,0:T(8,128)(2,1)} %get-tuple-element.30), channel_id=1, source_target_pairs={{0,3},{1,0},{2,1},{3,2},{4,7},{5,4},{6,5},{7,6},{8,11},{9,8},{10,9... | collective-permute-start | bytes 1572872 | tf_op jit(solution)/shard_map/ppermute | solution.py:33
  155.1 1.2 copy.23
  158.3 5.1 %collective-permute-done.20.refs_3_ = bf16[128,2048]{1,0:T(8,128)(2,1)S(1)} collective-permute-done((bf16[128,2048]{1,0:T(8,128)(2,1)}, bf16[128,2048]{1,0:T(8,128)(2,1)S(1)}, u32[]{:S(2)}, u32[]{:S(2)}) %collective-permute-start.20) | collective-permute-done | bytes 524320 | tf_op jit(solution)/shard_map/ppermute | solution.py:33
  164.2 1.2 copy-done.1
  165.4 1.0 copy-done.3
  166.5 1.0 copy-done.5
  167.5 1.0 copy-done.7
  168.6 1.0 copy-done.10
  169.6 1.0 copy-done.12
  170.6 8.9 %dispatch.1 = (bf16[1024,4608]{1,0:T(8,128)(2,1)S(1)}, f32[128,4096]{1,0:T(8,128)S(1)}) custom-call(s32[8]{0:T(128)S(1)} %concatenate.29.meta, bf16[128,2048]{1,0:T(8,128)(2,1)S(1)} %copy-done.12, bf16[128,2048]{1,0:T(8,128)(2,1)S(1)} %collective-permute-done.18.refs_1_, bf16[128,2048]{1,0:T(8,128)(2,1)S(1)} %copy-done.5, bf16[128,2048]{1,0:T(8,128)(2,1)S(1)} %copy-done.7, ...), custom_call_target="tpu_custom_call" | custom-call | flops 3000000000 | bytes 16000000 | tf_op jit(solution)/shard_map/dispatch/pallas_call | solution.py:250
  179.5 118.2 %all_to_all.10 = bf16[128,8,4608]{2,1,0:T(8,128)(2,1)} all-to-all(bf16[128,8,4608]{2,1,0:T(8,128)(2,1)S(1)} %bitcast.34), channel_id=1, replica_groups=mesh['dp'=4,'ctx'=2,'tp'=16] {'dp','ctx','tp'}, dimensions={0} | all-to-all | bytes 18874368 | tf_op jit(solution)/shard_map/all_to_all | solution.py:459
  297.8 32.6 %experts.1 = bf16[1024,4608]{1,0:T(8,128)(2,1)} custom-call(bf16[1024,4608]{1,0:T(8,128)(2,1)} %bitcast.37, bf16[1024,4608]{1,0:T(8,128)(2,1)} %bitcast.38, bf16[1,4096,768]{2,1,0:T(8,128)(2,1)} %up_ref.1, bf16[1,768,4096]{2,1,0:T(8,128)(2,1)} %down_ref.1), custom_call_target="tpu_custom_call" | custom-call | flops 14495514624 | bytes 32000000 | tf_op jit(solution)/shard_map/experts/pallas_call | solution.py:313
  330.3 6.9 %all-to-all-start.1 = ((bf16[128,8,4608]{2,1,0:T(8,128)(2,1)}), bf16[128,8,4608]{2,1,0:T(8,128)(2,1)}, u32[]{:S(2)}, u32[]{:S(2)}) async-start(bf16[128,8,4608]{2,1,0:T(8,128)(2,1)} %bitcast.36), calls=%async_computation.1 | async-start | bytes 18874368 | tf_op jit(solution)/shard_map/all_to_all | solution.py:459
  338.5 117.3 %all-to-all-done.1 = bf16[128,8,4608]{2,1,0:T(8,128)(2,1)} async-done(((bf16[128,8,4608]{2,1,0:T(8,128)(2,1)}), bf16[128,8,4608]{2,1,0:T(8,128)(2,1)}, u32[]{:S(2)}, u32[]{:S(2)}) %all-to-all-start.1) | async-done | bytes 9437216 | tf_op jit(solution)/shard_map/all_to_all | solution.py:459
  455.8 9.9 %combine.1 = bf16[128,4096]{1,0:T(8,128)(2,1)} custom-call(bf16[256,1024]{1,0:T(8,128)(2,1)S(1)} %pad_maximum_fusion.main, bf16[256,1024]{1,0:T(8,128)(2,1)S(1)} %pad_maximum_fusion.1.over, bf16[1024,4608]{1,0:T(8,128)(2,1)} %bitcast.23.rows_ref.over_ref, bf16[1024,4608]{1,0:T(8,128)(2,1)} %bitcast.23.rows_ref.over_ref, f32[128,4096]{1,0:T(8,128)S(1)} %get-tuple-element.40.state), custom_call_target="tpu_custom_call" | custom-call | flops 4000000000 | bytes 13000000 | tf_op jit(solution)/shard_map/combine/pallas_call | solution.py:345
  (106 shorter events, 14.1 us)
Async XLA Ops:
  0.0 9.9 %copy-start.17 = (bf16[128,512]{1,0:T(8,128)(2,1)S(1)}, bf16[128,512]{1,0:T(8,128)(2,1)}, u32[]{:S(2)}) copy-start(bf16[128,512]{1,0:T(8,128)(2,1)} %param.12) | copy-start | bytes 393220
  0.0 9.9 %copy-start.16 = (bf16[128,512]{1,0:T(8,128)(2,1)S(1)}, bf16[128,512]{1,0:T(8,128)(2,1)}, u32[]{:S(2)}) copy-start(bf16[128,512]{1,0:T(8,128)(2,1)} %param.13) | copy-start | bytes 393220
  2.5 16.4 %collective-permute-start.24 = (bf16[256,1024]{1,0:T(8,128)(2,1)}, bf16[256,1024]{1,0:T(8,128)(2,1)}, u32[]{:S(2)}, u32[]{:S(2)}) collective-permute-start(bf16[256,1024]{1,0:T(8,128)(2,1)} %get-tuple-element.48), channel_id=1, source_target_pairs={{0,1},{1,2},{2,3},{3,0},{4,5},{5,6},{6,7},{7,4},{8,9},{9,10},{10,1... | collective-permute-start | bytes 1572872 | tf_op jit(solution)/shard_map/ppermute | solution.py:33
  4.5 15.4 %collective-permute-start.26 = (bf16[256,1024]{1,0:T(8,128)(2,1)}, bf16[256,1024]{1,0:T(8,128)(2,1)S(1)}, u32[]{:S(2)}, u32[]{:S(2)}) collective-permute-start(bf16[256,1024]{1,0:T(8,128)(2,1)} %get-tuple-element.48), channel_id=1, source_target_pairs={{0,3},{1,0},{2,1},{3,2},{4,7},{5,4},{6,5},{7,6},{8,11},{9,8},{10,9... | collective-permute-start | bytes 1572872 | tf_op jit(solution)/shard_map/ppermute | solution.py:33
  6.7 31.7 %collective-permute-start.13 = (bf16[256,1024]{1,0:T(8,128)(2,1)}, bf16[256,1024]{1,0:T(8,128)(2,1)}, u32[]{:S(2)}, u32[]{:S(2)}) collective-permute-start(bf16[256,1024]{1,0:T(8,128)(2,1)} %get-tuple-element.52), channel_id=1, source_target_pairs={{0,4},{1,5},{2,6},{3,7},{4,8},{5,9},{6,10},{7,11},{8,12},{9,13},{1... | collective-permute-start | bytes 1572872 | tf_op jit(solution)/shard_map/ppermute | solution.py:25
  8.2 31.8 %collective-permute-start.15 = (bf16[256,1024]{1,0:T(8,128)(2,1)}, bf16[256,1024]{1,0:T(8,128)(2,1)S(1)}, u32[]{:S(2)}, u32[]{:S(2)}) collective-permute-start(bf16[256,1024]{1,0:T(8,128)(2,1)} %get-tuple-element.52), channel_id=1, source_target_pairs={{0,12},{1,13},{2,14},{3,15},{4,0},{5,1},{6,2},{7,3},{8,4},{9,5},{1... | collective-permute-start | bytes 1572872 | tf_op jit(solution)/shard_map/ppermute | solution.py:25
  10.0 25.1 %collective-permute-start = (bf16[128,256]{1,0:T(8,128)(2,1)S(1)}, bf16[128,256]{1,0:T(8,128)(2,1)S(1)}, u32[]{:S(2)}, u32[]{:S(2)}) collective-permute-start(bf16[128,256]{1,0:T(8,128)(2,1)S(1)} %pad_maximum_fusion.3), channel_id=1, source_target_pairs={{0,4},{1,5},{2,6},{3,7},{4,8},{5,9},{6,10},{7,11},{8,12},{9,13},{1... | collective-permute-start | bytes 196616 | tf_op jit(solution)/shard_map/ppermute | solution.py:25
  19.9 8.8 %collective-permute-start.25 = (bf16[128,1024]{1,0:T(8,128)(2,1)S(1)}, bf16[128,1024]{1,0:T(8,128)(2,1)S(1)}, u32[]{:S(2)}, u32[]{:S(2)}) collective-permute-start(bf16[128,1024]{1,0:T(8,128)(2,1)S(1)} %slice.18), channel_id=1, source_target_pairs={{0,1},{1,2},{2,3},{3,0},{4,5},{5,6},{6,7},{7,4},{8,9},{9,10},{10,1... | collective-permute-start | bytes 786440 | tf_op jit(solution)/shard_map/ppermute | solution.py:33
  20.0 12.4 %collective-permute-start.27 = (bf16[128,1024]{1,0:T(8,128)(2,1)S(1)}, bf16[128,1024]{1,0:T(8,128)(2,1)S(1)}, u32[]{:S(2)}, u32[]{:S(2)}) collective-permute-start(bf16[128,1024]{1,0:T(8,128)(2,1)S(1)} %slice.19), channel_id=1, source_target_pairs={{0,3},{1,0},{2,1},{3,2},{4,7},{5,4},{6,5},{7,6},{8,11},{9,8},{10,9... | collective-permute-start | bytes 786440 | tf_op jit(solution)/shard_map/ppermute | solution.py:33
  28.6 6.5 %collective-permute-start.1 = (bf16[128,256]{1,0:T(8,128)(2,1)S(1)}, bf16[128,256]{1,0:T(8,128)(2,1)S(1)}, u32[]{:S(2)}, u32[]{:S(2)}) collective-permute-start(bf16[128,256]{1,0:T(8,128)(2,1)S(1)} %pad_maximum_fusion.4), channel_id=1, source_target_pairs={{0,8},{1,9},{2,10},{3,11},{4,12},{5,13},{6,14},{7,15},{8,0},{9,1},... | collective-permute-start | bytes 196616 | tf_op jit(solution)/shard_map/ppermute | solution.py:25
  32.4 4.3 collective-permute-start.2
  35.1 77.2 %collective-permute-start.28 = (bf16[1024,1024]{1,0:T(8,128)(2,1)}, bf16[1024,1024]{1,0:T(8,128)(2,1)}, u32[]{:S(2)}, u32[]{:S(2)}) collective-permute-start(bf16[1024,1024]{1,0:T(8,128)(2,1)} %constant_dynamic-update-slice_fusion.5.refs_4_), channel_id=1, source_target_pairs={{0,32},{32,0},{64,96},{96,64},{1,33},{33,1},{65,97},{97,65},{2,34}... | collective-permute-start | bytes 6291464 | tf_op jit(solution)/shard_map/ppermute | solution.py:45
  36.7 24.0 %copy-start.20 = (s32[4]{0:T(128)S(1)}, s32[4]{0:T(128)}, u32[]{:S(2)}) copy-start(s32[4]{0:T(128)} %param.14) | copy-start | bytes 52
  36.7 7.9 %collective-permute-start.3 = (bf16[4,128,256]{2,1,0:T(8,128)(2,1)S(1)}, bf16[4,128,256]{2,1,0:T(8,128)(2,1)S(1)}, u32[]{:S(2)}, u32[]{:S(2)}) collective-permute-start(bf16[4,128,256]{2,1,0:T(8,128)(2,1)S(1)} %pad_maximum_fusion.2.refs_0_), channel_id=1, source_target_pairs={{0,16},{16,0},{1,17},{17,1},{2,18},{18,2},{3,19},{19,3},{4,20},{20... | collective-permute-start | bytes 786440 | tf_op jit(solution)/shard_map/ppermute | solution.py:41
  39.3 8.5 %collective-permute-start.14 = (bf16[128,1024]{1,0:T(8,128)(2,1)S(1)}, bf16[128,1024]{1,0:T(8,128)(2,1)S(1)}, u32[]{:S(2)}, u32[]{:S(2)}) collective-permute-start(bf16[128,1024]{1,0:T(8,128)(2,1)S(1)} %slice.16), channel_id=1, source_target_pairs={{0,4},{1,5},{2,6},{3,7},{4,8},{5,9},{6,10},{7,11},{8,12},{9,13},{1... | collective-permute-start | bytes 786440 | tf_op jit(solution)/shard_map/ppermute | solution.py:25
  40.8 7.7 %collective-permute-start.16 = (bf16[128,1024]{1,0:T(8,128)(2,1)S(1)}, bf16[128,1024]{1,0:T(8,128)(2,1)S(1)}, u32[]{:S(2)}, u32[]{:S(2)}) collective-permute-start(bf16[128,1024]{1,0:T(8,128)(2,1)S(1)} %slice.17), channel_id=1, source_target_pairs={{0,12},{1,13},{2,14},{3,15},{4,0},{5,1},{6,2},{7,3},{8,4},{9,5},{1... | collective-permute-start | bytes 786440 | tf_op jit(solution)/shard_map/ppermute | solution.py:25
  43.4 5.1 %copy-start.14 = (bf16[256,1024]{1,0:T(8,128)(2,1)S(1)}, bf16[256,1024]{1,0:T(8,128)(2,1)}, u32[]{:S(2)}) copy-start(bf16[256,1024]{1,0:T(8,128)(2,1)} %copy-done.13) | copy-start | bytes 1572868
  43.4 7.6 %collective-permute-start.4 = (bf16[4,128,256]{2,1,0:T(8,128)(2,1)S(1)}, bf16[4,128,256]{2,1,0:T(8,128)(2,1)S(1)}, u32[]{:S(2)}, u32[]{:S(2)}) collective-permute-start(bf16[4,128,256]{2,1,0:T(8,128)(2,1)S(1)} %pad_maximum_fusion.2.refs_0_), channel_id=1, source_target_pairs={{0,1},{1,2},{2,3},{3,0},{4,5},{5,6},{6,7},{7,4},{8,9},{9,10},{10,1... | collective-permute-start | bytes 786440 | tf_op jit(solution)/shard_map/ppermute | solution.py:33
  44.6 9.6 %collective-permute-start.6 = (bf16[4,128,256]{2,1,0:T(8,128)(2,1)S(1)}, bf16[4,128,256]{2,1,0:T(8,128)(2,1)S(1)}, u32[]{:S(2)}, u32[]{:S(2)}) collective-permute-start(bf16[4,128,256]{2,1,0:T(8,128)(2,1)S(1)} %pad_maximum_fusion.2.refs_0_), channel_id=1, source_target_pairs={{0,3},{1,0},{2,1},{3,2},{4,7},{5,4},{6,5},{7,6},{8,11},{9,8},{10,9... | collective-permute-start | bytes 786440 | tf_op jit(solution)/shard_map/ppermute | solution.py:33
  47.8 9.2 %collective-permute-start.7 = (bf16[4,128,256]{2,1,0:T(8,128)(2,1)S(1)}, bf16[4,128,256]{2,1,0:T(8,128)(2,1)S(1)}, u32[]{:S(2)}, u32[]{:S(2)}) collective-permute-start(bf16[4,128,256]{2,1,0:T(8,128)(2,1)S(1)} %collective-permute-done.3.refs_1_), channel_id=1, source_target_pairs={{0,3},{1,0},{2,1},{3,2},{4,7},{5,4},{6,5},{7,6},{8,11},{9,8},{10,9... | collective-permute-start | bytes 786440 | tf_op jit(solution)/shard_map/ppermute | solution.py:33
  48.6 75.8 %collective-permute-start.17 = (bf16[1024,1024]{1,0:T(8,128)(2,1)S(1)}, bf16[1024,1024]{1,0:T(8,128)(2,1)}, u32[]{:S(2)}, u32[]{:S(2)}) collective-permute-start(bf16[1024,1024]{1,0:T(8,128)(2,1)S(1)} %constant_dynamic-update-slice_fusion.refs_4_), channel_id=1, source_target_pairs={{0,32},{32,0},{64,96},{96,64},{1,33},{33,1},{65,97},{97,65},{2,34}... | collective-permute-start | bytes 6291464 | tf_op jit(solution)/shard_map/ppermute | solution.py:45
  51.0 10.5 %collective-permute-start.5 = (bf16[4,128,256]{2,1,0:T(8,128)(2,1)S(1)}, bf16[4,128,256]{2,1,0:T(8,128)(2,1)}, u32[]{:S(2)}, u32[]{:S(2)}) collective-permute-start(bf16[4,128,256]{2,1,0:T(8,128)(2,1)S(1)} %collective-permute-done.3.refs_1_), channel_id=1, source_target_pairs={{0,1},{1,2},{2,3},{3,0},{4,5},{5,6},{6,7},{7,4},{8,9},{9,10},{10,1... | collective-permute-start | bytes 786440 | tf_op jit(solution)/shard_map/ppermute | solution.py:33
  54.2 10.1 %collective-permute-start.8 = (bf16[4,128,256]{2,1,0:T(8,128)(2,1)S(1)}, bf16[4,128,256]{2,1,0:T(8,128)(2,1)}, u32[]{:S(2)}, u32[]{:S(2)}) collective-permute-start(bf16[4,128,256]{2,1,0:T(8,128)(2,1)S(1)} %collective-permute-done.4.refs_2_), channel_id=1, source_target_pairs={{0,1},{1,2},{2,3},{3,0},{4,5},{5,6},{6,7},{7,4},{8,9},{9,10},{10,1... | collective-permute-start | bytes 786440 | tf_op jit(solution)/shard_map/ppermute | solution.py:33
  57.0 7.6 %collective-permute-start.9 = (bf16[4,128,256]{2,1,0:T(8,128)(2,1)S(1)}, bf16[4,128,256]{2,1,0:T(8,128)(2,1)}, u32[]{:S(2)}, u32[]{:S(2)}) collective-permute-start(bf16[4,128,256]{2,1,0:T(8,128)(2,1)S(1)} %collective-permute-done.7.refs_5_), channel_id=1, source_target_pairs={{0,3},{1,0},{2,1},{3,2},{4,7},{5,4},{6,5},{7,6},{8,11},{9,8},{10,9... | collective-permute-start | bytes 786440 | tf_op jit(solution)/shard_map/ppermute | solution.py:33
  60.7 39.0 %copy-start.18 = (f32[128,8]{0,1:T(8,128)S(1)}, f32[128,8]{0,1:T(8,128)}, u32[]{:S(2)}) copy-start(f32[128,8]{0,1:T(8,128)} %param.19) | copy-start | bytes 12292
  64.6 1.2 copy-start
  65.8 33.8 %copy-start.19 = (s32[128,8]{0,1:T(8,128)S(1)}, s32[128,8]{0,1:T(8,128)}, u32[]{:S(2)}) copy-start(s32[128,8]{0,1:T(8,128)} %param.18) | copy-start | bytes 12292
  94.3 10.1 %collective-permute-start.21 = (bf16[512,256]{1,0:T(8,128)(2,1)S(1)}, bf16[512,256]{1,0:T(8,128)(2,1)S(1)}, u32[]{:S(2)}, u32[]{:S(2)}) collective-permute-start(bf16[512,256]{1,0:T(8,128)(2,1)S(1)} %get-tuple-element.32), channel_id=1, source_target_pairs={{0,1},{1,2},{2,3},{3,0},{4,5},{5,6},{6,7},{7,4},{8,9},{9,10},{10,1... | collective-permute-start | bytes 786440 | tf_op jit(solution)/shard_map/ppermute | solution.py:33
  94.4 12.8 %collective-permute-start.22 = (bf16[512,256]{1,0:T(8,128)(2,1)S(1)}, bf16[512,256]{1,0:T(8,128)(2,1)S(1)}, u32[]{:S(2)}, u32[]{:S(2)}) collective-permute-start(bf16[512,256]{1,0:T(8,128)(2,1)S(1)} %get-tuple-element.33), channel_id=1, source_target_pairs={{0,2},{1,3},{2,0},{3,1},{4,6},{5,7},{6,4},{7,5},{8,10},{9,11},{10,... | collective-permute-start | bytes 786440 | tf_op jit(solution)/shard_map/ppermute | solution.py:33
  99.7 12.6 %collective-permute-start.23 = (bf16[512,256]{1,0:T(8,128)(2,1)S(1)}, bf16[512,256]{1,0:T(8,128)(2,1)S(1)}, u32[]{:S(2)}, u32[]{:S(2)}) collective-permute-start(bf16[512,256]{1,0:T(8,128)(2,1)S(1)} %get-tuple-element.34), channel_id=1, source_target_pairs={{0,3},{1,0},{2,1},{3,2},{4,7},{5,4},{6,5},{7,6},{8,11},{9,8},{10,9... | collective-permute-start | bytes 786440 | tf_op jit(solution)/shard_map/ppermute | solution.py:33
  104.4 16.6 %collective-permute-start.10 = (bf16[512,256]{1,0:T(8,128)(2,1)S(1)}, bf16[512,256]{1,0:T(8,128)(2,1)S(1)}, u32[]{:S(2)}, u32[]{:S(2)}) collective-permute-start(bf16[512,256]{1,0:T(8,128)(2,1)S(1)} %get-tuple-element.24), channel_id=1, source_target_pairs={{0,4},{1,5},{2,6},{3,7},{4,8},{5,9},{6,10},{7,11},{8,12},{9,13},{1... | collective-permute-start | bytes 786440 | tf_op jit(solution)/shard_map/ppermute | solution.py:25
  107.2 17.0 %collective-permute-start.11 = (bf16[512,256]{1,0:T(8,128)(2,1)S(1)}, bf16[512,256]{1,0:T(8,128)(2,1)S(1)}, u32[]{:S(2)}, u32[]{:S(2)}) collective-permute-start(bf16[512,256]{1,0:T(8,128)(2,1)S(1)} %get-tuple-element.25), channel_id=1, source_target_pairs={{0,8},{1,9},{2,10},{3,11},{4,12},{5,13},{6,14},{7,15},{8,0},{9,1},... | collective-permute-start | bytes 786440 | tf_op jit(solution)/shard_map/ppermute | solution.py:25
  112.3 12.2 %collective-permute-start.12 = (bf16[512,256]{1,0:T(8,128)(2,1)S(1)}, bf16[512,256]{1,0:T(8,128)(2,1)S(1)}, u32[]{:S(2)}, u32[]{:S(2)}) collective-permute-start(bf16[512,256]{1,0:T(8,128)(2,1)S(1)} %get-tuple-element.26), channel_id=1, source_target_pairs={{0,12},{1,13},{2,14},{3,15},{4,0},{5,1},{6,2},{7,3},{8,4},{9,5},{1... | collective-permute-start | bytes 786440 | tf_op jit(solution)/shard_map/ppermute | solution.py:25
  118.1 6.4 %copy-start.9 = (bf16[128,2048]{1,0:T(8,128)(2,1)}, bf16[128,2048]{1,0:T(8,128)(2,1)S(1)}, u32[]{:S(2)}) copy-start(bf16[128,2048]{1,0:T(8,128)(2,1)S(1)} %get-tuple-element.35.refs_4_) | copy-start | bytes 1572868
  118.1 26.0 %collective-permute-start.29 = (bf16[128,2048]{1,0:T(8,128)(2,1)S(1)}, bf16[128,2048]{1,0:T(8,128)(2,1)S(1)}, u32[]{:S(2)}, u32[]{:S(2)}) collective-permute-start(bf16[128,2048]{1,0:T(8,128)(2,1)S(1)} %get-tuple-element.36), channel_id=1, source_target_pairs={{0,4},{1,5},{2,6},{3,7},{4,8},{5,9},{6,10},{7,11},{8,12},{9,13},{1... | collective-permute-start | bytes 1572872 | tf_op jit(solution)/shard_map/ppermute | solution.py:25
  121.1 36.4 %collective-permute-start.30 = (bf16[128,2048]{1,0:T(8,128)(2,1)}, bf16[128,2048]{1,0:T(8,128)(2,1)}, u32[]{:S(2)}, u32[]{:S(2)}) collective-permute-start(bf16[128,2048]{1,0:T(8,128)(2,1)} %get-tuple-element.37), channel_id=1, source_target_pairs={{0,8},{1,9},{2,10},{3,11},{4,12},{5,13},{6,14},{7,15},{8,0},{9,1},... | collective-permute-start | bytes 1572872 | tf_op jit(solution)/shard_map/ppermute | solution.py:25
  124.3 33.2 %collective-permute-start.31 = (bf16[128,2048]{1,0:T(8,128)(2,1)}, bf16[128,2048]{1,0:T(8,128)(2,1)}, u32[]{:S(2)}, u32[]{:S(2)}) collective-permute-start(bf16[128,2048]{1,0:T(8,128)(2,1)} %get-tuple-element.38), channel_id=1, source_target_pairs={{0,12},{1,13},{2,14},{3,15},{4,0},{5,1},{6,2},{7,3},{8,4},{9,5},{1... | collective-permute-start | bytes 1572872 | tf_op jit(solution)/shard_map/ppermute | solution.py:25
  130.6 33.6 %copy-start.8 = (f32[4096]{0:T(1024)S(1)}, f32[4096]{0:T(1024)}, u32[]{:S(2)}) copy-start(f32[4096]{0:T(1024)} %param.17) | copy-start | bytes 49156
  130.6 26.9 %collective-permute-start.18 = (bf16[128,2048]{1,0:T(8,128)(2,1)}, bf16[128,2048]{1,0:T(8,128)(2,1)S(1)}, u32[]{:S(2)}, u32[]{:S(2)}) collective-permute-start(bf16[128,2048]{1,0:T(8,128)(2,1)} %get-tuple-element.28), channel_id=1, source_target_pairs={{0,1},{1,2},{2,3},{3,0},{4,5},{5,6},{6,7},{7,4},{8,9},{9,10},{10,1... | collective-permute-start | bytes 1572872 | tf_op jit(solution)/shard_map/ppermute | solution.py:33
  130.6 26.9 %collective-permute-start.19 = (bf16[128,2048]{1,0:T(8,128)(2,1)}, bf16[128,2048]{1,0:T(8,128)(2,1)S(1)}, u32[]{:S(2)}, u32[]{:S(2)}) collective-permute-start(bf16[128,2048]{1,0:T(8,128)(2,1)} %get-tuple-element.29), channel_id=1, source_target_pairs={{0,2},{1,3},{2,0},{3,1},{4,6},{5,7},{6,4},{7,5},{8,10},{9,11},{10,... | collective-permute-start | bytes 1572872 | tf_op jit(solution)/shard_map/ppermute | solution.py:33
  144.1 20.1 %copy-start.2 = (bf16[128,2048]{1,0:T(8,128)(2,1)}, bf16[128,2048]{1,0:T(8,128)(2,1)S(1)}, u32[]{:S(2)}) copy-start(bf16[128,2048]{1,0:T(8,128)(2,1)S(1)} %collective-permute-done.29.refs_5_) | copy-start | bytes 1572868
  144.1 19.3 %collective-permute-start.20 = (bf16[128,2048]{1,0:T(8,128)(2,1)}, bf16[128,2048]{1,0:T(8,128)(2,1)S(1)}, u32[]{:S(2)}, u32[]{:S(2)}) collective-permute-start(bf16[128,2048]{1,0:T(8,128)(2,1)} %get-tuple-element.30), channel_id=1, source_target_pairs={{0,3},{1,0},{2,1},{3,2},{4,7},{5,4},{6,5},{7,6},{8,11},{9,8},{10,9... | collective-permute-start | bytes 1572872 | tf_op jit(solution)/shard_map/ppermute | solution.py:33
  164.2 1.2 copy-start.1
  165.4 1.0 copy-start.3
  166.5 1.0 copy-start.5
  167.5 1.0 copy-start.7
  168.6 1.0 copy-start.10
  330.3 125.4 %all-to-all-start.1 = ((bf16[128,8,4608]{2,1,0:T(8,128)(2,1)}), bf16[128,8,4608]{2,1,0:T(8,128)(2,1)}, u32[]{:S(2)}, u32[]{:S(2)}) async-start(bf16[128,8,4608]{2,1,0:T(8,128)(2,1)} %bitcast.36), calls=%async_computation.1 | async-start | bytes 18874368 | tf_op jit(solution)/shard_map/all_to_all | solution.py:459
  (6 other events, 5.2 us)

commit v2 on v1

v2 whole, which is shorter than its diff:
```python
import functools
import math

import jax
import jax.numpy as jnp
from jax import lax
from jax.experimental import pallas as pl
from jax.experimental.pallas import tpu as pltpu
from jax.sharding import PartitionSpec as P

HD = 128
KVH = 4
SIDE = 4
TOKENS = 128
SLOTS = 8
SEG = 512
ROWS = 256
BLOCK = 512
NEGATIVE = -1e30
MIB = 1 << 20
F32 = jnp.float32
BF16 = jnp.bfloat16


def shift_x(value, step):
    return lax.ppermute(
        value,
        "tp",
        [(x * SIDE + z, (x + step) % SIDE * SIDE + z) for x in range(SIDE) for z in range(SIDE)],
    )


def shift_z(value, step):
    return lax.ppermute(
        value,
        "tp",
        [(x * SIDE + z, x * SIDE + (z + step) % SIDE) for x in range(SIDE) for z in range(SIDE)],
    )


def swap_ctx(value):
    return lax.ppermute(value, "ctx", [(0, 1), (1, 0)])


def swap_core(value):
    return lax.ppermute(value, "dp", [(0, 1), (1, 0), (2, 3), (3, 2)])


GROUPS_X = [[x * SIDE + z for x in range(SIDE)] for z in range(SIDE)]
GROUPS_Z = [[x * SIDE + z for z in range(SIDE)] for x in range(SIDE)]


def exchange(shift, blocks):
    return [blocks[0], shift(blocks[1], 1), shift(blocks[2], 2), shift(blocks[3], -1)]


def call(kernel, name, out_shape, in_specs, out_specs, grid=(), scratch=(), limit=56, cost=None):
    return pl.pallas_call(
        kernel,
        name=name,
        out_shape=out_shape,
        grid=grid,
        in_specs=in_specs,
        out_specs=out_specs,
        scratch_shapes=list(scratch),
        compiler_params=pltpu.CompilerParams(vmem_limit_bytes=limit * MIB),
        cost_estimate=cost,
    )


def smem():
    return pl.BlockSpec(memory_space=pltpu.SMEM)


def vmem():
    return pl.BlockSpec(memory_space=pltpu.VMEM)


def whole(array):
    zeros = (0,) * array.ndim
    return pl.BlockSpec(array.shape, lambda *_: zeros, pipeline_mode=pl.Buffered(1))


def dot(left, right):
    return jnp.dot(left, right, preferred_element_type=F32)


def dot_nt(left, right):
    return lax.dot_general(left, right, (((1,), (1,)), ((), ())), preferred_element_type=F32)


def attention_kernel(meta, q_ref, *refs):
    pieces, refs = refs[:8], refs[8:]
    outs_x, outs_z, refs = refs[:4], refs[4:8], refs[8:]
    keys, values, sums, peaks, totals, context = refs[:6]
    even, odd = refs[6:8], refs[8:10]
    ctx, x, z = meta[4], meta[5], meta[6]
    factor = math.log2(math.e) / math.sqrt(HD)

    for number, piece in enumerate(pieces):
        part = lax.rem(ctx + number % 2, 2)
        back = (0, 1, 3, 2)[number // 2]
        z_of = lax.rem(z + SIDE - back, SIDE)
        for block in range(SIDE):
            x_of = lax.rem(x + SIDE - block, SIDE)
            place = meta[part * 2 + x_of // 2] * 8 + lax.rem(x_of, 2) * SIDE + z_of
            rows = pl.ds(pl.multiple_of(place * HD, HD), HD)
            keys[rows, :] = piece[block, :, :HD]
            values[:, rows] = piece[block, :, HD:].T

    def rows_of(chunk):
        return pl.ds(pl.multiple_of(chunk * BLOCK, BLOCK), BLOCK)

    @pl.loop(0, SIDE)
    def _(chunk):
        mine = meta[ctx * 2 + chunk // 2] * 2 + lax.rem(chunk, 2)
        heads = [q_ref[rows_of(chunk), head * HD : (head + 1) * HD] for head in range(2)]
        for head in range(2):
            sums[head] = jnp.zeros((HD, BLOCK), F32)
            peaks[head] = jnp.full((1, BLOCK), NEGATIVE, F32)
            totals[head] = jnp.zeros((1, BLOCK), F32)

        def score(number, held):
            key_block = keys[rows_of(number), :]
            for head in range(2):
                held[head][...] = dot_nt(key_block, heads[head])

        def process(number, held, masked):
            value_block = values[:, rows_of(number)]
            for head in range(2):
                scores = held[head][...]
                if masked:
                    seen = lax.broadcasted_iota(
                        jnp.int32, (BLOCK, BLOCK), 0
                    ) <= lax.broadcasted_iota(jnp.int32, (BLOCK, BLOCK), 1)
                    scores = jnp.where(seen, scores, NEGATIVE)
                peak = peaks[head]
                new_peak = jnp.maximum(peak, jnp.max(scores, axis=0, keepdims=True))
                weights = jnp.exp2(scores * factor - new_peak * factor)
                fading = jnp.exp2((peak - new_peak) * factor)
                peaks[head] = new_peak
                totals[head] = totals[head] * fading + jnp.sum(weights, axis=0, keepdims=True)
                sums[head] = sums[head] * fading + dot(value_block, weights.astype(BF16))

        score(0, even)

        def two(pair, carry):
            score(2 * pair + 1, odd)
            process(2 * pair, even, False)
            score(2 * pair + 2, even)
            process(2 * pair + 1, odd, False)
            return carry

        lax.fori_loop(0, mine // 2, two, 0)

        @pl.when(lax.rem(mine, 2) == 1)
        def _():
            score(mine, odd)
            process(mine - 1, even, False)
            process(mine, odd, True)

        @pl.when(lax.rem(mine, 2) == 0)
        def _():
            process(mine, even, True)

        for head in range(2):
            context[rows_of(chunk), head * HD : (head + 1) * HD] = (
                (sums[head] / totals[head]).T.astype(BF16)
            )

    for step_of in range(SIDE):
        to_x = lax.rem(x + step_of, SIDE)
        to_z = lax.rem(z + step_of, SIDE)
        outs_x[step_of][...] = context[pl.ds(pl.multiple_of(to_x * BLOCK, BLOCK), BLOCK), :]
        for block in range(SIDE):
            rows = pl.ds(pl.multiple_of(block * BLOCK + to_z * TOKENS, TOKENS), TOKENS)
            outs_z[step_of][block * TOKENS : (block + 1) * TOKENS, :] = context[rows, :]


def attention(meta, queries, pieces):
    rows, width = queries.shape
    return call(
        attention_kernel,
        "attention",
        [jax.ShapeDtypeStruct((BLOCK, width), BF16)] * 8,
        [smem(), whole(queries)] + [whole(piece) for piece in pieces],
        [pl.BlockSpec((BLOCK, width), lambda: (0, 0))] * 8,
        scratch=[
            pltpu.VMEM((2 * rows, HD), BF16),
            pltpu.VMEM((HD, 2 * rows), BF16),
            pltpu.VMEM((2, HD, BLOCK), F32),
            pltpu.VMEM((2, 1, BLOCK), F32),
            pltpu.VMEM((2, 1, BLOCK), F32),
            pltpu.VMEM((rows, width), BF16),
        ]
        + [pltpu.VMEM((BLOCK, BLOCK), F32)] * 4,
        cost=pl.CostEstimate(
            flops=7 * 10**9, bytes_accessed=5 * 10**6, transcendentals=14 * 10**6
        ),
    )(meta, queries, *pieces)


def projection_kernel(axis_in, axis_out, meta, *refs):
    context, weights, outs, held = refs[:4], refs[4:6], refs[6:10], refs[10]
    me_in, me = meta[axis_in], meta[axis_out]
    width = context[0].shape[1]
    columns = 256
    for side, weight in enumerate(weights):
        for start in range(0, weight.shape[1], columns):
            total = None
            for number, rows in enumerate(context):
                source = lax.rem(me_in + SIDE - number, SIDE)
                part = pl.ds(pl.multiple_of(source * width, width), width)
                term = dot(rows[...], weight[part, start : start + columns])
                total = term if total is None else total + term
            held[:, side * weight.shape[1] + start : side * weight.shape[1] + start + columns] = (
                total.astype(BF16)
            )
    for number, out in enumerate(outs):
        to = lax.rem(me + number, SIDE)
        out[...] = held[pl.ds(pl.multiple_of(to * TOKENS, TOKENS), TOKENS), :]


def projection(axis_in, axis_out, meta, context, weights):
    columns = 2 * weights[0].shape[1]
    return call(
        functools.partial(projection_kernel, axis_in, axis_out),
        "projection",
        [jax.ShapeDtypeStruct((TOKENS, columns), BF16)] * 4,
        [smem()] + [whole(array) for array in (*context, *weights)],
        [pl.BlockSpec((TOKENS, columns), lambda: (0, 0))] * 4,
        scratch=[pltpu.VMEM((SIDE * TOKENS, columns), BF16)],
        cost=pl.CostEstimate(
            flops=2 * 512 * 1024 * columns, bytes_accessed=7 * 10**6, transcendentals=0
        ),
    )(meta, *context, *weights)


def wide_scratch():
    return pltpu.VMEM((SEG // HD, TOKENS * SLOTS, HD), F32)


def widen(wide, rows_ref):
    for part in range(SEG // HD):
        wide[part] = rows_ref[:, part * HD : (part + 1) * HD].astype(F32)


def narrow(wide):
    return jnp.concatenate([wide[part].astype(BF16) for part in range(SEG // HD)], axis=1)


def gather_rows(wide, segment):
    rows = pl.ds(segment, TOKENS, stride=SLOTS)
    return jnp.concatenate([wide[part, rows, :] for part in range(SEG // HD)], axis=1).astype(BF16)


def scatter_rows(wide, segment, value):
    rows = pl.ds(segment, TOKENS, stride=SLOTS)
    for part in range(SEG // HD):
        wide[part, rows, :] = value[:, part * HD : (part + 1) * HD]


def dispatch_kernel(meta, *refs):
    terms_z, terms_x, refs = refs[:4], refs[4:8], refs[8:]
    residual, gain, main, late, outgoing, state, normed, wide, spread = refs
    step = pl.program_id(0)
    half = terms_z[0].shape[1]
    quarter = half // 2
    core = meta[7]

    @pl.when(step == 0)
    def _():
        for base, terms in ((0, terms_z), (half, terms_x)):
            for side in range(2):
                place = base + quarter * lax.rem(core + side, 2)
                columns = pl.ds(pl.multiple_of(place, quarter), quarter)
                part = slice(side * quarter, (side + 1) * quarter)
                total = terms[0][:, part].astype(F32)
                for term in terms[1:]:
                    total = total + term[:, part].astype(F32)
                state[:, columns] = residual[:, columns].astype(F32) + total
        value = state[...]
        scale = lax.rsqrt(jnp.mean(value * value, axis=1, keepdims=True) + 1e-06)
        for segment in range(SLOTS):
            columns = slice(segment * SEG, (segment + 1) * SEG)
            normed[segment] = (state[:, columns] * scale * gain[:, columns]).astype(BF16)

        for segment in range(SLOTS):
            scatter_rows(wide, segment, dot(late[...], normed[segment]))
        spread[...] = narrow(wide)

    for segment in range(SLOTS):
        columns = slice(segment * SEG, (segment + 1) * SEG)
        outgoing[:, columns] = dot(main[...], normed[segment]).astype(BF16)
    rows = outgoing.shape[0]
    outgoing[:, 2 * half :] = spread[pl.ds(pl.multiple_of(step * rows, rows), rows), :]


def dispatch(meta, terms_z, terms_x, residual, gain, main, late):
    rows, width = main.shape[0], residual.shape[1]
    arrays = (*terms_z, *terms_x, residual, gain)
    return call(
        dispatch_kernel,
        "dispatch",
        [
            jax.ShapeDtypeStruct((rows, width + SEG), BF16),
            jax.ShapeDtypeStruct((TOKENS, width), F32),
        ],
        [smem()]
        + [whole(a) for a in arrays]
        + [pl.BlockSpec((ROWS, TOKENS), lambda i: (i, 0)), whole(late)],
        [
            pl.BlockSpec((ROWS, width + SEG), lambda i: (i, 0)),
            pl.BlockSpec((TOKENS, width), lambda i: (0, 0)),
        ],
        grid=(rows // ROWS,),
        scratch=[
            pltpu.VMEM((SLOTS, TOKENS, SEG), BF16),
            wide_scratch(),
            pltpu.VMEM((rows, SEG), BF16),
        ],
        cost=pl.CostEstimate(flops=3 * 10**9, bytes_accessed=16 * 10**6, transcendentals=0),
    )(meta, *arrays, main, late)


def expert_kernel(rows_ref, over_ref, up_ref, down_ref, out_ref, wide, spread):
    step = pl.program_id(0)
    width = down_ref.shape[2]

    def act(value):
        return (value / (1.0 + jnp.exp(-value))).astype(BF16)

    @pl.when(step == 0)
    def _():
        widen(wide, over_ref)
        total = None
        for segment in range(SLOTS):
            part = up_ref[0, segment * SEG : (segment + 1) * SEG, :]
            term = dot(gather_rows(wide, segment), part)
            total = term if total is None else total + term
        inner = act(total)
        for segment in range(SLOTS):
            part = down_ref[0, :, segment * SEG : (segment + 1) * SEG]
            scatter_rows(wide, segment, dot(inner, part))
        spread[...] = narrow(wide)

    inner = act(dot(rows_ref[:, :width], up_ref[0]))
    for segment in range(SLOTS):
        columns = slice(segment * SEG, (segment + 1) * SEG)
        out_ref[:, columns] = dot(inner, down_ref[0, :, columns]).astype(BF16)
    mine = pl.ds(pl.multiple_of(step * ROWS, ROWS), ROWS)
    out_ref[:, width:] = spread[mine, :]


def experts(arrived, up, down):
    rows, columns = arrived.shape
    inner = up.shape[2]
    return call(
        expert_kernel,
        "experts",
        jax.ShapeDtypeStruct((rows, columns), BF16),
        [
            pl.BlockSpec((ROWS, columns), lambda i: (i, 0)),
            pl.BlockSpec((rows, SEG), lambda i: (0, SLOTS)),
            vmem(),
            vmem(),
        ],
        pl.BlockSpec((ROWS, columns), lambda i: (i, 0)),
        grid=(rows // ROWS,),
        scratch=[wide_scratch(), pltpu.VMEM((rows, SEG), BF16)],
        limit=40,
        cost=pl.CostEstimate(
            flops=4 * rows * columns * inner,
            bytes_accessed=32 * 10**6,
            transcendentals=rows * inner,
        ),
    )(arrived, arrived, up, down)


def combine_kernel(main, late, rows_ref, over_ref, state, out, total, wide):
    step = pl.program_id(0)
    segments = [(i, slice(i * SEG, (i + 1) * SEG)) for i in range(SLOTS)]

    def both(value):
        return value[:TOKENS] + value[TOKENS:]

    @pl.when(step == 0)
    def _():
        widen(wide, over_ref)
        for segment, columns in segments:
            late_part = both(dot(late[...], gather_rows(wide, segment)))
            total[:, columns] = state[:, columns] + late_part

    for segment, columns in segments:
        total[:, columns] += both(dot(main[...], rows_ref[:, columns]))

    @pl.when(step == pl.num_programs(0) - 1)
    def _():
        out[...] = total[...].astype(BF16)


def combine(main, late, returned, state):
    rows, columns = returned.shape
    return call(
        combine_kernel,
        "combine",
        jax.ShapeDtypeStruct(state.shape, BF16),
        [
            pl.BlockSpec((2 * TOKENS, ROWS), lambda i: (0, i)),
            whole(late),
            pl.BlockSpec((ROWS, columns), lambda i: (i, 0)),
            pl.BlockSpec((rows, SEG), lambda i: (0, SLOTS), pipeline_mode=pl.Buffered(1)),
            whole(state),
        ],
        pl.BlockSpec(state.shape, lambda i: (0, 0)),
        grid=(rows // ROWS,),
        scratch=[pltpu.VMEM(state.shape, F32), wide_scratch()],
        cost=pl.CostEstimate(flops=4 * 10**9, bytes_accessed=13 * 10**6, transcendentals=0),
    )(main, late, returned, returned, state)


def routes(expert_ids, route_weights, n_experts):
    tokens = expert_ids.shape[0]
    chosen = expert_ids.T[:, None, :] == jnp.arange(n_experts, dtype=jnp.int32)[None, :, None]
    named = jnp.sum(chosen.astype(F32), axis=0)
    weight = jnp.sum(jnp.where(chosen, route_weights.T[:, None, :], 0.0), axis=0)
    order = jnp.arange(tokens, dtype=jnp.int32)
    earlier = (order[:, None] < order[None, :]).astype(BF16)
    rank = dot(named.astype(BF16), earlier)
    rank = jnp.where(named > 0, rank, -1.0)
    slots = jnp.arange(SLOTS, dtype=jnp.int32).astype(F32)
    hit = rank[:, None, :] == slots[None, :, None]
    late = rank == SLOTS
    high = lax.reduce_precision(weight, 8, 7)
    low = weight - high

    def rows(value):
        spread = jnp.where(hit, value, 0.0)
        return spread.astype(BF16).reshape(n_experts * SLOTS, tokens)

    back_main = jnp.concatenate([rows(high[:, None, :]).T, rows(low[:, None, :]).T], axis=0)
    back_late = jnp.concatenate(
        [jnp.where(late, value, 0.0).astype(BF16).T for value in (high, low)], axis=0
    )
    return rows(1.0), late.astype(BF16), back_main, back_late


def local(
    queries,
    key_rows,
    value_rows,
    span_order,
    out_proj,
    residual,
    norm_gain,
    expert_ids,
    route_weights,
    w_up,
    w_down,
):
    n_devices = lax.axis_size("dp") * lax.axis_size("ctx") * lax.axis_size("tp")
    core = lax.axis_index("dp") % 2
    ctx = lax.axis_index("ctx")
    x, z = lax.axis_index("tp") // SIDE, lax.axis_index("tp") % SIDE
    meta = jnp.concatenate([span_order, jnp.stack([ctx, x, z, core]).astype(jnp.int32)])

    def head_block(step):
        start = (x + step) % SIDE * HD
        return jnp.concatenate(
            [
                lax.dynamic_slice_in_dim(key_rows, start, HD, 1),
                lax.dynamic_slice_in_dim(value_rows, start, HD, 1),
            ],
            axis=1,
        )

    width = out_proj.shape[1]
    quarter = width // 4

    def weights_part(base):
        return lax.dynamic_slice_in_dim(out_proj, base + core * quarter, quarter, 1)

    def gathered(part, groups):
        return lax.all_gather(part, "tp", axis=0, tiled=True, axis_index_groups=groups)

    own = jnp.stack(exchange(shift_x, [head_block(step) for step in range(SIDE)]))
    own, part_x, part_z = lax.optimization_barrier(
        (own, weights_part(0), weights_part(width // 2))
    )
    weights_x = gathered(part_x, GROUPS_X)
    weights_z = gathered(part_z, GROUPS_Z)
    other = swap_ctx(own)
    before_own, after_own = shift_z(own, 1), shift_z(own, -1)
    before_other, after_other = shift_z(other, 1), shift_z(other, -1)
    far_own = shift_z(before_own, 1)
    far_other = shift_z(after_other, -1)
    pieces = [
        own,
        other,
        before_own,
        before_other,
        after_own,
        after_other,
        far_own,
        far_other,
    ]

    maps = routes(expert_ids, route_weights, n_devices)

    parts = attention(meta, queries, pieces)
    parts, weights_x = lax.optimization_barrier((parts, weights_x))
    other_x = swap_core(weights_x)
    context_x = exchange(shift_x, parts[:4])
    context_z = exchange(shift_z, parts[4:])
    context_x, context_z = lax.optimization_barrier((context_x, context_z))
    terms_z = projection(5, 6, meta, context_x, [weights_x, other_x])
    terms_z, weights_z = lax.optimization_barrier((terms_z, weights_z))
    other_z = swap_core(weights_z)
    terms_x = projection(6, 5, meta, context_z, [weights_z, other_z])
    terms_z, terms_x = exchange(shift_z, terms_z), exchange(shift_x, terms_x)
    main, late, back_main, back_late = maps

    outgoing, state = dispatch(
        meta, terms_z, terms_x, residual, norm_gain[None, :], main, late
    )

    def all_to_all(rows):
        blocks = rows.reshape(n_devices, SLOTS, rows.shape[1])
        return lax.all_to_all(
            blocks, ("dp", "ctx", "tp"), split_axis=0, concat_axis=0, tiled=True
        ).reshape(rows.shape)

    arrived = all_to_all(outgoing)
    returned = all_to_all(experts(arrived, w_up, w_down))
    return combine(back_main, back_late, returned, state)


def solution(mesh):
    return jax.shard_map(
        local,
        mesh=mesh,
        in_specs=(
            P(("dp", "ctx"), "tp"),
            P(("dp", "ctx", "tp"), None),
            P(("dp", "ctx", "tp"), None),
            P(),
            P("tp", None),
            P(("dp", "ctx", "tp"), None),
            P(),
            P(("dp", "ctx", "tp"), None),
            P(("dp", "ctx", "tp"), None),
            P(("dp", "ctx", "tp"), None, None),
            P(("dp", "ctx", "tp"), None, None),
        ),
        out_specs=P(("dp", "ctx", "tp"), None),
        check_vma=False,
    )
```

time: 473 us -> 445 us (0.941)
  starting transfers between devices: 62.4 us -> 46.9 us
  between operations: 0.57 us -> 13.7 us
  Pallas kernels: 90.9 us -> 80.5 us
  local copies, waits for them, and re-layouts: 24.1 us -> 14.9 us
  waiting for transfers between devices: 168 us -> 163 us
    ppermute x16 -> x12, waiting for transfers between devices: 36.7 us -> 22.2 us  [shift_z(): lax.ppermute(value, 'tp', [(x * SIDE + z, x * SIDE + (z + step) % SIDE) f...]
    unnamed x49 -> x54, local copies, waits for them, and re-layouts: 18.1 us -> 8.56 us
    ppermute x16 -> x12, starting transfers between devices: 32.3 us -> 23.3 us  [shift_z(): lax.ppermute(value, 'tp', [(x * SIDE + z, x * SIDE + (z + step) % SIDE) f...]
    pallas_call x1, Pallas kernels: 32.6 us -> 24.6 us  [experts(): call(expert_kernel, 'experts', jax.ShapeDtypeStruct((rows, columns), BF16...]
    ppermute x13 -> x9, waiting for transfers between devices: 14.2 us -> 21.5 us  [shift_x(): lax.ppermute(value, 'tp', [(x * SIDE + z, (x + step) % SIDE * SIDE + z) f...]
    ppermute x13 -> x9, starting transfers between devices: 21.5 us -> 14.9 us  [shift_x(): lax.ppermute(value, 'tp', [(x * SIDE + z, (x + step) % SIDE * SIDE + z) f...]
  transfers between devices with their start and end apart: 33 -> 27, of which waited for: 14 -> 17; matrix products, arithmetic and copies ran while one was open for 3% -> 2% of each run, Pallas kernels for 8% -> 8%
where the time goes in v2:
time: 445 us; the launch traced here: 440 us
  waiting for transfers between devices  163 us (37%)
  blocking collectives  118 us (27%)
  Pallas kernels  80.5 us (18%)
  starting transfers between devices  46.9 us (11%)
  local copies, waits for them, and re-layouts  14.9 us (3%)
  between operations  13.7 us (3%)
    all_to_all x1, blocking collectives, all_to_all(): lax.all_to_all(blocks, ('dp', 'ctx', 'tp'), split_axis=0, concat_axis=0,...  118 us
    all_to_all x1, waiting for transfers between devices, all_to_all(): lax.all_to_all(blocks, ('dp', 'ctx', 'tp'), split_axis=0, concat_axis=0,...  116 us
    pallas_call x1, Pallas kernels, experts(): call(expert_kernel, 'experts', jax.ShapeDtypeStruct((rows, columns), BF16...  24.6 us
    pallas_call x1, Pallas kernels, attention(): call(attention_kernel, 'attention', [jax.ShapeDtypeStruct((BLOCK, width),...  23.9 us
    ppermute x12, starting transfers between devices, shift_z(): lax.ppermute(value, 'tp', [(x * SIDE + z, x * SIDE + (z + step) % SIDE) f...  23.3 us
    ppermute x12, waiting for transfers between devices, shift_z(): lax.ppermute(value, 'tp', [(x * SIDE + z, x * SIDE + (z + step) % SIDE) f...  22.2 us
    ppermute x9, waiting for transfers between devices, shift_x(): lax.ppermute(value, 'tp', [(x * SIDE + z, (x + step) % SIDE * SIDE + z) f...  21.5 us
    ppermute x9, starting transfers between devices, shift_x(): lax.ppermute(value, 'tp', [(x * SIDE + z, (x + step) % SIDE * SIDE + z) f...  14.9 us
  transfers between devices with their start and end apart: 27, of which 17 were waited for; matrix products, arithmetic and copies ran while one was open for 2% of the time, Pallas kernels for 8%

profile of v2, /device:TPU:0, one launch (start us, length us, event | category | flops | bytes accessed | tf_op | source)
XLA Modules:
  0.0 439.7 jit_solution(33298473805240654)
XLA Ops:
  6.5 0.9 constant_dynamic-slice_fusion.8
  7.5 1.6 collective-permute-start
  9.1 2.8 collective-permute-start.1
  11.9 1.5 collective-permute-start.2
  13.4 2.3 constant_dynamic-slice_fusion
  16.4 1.7 collective-permute-start.3
  18.1 1.9 collective-permute-start.4
  20.0 3.2 collective-permute-done.3.refs_1_
  23.2 4.1 collective-permute-start.7
  27.7 1.6 collective-permute-start.5
  29.4 4.7 %collective-permute-done.7.refs_5_ = bf16[4,128,256]{2,1,0:T(8,128)(2,1)S(1)} collective-permute-done((bf16[4,128,256]{2,1,0:T(8,128)(2,1)S(1)}, bf16[4,128,256]{2,1,0:T(8,128)(2,1)S(1)}, u32[]{:S(2)}, u32[]{:S(2)}) %collective-permute-start.7) | collective-permute-done | bytes 262176 | tf_op jit(solution)/shard_map/ppermute | solution.py:34
  34.1 3.7 collective-permute-start.9
  37.8 0.7 concatenate.23.meta
  38.5 0.6 collective-permute-done.6.refs_4_
  39.1 0.7 collective-permute-done.8.refs_6_
  39.9 2.1 collective-permute-done.9.refs_7_
  42.0 0.7 copy-done.21
  42.7 23.9 %attention.1 = (bf16[512,256]{1,0:T(8,128)(2,1)}, bf16[512,256]{1,0:T(8,128)(2,1)}, bf16[512,256]{1,0:T(8,128)(2,1)}, bf16[512,256]{1,0:T(8,128)(2,1)}, bf16[512...) custom-call(s32[8]{0:T(128)} %concatenate.23.meta, ...), custom_call_target="tpu_custom_call" | custom-call | flops 7000000000 | bytes 5000000 | tf_op jit(solution)/shard_map/attention/pallas_call | solution.py:182
  67.2 3.2 collective-permute-start.11
  71.1 5.9 %collective-permute-done.10.refs_1_ = bf16[512,256]{1,0:T(8,128)(2,1)S(1)} collective-permute-done((bf16[512,256]{1,0:T(8,128)(2,1)}, bf16[512,256]{1,0:T(8,128)(2,1)S(1)}, u32[]{:S(2)}, u32[]{:S(2)}) %collective-permute-start.10) | collective-permute-done | bytes 262176 | tf_op jit(solution)/shard_map/ppermute | solution.py:26
  77.0 2.3 collective-permute-start.14
  79.4 3.5 collective-permute-done.11.refs_2_
  82.9 3.7 collective-permute-start.15
  86.9 6.2 %collective-permute-done.14.refs_2_ = bf16[512,256]{1,0:T(8,128)(2,1)S(1)} collective-permute-done((bf16[512,256]{1,0:T(8,128)(2,1)}, bf16[512,256]{1,0:T(8,128)(2,1)S(1)}, u32[]{:S(2)}, u32[]{:S(2)}) %collective-permute-start.14) | collective-permute-done | bytes 262176 | tf_op jit(solution)/shard_map/ppermute | solution.py:34
  94.0 1.4 copy-done.5
  95.3 6.5 %projection.2 = (bf16[128,2048]{1,0:T(8,128)(2,1)}, bf16[128,2048]{1,0:T(8,128)(2,1)}, bf16[128,2048]{1,0:T(8,128)(2,1)}, bf16[128,2048]{1,0:T(8,128)(2,1)}) custom-call(s32[8]{0:T(128)} %concatenate.23.meta, bf16[512,256]{1,0:T(8,128)(2,1)} %get-tuple-element.66.refs_0_, bf16[512,256]{1,0:T(8,128)(2,1)} %copy-done.22, bf16[512,256]{1,0:T(8,128)(2,1)} %copy-done.23, ...), custom_call_target="tpu_custom_call" | custom-call | flops 2147483648 | bytes 7000000 | tf_op jit(solution)/shard_map/projection/pallas_call | solution.py:226
  101.8 1.0 collective-permute-start.17
  103.3 4.0 collective-permute-start.18
  107.3 1.3 copy-done.6
  108.7 6.5 %projection.3 = (bf16[128,2048]{1,0:T(8,128)(2,1)}, bf16[128,2048]{1,0:T(8,128)(2,1)}, bf16[128,2048]{1,0:T(8,128)(2,1)}, bf16[128,2048]{1,0:T(8,128)(2,1)}) custom-call(s32[8]{0:T(128)} %concatenate.23.meta, bf16[512,256]{1,0:T(8,128)(2,1)} %get-tuple-element.80.refs_0_, bf16[512,256]{1,0:T(8,128)(2,1)} %copy-done.12, bf16[512,256]{1,0:T(8,128)(2,1)} %copy-done.15, ...), custom_call_target="tpu_custom_call" | custom-call | flops 2147483648 | bytes 7000000 | tf_op jit(solution)/shard_map/projection/pallas_call | solution.py:226
  115.1 0.8 collective-permute-start.21
  115.9 2.7 collective-permute-start.22
  118.6 0.8 copy-done.7
  119.4 1.7 collective-permute-start.23
  121.5 0.8 copy.31.refs_10_
  122.4 0.7 copy.32.refs_11_
  123.1 7.3 %collective-permute-done.18.refs_2_ = bf16[128,2048]{1,0:T(8,128)(2,1)S(1)} collective-permute-done((bf16[128,2048]{1,0:T(8,128)(2,1)}, bf16[128,2048]{1,0:T(8,128)(2,1)S(1)}, u32[]{:S(2)}, u32[]{:S(2)}) %collective-permute-start.18) | collective-permute-done | bytes 524320 | tf_op jit(solution)/shard_map/ppermute | solution.py:34
  130.5 0.9 collective-permute-done.21.refs_5_
  131.4 10.1 %collective-permute-done.22.refs_6_ = bf16[128,2048]{1,0:T(8,128)(2,1)S(1)} collective-permute-done((bf16[128,2048]{1,0:T(8,128)(2,1)}, bf16[128,2048]{1,0:T(8,128)(2,1)S(1)}, u32[]{:S(2)}, u32[]{:S(2)}) %collective-permute-start.22) | collective-permute-done | bytes 524320 | tf_op jit(solution)/shard_map/ppermute | solution.py:26
  142.9 10.1 %dispatch.1 = (bf16[1024,4608]{1,0:T(8,128)(2,1)}, f32[128,4096]{1,0:T(8,128)}) custom-call(s32[8]{0:T(128)} %concatenate.23.meta, bf16[128,2048]{1,0:T(8,128)(2,1)} %get-tuple-element.76.refs_0_, bf16[128,2048]{1,0:T(8,128)(2,1)} %copy-done.7, bf16[128,2048]{1,0:T(8,128)(2,1)} %copy-done.8, bf16[128,2048]{1,0:T(8,128)(2,1)} %collective-permute-done.19.refs_3_, ...), custom_call_target="tpu_custom_call" | custom-call | flops 3000000000 | bytes 16000000 | tf_op jit(solution)/shard_map/dispatch/pallas_call | solution.py:302
  152.9 118.2 %all_to_all.10 = bf16[128,8,4608]{2,1,0:T(8,128)(2,1)} all-to-all(bf16[128,8,4608]{2,1,0:T(8,128)(2,1)} %bitcast.35), channel_id=1, replica_groups=mesh['dp'=4,'ctx'=2,'tp'=16] {'dp','ctx','tp'}, dimensions={0} | all-to-all | bytes 18874368 | tf_op jit(solution)/shard_map/all_to_all | solution.py:529
  271.1 2.8 copy-done
  273.9 24.6 %experts.1 = bf16[1024,4608]{1,0:T(8,128)(2,1)} custom-call(bf16[1024,4608]{1,0:T(8,128)(2,1)} %bitcast.36, bf16[1024,4608]{1,0:T(8,128)(2,1)} %bitcast.37, bf16[1,4096,768]{2,1,0:T(8,128)(2,1)S(1)} %bitcast.33, bf16[1,768,4096]{2,1,0:T(8,128)(2,1)S(1)} %copy-done), custom_call_target="tpu_custom_call" | custom-call | flops 14495514624 | bytes 32000000 | tf_op jit(solution)/shard_map/experts/pallas_call | solution.py:358
  298.5 6.9 %all-to-all-start.1 = ((bf16[128,8,4608]{2,1,0:T(8,128)(2,1)}), bf16[128,8,4608]{2,1,0:T(8,128)(2,1)}, u32[]{:S(2)}, u32[]{:S(2)}) async-start(bf16[128,8,4608]{2,1,0:T(8,128)(2,1)} %bitcast.34), calls=%async_computation.1 | async-start | bytes 18874368 | tf_op jit(solution)/shard_map/all_to_all | solution.py:529
  305.9 0.6 pad_maximum_fusion.2.late
  306.7 0.8 pad_maximum_fusion.main
  307.5 116.4 %all-to-all-done.1 = bf16[128,8,4608]{2,1,0:T(8,128)(2,1)} async-done(((bf16[128,8,4608]{2,1,0:T(8,128)(2,1)}), bf16[128,8,4608]{2,1,0:T(8,128)(2,1)}, u32[]{:S(2)}, u32[]{:S(2)}) %all-to-all-start.1) | async-done | bytes 9437216 | tf_op jit(solution)/shard_map/all_to_all | solution.py:529
  423.9 8.9 %combine.1 = bf16[128,4096]{1,0:T(8,128)(2,1)} custom-call(bf16[256,1024]{1,0:T(8,128)(2,1)} %pad_maximum_fusion.main, bf16[256,128]{1,0:T(8,128)(2,1)} %pad_maximum_fusion.2.late, bf16[1024,4608]{1,0:T(8,128)(2,1)} %bitcast.21.rows_ref.over_ref, bf16[1024,4608]{1,0:T(8,128)(2,1)} %bitcast.21.rows_ref.over_ref, f32[128,4096]{1,0:T(8,128)} %get-tuple-element.90.state), custom_call_target="tpu_custom_call" | custom-call | flops 4000000000 | bytes 13000000 | tf_op jit(solution)/shard_map/combine/pallas_call | solution.py:404
  (99 shorter events, 6.7 us)
Async XLA Ops:
  6.5 60.1 %all-gather.3.cloned.1.call-start = ((), (), s32[]{:S(2)}) async-start(), calls=%async_computation.2 | async-start | bytes 2621440 | tf_op jit(solution)/shard_map/all_gather | solution.py:484
  7.5 30.4 %copy-start.4 = (s32[4]{0:T(128)S(1)}, s32[4]{0:T(128)}, u32[]{:S(2)}) copy-start(s32[4]{0:T(128)} %param.14) | copy-start | bytes 52
  7.5 8.2 %collective-permute-start = (bf16[128,256]{1,0:T(8,128)(2,1)S(1)}, bf16[128,256]{1,0:T(8,128)(2,1)S(1)}, u32[]{:S(2)}, u32[]{:S(2)}) collective-permute-start(bf16[128,256]{1,0:T(8,128)(2,1)S(1)} %pad_maximum_fusion.3), channel_id=1, source_target_pairs={{0,4},{1,5},{2,6},{3,7},{4,8},{5,9},{6,10},{7,11},{8,12},{9,13},{1... | collective-permute-start | bytes 196616 | tf_op jit(solution)/shard_map/ppermute | solution.py:26
  9.1 6.6 %collective-permute-start.1 = (bf16[128,256]{1,0:T(8,128)(2,1)S(1)}, bf16[128,256]{1,0:T(8,128)(2,1)S(1)}, u32[]{:S(2)}, u32[]{:S(2)}) collective-permute-start(bf16[128,256]{1,0:T(8,128)(2,1)S(1)} %pad_maximum_fusion.4), channel_id=1, source_target_pairs={{0,8},{1,9},{2,10},{3,11},{4,12},{5,13},{6,14},{7,15},{8,0},{9,1},... | collective-permute-start | bytes 196616 | tf_op jit(solution)/shard_map/ppermute | solution.py:26
  11.9 4.3 collective-permute-start.2
  16.3 25.6 %copy-start.1 = (bf16[4,128,256]{2,1,0:T(8,128)(2,1)}, bf16[4,128,256]{2,1,0:T(8,128)(2,1)S(1)}, u32[]{:S(2)}) copy-start(bf16[4,128,256]{2,1,0:T(8,128)(2,1)S(1)} %pad_maximum_fusion.1.refs_0_) | copy-start | bytes 786436
  16.4 85.5 %all-gather.5.cloned.1.call-start = ((), (), s32[]{:S(2)}) async-start(), calls=%async_computation.3 | async-start | bytes 2621440 | tf_op jit(solution)/shard_map/all_gather | solution.py:484
  16.4 6.8 %collective-permute-start.3 = (bf16[4,128,256]{2,1,0:T(8,128)(2,1)S(1)}, bf16[4,128,256]{2,1,0:T(8,128)(2,1)S(1)}, u32[]{:S(2)}, u32[]{:S(2)}) collective-permute-start(bf16[4,128,256]{2,1,0:T(8,128)(2,1)S(1)} %pad_maximum_fusion.1.refs_0_), channel_id=1, source_target_pairs={{0,16},{16,0},{1,17},{17,1},{2,18},{18,2},{3,19},{19,3},{4,20},{20... | collective-permute-start | bytes 786440 | tf_op jit(solution)/shard_map/ppermute | solution.py:42
  18.1 11.3 %collective-permute-start.4 = (bf16[4,128,256]{2,1,0:T(8,128)(2,1)S(1)}, bf16[4,128,256]{2,1,0:T(8,128)(2,1)S(1)}, u32[]{:S(2)}, u32[]{:S(2)}) collective-permute-start(bf16[4,128,256]{2,1,0:T(8,128)(2,1)S(1)} %pad_maximum_fusion.1.refs_0_), channel_id=1, source_target_pairs={{0,1},{1,2},{2,3},{3,0},{4,5},{5,6},{6,7},{7,4},{8,9},{9,10},{10,1... | collective-permute-start | bytes 786440 | tf_op jit(solution)/shard_map/ppermute | solution.py:34
  23.2 18.8 %copy-start.13 = (bf16[4,128,256]{2,1,0:T(8,128)(2,1)}, bf16[4,128,256]{2,1,0:T(8,128)(2,1)S(1)}, u32[]{:S(2)}) copy-start(bf16[4,128,256]{2,1,0:T(8,128)(2,1)S(1)} %collective-permute-done.3.refs_1_) | copy-start | bytes 786436
  23.2 10.9 %collective-permute-start.7 = (bf16[4,128,256]{2,1,0:T(8,128)(2,1)S(1)}, bf16[4,128,256]{2,1,0:T(8,128)(2,1)S(1)}, u32[]{:S(2)}, u32[]{:S(2)}) collective-permute-start(bf16[4,128,256]{2,1,0:T(8,128)(2,1)S(1)} %collective-permute-done.3.refs_1_), channel_id=1, source_target_pairs={{0,3},{1,0},{2,1},{3,2},{4,7},{5,4},{6,5},{7,6},{8,11},{9,8},{10,9... | collective-permute-start | bytes 786440 | tf_op jit(solution)/shard_map/ppermute | solution.py:34
  27.3 11.8 %collective-permute-start.6 = (bf16[4,128,256]{2,1,0:T(8,128)(2,1)S(1)}, bf16[4,128,256]{2,1,0:T(8,128)(2,1)S(1)}, u32[]{:S(2)}, u32[]{:S(2)}) collective-permute-start(bf16[4,128,256]{2,1,0:T(8,128)(2,1)S(1)} %pad_maximum_fusion.1.refs_0_), channel_id=1, source_target_pairs={{0,3},{1,0},{2,1},{3,2},{4,7},{5,4},{6,5},{7,6},{8,11},{9,8},{10,9... | collective-permute-start | bytes 786440 | tf_op jit(solution)/shard_map/ppermute | solution.py:34
  27.7 11.4 %collective-permute-start.5 = (bf16[4,128,256]{2,1,0:T(8,128)(2,1)S(1)}, bf16[4,128,256]{2,1,0:T(8,128)(2,1)S(1)}, u32[]{:S(2)}, u32[]{:S(2)}) collective-permute-start(bf16[4,128,256]{2,1,0:T(8,128)(2,1)S(1)} %collective-permute-done.3.refs_1_), channel_id=1, source_target_pairs={{0,1},{1,2},{2,3},{3,0},{4,5},{5,6},{6,7},{7,4},{8,9},{9,10},{10,1... | collective-permute-start | bytes 786440 | tf_op jit(solution)/shard_map/ppermute | solution.py:34
  29.3 12.6 %copy-start.14 = (bf16[4,128,256]{2,1,0:T(8,128)(2,1)}, bf16[4,128,256]{2,1,0:T(8,128)(2,1)S(1)}, u32[]{:S(2)}) copy-start(bf16[4,128,256]{2,1,0:T(8,128)(2,1)S(1)} %collective-permute-done.4.refs_2_) | copy-start | bytes 786436
  29.3 10.5 %collective-permute-start.8 = (bf16[4,128,256]{2,1,0:T(8,128)(2,1)S(1)}, bf16[4,128,256]{2,1,0:T(8,128)(2,1)S(1)}, u32[]{:S(2)}, u32[]{:S(2)}) collective-permute-start(bf16[4,128,256]{2,1,0:T(8,128)(2,1)S(1)} %collective-permute-done.4.refs_2_), channel_id=1, source_target_pairs={{0,1},{1,2},{2,3},{3,0},{4,5},{5,6},{6,7},{7,4},{8,9},{9,10},{10,1... | collective-permute-start | bytes 786440 | tf_op jit(solution)/shard_map/ppermute | solution.py:34
  34.1 7.9 %copy-start.16 = (bf16[4,128,256]{2,1,0:T(8,128)(2,1)}, bf16[4,128,256]{2,1,0:T(8,128)(2,1)S(1)}, u32[]{:S(2)}) copy-start(bf16[4,128,256]{2,1,0:T(8,128)(2,1)S(1)} %collective-permute-done.7.refs_5_) | copy-start | bytes 786436
  34.1 7.9 %collective-permute-start.9 = (bf16[4,128,256]{2,1,0:T(8,128)(2,1)S(1)}, bf16[4,128,256]{2,1,0:T(8,128)(2,1)S(1)}, u32[]{:S(2)}, u32[]{:S(2)}) collective-permute-start(bf16[4,128,256]{2,1,0:T(8,128)(2,1)S(1)} %collective-permute-done.7.refs_5_), channel_id=1, source_target_pairs={{0,3},{1,0},{2,1},{3,2},{4,7},{5,4},{6,5},{7,6},{8,11},{9,8},{10,9... | collective-permute-start | bytes 786440 | tf_op jit(solution)/shard_map/ppermute | solution.py:34
  39.1 2.8 copy-start.18
  39.1 2.8 copy-start.19
  39.9 2.1 copy-start.20
  66.6 36.1 %copy-start.2 = (f32[128,8]{0,1:T(8,128)S(1)}, f32[128,8]{0,1:T(8,128)}, u32[]{:S(2)}) copy-start(f32[128,8]{0,1:T(8,128)} %param.19) | copy-start | bytes 12292
  66.7 36.1 %copy-start.3 = (s32[128,8]{0,1:T(8,128)S(1)}, s32[128,8]{0,1:T(8,128)}, u32[]{:S(2)}) copy-start(s32[128,8]{0,1:T(8,128)} %param.18) | copy-start | bytes 12292
  66.7 26.6 %collective-permute-start.16 = (bf16[1024,1024]{1,0:T(8,128)(2,1)}, bf16[1024,1024]{1,0:T(8,128)(2,1)S(1)}, u32[]{:S(2)}, u32[]{:S(2)}) collective-permute-start(bf16[1024,1024]{1,0:T(8,128)(2,1)} %all-gather.3.cloned.1.call-done.refs_4_), channel_id=1, source_target_pairs={{0,32},{32,0},{64,96},{96,64},{1,33},{33,1},{65,97},{97,65},{2,34}... | collective-permute-start | bytes 6291464 | tf_op jit(solution)/shard_map/ppermute | solution.py:46
  66.8 10.3 %collective-permute-start.10 = (bf16[512,256]{1,0:T(8,128)(2,1)}, bf16[512,256]{1,0:T(8,128)(2,1)S(1)}, u32[]{:S(2)}, u32[]{:S(2)}) collective-permute-start(bf16[512,256]{1,0:T(8,128)(2,1)} %get-tuple-element.59), channel_id=1, source_target_pairs={{0,4},{1,5},{2,6},{3,7},{4,8},{5,9},{6,10},{7,11},{8,12},{9,13},{1... | collective-permute-start | bytes 786440 | tf_op jit(solution)/shard_map/ppermute | solution.py:26
  67.2 15.7 %collective-permute-start.11 = (bf16[512,256]{1,0:T(8,128)(2,1)}, bf16[512,256]{1,0:T(8,128)(2,1)S(1)}, u32[]{:S(2)}, u32[]{:S(2)}) collective-permute-start(bf16[512,256]{1,0:T(8,128)(2,1)} %get-tuple-element.60), channel_id=1, source_target_pairs={{0,8},{1,9},{2,10},{3,11},{4,12},{5,13},{6,14},{7,15},{8,0},{9,1},... | collective-permute-start | bytes 786440 | tf_op jit(solution)/shard_map/ppermute | solution.py:26
  70.4 16.1 %collective-permute-start.12 = (bf16[512,256]{1,0:T(8,128)(2,1)}, bf16[512,256]{1,0:T(8,128)(2,1)S(1)}, u32[]{:S(2)}, u32[]{:S(2)}) collective-permute-start(bf16[512,256]{1,0:T(8,128)(2,1)} %get-tuple-element.61), channel_id=1, source_target_pairs={{0,12},{1,13},{2,14},{3,15},{4,0},{5,1},{6,2},{7,3},{8,4},{9,5},{1... | collective-permute-start | bytes 786440 | tf_op jit(solution)/shard_map/ppermute | solution.py:26
  70.6 16.3 %collective-permute-start.13 = (bf16[512,256]{1,0:T(8,128)(2,1)}, bf16[512,256]{1,0:T(8,128)(2,1)S(1)}, u32[]{:S(2)}, u32[]{:S(2)}) collective-permute-start(bf16[512,256]{1,0:T(8,128)(2,1)} %get-tuple-element.63), channel_id=1, source_target_pairs={{0,1},{1,2},{2,3},{3,0},{4,5},{5,6},{6,7},{7,4},{8,9},{9,10},{10,1... | collective-permute-start | bytes 786440 | tf_op jit(solution)/shard_map/ppermute | solution.py:34
  77.0 16.2 %copy-start.22 = (bf16[512,256]{1,0:T(8,128)(2,1)}, bf16[512,256]{1,0:T(8,128)(2,1)S(1)}, u32[]{:S(2)}) copy-start(bf16[512,256]{1,0:T(8,128)(2,1)S(1)} %collective-permute-done.10.refs_1_) | copy-start | bytes 786436
  77.0 16.1 %collective-permute-start.14 = (bf16[512,256]{1,0:T(8,128)(2,1)}, bf16[512,256]{1,0:T(8,128)(2,1)S(1)}, u32[]{:S(2)}, u32[]{:S(2)}) collective-permute-start(bf16[512,256]{1,0:T(8,128)(2,1)} %get-tuple-element.64), channel_id=1, source_target_pairs={{0,2},{1,3},{2,0},{3,1},{4,6},{5,7},{6,4},{7,5},{8,10},{9,11},{10,... | collective-permute-start | bytes 786440 | tf_op jit(solution)/shard_map/ppermute | solution.py:34
  82.9 10.4 %copy-start.23 = (bf16[512,256]{1,0:T(8,128)(2,1)}, bf16[512,256]{1,0:T(8,128)(2,1)S(1)}, u32[]{:S(2)}) copy-start(bf16[512,256]{1,0:T(8,128)(2,1)S(1)} %collective-permute-done.11.refs_2_) | copy-start | bytes 786436
  82.9 10.4 %collective-permute-start.15 = (bf16[512,256]{1,0:T(8,128)(2,1)}, bf16[512,256]{1,0:T(8,128)(2,1)S(1)}, u32[]{:S(2)}, u32[]{:S(2)}) collective-permute-start(bf16[512,256]{1,0:T(8,128)(2,1)} %get-tuple-element.65), channel_id=1, source_target_pairs={{0,3},{1,0},{2,1},{3,2},{4,7},{5,4},{6,5},{7,6},{8,11},{9,8},{10,9... | collective-permute-start | bytes 786440 | tf_op jit(solution)/shard_map/ppermute | solution.py:34
  86.5 6.7 %copy-start.24 = (bf16[512,256]{1,0:T(8,128)(2,1)}, bf16[512,256]{1,0:T(8,128)(2,1)S(1)}, u32[]{:S(2)}) copy-start(bf16[512,256]{1,0:T(8,128)(2,1)S(1)} %collective-permute-done.12.refs_3_) | copy-start | bytes 786436
  86.9 6.4 %copy-start.12 = (bf16[512,256]{1,0:T(8,128)(2,1)}, bf16[512,256]{1,0:T(8,128)(2,1)S(1)}, u32[]{:S(2)}) copy-start(bf16[512,256]{1,0:T(8,128)(2,1)S(1)} %collective-permute-done.13.refs_1_) | copy-start | bytes 786436
  94.0 1.4 copy-start.5
  101.8 5.5 %collective-permute-start.20 = (bf16[1024,1024]{1,0:T(8,128)(2,1)}, bf16[1024,1024]{1,0:T(8,128)(2,1)S(1)}, u32[]{:S(2)}, u32[]{:S(2)}) collective-permute-start(bf16[1024,1024]{1,0:T(8,128)(2,1)} %all-gather.5.cloned.1.call-done.refs_4_), channel_id=1, source_target_pairs={{0,32},{32,0},{64,96},{96,64},{1,33},{33,1},{65,97},{97,65},{2,34}... | collective-permute-start | bytes 6291464 | tf_op jit(solution)/shard_map/ppermute | solution.py:46
  101.8 16.8 %collective-permute-start.17 = (bf16[128,2048]{1,0:T(8,128)(2,1)}, bf16[128,2048]{1,0:T(8,128)(2,1)S(1)}, u32[]{:S(2)}, u32[]{:S(2)}) collective-permute-start(bf16[128,2048]{1,0:T(8,128)(2,1)} %get-tuple-element.77), channel_id=1, source_target_pairs={{0,1},{1,2},{2,3},{3,0},{4,5},{5,6},{6,7},{7,4},{8,9},{9,10},{10,1... | collective-permute-start | bytes 1572872 | tf_op jit(solution)/shard_map/ppermute | solution.py:34
  103.3 27.1 %collective-permute-start.18 = (bf16[128,2048]{1,0:T(8,128)(2,1)}, bf16[128,2048]{1,0:T(8,128)(2,1)S(1)}, u32[]{:S(2)}, u32[]{:S(2)}) collective-permute-start(bf16[128,2048]{1,0:T(8,128)(2,1)} %get-tuple-element.78), channel_id=1, source_target_pairs={{0,2},{1,3},{2,0},{3,1},{4,6},{5,7},{6,4},{7,5},{8,10},{9,11},{10,... | collective-permute-start | bytes 1572872 | tf_op jit(solution)/shard_map/ppermute | solution.py:34
  107.3 23.3 %collective-permute-start.19 = (bf16[128,2048]{1,0:T(8,128)(2,1)}, bf16[128,2048]{1,0:T(8,128)(2,1)}, u32[]{:S(2)}, u32[]{:S(2)}) collective-permute-start(bf16[128,2048]{1,0:T(8,128)(2,1)} %get-tuple-element.79), channel_id=1, source_target_pairs={{0,3},{1,0},{2,1},{3,2},{4,7},{5,4},{6,5},{7,6},{8,11},{9,8},{10,9... | collective-permute-start | bytes 1572872 | tf_op jit(solution)/shard_map/ppermute | solution.py:34
  107.3 1.3 copy-start.6
  115.1 16.3 %collective-permute-start.21 = (bf16[128,2048]{1,0:T(8,128)(2,1)}, bf16[128,2048]{1,0:T(8,128)(2,1)S(1)}, u32[]{:S(2)}, u32[]{:S(2)}) collective-permute-start(bf16[128,2048]{1,0:T(8,128)(2,1)} %get-tuple-element.86), channel_id=1, source_target_pairs={{0,4},{1,5},{2,6},{3,7},{4,8},{5,9},{6,10},{7,11},{8,12},{9,13},{1... | collective-permute-start | bytes 1572872 | tf_op jit(solution)/shard_map/ppermute | solution.py:26
  115.9 25.7 %collective-permute-start.22 = (bf16[128,2048]{1,0:T(8,128)(2,1)}, bf16[128,2048]{1,0:T(8,128)(2,1)S(1)}, u32[]{:S(2)}, u32[]{:S(2)}) collective-permute-start(bf16[128,2048]{1,0:T(8,128)(2,1)} %get-tuple-element.87), channel_id=1, source_target_pairs={{0,8},{1,9},{2,10},{3,11},{4,12},{5,13},{6,14},{7,15},{8,0},{9,1},... | collective-permute-start | bytes 1572872 | tf_op jit(solution)/shard_map/ppermute | solution.py:26
  119.4 22.7 %collective-permute-start.23 = (bf16[128,2048]{1,0:T(8,128)(2,1)}, bf16[128,2048]{1,0:T(8,128)(2,1)S(1)}, u32[]{:S(2)}, u32[]{:S(2)}) collective-permute-start(bf16[128,2048]{1,0:T(8,128)(2,1)} %get-tuple-element.88), channel_id=1, source_target_pairs={{0,12},{1,13},{2,14},{3,15},{4,0},{5,1},{6,2},{7,3},{8,4},{9,5},{1... | collective-permute-start | bytes 1572872 | tf_op jit(solution)/shard_map/ppermute | solution.py:26
  130.4 11.7 %copy-start.8 = (bf16[128,2048]{1,0:T(8,128)(2,1)}, bf16[128,2048]{1,0:T(8,128)(2,1)S(1)}, u32[]{:S(2)}) copy-start(bf16[128,2048]{1,0:T(8,128)(2,1)S(1)} %collective-permute-done.18.refs_2_) | copy-start | bytes 1572868
  131.4 10.7 %copy-start.9 = (bf16[128,2048]{1,0:T(8,128)(2,1)}, bf16[128,2048]{1,0:T(8,128)(2,1)S(1)}, u32[]{:S(2)}) copy-start(bf16[128,2048]{1,0:T(8,128)(2,1)S(1)} %collective-permute-done.21.refs_5_) | copy-start | bytes 1572868
  142.9 128.3 %slice-start = ((s8[6291456]{0:T(1024)(128)(4,1)}), s8[2097152]{0:T(1024)(128)(4,1)S(1)}, s32[]{:S(2)}) async-start(s8[6291456]{0:T(1024)(128)(4,1)} %bitcast.32), calls=%async_computation.4 | async-start | bytes 4194304
  152.9 118.2 %slice-start.1 = ((s8[6291456]{0:T(1024)(128)(4,1)}), s8[4194304]{0:T(1024)(128)(4,1)S(1)}, s32[]{:S(2)}) async-start(s8[6291456]{0:T(1024)(128)(4,1)} %bitcast.32), calls=%async_computation.5 | async-start | bytes 8388608
  271.1 2.8 copy-start
  298.5 125.4 %all-to-all-start.1 = ((bf16[128,8,4608]{2,1,0:T(8,128)(2,1)}), bf16[128,8,4608]{2,1,0:T(8,128)(2,1)}, u32[]{:S(2)}, u32[]{:S(2)}) async-start(bf16[128,8,4608]{2,1,0:T(8,128)(2,1)} %bitcast.34), calls=%async_computation.1 | async-start | bytes 18874368 | tf_op jit(solution)/shard_map/all_to_all | solution.py:529
  (6 other events, 4.6 us)
Sparse Core Ops, SparseCore 0:
  16.5 32.7 all-gather.2
  51.0 36.9 all-gather.4

commit v3 on v2

--- a/solution.py
+++ b/solution.py
@@ -46,8 +46,8 @@
     return lax.ppermute(value, "dp", [(0, 1), (1, 0), (2, 3), (3, 2)])
 
 
-GROUPS_X = [[x * SIDE + z for x in range(SIDE)] for z in range(SIDE)]
-GROUPS_Z = [[x * SIDE + z for z in range(SIDE)] for x in range(SIDE)]
+def gather_rows_of(shift, rows):
+    return [rows, shift(rows, 1), shift(rows, 2), shift(rows, -1)]
 
 
 def exchange(shift, blocks):
@@ -200,18 +200,25 @@
     )(meta, queries, *pieces)
 
 
-def projection_kernel(axis_in, axis_out, meta, *refs):
-    context, weights, outs, held = refs[:4], refs[4:6], refs[6:10], refs[10]
-    me_in, me = meta[axis_in], meta[axis_out]
+def projection_kernel(axis, n_pieces, meta, *refs):
+    context, weights, pieces, refs = refs[:4], refs[4:6], refs[6 : 6 + n_pieces], refs[6 + n_pieces :]
+    outs, refs = refs[:4], refs[4:]
+    joined, held, done = refs if n_pieces else (None, *refs)
+    me = meta[axis]
     width = context[0].shape[1]
     columns = 256
+    copies = [
+        pltpu.make_async_copy(piece, joined.at[pl.ds(i * width, width), :], done.at[i])
+        for i, piece in enumerate(pieces)
+    ]
+    for copy in copies:
+        copy.start()
     for side, weight in enumerate(weights):
         for start in range(0, weight.shape[1], columns):
             total = None
             for number, rows in enumerate(context):
-                source = lax.rem(me_in + SIDE - number, SIDE)
-                part = pl.ds(pl.multiple_of(source * width, width), width)
-                term = dot(rows[...], weight[part, start : start + columns])
+                part = weight[number * width : (number + 1) * width, start : start + columns]
+                term = dot(rows[...], part)
                 total = term if total is None else total + term
             held[:, side * weight.shape[1] + start : side * weight.shape[1] + start + columns] = (
                 total.astype(BF16)
@@ -219,21 +226,30 @@
     for number, out in enumerate(outs):
         to = lax.rem(me + number, SIDE)
         out[...] = held[pl.ds(pl.multiple_of(to * TOKENS, TOKENS), TOKENS), :]
-
-
-def projection(axis_in, axis_out, meta, context, weights):
+    for copy in copies:
+        copy.wait()
+
+
+def projection(axis, meta, context, weights, pieces=()):
     columns = 2 * weights[0].shape[1]
+    any_space = pl.BlockSpec(memory_space=pl.ANY)
+    joined = [jax.ShapeDtypeStruct(weights[0].shape, BF16)] if pieces else []
     return call(
-        functools.partial(projection_kernel, axis_in, axis_out),
+        functools.partial(projection_kernel, axis, len(pieces)),
         "projection",
-        [jax.ShapeDtypeStruct((TOKENS, columns), BF16)] * 4,
-        [smem()] + [whole(array) for array in (*context, *weights)],
-        [pl.BlockSpec((TOKENS, columns), lambda: (0, 0))] * 4,
-        scratch=[pltpu.VMEM((SIDE * TOKENS, columns), BF16)],
+        [jax.ShapeDtypeStruct((TOKENS, columns), BF16)] * 4 + joined,
+        [smem()]
+        + [whole(array) for array in (*context, *weights)]
+        + [any_space for _ in pieces],
+        [pl.BlockSpec((TOKENS, columns), lambda: (0, 0))] * 4 + [any_space for _ in joined],
+        scratch=[
+            pltpu.VMEM((SIDE * TOKENS, columns), BF16),
+            pltpu.SemaphoreType.DMA((SIDE,)),
+        ],
         cost=pl.CostEstimate(
             flops=2 * 512 * 1024 * columns, bytes_accessed=7 * 10**6, transcendentals=0
         ),
-    )(meta, *context, *weights)
+    )(meta, *context, *weights, *pieces)
 
 
 def wide_scratch():
@@ -323,15 +339,17 @@
     )(meta, *arrays, main, late)
 
 
-def expert_kernel(rows_ref, over_ref, up_ref, down_ref, out_ref, wide, spread):
+def expert_kernel(rows_ref, over_ref, up_ref, down_hbm, out_ref, wide, spread, down_ref, done):
     step = pl.program_id(0)
     width = down_ref.shape[2]
+    fetch = pltpu.make_async_copy(down_hbm, down_ref, done)
 
     def act(value):
         return (value / (1.0 + jnp.exp(-value))).astype(BF16)
 
     @pl.when(step == 0)
     def _():
+        fetch.start()
         widen(wide, over_ref)
         total = None
         for segment in range(SLOTS):
@@ -339,6 +357,7 @@
             term = dot(gather_rows(wide, segment), part)
             total = term if total is None else total + term
         inner = act(total)
+        fetch.wait()
         for segment in range(SLOTS):
             part = down_ref[0, :, segment * SEG : (segment + 1) * SEG]
             scatter_rows(wide, segment, dot(inner, part))
@@ -363,12 +382,17 @@
             pl.BlockSpec((ROWS, columns), lambda i: (i, 0)),
             pl.BlockSpec((rows, SEG), lambda i: (0, SLOTS)),
             vmem(),
-            vmem(),
+            pl.BlockSpec(memory_space=pl.ANY),
         ],
         pl.BlockSpec((ROWS, columns), lambda i: (i, 0)),
         grid=(rows // ROWS,),
-        scratch=[wide_scratch(), pltpu.VMEM((rows, SEG), BF16)],
-        limit=40,
+        scratch=[
+            wide_scratch(),
+            pltpu.VMEM((rows, SEG), BF16),
+            pltpu.VMEM(down.shape, BF16),
+            pltpu.SemaphoreType.DMA,
+        ],
+        limit=46,
         cost=pl.CostEstimate(
             flops=4 * rows * columns * inner,
             bytes_accessed=32 * 10**6,
@@ -480,20 +504,19 @@
     def weights_part(base):
         return lax.dynamic_slice_in_dim(out_proj, base + core * quarter, quarter, 1)
 
-    def gathered(part, groups):
-        return lax.all_gather(part, "tp", axis=0, tiled=True, axis_index_groups=groups)
-
     own = jnp.stack(exchange(shift_x, [head_block(step) for step in range(SIDE)]))
-    own, part_x, part_z = lax.optimization_barrier(
-        (own, weights_part(0), weights_part(width // 2))
-    )
-    weights_x = gathered(part_x, GROUPS_X)
-    weights_z = gathered(part_z, GROUPS_Z)
+    own, part_x = lax.optimization_barrier((own, weights_part(0)))
     other = swap_ctx(own)
     before_own, after_own = shift_z(own, 1), shift_z(own, -1)
+    before_own, after_own, part_z = lax.optimization_barrier(
+        (before_own, after_own, weights_part(width // 2))
+    )
     before_other, after_other = shift_z(other, 1), shift_z(other, -1)
     far_own = shift_z(before_own, 1)
     far_other = shift_z(after_other, -1)
+    weights_x = jnp.concatenate(gather_rows_of(shift_x, part_x), axis=0)
+    other_x = swap_core(weights_x)
+    weights_z = gather_rows_of(shift_z, part_z)
     pieces = [
         own,
         other,
@@ -508,15 +531,11 @@
     maps = routes(expert_ids, route_weights, n_devices)
 
     parts = attention(meta, queries, pieces)
-    parts, weights_x = lax.optimization_barrier((parts, weights_x))
-    other_x = swap_core(weights_x)
     context_x = exchange(shift_x, parts[:4])
     context_z = exchange(shift_z, parts[4:])
-    context_x, context_z = lax.optimization_barrier((context_x, context_z))
-    terms_z = projection(5, 6, meta, context_x, [weights_x, other_x])
-    terms_z, weights_z = lax.optimization_barrier((terms_z, weights_z))
-    other_z = swap_core(weights_z)
-    terms_x = projection(6, 5, meta, context_z, [weights_z, other_z])
+    context_x, context_z, weights_z = lax.optimization_barrier((context_x, context_z, weights_z))
+    *terms_z, weights_z = projection(6, meta, context_x, [weights_x, other_x], weights_z)
+    terms_x = projection(5, meta, context_z, [weights_z, swap_core(weights_z)])
     terms_z, terms_x = exchange(shift_z, terms_z), exchange(shift_x, terms_x)
     main, late, back_main, back_late = maps
 

time: 445 us -> 518 us (1.16)
  Pallas kernels: 80.5 us -> 139 us
  waiting for transfers between devices: 163 us -> 190 us
  between operations: 13.7 us -> 0.47 us
  starting transfers between devices: 46.9 us -> 54.8 us
  local copies, waits for them, and re-layouts: 14.9 us -> 8.45 us
    pallas_call x2, Pallas kernels: 13 us -> 75.2 us  [projection(): call(functools.partial(projection_kernel, axis, len(pieces)), 'projection...]
    ppermute x9 -> x12, waiting for transfers between devices: 21.5 us -> 39.6 us  [shift_x(): lax.ppermute(value, 'tp', [(x * SIDE + z, (x + step) % SIDE * SIDE + z) f...]
    ppermute x12 -> x15, waiting for transfers between devices: 22.2 us -> 30.7 us  [shift_z(): lax.ppermute(value, 'tp', [(x * SIDE + z, x * SIDE + (z + step) % SIDE) f...]
    pallas_call x1, Pallas kernels: 23.9 us -> 18.2 us  [attention(): call(attention_kernel, 'attention', [jax.ShapeDtypeStruct((BLOCK, width),...]
    unnamed x54 -> x55, local copies, waits for them, and re-layouts: 8.56 us -> 3.09 us
    ppermute x12 -> x15, starting transfers between devices: 23.3 us -> 28.2 us  [shift_z(): lax.ppermute(value, 'tp', [(x * SIDE + z, x * SIDE + (z + step) % SIDE) f...]
    ppermute x9 -> x12, starting transfers between devices: 14.9 us -> 17.8 us  [shift_x(): lax.ppermute(value, 'tp', [(x * SIDE + z, (x + step) % SIDE * SIDE + z) f...]
  transfers between devices with their start and end apart: 27 -> 31, of which waited for: 17 -> 19; matrix products, arithmetic and copies ran while one was open for 2% -> 1% of each run, Pallas kernels for 8% -> 5%
where the time goes in v3:
time: 518 us; the launch traced here: 512 us
  waiting for transfers between devices  190 us (37%)
  Pallas kernels  139 us (27%)
  blocking collectives  118 us (23%)
  starting transfers between devices  54.8 us (11%)
  local copies, waits for them, and re-layouts  8.45 us (2%)
    all_to_all x1, blocking collectives, all_to_all(): lax.all_to_all(blocks, ('dp', 'ctx', 'tp'), split_axis=0, concat_axis=0,...  118 us
    all_to_all x1, waiting for transfers between devices, all_to_all(): lax.all_to_all(blocks, ('dp', 'ctx', 'tp'), split_axis=0, concat_axis=0,...  116 us
    pallas_call x2, Pallas kernels, projection(): call(functools.partial(projection_kernel, axis, len(pieces)), 'projection...  75.2 us
    ppermute x12, waiting for transfers between devices, shift_x(): lax.ppermute(value, 'tp', [(x * SIDE + z, (x + step) % SIDE * SIDE + z) f...  39.6 us
    ppermute x15, waiting for transfers between devices, shift_z(): lax.ppermute(value, 'tp', [(x * SIDE + z, x * SIDE + (z + step) % SIDE) f...  30.7 us
    ppermute x15, starting transfers between devices, shift_z(): lax.ppermute(value, 'tp', [(x * SIDE + z, x * SIDE + (z + step) % SIDE) f...  28.2 us
    pallas_call x1, Pallas kernels, experts(): call(expert_kernel, 'experts', jax.ShapeDtypeStruct((rows, columns), BF16...  26.1 us
    pallas_call x1, Pallas kernels, attention(): call(attention_kernel, 'attention', [jax.ShapeDtypeStruct((BLOCK, width),...  18.2 us
  transfers between devices with their start and end apart: 31, of which 19 were waited for; matrix products, arithmetic and copies ran while one was open for 1% of the time, Pallas kernels for 5%

profile of v3, /device:TPU:0, one launch (start us, length us, event | category | flops | bytes accessed | tf_op | source)
XLA Modules:
  0.0 512.1 jit_solution(6512350322883332520)
XLA Ops:
  0.0 0.9 constant_dynamic-slice_fusion.8
  0.9 1.6 collective-permute-start
  2.6 2.8 collective-permute-start.1
  5.4 1.5 collective-permute-start.2
  6.9 1.3 constant_dynamic-slice_fusion
  8.5 1.2 collective-permute-done.2
  10.4 3.6 collective-permute-start.20
  14.0 11.6 %collective-permute-done.19 = bf16[256,1024]{1,0:T(8,128)(2,1)S(1)} collective-permute-done((bf16[256,1024]{1,0:T(8,128)(2,1)S(1)}, bf16[256,1024]{1,0:T(8,128)(2,1)S(1)}, u32[]{:S(2)}, u32[]{:S(2)}) %collective-permute-start.19) | collective-permute-done | bytes 524320 | tf_op jit(solution)/shard_map/ppermute | solution.py:26
  25.6 9.6 %collective-permute-done.20 = bf16[256,1024]{1,0:T(8,128)(2,1)S(1)} collective-permute-done((bf16[256,1024]{1,0:T(8,128)(2,1)S(1)}, bf16[256,1024]{1,0:T(8,128)(2,1)S(1)}, u32[]{:S(2)}, u32[]{:S(2)}) %collective-permute-start.20) | collective-permute-done | bytes 524320 | tf_op jit(solution)/shard_map/ppermute | solution.py:26
  35.4 1.7 collective-permute-start.3
  37.2 1.9 collective-permute-start.4
  39.1 2.1 collective-permute-start.5
  41.2 2.9 collective-permute-done.3.refs_1_
  44.2 4.1 collective-permute-start.7
  48.3 1.3 collective-permute-start.8
  49.6 1.5 collective-permute-start.6
  51.1 2.6 collective-permute-done.7.refs_5_
  53.6 3.8 collective-permute-start.9
  58.1 0.8 collective-permute-done.8.refs_6_
  58.9 1.5 collective-permute-start.17
  60.5 4.1 collective-permute-done.6.refs_3_
  64.5 1.2 collective-permute-start.18
  65.8 9.6 %collective-permute-done.9.refs_7_ = bf16[4,128,256]{2,1,0:T(8,128)(2,1)} collective-permute-done((bf16[4,128,256]{2,1,0:T(8,128)(2,1)}, bf16[4,128,256]{2,1,0:T(8,128)(2,1)}, u32[]{:S(2)}, u32[]{:S(2)}) %collective-permute-start.9) | collective-permute-done | bytes 262176 | tf_op jit(solution)/shard_map/ppermute | solution.py:34
  75.3 18.2 %attention.1 = (bf16[512,256]{1,0:T(8,128)(2,1)}, bf16[512,256]{1,0:T(8,128)(2,1)}, bf16[512,256]{1,0:T(8,128)(2,1)}, bf16[512,256]{1,0:T(8,128)(2,1)}, bf16[512...) custom-call(s32[8]{0:T(128)} %concatenate.26.meta, ...), custom_call_target="tpu_custom_call" | custom-call | flops 7000000000 | bytes 5000000 | tf_op jit(solution)/shard_map/attention/pallas_call | solution.py:182
  94.3 3.4 collective-permute-start.11
  98.0 3.4 collective-permute-done.10.refs_1_
  101.4 1.9 collective-permute-start.14
  103.3 1.8 collective-permute-done.11.refs_2_
  105.1 3.8 collective-permute-start.15
  108.9 1.7 collective-permute-done.14.refs_2_
  110.7 2.8 collective-permute-done.15.refs_3_
  113.6 68.6 %projection.2 = (bf16[128,2048]{1,0:T(8,128)(2,1)}, bf16[128,2048]{1,0:T(8,128)(2,1)}, bf16[128,2048]{1,0:T(8,128)(2,1)}, bf16[128,2048]{1,0:T(8,128)(2,1)}, bf16[1024,1024]{1,0:T(8,128)(2,1)}) custom-call(s32[8]{0:T(128)} %concatenate.26.meta, bf16[512,256]{1,0:T(8,128)(2,1)} %get-tuple-element.53.refs_0_, bf16[512,256]{1,0:T(8,128)(2,1)} %copy-done.21, ...), custom_call_target="tpu_custom_call" | custom-call | flops 2147483648 | bytes 7000000 | tf_op jit(solution)/shard_map/projection/pallas_call | solution.py:237
  183.0 4.7 collective-permute-start.24
  187.7 1.3 copy-done.6
  189.0 6.5 %projection.3 = (bf16[128,2048]{1,0:T(8,128)(2,1)}, bf16[128,2048]{1,0:T(8,128)(2,1)}, bf16[128,2048]{1,0:T(8,128)(2,1)}, bf16[128,2048]{1,0:T(8,128)(2,1)}) custom-call(s32[8]{0:T(128)} %concatenate.26.meta, bf16[512,256]{1,0:T(8,128)(2,1)} %get-tuple-element.66.refs_0_, bf16[512,256]{1,0:T(8,128)(2,1)} %copy-done.17, bf16[512,256]{1,0:T(8,128)(2,1)} %copy-done.19, ...), custom_call_target="tpu_custom_call" | custom-call | flops 2147483648 | bytes 7000000 | tf_op jit(solution)/shard_map/projection/pallas_call | solution.py:237
  195.6 2.3 collective-permute-start.28
  198.3 0.8 copy-done.9
  199.1 1.2 collective-permute-start.29
  200.8 0.8 copy.31.refs_10_
  202.3 8.5 %collective-permute-done.24.refs_2_ = bf16[128,2048]{1,0:T(8,128)(2,1)S(1)} collective-permute-done((bf16[128,2048]{1,0:T(8,128)(2,1)}, bf16[128,2048]{1,0:T(8,128)(2,1)S(1)}, u32[]{:S(2)}, u32[]{:S(2)}) %collective-permute-start.24) | collective-permute-done | bytes 524320 | tf_op jit(solution)/shard_map/ppermute | solution.py:34
  210.9 11.0 %collective-permute-done.27.refs_5_ = bf16[128,2048]{1,0:T(8,128)(2,1)S(1)} collective-permute-done((bf16[128,2048]{1,0:T(8,128)(2,1)}, bf16[128,2048]{1,0:T(8,128)(2,1)S(1)}, u32[]{:S(2)}, u32[]{:S(2)}) %collective-permute-start.27) | collective-permute-done | bytes 524320 | tf_op jit(solution)/shard_map/ppermute | solution.py:26
  223.4 10.0 %dispatch.1 = (bf16[1024,4608]{1,0:T(8,128)(2,1)}, f32[128,4096]{1,0:T(8,128)}) custom-call(s32[8]{0:T(128)} %concatenate.26.meta, bf16[128,2048]{1,0:T(8,128)(2,1)} %get-tuple-element.62.refs_0_, bf16[128,2048]{1,0:T(8,128)(2,1)} %copy-done.9, bf16[128,2048]{1,0:T(8,128)(2,1)} %copy-done.11, bf16[128,2048]{1,0:T(8,128)(2,1)} %collective-permute-done.25.refs_3_, ...), custom_call_target="tpu_custom_call" | custom-call | flops 3000000000 | bytes 16000000 | tf_op jit(solution)/shard_map/dispatch/pallas_call | solution.py:318
  233.4 118.2 %all_to_all.10 = bf16[128,8,4608]{2,1,0:T(8,128)(2,1)} all-to-all(bf16[128,8,4608]{2,1,0:T(8,128)(2,1)} %bitcast.35), channel_id=1, replica_groups=mesh['dp'=4,'ctx'=2,'tp'=16] {'dp','ctx','tp'}, dimensions={0} | all-to-all | bytes 18874368 | tf_op jit(solution)/shard_map/all_to_all | solution.py:548
  351.6 26.1 %experts.1 = bf16[1024,4608]{1,0:T(8,128)(2,1)} custom-call(bf16[1024,4608]{1,0:T(8,128)(2,1)} %bitcast.36, bf16[1024,4608]{1,0:T(8,128)(2,1)} %bitcast.37, bf16[1,4096,768]{2,1,0:T(8,128)(2,1)S(1)} %bitcast.33, bf16[1,768,4096]{2,1,0:T(8,128)(2,1)} %down_hbm.1), custom_call_target="tpu_custom_call" | custom-call | flops 14495514624 | bytes 32000000 | tf_op jit(solution)/shard_map/experts/pallas_call | solution.py:377
  377.8 6.9 %all-to-all-start.1 = ((bf16[128,8,4608]{2,1,0:T(8,128)(2,1)}), bf16[128,8,4608]{2,1,0:T(8,128)(2,1)}, u32[]{:S(2)}, u32[]{:S(2)}) async-start(bf16[128,8,4608]{2,1,0:T(8,128)(2,1)} %bitcast.34), calls=%async_computation.1 | async-start | bytes 18874368 | tf_op jit(solution)/shard_map/all_to_all | solution.py:548
  385.9 0.8 pad_maximum_fusion.main
  386.7 116.4 %all-to-all-done.1 = bf16[128,8,4608]{2,1,0:T(8,128)(2,1)} async-done(((bf16[128,8,4608]{2,1,0:T(8,128)(2,1)}), bf16[128,8,4608]{2,1,0:T(8,128)(2,1)}, u32[]{:S(2)}, u32[]{:S(2)}) %all-to-all-start.1) | async-done | bytes 9437216 | tf_op jit(solution)/shard_map/all_to_all | solution.py:548
  503.2 8.9 %combine.1 = bf16[128,4096]{1,0:T(8,128)(2,1)} custom-call(bf16[256,1024]{1,0:T(8,128)(2,1)} %pad_maximum_fusion.main, bf16[256,128]{1,0:T(8,128)(2,1)} %pad_maximum_fusion.2.late, bf16[1024,4608]{1,0:T(8,128)(2,1)} %bitcast.21.rows_ref.over_ref, bf16[1024,4608]{1,0:T(8,128)(2,1)} %bitcast.21.rows_ref.over_ref, f32[128,4096]{1,0:T(8,128)} %get-tuple-element.76.state), custom_call_target="tpu_custom_call" | custom-call | flops 4000000000 | bytes 13000000 | tf_op jit(solution)/shard_map/combine/pallas_call | solution.py:428
  (107 shorter events, 8.0 us)
Async XLA Ops:
  0.9 7.3 %collective-permute-start = (bf16[128,256]{1,0:T(8,128)(2,1)S(1)}, bf16[128,256]{1,0:T(8,128)(2,1)S(1)}, u32[]{:S(2)}, u32[]{:S(2)}) collective-permute-start(bf16[128,256]{1,0:T(8,128)(2,1)S(1)} %pad_maximum_fusion.3), channel_id=1, source_target_pairs={{0,4},{1,5},{2,6},{3,7},{4,8},{5,9},{6,10},{7,11},{8,12},{9,13},{1... | collective-permute-start | bytes 196616 | tf_op jit(solution)/shard_map/ppermute | solution.py:26
  2.6 5.9 %collective-permute-start.1 = (bf16[128,256]{1,0:T(8,128)(2,1)S(1)}, bf16[128,256]{1,0:T(8,128)(2,1)S(1)}, u32[]{:S(2)}, u32[]{:S(2)}) collective-permute-start(bf16[128,256]{1,0:T(8,128)(2,1)S(1)} %pad_maximum_fusion.4), channel_id=1, source_target_pairs={{0,8},{1,9},{2,10},{3,11},{4,12},{5,13},{6,14},{7,15},{8,0},{9,1},... | collective-permute-start | bytes 196616 | tf_op jit(solution)/shard_map/ppermute | solution.py:26
  5.4 4.3 collective-permute-start.2
  8.2 56.4 %copy-start = (bf16[256,1024]{1,0:T(8,128)(2,1)}, bf16[256,1024]{1,0:T(8,128)(2,1)S(1)}, u32[]{:S(2)}) copy-start(bf16[256,1024]{1,0:T(8,128)(2,1)S(1)} %get-tuple-element.58.refs_6_) | copy-start | bytes 1572868
  9.8 29.3 %copy-start.1 = (bf16[4,128,256]{2,1,0:T(8,128)(2,1)}, bf16[4,128,256]{2,1,0:T(8,128)(2,1)S(1)}, u32[]{:S(2)}) copy-start(bf16[4,128,256]{2,1,0:T(8,128)(2,1)S(1)} %pad_maximum_fusion.1.refs_0_) | copy-start | bytes 786436
  9.8 47.7 %copy-start.5 = (s32[4]{0:T(128)S(1)}, s32[4]{0:T(128)}, u32[]{:S(2)}) copy-start(s32[4]{0:T(128)} %param.14) | copy-start | bytes 52
  9.8 15.8 %collective-permute-start.19 = (bf16[256,1024]{1,0:T(8,128)(2,1)S(1)}, bf16[256,1024]{1,0:T(8,128)(2,1)S(1)}, u32[]{:S(2)}, u32[]{:S(2)}) collective-permute-start(bf16[256,1024]{1,0:T(8,128)(2,1)S(1)} %get-tuple-element.57), channel_id=1, source_target_pairs={{0,4},{1,5},{2,6},{3,7},{4,8},{5,9},{6,10},{7,11},{8,12},{9,13},{1... | collective-permute-start | bytes 1572872 | tf_op jit(solution)/shard_map/ppermute | solution.py:26
  10.4 24.9 %collective-permute-start.20 = (bf16[256,1024]{1,0:T(8,128)(2,1)S(1)}, bf16[256,1024]{1,0:T(8,128)(2,1)S(1)}, u32[]{:S(2)}, u32[]{:S(2)}) collective-permute-start(bf16[256,1024]{1,0:T(8,128)(2,1)S(1)} %get-tuple-element.57), channel_id=1, source_target_pairs={{0,8},{1,9},{2,10},{3,11},{4,12},{5,13},{6,14},{7,15},{8,0},{9,1},... | collective-permute-start | bytes 1572872 | tf_op jit(solution)/shard_map/ppermute | solution.py:26
  14.0 21.3 %collective-permute-start.21 = (bf16[256,1024]{1,0:T(8,128)(2,1)S(1)}, bf16[256,1024]{1,0:T(8,128)(2,1)S(1)}, u32[]{:S(2)}, u32[]{:S(2)}) collective-permute-start(bf16[256,1024]{1,0:T(8,128)(2,1)S(1)} %get-tuple-element.57), channel_id=1, source_target_pairs={{0,12},{1,13},{2,14},{3,15},{4,0},{5,1},{6,2},{7,3},{8,4},{9,5},{1... | collective-permute-start | bytes 1572872 | tf_op jit(solution)/shard_map/ppermute | solution.py:26
  35.3 58.2 %copy-start.2 = (bf16[1024,1024]{1,0:T(8,128)(2,1)}, bf16[1024,1024]{1,0:T(8,128)(2,1)S(1)}, u32[]{:S(2)}) copy-start(bf16[1024,1024]{1,0:T(8,128)(2,1)S(1)} %constant_dynamic-update-slice_fusion.refs_4_) | copy-start | bytes 6291460
  35.3 78.2 %collective-permute-start.22 = (bf16[1024,1024]{1,0:T(8,128)(2,1)S(1)}, bf16[1024,1024]{1,0:T(8,128)(2,1)}, u32[]{:S(2)}, u32[]{:S(2)}) collective-permute-start(bf16[1024,1024]{1,0:T(8,128)(2,1)S(1)} %constant_dynamic-update-slice_fusion.refs_4_), channel_id=1, source_target_pairs={{0,32},{32,0},{64,96},{96,64},{1,33},{33,1},{65,97},{97,65},{2,34}... | collective-permute-start | bytes 6291464 | tf_op jit(solution)/shard_map/ppermute | solution.py:46
  35.4 8.7 %collective-permute-start.3 = (bf16[4,128,256]{2,1,0:T(8,128)(2,1)S(1)}, bf16[4,128,256]{2,1,0:T(8,128)(2,1)S(1)}, u32[]{:S(2)}, u32[]{:S(2)}) collective-permute-start(bf16[4,128,256]{2,1,0:T(8,128)(2,1)S(1)} %pad_maximum_fusion.1.refs_0_), channel_id=1, source_target_pairs={{0,16},{16,0},{1,17},{17,1},{2,18},{18,2},{3,19},{19,3},{4,20},{20... | collective-permute-start | bytes 786440 | tf_op jit(solution)/shard_map/ppermute | solution.py:42
  37.2 11.1 %collective-permute-start.4 = (bf16[4,128,256]{2,1,0:T(8,128)(2,1)S(1)}, bf16[4,128,256]{2,1,0:T(8,128)(2,1)S(1)}, u32[]{:S(2)}, u32[]{:S(2)}) collective-permute-start(bf16[4,128,256]{2,1,0:T(8,128)(2,1)S(1)} %pad_maximum_fusion.1.refs_0_), channel_id=1, source_target_pairs={{0,1},{1,2},{2,3},{3,0},{4,5},{5,6},{6,7},{7,4},{8,9},{9,10},{10,1... | collective-permute-start | bytes 786440 | tf_op jit(solution)/shard_map/ppermute | solution.py:34
  39.1 9.2 %collective-permute-start.5 = (bf16[4,128,256]{2,1,0:T(8,128)(2,1)S(1)}, bf16[4,128,256]{2,1,0:T(8,128)(2,1)S(1)}, u32[]{:S(2)}, u32[]{:S(2)}) collective-permute-start(bf16[4,128,256]{2,1,0:T(8,128)(2,1)S(1)} %pad_maximum_fusion.1.refs_0_), channel_id=1, source_target_pairs={{0,3},{1,0},{2,1},{3,2},{4,7},{5,4},{6,5},{7,6},{8,11},{9,8},{10,9... | collective-permute-start | bytes 786440 | tf_op jit(solution)/shard_map/ppermute | solution.py:34
  44.2 31.2 %copy-start.15 = (bf16[4,128,256]{2,1,0:T(8,128)(2,1)}, bf16[4,128,256]{2,1,0:T(8,128)(2,1)S(1)}, u32[]{:S(2)}) copy-start(bf16[4,128,256]{2,1,0:T(8,128)(2,1)S(1)} %collective-permute-done.3.refs_1_) | copy-start | bytes 786436
  44.2 9.5 %collective-permute-start.7 = (bf16[4,128,256]{2,1,0:T(8,128)(2,1)S(1)}, bf16[4,128,256]{2,1,0:T(8,128)(2,1)}, u32[]{:S(2)}, u32[]{:S(2)}) collective-permute-start(bf16[4,128,256]{2,1,0:T(8,128)(2,1)S(1)} %collective-permute-done.3.refs_1_), channel_id=1, source_target_pairs={{0,3},{1,0},{2,1},{3,2},{4,7},{5,4},{6,5},{7,6},{8,11},{9,8},{10,9... | collective-permute-start | bytes 786440 | tf_op jit(solution)/shard_map/ppermute | solution.py:34
  48.3 27.0 %copy-start.16 = (bf16[4,128,256]{2,1,0:T(8,128)(2,1)}, bf16[4,128,256]{2,1,0:T(8,128)(2,1)S(1)}, u32[]{:S(2)}) copy-start(bf16[4,128,256]{2,1,0:T(8,128)(2,1)S(1)} %collective-permute-done.4.refs_2_) | copy-start | bytes 786436
  48.3 27.0 %copy-start.18 = (bf16[4,128,256]{2,1,0:T(8,128)(2,1)}, bf16[4,128,256]{2,1,0:T(8,128)(2,1)S(1)}, u32[]{:S(2)}) copy-start(bf16[4,128,256]{2,1,0:T(8,128)(2,1)S(1)} %collective-permute-done.5.refs_4_) | copy-start | bytes 786436
  48.3 10.6 %collective-permute-start.8 = (bf16[4,128,256]{2,1,0:T(8,128)(2,1)S(1)}, bf16[4,128,256]{2,1,0:T(8,128)(2,1)}, u32[]{:S(2)}, u32[]{:S(2)}) collective-permute-start(bf16[4,128,256]{2,1,0:T(8,128)(2,1)S(1)} %collective-permute-done.4.refs_2_), channel_id=1, source_target_pairs={{0,1},{1,2},{2,3},{3,0},{4,5},{5,6},{6,7},{7,4},{8,9},{9,10},{10,1... | collective-permute-start | bytes 786440 | tf_op jit(solution)/shard_map/ppermute | solution.py:34
  49.6 15.0 %collective-permute-start.6 = (bf16[4,128,256]{2,1,0:T(8,128)(2,1)S(1)}, bf16[4,128,256]{2,1,0:T(8,128)(2,1)}, u32[]{:S(2)}, u32[]{:S(2)}) collective-permute-start(bf16[4,128,256]{2,1,0:T(8,128)(2,1)S(1)} %collective-permute-done.3.refs_1_), channel_id=1, source_target_pairs={{0,1},{1,2},{2,3},{3,0},{4,5},{5,6},{6,7},{7,4},{8,9},{9,10},{10,1... | collective-permute-start | bytes 786440 | tf_op jit(solution)/shard_map/ppermute | solution.py:34
  53.6 21.7 %collective-permute-start.9 = (bf16[4,128,256]{2,1,0:T(8,128)(2,1)}, bf16[4,128,256]{2,1,0:T(8,128)(2,1)}, u32[]{:S(2)}, u32[]{:S(2)}) collective-permute-start(bf16[4,128,256]{2,1,0:T(8,128)(2,1)} %collective-permute-done.7.refs_5_), channel_id=1, source_target_pairs={{0,3},{1,0},{2,1},{3,2},{4,7},{5,4},{6,5},{7,6},{8,11},{9,8},{10,9... | collective-permute-start | bytes 786440 | tf_op jit(solution)/shard_map/ppermute | solution.py:34
  58.1 36.2 %collective-permute-start.16 = (bf16[256,1024]{1,0:T(8,128)(2,1)S(1)}, bf16[256,1024]{1,0:T(8,128)(2,1)S(1)}, u32[]{:S(2)}, u32[]{:S(2)}) collective-permute-start(bf16[256,1024]{1,0:T(8,128)(2,1)S(1)} %get-tuple-element.58.refs_6_), channel_id=1, source_target_pairs={{0,1},{1,2},{2,3},{3,0},{4,5},{5,6},{6,7},{7,4},{8,9},{9,10},{10,1... | collective-permute-start | bytes 1572872 | tf_op jit(solution)/shard_map/ppermute | solution.py:34
  58.9 38.8 %collective-permute-start.17 = (bf16[256,1024]{1,0:T(8,128)(2,1)S(1)}, bf16[256,1024]{1,0:T(8,128)(2,1)S(1)}, u32[]{:S(2)}, u32[]{:S(2)}) collective-permute-start(bf16[256,1024]{1,0:T(8,128)(2,1)S(1)} %get-tuple-element.58.refs_6_), channel_id=1, source_target_pairs={{0,2},{1,3},{2,0},{3,1},{4,6},{5,7},{6,4},{7,5},{8,10},{9,11},{10,... | collective-permute-start | bytes 1572872 | tf_op jit(solution)/shard_map/ppermute | solution.py:34
  64.5 33.2 %collective-permute-start.18 = (bf16[256,1024]{1,0:T(8,128)(2,1)S(1)}, bf16[256,1024]{1,0:T(8,128)(2,1)S(1)}, u32[]{:S(2)}, u32[]{:S(2)}) collective-permute-start(bf16[256,1024]{1,0:T(8,128)(2,1)S(1)} %get-tuple-element.58.refs_6_), channel_id=1, source_target_pairs={{0,3},{1,0},{2,1},{3,2},{4,7},{5,4},{6,5},{7,6},{8,11},{9,8},{10,9... | collective-permute-start | bytes 1572872 | tf_op jit(solution)/shard_map/ppermute | solution.py:34
  93.6 7.9 %collective-permute-start.10 = (bf16[512,256]{1,0:T(8,128)(2,1)}, bf16[512,256]{1,0:T(8,128)(2,1)S(1)}, u32[]{:S(2)}, u32[]{:S(2)}) collective-permute-start(bf16[512,256]{1,0:T(8,128)(2,1)} %get-tuple-element.45), channel_id=1, source_target_pairs={{0,4},{1,5},{2,6},{3,7},{4,8},{5,9},{6,10},{7,11},{8,12},{9,13},{1... | collective-permute-start | bytes 786440 | tf_op jit(solution)/shard_map/ppermute | solution.py:26
  94.3 19.3 %copy-start.7 = (bf16[256,1024]{1,0:T(8,128)(2,1)}, bf16[256,1024]{1,0:T(8,128)(2,1)S(1)}, u32[]{:S(2)}) copy-start(bf16[256,1024]{1,0:T(8,128)(2,1)S(1)} %collective-permute-done.16.refs_7_) | copy-start | bytes 1572868
  94.3 10.8 %collective-permute-start.11 = (bf16[512,256]{1,0:T(8,128)(2,1)}, bf16[512,256]{1,0:T(8,128)(2,1)S(1)}, u32[]{:S(2)}, u32[]{:S(2)}) collective-permute-start(bf16[512,256]{1,0:T(8,128)(2,1)} %get-tuple-element.46), channel_id=1, source_target_pairs={{0,8},{1,9},{2,10},{3,11},{4,12},{5,13},{6,14},{7,15},{8,0},{9,1},... | collective-permute-start | bytes 786440 | tf_op jit(solution)/shard_map/ppermute | solution.py:26
  97.7 15.8 %copy-start.8 = (bf16[256,1024]{1,0:T(8,128)(2,1)}, bf16[256,1024]{1,0:T(8,128)(2,1)S(1)}, u32[]{:S(2)}) copy-start(bf16[256,1024]{1,0:T(8,128)(2,1)S(1)} %collective-permute-done.17.refs_8_) | copy-start | bytes 1572868
  97.7 11.2 %collective-permute-start.12 = (bf16[512,256]{1,0:T(8,128)(2,1)}, bf16[512,256]{1,0:T(8,128)(2,1)S(1)}, u32[]{:S(2)}, u32[]{:S(2)}) collective-permute-start(bf16[512,256]{1,0:T(8,128)(2,1)} %get-tuple-element.47), channel_id=1, source_target_pairs={{0,12},{1,13},{2,14},{3,15},{4,0},{5,1},{6,2},{7,3},{8,4},{9,5},{1... | collective-permute-start | bytes 786440 | tf_op jit(solution)/shard_map/ppermute | solution.py:26
  97.7 15.8 %copy-start.10 = (bf16[256,1024]{1,0:T(8,128)(2,1)}, bf16[256,1024]{1,0:T(8,128)(2,1)S(1)}, u32[]{:S(2)}) copy-start(bf16[256,1024]{1,0:T(8,128)(2,1)S(1)} %collective-permute-done.18.refs_9_) | copy-start | bytes 1572868
  97.7 11.2 %collective-permute-start.13 = (bf16[512,256]{1,0:T(8,128)(2,1)}, bf16[512,256]{1,0:T(8,128)(2,1)S(1)}, u32[]{:S(2)}, u32[]{:S(2)}) collective-permute-start(bf16[512,256]{1,0:T(8,128)(2,1)} %get-tuple-element.49), channel_id=1, source_target_pairs={{0,1},{1,2},{2,3},{3,0},{4,5},{5,6},{6,7},{7,4},{8,9},{9,10},{10,1... | collective-permute-start | bytes 786440 | tf_op jit(solution)/shard_map/ppermute | solution.py:34
  101.4 12.1 %copy-start.21 = (bf16[512,256]{1,0:T(8,128)(2,1)}, bf16[512,256]{1,0:T(8,128)(2,1)S(1)}, u32[]{:S(2)}) copy-start(bf16[512,256]{1,0:T(8,128)(2,1)S(1)} %collective-permute-done.10.refs_1_) | copy-start | bytes 786436
  101.4 9.2 %collective-permute-start.14 = (bf16[512,256]{1,0:T(8,128)(2,1)}, bf16[512,256]{1,0:T(8,128)(2,1)S(1)}, u32[]{:S(2)}, u32[]{:S(2)}) collective-permute-start(bf16[512,256]{1,0:T(8,128)(2,1)} %get-tuple-element.50), channel_id=1, source_target_pairs={{0,2},{1,3},{2,0},{3,1},{4,6},{5,7},{6,4},{7,5},{8,10},{9,11},{10,... | collective-permute-start | bytes 786440 | tf_op jit(solution)/shard_map/ppermute | solution.py:34
  105.1 8.4 %collective-permute-start.15 = (bf16[512,256]{1,0:T(8,128)(2,1)}, bf16[512,256]{1,0:T(8,128)(2,1)S(1)}, u32[]{:S(2)}, u32[]{:S(2)}) collective-permute-start(bf16[512,256]{1,0:T(8,128)(2,1)} %get-tuple-element.51), channel_id=1, source_target_pairs={{0,3},{1,0},{2,1},{3,2},{4,7},{5,4},{6,5},{7,6},{8,11},{9,8},{10,9... | collective-permute-start | bytes 786440 | tf_op jit(solution)/shard_map/ppermute | solution.py:34
  110.7 71.6 %copy-start.19 = (bf16[512,256]{1,0:T(8,128)(2,1)}, bf16[512,256]{1,0:T(8,128)(2,1)S(1)}, u32[]{:S(2)}) copy-start(bf16[512,256]{1,0:T(8,128)(2,1)S(1)} %collective-permute-done.14.refs_2_) | copy-start | bytes 786436
  113.5 68.7 %copy-start.20 = (bf16[512,256]{1,0:T(8,128)(2,1)}, bf16[512,256]{1,0:T(8,128)(2,1)S(1)}, u32[]{:S(2)}) copy-start(bf16[512,256]{1,0:T(8,128)(2,1)S(1)} %collective-permute-done.15.refs_3_) | copy-start | bytes 786436
  113.5 68.9 %copy-start.3 = (f32[128,8]{0,1:T(8,128)S(1)}, f32[128,8]{0,1:T(8,128)}, u32[]{:S(2)}) copy-start(f32[128,8]{0,1:T(8,128)} %param.19) | copy-start | bytes 12292
  113.5 68.9 %copy-start.4 = (s32[128,8]{0,1:T(8,128)S(1)}, s32[128,8]{0,1:T(8,128)}, u32[]{:S(2)}) copy-start(s32[128,8]{0,1:T(8,128)} %param.18) | copy-start | bytes 12292
  182.3 5.4 %collective-permute-start.26 = (bf16[1024,1024]{1,0:T(8,128)(2,1)}, bf16[1024,1024]{1,0:T(8,128)(2,1)S(1)}, u32[]{:S(2)}, u32[]{:S(2)}) collective-permute-start(bf16[1024,1024]{1,0:T(8,128)(2,1)} %get-tuple-element.70.refs_4_), channel_id=1, source_target_pairs={{0,32},{32,0},{64,96},{96,64},{1,33},{33,1},{65,97},{97,65},{2,34}... | collective-permute-start | bytes 6291464 | tf_op jit(solution)/shard_map/ppermute | solution.py:46
  182.3 16.0 %collective-permute-start.23 = (bf16[128,2048]{1,0:T(8,128)(2,1)}, bf16[128,2048]{1,0:T(8,128)(2,1)S(1)}, u32[]{:S(2)}, u32[]{:S(2)}) collective-permute-start(bf16[128,2048]{1,0:T(8,128)(2,1)} %get-tuple-element.63), channel_id=1, source_target_pairs={{0,1},{1,2},{2,3},{3,0},{4,5},{5,6},{6,7},{7,4},{8,9},{9,10},{10,1... | collective-permute-start | bytes 1572872 | tf_op jit(solution)/shard_map/ppermute | solution.py:34
  183.0 27.8 %collective-permute-start.24 = (bf16[128,2048]{1,0:T(8,128)(2,1)}, bf16[128,2048]{1,0:T(8,128)(2,1)S(1)}, u32[]{:S(2)}, u32[]{:S(2)}) collective-permute-start(bf16[128,2048]{1,0:T(8,128)(2,1)} %get-tuple-element.64), channel_id=1, source_target_pairs={{0,2},{1,3},{2,0},{3,1},{4,6},{5,7},{6,4},{7,5},{8,10},{9,11},{10,... | collective-permute-start | bytes 1572872 | tf_op jit(solution)/shard_map/ppermute | solution.py:34
  187.7 23.3 %collective-permute-start.25 = (bf16[128,2048]{1,0:T(8,128)(2,1)}, bf16[128,2048]{1,0:T(8,128)(2,1)}, u32[]{:S(2)}, u32[]{:S(2)}) collective-permute-start(bf16[128,2048]{1,0:T(8,128)(2,1)} %get-tuple-element.65), channel_id=1, source_target_pairs={{0,3},{1,0},{2,1},{3,2},{4,7},{5,4},{6,5},{7,6},{8,11},{9,8},{10,9... | collective-permute-start | bytes 1572872 | tf_op jit(solution)/shard_map/ppermute | solution.py:34
  195.5 26.4 %collective-permute-start.27 = (bf16[128,2048]{1,0:T(8,128)(2,1)}, bf16[128,2048]{1,0:T(8,128)(2,1)S(1)}, u32[]{:S(2)}, u32[]{:S(2)}) collective-permute-start(bf16[128,2048]{1,0:T(8,128)(2,1)} %get-tuple-element.72), channel_id=1, source_target_pairs={{0,4},{1,5},{2,6},{3,7},{4,8},{5,9},{6,10},{7,11},{8,12},{9,13},{1... | collective-permute-start | bytes 1572872 | tf_op jit(solution)/shard_map/ppermute | solution.py:26
  195.6 26.4 %collective-permute-start.28 = (bf16[128,2048]{1,0:T(8,128)(2,1)}, bf16[128,2048]{1,0:T(8,128)(2,1)S(1)}, u32[]{:S(2)}, u32[]{:S(2)}) collective-permute-start(bf16[128,2048]{1,0:T(8,128)(2,1)} %get-tuple-element.73), channel_id=1, source_target_pairs={{0,8},{1,9},{2,10},{3,11},{4,12},{5,13},{6,14},{7,15},{8,0},{9,1},... | collective-permute-start | bytes 1572872 | tf_op jit(solution)/shard_map/ppermute | solution.py:26
  199.1 23.5 %collective-permute-start.29 = (bf16[128,2048]{1,0:T(8,128)(2,1)}, bf16[128,2048]{1,0:T(8,128)(2,1)S(1)}, u32[]{:S(2)}, u32[]{:S(2)}) collective-permute-start(bf16[128,2048]{1,0:T(8,128)(2,1)} %get-tuple-element.74), channel_id=1, source_target_pairs={{0,12},{1,13},{2,14},{3,15},{4,0},{5,1},{6,2},{7,3},{8,4},{9,5},{1... | collective-permute-start | bytes 1572872 | tf_op jit(solution)/shard_map/ppermute | solution.py:26
  223.4 128.2 %slice-start = ((s8[6291456]{0:T(1024)(128)(4,1)}), s8[2097152]{0:T(1024)(128)(4,1)S(1)}, s32[]{:S(2)}) async-start(s8[6291456]{0:T(1024)(128)(4,1)} %bitcast.32), calls=%async_computation.2 | async-start | bytes 4194304
  233.4 118.2 %slice-start.1 = ((s8[6291456]{0:T(1024)(128)(4,1)}), s8[4194304]{0:T(1024)(128)(4,1)S(1)}, s32[]{:S(2)}) async-start(s8[6291456]{0:T(1024)(128)(4,1)} %bitcast.32), calls=%async_computation.3 | async-start | bytes 8388608
  377.8 125.4 %all-to-all-start.1 = ((bf16[128,8,4608]{2,1,0:T(8,128)(2,1)}), bf16[128,8,4608]{2,1,0:T(8,128)(2,1)}, u32[]{:S(2)}, u32[]{:S(2)}) async-start(bf16[128,8,4608]{2,1,0:T(8,128)(2,1)} %bitcast.34), calls=%async_computation.1 | async-start | bytes 18874368 | tf_op jit(solution)/shard_map/all_to_all | solution.py:548
  (9 other events, 34.4 us)

commit v4 on v3

--- a/solution.py
+++ b/solution.py
@@ -89,14 +89,88 @@
     return lax.dot_general(left, right, (((1,), (1,)), ((), ())), preferred_element_type=F32)
 
 
+def rows_of(chunk):
+    return pl.ds(pl.multiple_of(chunk * BLOCK, BLOCK), BLOCK)
+
+
+def attend(meta, chunk, q_ref, keys, values, scratch):
+    sums, peaks, totals, even, odd = scratch[0], scratch[1], scratch[2], scratch[3:5], scratch[5:7]
+    factor = math.log2(math.e) / math.sqrt(HD)
+    mine = meta[meta[4] * 2 + chunk // 2] * 2 + lax.rem(chunk, 2)
+    heads = [q_ref[rows_of(chunk), head * HD : (head + 1) * HD] for head in range(2)]
+    for head in range(2):
+        sums[head] = jnp.zeros((HD, BLOCK), F32)
+        peaks[head] = jnp.full((1, BLOCK), NEGATIVE, F32)
+        totals[head] = jnp.zeros((1, BLOCK), F32)
+
+    def score(number, held):
+        key_block = keys[rows_of(number), :]
+        for head in range(2):
+            held[head][...] = dot_nt(key_block, heads[head])
+
+    def process(number, held, masked):
+        value_block = values[:, rows_of(number)]
+        for head in range(2):
+            scores = held[head][...]
+            if masked:
+                seen = lax.broadcasted_iota(
+                    jnp.int32, (BLOCK, BLOCK), 0
+                ) <= lax.broadcasted_iota(jnp.int32, (BLOCK, BLOCK), 1)
+                scores = jnp.where(seen, scores, NEGATIVE)
+            peak = peaks[head]
+            new_peak = jnp.maximum(peak, jnp.max(scores, axis=0, keepdims=True))
+            weights = jnp.exp2(scores * factor - new_peak * factor)
+            fading = jnp.exp2((peak - new_peak) * factor)
+            peaks[head] = new_peak
+            totals[head] = totals[head] * fading + jnp.sum(weights, axis=0, keepdims=True)
+            sums[head] = sums[head] * fading + dot(value_block, weights.astype(BF16))
+
+    score(0, even)
+
+    def two(pair, carry):
+        score(2 * pair + 1, odd)
+        process(2 * pair, even, False)
+        score(2 * pair + 2, even)
+        process(2 * pair + 1, odd, False)
+        return carry
+
+    lax.fori_loop(0, mine // 2, two, 0)
+
+    @pl.when(lax.rem(mine, 2) == 1)
+    def _():
+        score(mine, odd)
+        process(mine - 1, even, False)
+        process(mine, odd, True)
+
+    @pl.when(lax.rem(mine, 2) == 0)
+    def _():
+        process(mine, even, True)
+
+    return jnp.concatenate(
+        [(sums[head] / totals[head]).T.astype(BF16) for head in range(2)], axis=1
+    )
+
+
+def attend_scratch():
+    return [
+        pltpu.VMEM((2, HD, BLOCK), F32),
+        pltpu.VMEM((2, 1, BLOCK), F32),
+        pltpu.VMEM((2, 1, BLOCK), F32),
+    ] + [pltpu.VMEM((BLOCK, BLOCK), F32)] * 4
+
+
+def join(pieces, joined):
+    rows = pieces[0].shape[0]
+    for number, piece in enumerate(pieces):
+        joined[number * rows : (number + 1) * rows, :] = piece[...]
+
+
 def attention_kernel(meta, q_ref, *refs):
-    pieces, refs = refs[:8], refs[8:]
-    outs_x, outs_z, refs = refs[:4], refs[4:8], refs[8:]
-    keys, values, sums, peaks, totals, context = refs[:6]
-    even, odd = refs[6:8], refs[8:10]
+    pieces, weights, refs = refs[:8], refs[8:12], refs[12:]
+    outs, keys, values, joined, context, scratch = refs[:3], *refs[3:7], refs[7:]
     ctx, x, z = meta[4], meta[5], meta[6]
-    factor = math.log2(math.e) / math.sqrt(HD)
-
+
+    join(weights, joined)
     for number, piece in enumerate(pieces):
         part = lax.rem(ctx + number % 2, 2)
         back = (0, 1, 3, 2)[number // 2]
@@ -108,111 +182,74 @@
             keys[rows, :] = piece[block, :, :HD]
             values[:, rows] = piece[block, :, HD:].T
 
-    def rows_of(chunk):
-        return pl.ds(pl.multiple_of(chunk * BLOCK, BLOCK), BLOCK)
-
-    @pl.loop(0, SIDE)
-    def _(chunk):
-        mine = meta[ctx * 2 + chunk // 2] * 2 + lax.rem(chunk, 2)
-        heads = [q_ref[rows_of(chunk), head * HD : (head + 1) * HD] for head in range(2)]
-        for head in range(2):
-            sums[head] = jnp.zeros((HD, BLOCK), F32)
-            peaks[head] = jnp.full((1, BLOCK), NEGATIVE, F32)
-            totals[head] = jnp.zeros((1, BLOCK), F32)
-
-        def score(number, held):
-            key_block = keys[rows_of(number), :]
-            for head in range(2):
-                held[head][...] = dot_nt(key_block, heads[head])
-
-        def process(number, held, masked):
-            value_block = values[:, rows_of(number)]
-            for head in range(2):
-                scores = held[head][...]
-                if masked:
-                    seen = lax.broadcasted_iota(
-                        jnp.int32, (BLOCK, BLOCK), 0
-                    ) <= lax.broadcasted_iota(jnp.int32, (BLOCK, BLOCK), 1)
-                    scores = jnp.where(seen, scores, NEGATIVE)
-                peak = peaks[head]
-                new_peak = jnp.maximum(peak, jnp.max(scores, axis=0, keepdims=True))
-                weights = jnp.exp2(scores * factor - new_peak * factor)
-                fading = jnp.exp2((peak - new_peak) * factor)
-                peaks[head] = new_peak
-                totals[head] = totals[head] * fading + jnp.sum(weights, axis=0, keepdims=True)
-                sums[head] = sums[head] * fading + dot(value_block, weights.astype(BF16))
-
-        score(0, even)
-
-        def two(pair, carry):
-            score(2 * pair + 1, odd)
-            process(2 * pair, even, False)
-            score(2 * pair + 2, even)
-            process(2 * pair + 1, odd, False)
-            return carry
-
-        lax.fori_loop(0, mine // 2, two, 0)
-
-        @pl.when(lax.rem(mine, 2) == 1)
-        def _():
-            score(mine, odd)
-            process(mine - 1, even, False)
-            process(mine, odd, True)
-
-        @pl.when(lax.rem(mine, 2) == 0)
-        def _():
-            process(mine, even, True)
-
-        for head in range(2):
-            context[rows_of(chunk), head * HD : (head + 1) * HD] = (
-                (sums[head] / totals[head]).T.astype(BF16)
-            )
-
-    for step_of in range(SIDE):
-        to_x = lax.rem(x + step_of, SIDE)
-        to_z = lax.rem(z + step_of, SIDE)
-        outs_x[step_of][...] = context[pl.ds(pl.multiple_of(to_x * BLOCK, BLOCK), BLOCK), :]
-        for block in range(SIDE):
-            rows = pl.ds(pl.multiple_of(block * BLOCK + to_z * TOKENS, TOKENS), TOKENS)
-            outs_z[step_of][block * TOKENS : (block + 1) * TOKENS, :] = context[rows, :]
-
-
-def attention(meta, queries, pieces):
+    @pl.loop(0, SIDE - 1)
+    def _(number):
+        chunk = lax.rem(x + 1 + number, SIDE)
+        context[number] = attend(meta, chunk, q_ref, keys, values, scratch)
+
+    for number, out in enumerate(outs):
+        out[...] = context[number]
+
+
+def attention(meta, queries, pieces, weights):
     rows, width = queries.shape
+    arrays = (queries, *pieces, *weights)
+    outs = [jax.ShapeDtypeStruct((BLOCK, width), BF16)] * 3 + [
+        jax.ShapeDtypeStruct((2 * rows, HD), BF16),
+        jax.ShapeDtypeStruct((HD, 2 * rows), BF16),
+        jax.ShapeDtypeStruct((SIDE * weights[0].shape[0], weights[0].shape[1]), BF16),
+    ]
     return call(
         attention_kernel,
         "attention",
-        [jax.ShapeDtypeStruct((BLOCK, width), BF16)] * 8,
-        [smem(), whole(queries)] + [whole(piece) for piece in pieces],
-        [pl.BlockSpec((BLOCK, width), lambda: (0, 0))] * 8,
-        scratch=[
-            pltpu.VMEM((2 * rows, HD), BF16),
-            pltpu.VMEM((HD, 2 * rows), BF16),
-            pltpu.VMEM((2, HD, BLOCK), F32),
-            pltpu.VMEM((2, 1, BLOCK), F32),
-            pltpu.VMEM((2, 1, BLOCK), F32),
-            pltpu.VMEM((rows, width), BF16),
-        ]
-        + [pltpu.VMEM((BLOCK, BLOCK), F32)] * 4,
+        outs,
+        [smem()] + [whole(array) for array in arrays],
+        [pl.BlockSpec(out.shape, lambda: (0, 0)) for out in outs],
+        scratch=[pltpu.VMEM((3, BLOCK, width), BF16), *attend_scratch()],
         cost=pl.CostEstimate(
-            flops=7 * 10**9, bytes_accessed=5 * 10**6, transcendentals=14 * 10**6
+            flops=16 * 10**9, bytes_accessed=7 * 10**6, transcendentals=10 * 10**6
         ),
-    )(meta, queries, *pieces)
-
-
-def projection_kernel(axis, n_pieces, meta, *refs):
-    context, weights, pieces, refs = refs[:4], refs[4:6], refs[6 : 6 + n_pieces], refs[6 + n_pieces :]
-    outs, refs = refs[:4], refs[4:]
-    joined, held, done = refs if n_pieces else (None, *refs)
+    )(meta, *arrays)
+
+
+def attention_end_kernel(meta, q_ref, keys, values, *refs):
+    others, weights, out, refs = refs[:3], refs[3:7], refs[7], refs[8:]
+    outs_z, joined, scratch = refs[:4], refs[4], refs[5:]
+    x, z = meta[5], meta[6]
+    join(weights, joined)
+    out[...] = attend(meta, x, q_ref, keys, values, scratch)
+    for number, context in enumerate((out, *others)):
+        x_of = lax.rem(x + number, SIDE)
+        rows = pl.ds(pl.multiple_of(x_of * TOKENS, TOKENS), TOKENS)
+        for step_of in range(SIDE):
+            to_z = lax.rem(z + step_of, SIDE)
+            part = pl.ds(pl.multiple_of(to_z * TOKENS, TOKENS), TOKENS)
+            outs_z[step_of][rows, :] = context[part, :]
+
+
+def attention_end(meta, queries, keys, values, others, weights):
+    width = queries.shape[1]
+    arrays = (queries, keys, values, *others, *weights)
+    outs = [jax.ShapeDtypeStruct((BLOCK, width), BF16)] * 5
+    outs.append(jax.ShapeDtypeStruct((SIDE * weights[0].shape[0], weights[0].shape[1]), BF16))
+    return call(
+        attention_end_kernel,
+        "attention_end",
+        outs,
+        [smem()] + [whole(array) for array in arrays],
+        [pl.BlockSpec(out.shape, lambda: (0, 0)) for out in outs],
+        scratch=attend_scratch(),
+        cost=pl.CostEstimate(
+            flops=6 * 10**9, bytes_accessed=7 * 10**6, transcendentals=3 * 10**6
+        ),
+    )(meta, *arrays)
+
+
+def projection_kernel(axis, meta, *refs):
+    context, weights, outs, held = refs[:4], refs[4:6], refs[6:10], refs[10]
     me = meta[axis]
     width = context[0].shape[1]
     columns = 256
-    copies = [
-        pltpu.make_async_copy(piece, joined.at[pl.ds(i * width, width), :], done.at[i])
-        for i, piece in enumerate(pieces)
-    ]
-    for copy in copies:
-        copy.start()
     for side, weight in enumerate(weights):
         for start in range(0, weight.shape[1], columns):
             total = None
@@ -226,30 +263,22 @@
     for number, out in enumerate(outs):
         to = lax.rem(me + number, SIDE)
         out[...] = held[pl.ds(pl.multiple_of(to * TOKENS, TOKENS), TOKENS), :]
-    for copy in copies:
-        copy.wait()
-
-
-def projection(axis, meta, context, weights, pieces=()):
+
+
+def projection(axis, meta, context, weights):
     columns = 2 * weights[0].shape[1]
-    any_space = pl.BlockSpec(memory_space=pl.ANY)
-    joined = [jax.ShapeDtypeStruct(weights[0].shape, BF16)] if pieces else []
+    arrays = (*context, *weights)
     return call(
-        functools.partial(projection_kernel, axis, len(pieces)),
+        functools.partial(projection_kernel, axis),
         "projection",
-        [jax.ShapeDtypeStruct((TOKENS, columns), BF16)] * 4 + joined,
-        [smem()]
-        + [whole(array) for array in (*context, *weights)]
-        + [any_space for _ in pieces],
-        [pl.BlockSpec((TOKENS, columns), lambda: (0, 0))] * 4 + [any_space for _ in joined],
-        scratch=[
-            pltpu.VMEM((SIDE * TOKENS, columns), BF16),
-            pltpu.SemaphoreType.DMA((SIDE,)),
-        ],
+        [jax.ShapeDtypeStruct((TOKENS, columns), BF16)] * 4,
+        [smem()] + [whole(array) for array in arrays],
+        [pl.BlockSpec((TOKENS, columns), lambda: (0, 0))] * 4,
+        scratch=[pltpu.VMEM((SIDE * TOKENS, columns), BF16)],
         cost=pl.CostEstimate(
             flops=2 * 512 * 1024 * columns, bytes_accessed=7 * 10**6, transcendentals=0
         ),
-    )(meta, *context, *weights, *pieces)
+    )(meta, *arrays)
 
 
 def wide_scratch():
@@ -504,19 +533,17 @@
     def weights_part(base):
         return lax.dynamic_slice_in_dim(out_proj, base + core * quarter, quarter, 1)
 
+    def after(value, *others):
+        return lax.optimization_barrier((value, *others))[0]
+
     own = jnp.stack(exchange(shift_x, [head_block(step) for step in range(SIDE)]))
-    own, part_x = lax.optimization_barrier((own, weights_part(0)))
     other = swap_ctx(own)
     before_own, after_own = shift_z(own, 1), shift_z(own, -1)
-    before_own, after_own, part_z = lax.optimization_barrier(
-        (before_own, after_own, weights_part(width // 2))
-    )
     before_other, after_other = shift_z(other, 1), shift_z(other, -1)
     far_own = shift_z(before_own, 1)
     far_other = shift_z(after_other, -1)
-    weights_x = jnp.concatenate(gather_rows_of(shift_x, part_x), axis=0)
-    other_x = swap_core(weights_x)
-    weights_z = gather_rows_of(shift_z, part_z)
+    weights_x = gather_rows_of(shift_x, after(weights_part(0), own))
+    weights_z = gather_rows_of(shift_z, after(weights_part(width // 2), far_own, far_other))
     pieces = [
         own,
         other,
@@ -530,12 +557,14 @@
 
     maps = routes(expert_ids, route_weights, n_devices)
 
-    parts = attention(meta, queries, pieces)
-    context_x = exchange(shift_x, parts[:4])
-    context_z = exchange(shift_z, parts[4:])
-    context_x, context_z, weights_z = lax.optimization_barrier((context_x, context_z, weights_z))
-    *terms_z, weights_z = projection(6, meta, context_x, [weights_x, other_x], weights_z)
-    terms_x = projection(5, meta, context_z, [weights_z, swap_core(weights_z)])
+    *far, keys, values, weights_x = attention(meta, queries, pieces, weights_x)
+    other_x = swap_core(weights_x)
+    mine, *parts, weights_z = attention_end(meta, queries, keys, values, far, weights_z)
+    other_z = swap_core(weights_z)
+    context_x = exchange(shift_x, [mine, *far])
+    context_z = exchange(shift_z, parts)
+    terms_z = projection(6, meta, context_x, [weights_x, other_x])
+    terms_x = projection(5, meta, context_z, [weights_z, other_z])
     terms_z, terms_x = exchange(shift_z, terms_z), exchange(shift_x, terms_x)
     main, late, back_main, back_late = maps
 

time: 518 us -> 441 us (0.85)
  Pallas kernels: 139 us -> 76.9 us
  waiting for transfers between devices: 190 us -> 168 us
  blocking collectives: 118 us -> 127 us
  starting transfers between devices: 54.8 us -> 48.5 us
    pallas_call x3 -> x4, Pallas kernels: 93.4 us -> 31.7 us  [the longest x2 12.9 us: projection(): call(functools.partial(projection_kernel, axis), 'projection', [jax.Shape...]
    ppermute x12, waiting for transfers between devices: 39.6 us -> 22.2 us  [shift_x(): lax.ppermute(value, 'tp', [(x * SIDE + z, (x + step) % SIDE * SIDE + z) f...]
    all_to_all x1, blocking collectives: 118 us -> 127 us  [all_to_all(): lax.all_to_all(blocks, ('dp', 'ctx', 'tp'), split_axis=0, concat_axis=0,...]
    ppermute x15, starting transfers between devices: 28.2 us -> 22.9 us  [shift_z(): lax.ppermute(value, 'tp', [(x * SIDE + z, x * SIDE + (z + step) % SIDE) f...]
  transfers between devices with their start and end apart: 31 -> 31, of which waited for: 19 -> 13; matrix products, arithmetic and copies ran while one was open for 1% -> 1% of each run, Pallas kernels for 5% -> 7%
where the time goes in v4:
time: 441 us; the launch traced here: 436 us
  waiting for transfers between devices  168 us (38%)
  blocking collectives  127 us (29%)
  Pallas kernels  76.9 us (17%)
  starting transfers between devices  48.5 us (11%)
  local copies, waits for them, and re-layouts  13 us (3%)
    all_to_all x1, blocking collectives, all_to_all(): lax.all_to_all(blocks, ('dp', 'ctx', 'tp'), split_axis=0, concat_axis=0,...  127 us
    all_to_all x1, waiting for transfers between devices, all_to_all(): lax.all_to_all(blocks, ('dp', 'ctx', 'tp'), split_axis=0, concat_axis=0,...  116 us
    pallas_call x1, Pallas kernels, experts(): call(expert_kernel, 'experts', jax.ShapeDtypeStruct((rows, columns), BF16...  26.1 us
    ppermute x15, waiting for transfers between devices, shift_z(): lax.ppermute(value, 'tp', [(x * SIDE + z, x * SIDE + (z + step) % SIDE) f...  26.1 us
    ppermute x15, starting transfers between devices, shift_z(): lax.ppermute(value, 'tp', [(x * SIDE + z, x * SIDE + (z + step) % SIDE) f...  22.9 us
    ppermute x12, waiting for transfers between devices, shift_x(): lax.ppermute(value, 'tp', [(x * SIDE + z, (x + step) % SIDE * SIDE + z) f...  22.2 us
    ppermute x12, starting transfers between devices, shift_x(): lax.ppermute(value, 'tp', [(x * SIDE + z, (x + step) % SIDE * SIDE + z) f...  17 us
    pallas_call x2, Pallas kernels, projection(): call(functools.partial(projection_kernel, axis), 'projection', [jax.Shape...  12.9 us
  transfers between devices with their start and end apart: 31, of which 13 were waited for; matrix products, arithmetic and copies ran while one was open for 1% of the time, Pallas kernels for 7%

profile of v4, /device:TPU:0, one launch (start us, length us, event | category | flops | bytes accessed | tf_op | source)
XLA Modules:
  0.0 435.7 jit_solution(6764570624803802662)
XLA Ops:
  0.0 0.9 constant_dynamic-slice_fusion.8
  0.9 1.6 collective-permute-start
  2.6 2.8 collective-permute-start.1
  5.4 1.5 collective-permute-start.2
  6.9 1.6 collective-permute-done.1
  8.5 1.2 collective-permute-done.2
  9.8 1.7 collective-permute-start.3
  11.4 1.9 collective-permute-start.4
  13.4 3.2 collective-permute-done.3.refs_1_
  16.6 4.1 collective-permute-start.7
  20.7 1.3 constant_dynamic-slice_fusion
  22.3 3.7 collective-permute-start.11
  26.1 3.2 collective-permute-start.9
  30.4 3.9 collective-permute-done.9.refs_7_
  35.6 7.0 %collective-permute-done.6.refs_4_ = bf16[4,128,256]{2,1,0:T(8,128)(2,1)} collective-permute-done((bf16[4,128,256]{2,1,0:T(8,128)(2,1)S(1)}, bf16[4,128,256]{2,1,0:T(8,128)(2,1)}, u32[]{:S(2)}, u32[]{:S(2)}) %collective-permute-start.6) | collective-permute-done | bytes 262176 | tf_op jit(solution)/shard_map/ppermute | solution.py:34
  42.7 5.2 %collective-permute-start.14 = (bf16[256,1024]{1,0:T(8,128)(2,1)S(1)}, bf16[256,1024]{1,0:T(8,128)(2,1)S(1)}, u32[]{:S(2)}, u32[]{:S(2)}) collective-permute-start(bf16[256,1024]{1,0:T(8,128)(2,1)S(1)} %get-tuple-element.35.refs_3_), channel_id=1, source_target_pairs={{0,2},{1,3},{2,0},{3,1},{4,6},{5,7},{6,4},{7,5},{8,10},{9,11},{10,... | collective-permute-start | bytes 1572872 | tf_op jit(solution)/shard_map/ppermute | solution.py:34
  47.9 1.1 collective-permute-start.15
  49.1 0.7 copy-done.12
  49.8 11.4 %attention.1 = (bf16[512,256]{1,0:T(8,128)(2,1)}, bf16[512,256]{1,0:T(8,128)(2,1)}, bf16[512,256]{1,0:T(8,128)(2,1)}, bf16[4096,128]{1,0:T(8,128)(2,1)}, bf16[12...) custom-call(s32[8]{0:T(128)} %concatenate.23.meta, bf16[2048,256]{1,0:T(8,128)(2,1)} %q_ref.3, ...), custom_call_target="tpu_custom_call" | custom-call | flops 16000000000 | bytes 7000000 | tf_op jit(solution)/shard_map/attention/pallas_call | solution.py:202
  61.4 1.9 collective-permute-done.14.refs_5_
  63.3 0.8 copy-done.16
  64.3 7.4 %attention_end.1 = (bf16[512,256]{1,0:T(8,128)(2,1)}, bf16[512,256]{1,0:T(8,128)(2,1)}, bf16[512,256]{1,0:T(8,128)(2,1)}, bf16[512,256]{1,0:T(8,128)(2,1)}, bf16...) custom-call(s32[8]{0:T(128)} %concatenate.23.meta, bf16[2048,256]{1,0:T(8,128)(2,1)} %q_ref.3, ...), custom_call_target="tpu_custom_call" | custom-call | flops 6000000000 | bytes 7000000 | tf_op jit(solution)/shard_map/attention_end/pallas_call | solution.py:235
  71.7 2.2 collective-permute-start.16
  74.6 2.1 collective-permute-start.18
  76.7 10.5 %collective-permute-done.16.refs_1_ = bf16[512,256]{1,0:T(8,128)(2,1)S(1)} collective-permute-done((bf16[512,256]{1,0:T(8,128)(2,1)S(1)}, bf16[512,256]{1,0:T(8,128)(2,1)S(1)}, u32[]{:S(2)}, u32[]{:S(2)}) %collective-permute-start.16) | collective-permute-done | bytes 262176 | tf_op jit(solution)/shard_map/ppermute | solution.py:26
  87.2 3.6 collective-permute-start.24
  91.6 0.7 copy-done.7
  92.3 6.5 %projection.2 = (bf16[128,2048]{1,0:T(8,128)(2,1)}, bf16[128,2048]{1,0:T(8,128)(2,1)}, bf16[128,2048]{1,0:T(8,128)(2,1)}, bf16[128,2048]{1,0:T(8,128)(2,1)}) custom-call(s32[8]{0:T(128)} %concatenate.23.meta, bf16[512,256]{1,0:T(8,128)(2,1)} %get-tuple-element.36.refs_0_, bf16[512,256]{1,0:T(8,128)(2,1)} %copy-done.26, bf16[512,256]{1,0:T(8,128)(2,1)} %copy-done.27, ...), custom_call_target="tpu_custom_call" | custom-call | flops 2147483648 | bytes 7000000 | tf_op jit(solution)/shard_map/projection/pallas_call | solution.py:271
  98.8 1.9 collective-permute-start.20
  101.3 0.7 copy-done.22
  102.5 1.5 collective-permute-done.24.refs_2_
  104.0 1.1 collective-permute-start.22
  105.1 1.3 copy-done.6
  106.4 6.4 %projection.3 = (bf16[128,2048]{1,0:T(8,128)(2,1)}, bf16[128,2048]{1,0:T(8,128)(2,1)}, bf16[128,2048]{1,0:T(8,128)(2,1)}, bf16[128,2048]{1,0:T(8,128)(2,1)}) custom-call(s32[8]{0:T(128)} %concatenate.23.meta, bf16[512,256]{1,0:T(8,128)(2,1)} %get-tuple-element.42.refs_0_, bf16[512,256]{1,0:T(8,128)(2,1)} %copy-done.22, ...), custom_call_target="tpu_custom_call" | custom-call | flops 2147483648 | bytes 7000000 | tf_op jit(solution)/shard_map/projection/pallas_call | solution.py:271
  112.9 1.1 collective-permute-start.28
  114.0 11.3 %collective-permute-done.20.refs_1_ = bf16[128,2048]{1,0:T(8,128)(2,1)S(1)} collective-permute-done((bf16[128,2048]{1,0:T(8,128)(2,1)}, bf16[128,2048]{1,0:T(8,128)(2,1)S(1)}, u32[]{:S(2)}, u32[]{:S(2)}) %collective-permute-start.20) | collective-permute-done | bytes 524320 | tf_op jit(solution)/shard_map/ppermute | solution.py:34
  125.4 0.8 copy-done.8
  126.2 0.9 collective-permute-start.29
  127.5 0.8 copy.31.refs_10_
  129.1 8.1 %collective-permute-done.27.refs_5_ = bf16[128,2048]{1,0:T(8,128)(2,1)S(1)} collective-permute-done((bf16[128,2048]{1,0:T(8,128)(2,1)}, bf16[128,2048]{1,0:T(8,128)(2,1)S(1)}, u32[]{:S(2)}, u32[]{:S(2)}) %collective-permute-start.27) | collective-permute-done | bytes 524320 | tf_op jit(solution)/shard_map/ppermute | solution.py:26
  137.2 0.7 collective-permute-done.29.refs_7_
  138.1 10.0 %dispatch.1 = (bf16[1024,4608]{1,0:T(8,128)(2,1)}, f32[128,4096]{1,0:T(8,128)}) custom-call(s32[8]{0:T(128)} %concatenate.23.meta, bf16[128,2048]{1,0:T(8,128)(2,1)} %get-tuple-element.38.refs_0_, bf16[128,2048]{1,0:T(8,128)(2,1)} %copy-done.8, bf16[128,2048]{1,0:T(8,128)(2,1)} %copy-done.11, bf16[128,2048]{1,0:T(8,128)(2,1)} %collective-permute-done.22.refs_3_, ...), custom_call_target="tpu_custom_call" | custom-call | flops 3000000000 | bytes 16000000 | tf_op jit(solution)/shard_map/dispatch/pallas_call | solution.py:347
  148.2 127.0 %all_to_all.10 = bf16[128,8,4608]{2,1,0:T(8,128)(2,1)} all-to-all(bf16[128,8,4608]{2,1,0:T(8,128)(2,1)} %bitcast.35), channel_id=1, replica_groups=mesh['dp'=4,'ctx'=2,'tp'=16] {'dp','ctx','tp'}, dimensions={0} | all-to-all | bytes 18874368 | tf_op jit(solution)/shard_map/all_to_all | solution.py:577
  275.2 26.1 %experts.1 = bf16[1024,4608]{1,0:T(8,128)(2,1)} custom-call(bf16[1024,4608]{1,0:T(8,128)(2,1)} %bitcast.36, bf16[1024,4608]{1,0:T(8,128)(2,1)} %bitcast.37, bf16[1,4096,768]{2,1,0:T(8,128)(2,1)S(1)} %bitcast.33, bf16[1,768,4096]{2,1,0:T(8,128)(2,1)} %down_hbm.1), custom_call_target="tpu_custom_call" | custom-call | flops 14495514624 | bytes 32000000 | tf_op jit(solution)/shard_map/experts/pallas_call | solution.py:406
  301.4 6.9 %all-to-all-start.1 = ((bf16[128,8,4608]{2,1,0:T(8,128)(2,1)}), bf16[128,8,4608]{2,1,0:T(8,128)(2,1)}, u32[]{:S(2)}, u32[]{:S(2)}) async-start(bf16[128,8,4608]{2,1,0:T(8,128)(2,1)} %bitcast.34), calls=%async_computation.1 | async-start | bytes 18874368 | tf_op jit(solution)/shard_map/all_to_all | solution.py:577
  309.6 0.8 pad_maximum_fusion.main
  310.4 116.4 %all-to-all-done.1 = bf16[128,8,4608]{2,1,0:T(8,128)(2,1)} async-done(((bf16[128,8,4608]{2,1,0:T(8,128)(2,1)}), bf16[128,8,4608]{2,1,0:T(8,128)(2,1)}, u32[]{:S(2)}, u32[]{:S(2)}) %all-to-all-start.1) | async-done | bytes 9437216 | tf_op jit(solution)/shard_map/all_to_all | solution.py:577
  426.8 8.9 %combine.1 = bf16[128,4096]{1,0:T(8,128)(2,1)} custom-call(bf16[256,1024]{1,0:T(8,128)(2,1)} %pad_maximum_fusion.main, bf16[256,128]{1,0:T(8,128)(2,1)} %pad_maximum_fusion.2.late, bf16[1024,4608]{1,0:T(8,128)(2,1)} %bitcast.21.rows_ref.over_ref, bf16[1024,4608]{1,0:T(8,128)(2,1)} %bitcast.21.rows_ref.over_ref, f32[128,4096]{1,0:T(8,128)} %get-tuple-element.52.state), custom_call_target="tpu_custom_call" | custom-call | flops 4000000000 | bytes 13000000 | tf_op jit(solution)/shard_map/combine/pallas_call | solution.py:457
  (114 shorter events, 8.3 us)
Async XLA Ops:
  0.0 35.0 %copy-start.5 = (s32[4]{0:T(128)S(1)}, s32[4]{0:T(128)}, u32[]{:S(2)}) copy-start(s32[4]{0:T(128)} %param.14) | copy-start | bytes 52
  0.9 6.0 %collective-permute-start = (bf16[128,256]{1,0:T(8,128)(2,1)S(1)}, bf16[128,256]{1,0:T(8,128)(2,1)S(1)}, u32[]{:S(2)}, u32[]{:S(2)}) collective-permute-start(bf16[128,256]{1,0:T(8,128)(2,1)S(1)} %pad_maximum_fusion.3), channel_id=1, source_target_pairs={{0,4},{1,5},{2,6},{3,7},{4,8},{5,9},{6,10},{7,11},{8,12},{9,13},{1... | collective-permute-start | bytes 196616 | tf_op jit(solution)/shard_map/ppermute | solution.py:26
  2.6 5.9 %collective-permute-start.1 = (bf16[128,256]{1,0:T(8,128)(2,1)S(1)}, bf16[128,256]{1,0:T(8,128)(2,1)S(1)}, u32[]{:S(2)}, u32[]{:S(2)}) collective-permute-start(bf16[128,256]{1,0:T(8,128)(2,1)S(1)} %pad_maximum_fusion.4), channel_id=1, source_target_pairs={{0,8},{1,9},{2,10},{3,11},{4,12},{5,13},{6,14},{7,15},{8,0},{9,1},... | collective-permute-start | bytes 196616 | tf_op jit(solution)/shard_map/ppermute | solution.py:26
  5.4 4.3 collective-permute-start.2
  9.8 39.3 %copy-start.2 = (bf16[4,128,256]{2,1,0:T(8,128)(2,1)}, bf16[4,128,256]{2,1,0:T(8,128)(2,1)S(1)}, u32[]{:S(2)}) copy-start(bf16[4,128,256]{2,1,0:T(8,128)(2,1)S(1)} %pad_maximum_fusion.1.refs_0_) | copy-start | bytes 786436
  9.8 6.8 %collective-permute-start.3 = (bf16[4,128,256]{2,1,0:T(8,128)(2,1)S(1)}, bf16[4,128,256]{2,1,0:T(8,128)(2,1)S(1)}, u32[]{:S(2)}, u32[]{:S(2)}) collective-permute-start(bf16[4,128,256]{2,1,0:T(8,128)(2,1)S(1)} %pad_maximum_fusion.1.refs_0_), channel_id=1, source_target_pairs={{0,16},{16,0},{1,17},{17,1},{2,18},{18,2},{3,19},{19,3},{4,20},{20... | collective-permute-start | bytes 786440 | tf_op jit(solution)/shard_map/ppermute | solution.py:42
  11.4 10.6 %collective-permute-start.4 = (bf16[4,128,256]{2,1,0:T(8,128)(2,1)S(1)}, bf16[4,128,256]{2,1,0:T(8,128)(2,1)S(1)}, u32[]{:S(2)}, u32[]{:S(2)}) collective-permute-start(bf16[4,128,256]{2,1,0:T(8,128)(2,1)S(1)} %pad_maximum_fusion.1.refs_0_), channel_id=1, source_target_pairs={{0,1},{1,2},{2,3},{3,0},{4,5},{5,6},{6,7},{7,4},{8,9},{9,10},{10,1... | collective-permute-start | bytes 786440 | tf_op jit(solution)/shard_map/ppermute | solution.py:34
  16.6 32.5 %copy-start.18 = (bf16[4,128,256]{2,1,0:T(8,128)(2,1)}, bf16[4,128,256]{2,1,0:T(8,128)(2,1)S(1)}, u32[]{:S(2)}) copy-start(bf16[4,128,256]{2,1,0:T(8,128)(2,1)S(1)} %collective-permute-done.3.refs_1_) | copy-start | bytes 786436
  16.6 9.5 %collective-permute-start.7 = (bf16[4,128,256]{2,1,0:T(8,128)(2,1)S(1)}, bf16[4,128,256]{2,1,0:T(8,128)(2,1)}, u32[]{:S(2)}, u32[]{:S(2)}) collective-permute-start(bf16[4,128,256]{2,1,0:T(8,128)(2,1)S(1)} %collective-permute-done.3.refs_1_), channel_id=1, source_target_pairs={{0,3},{1,0},{2,1},{3,2},{4,7},{5,4},{6,5},{7,6},{8,11},{9,8},{10,9... | collective-permute-start | bytes 786440 | tf_op jit(solution)/shard_map/ppermute | solution.py:34
  22.0 27.1 %copy-start.1 = (bf16[256,1024]{1,0:T(8,128)(2,1)}, bf16[256,1024]{1,0:T(8,128)(2,1)S(1)}, u32[]{:S(2)}) copy-start(bf16[256,1024]{1,0:T(8,128)(2,1)S(1)} %get-tuple-element.29.refs_8_) | copy-start | bytes 1572868
  22.0 39.3 %copy-start = (bf16[256,1024]{1,0:T(8,128)(2,1)}, bf16[256,1024]{1,0:T(8,128)(2,1)S(1)}, u32[]{:S(2)}) copy-start(bf16[256,1024]{1,0:T(8,128)(2,1)S(1)} %get-tuple-element.35.refs_3_) | copy-start | bytes 1572868
  22.0 27.1 %copy-start.19 = (bf16[4,128,256]{2,1,0:T(8,128)(2,1)}, bf16[4,128,256]{2,1,0:T(8,128)(2,1)S(1)}, u32[]{:S(2)}) copy-start(bf16[4,128,256]{2,1,0:T(8,128)(2,1)S(1)} %collective-permute-done.4.refs_2_) | copy-start | bytes 786436
  22.0 7.7 %collective-permute-start.8 = (bf16[4,128,256]{2,1,0:T(8,128)(2,1)S(1)}, bf16[4,128,256]{2,1,0:T(8,128)(2,1)S(1)}, u32[]{:S(2)}, u32[]{:S(2)}) collective-permute-start(bf16[4,128,256]{2,1,0:T(8,128)(2,1)S(1)} %collective-permute-done.4.refs_2_), channel_id=1, source_target_pairs={{0,1},{1,2},{2,3},{3,0},{4,5},{5,6},{6,7},{7,4},{8,9},{9,10},{10,1... | collective-permute-start | bytes 786440 | tf_op jit(solution)/shard_map/ppermute | solution.py:34
  22.1 20.6 %collective-permute-start.10 = (bf16[256,1024]{1,0:T(8,128)(2,1)S(1)}, bf16[256,1024]{1,0:T(8,128)(2,1)S(1)}, u32[]{:S(2)}, u32[]{:S(2)}) collective-permute-start(bf16[256,1024]{1,0:T(8,128)(2,1)S(1)} %get-tuple-element.29.refs_8_), channel_id=1, source_target_pairs={{0,4},{1,5},{2,6},{3,7},{4,8},{5,9},{6,10},{7,11},{8,12},{9,13},{1... | collective-permute-start | bytes 1572872 | tf_op jit(solution)/shard_map/ppermute | solution.py:26
  22.3 25.6 %collective-permute-start.11 = (bf16[256,1024]{1,0:T(8,128)(2,1)S(1)}, bf16[256,1024]{1,0:T(8,128)(2,1)S(1)}, u32[]{:S(2)}, u32[]{:S(2)}) collective-permute-start(bf16[256,1024]{1,0:T(8,128)(2,1)S(1)} %get-tuple-element.29.refs_8_), channel_id=1, source_target_pairs={{0,8},{1,9},{2,10},{3,11},{4,12},{5,13},{6,14},{7,15},{8,0},{9,1},... | collective-permute-start | bytes 1572872 | tf_op jit(solution)/shard_map/ppermute | solution.py:26
  26.0 23.0 %collective-permute-start.12 = (bf16[256,1024]{1,0:T(8,128)(2,1)S(1)}, bf16[256,1024]{1,0:T(8,128)(2,1)S(1)}, u32[]{:S(2)}, u32[]{:S(2)}) collective-permute-start(bf16[256,1024]{1,0:T(8,128)(2,1)S(1)} %get-tuple-element.29.refs_8_), channel_id=1, source_target_pairs={{0,12},{1,13},{2,14},{3,15},{4,0},{5,1},{6,2},{7,3},{8,4},{9,5},{1... | collective-permute-start | bytes 1572872 | tf_op jit(solution)/shard_map/ppermute | solution.py:26
  26.1 8.2 %collective-permute-start.9 = (bf16[4,128,256]{2,1,0:T(8,128)(2,1)}, bf16[4,128,256]{2,1,0:T(8,128)(2,1)S(1)}, u32[]{:S(2)}, u32[]{:S(2)}) collective-permute-start(bf16[4,128,256]{2,1,0:T(8,128)(2,1)} %collective-permute-done.7.refs_5_), channel_id=1, source_target_pairs={{0,3},{1,0},{2,1},{3,2},{4,7},{5,4},{6,5},{7,6},{8,11},{9,8},{10,9... | collective-permute-start | bytes 786440 | tf_op jit(solution)/shard_map/ppermute | solution.py:34
  29.7 13.0 %collective-permute-start.6 = (bf16[4,128,256]{2,1,0:T(8,128)(2,1)S(1)}, bf16[4,128,256]{2,1,0:T(8,128)(2,1)}, u32[]{:S(2)}, u32[]{:S(2)}) collective-permute-start(bf16[4,128,256]{2,1,0:T(8,128)(2,1)S(1)} %pad_maximum_fusion.1.refs_0_), channel_id=1, source_target_pairs={{0,3},{1,0},{2,1},{3,2},{4,7},{5,4},{6,5},{7,6},{8,11},{9,8},{10,9... | collective-permute-start | bytes 786440 | tf_op jit(solution)/shard_map/ppermute | solution.py:34
  35.0 14.0 %collective-permute-start.5 = (bf16[4,128,256]{2,1,0:T(8,128)(2,1)S(1)}, bf16[4,128,256]{2,1,0:T(8,128)(2,1)}, u32[]{:S(2)}, u32[]{:S(2)}) collective-permute-start(bf16[4,128,256]{2,1,0:T(8,128)(2,1)S(1)} %collective-permute-done.3.refs_1_), channel_id=1, source_target_pairs={{0,1},{1,2},{2,3},{3,0},{4,5},{5,6},{6,7},{7,4},{8,9},{9,10},{10,1... | collective-permute-start | bytes 786440 | tf_op jit(solution)/shard_map/ppermute | solution.py:34
  42.7 18.7 %collective-permute-start.13 = (bf16[256,1024]{1,0:T(8,128)(2,1)S(1)}, bf16[256,1024]{1,0:T(8,128)(2,1)S(1)}, u32[]{:S(2)}, u32[]{:S(2)}) collective-permute-start(bf16[256,1024]{1,0:T(8,128)(2,1)S(1)} %get-tuple-element.35.refs_3_), channel_id=1, source_target_pairs={{0,1},{1,2},{2,3},{3,0},{4,5},{5,6},{6,7},{7,4},{8,9},{9,10},{10,1... | collective-permute-start | bytes 1572872 | tf_op jit(solution)/shard_map/ppermute | solution.py:34
  42.7 6.4 %copy-start.9 = (bf16[256,1024]{1,0:T(8,128)(2,1)}, bf16[256,1024]{1,0:T(8,128)(2,1)S(1)}, u32[]{:S(2)}) copy-start(bf16[256,1024]{1,0:T(8,128)(2,1)S(1)} %collective-permute-done.10.refs_9_) | copy-start | bytes 1572868
  42.7 20.6 %collective-permute-start.14 = (bf16[256,1024]{1,0:T(8,128)(2,1)S(1)}, bf16[256,1024]{1,0:T(8,128)(2,1)S(1)}, u32[]{:S(2)}, u32[]{:S(2)}) collective-permute-start(bf16[256,1024]{1,0:T(8,128)(2,1)S(1)} %get-tuple-element.35.refs_3_), channel_id=1, source_target_pairs={{0,2},{1,3},{2,0},{3,1},{4,6},{5,7},{6,4},{7,5},{8,10},{9,11},{10,... | collective-permute-start | bytes 1572872 | tf_op jit(solution)/shard_map/ppermute | solution.py:34
  47.9 15.4 %collective-permute-start.15 = (bf16[256,1024]{1,0:T(8,128)(2,1)S(1)}, bf16[256,1024]{1,0:T(8,128)(2,1)S(1)}, u32[]{:S(2)}, u32[]{:S(2)}) collective-permute-start(bf16[256,1024]{1,0:T(8,128)(2,1)S(1)} %get-tuple-element.35.refs_3_), channel_id=1, source_target_pairs={{0,3},{1,0},{2,1},{3,2},{4,7},{5,4},{6,5},{7,6},{8,11},{9,8},{10,9... | collective-permute-start | bytes 1572872 | tf_op jit(solution)/shard_map/ppermute | solution.py:34
  61.3 29.6 %collective-permute-start.19 = (bf16[1024,1024]{1,0:T(8,128)(2,1)}, bf16[1024,1024]{1,0:T(8,128)(2,1)S(1)}, u32[]{:S(2)}, u32[]{:S(2)}) collective-permute-start(bf16[1024,1024]{1,0:T(8,128)(2,1)} %get-tuple-element.37.refs_4_), channel_id=1, source_target_pairs={{0,32},{32,0},{64,96},{96,64},{1,33},{33,1},{65,97},{97,65},{2,34}... | collective-permute-start | bytes 6291464 | tf_op jit(solution)/shard_map/ppermute | solution.py:46
  64.3 7.4 %copy-start.25 = (bf16[512,256]{1,0:T(8,128)(2,1)S(1)}, bf16[512,256]{1,0:T(8,128)(2,1)}, u32[]{:S(2)}) copy-start(bf16[512,256]{1,0:T(8,128)(2,1)} %get-tuple-element.32.refs_0_) | copy-start | bytes 786436
  64.3 9.6 %copy-start.24 = (bf16[512,256]{1,0:T(8,128)(2,1)S(1)}, bf16[512,256]{1,0:T(8,128)(2,1)}, u32[]{:S(2)}) copy-start(bf16[512,256]{1,0:T(8,128)(2,1)} %get-tuple-element.33.refs_1_) | copy-start | bytes 786436
  64.3 10.3 %copy-start.23 = (bf16[512,256]{1,0:T(8,128)(2,1)S(1)}, bf16[512,256]{1,0:T(8,128)(2,1)}, u32[]{:S(2)}) copy-start(bf16[512,256]{1,0:T(8,128)(2,1)} %get-tuple-element.34.refs_2_) | copy-start | bytes 786436
  71.7 33.5 %collective-permute-start.26 = (bf16[1024,1024]{1,0:T(8,128)(2,1)}, bf16[1024,1024]{1,0:T(8,128)(2,1)S(1)}, u32[]{:S(2)}, u32[]{:S(2)}) collective-permute-start(bf16[1024,1024]{1,0:T(8,128)(2,1)} %get-tuple-element.46.refs_4_), channel_id=1, source_target_pairs={{0,32},{32,0},{64,96},{96,64},{1,33},{33,1},{65,97},{97,65},{2,34}... | collective-permute-start | bytes 6291464 | tf_op jit(solution)/shard_map/ppermute | solution.py:46
  71.7 15.5 %collective-permute-start.16 = (bf16[512,256]{1,0:T(8,128)(2,1)S(1)}, bf16[512,256]{1,0:T(8,128)(2,1)S(1)}, u32[]{:S(2)}, u32[]{:S(2)}) collective-permute-start(bf16[512,256]{1,0:T(8,128)(2,1)S(1)} %copy-done.25), channel_id=1, source_target_pairs={{0,4},{1,5},{2,6},{3,7},{4,8},{5,9},{6,10},{7,11},{8,12},{9,13},{1... | collective-permute-start | bytes 786440 | tf_op jit(solution)/shard_map/ppermute | solution.py:26
  73.9 13.3 %collective-permute-start.17 = (bf16[512,256]{1,0:T(8,128)(2,1)S(1)}, bf16[512,256]{1,0:T(8,128)(2,1)S(1)}, u32[]{:S(2)}, u32[]{:S(2)}) collective-permute-start(bf16[512,256]{1,0:T(8,128)(2,1)S(1)} %copy-done.24), channel_id=1, source_target_pairs={{0,8},{1,9},{2,10},{3,11},{4,12},{5,13},{6,14},{7,15},{8,0},{9,1},... | collective-permute-start | bytes 786440 | tf_op jit(solution)/shard_map/ppermute | solution.py:26
  74.6 16.3 %collective-permute-start.18 = (bf16[512,256]{1,0:T(8,128)(2,1)S(1)}, bf16[512,256]{1,0:T(8,128)(2,1)S(1)}, u32[]{:S(2)}, u32[]{:S(2)}) collective-permute-start(bf16[512,256]{1,0:T(8,128)(2,1)S(1)} %copy-done.23), channel_id=1, source_target_pairs={{0,12},{1,13},{2,14},{3,15},{4,0},{5,1},{6,2},{7,3},{8,4},{9,5},{1... | collective-permute-start | bytes 786440 | tf_op jit(solution)/shard_map/ppermute | solution.py:26
  87.2 3.7 copy-start.26
  87.2 14.0 %collective-permute-start.23 = (bf16[512,256]{1,0:T(8,128)(2,1)}, bf16[512,256]{1,0:T(8,128)(2,1)S(1)}, u32[]{:S(2)}, u32[]{:S(2)}) collective-permute-start(bf16[512,256]{1,0:T(8,128)(2,1)} %get-tuple-element.43), channel_id=1, source_target_pairs={{0,1},{1,2},{2,3},{3,0},{4,5},{5,6},{6,7},{7,4},{8,9},{9,10},{10,1... | collective-permute-start | bytes 786440 | tf_op jit(solution)/shard_map/ppermute | solution.py:34
  87.2 3.7 copy-start.27
  87.2 16.8 %collective-permute-start.24 = (bf16[512,256]{1,0:T(8,128)(2,1)}, bf16[512,256]{1,0:T(8,128)(2,1)}, u32[]{:S(2)}, u32[]{:S(2)}) collective-permute-start(bf16[512,256]{1,0:T(8,128)(2,1)} %get-tuple-element.44), channel_id=1, source_target_pairs={{0,2},{1,3},{2,0},{3,1},{4,6},{5,7},{6,4},{7,5},{8,10},{9,11},{10,... | collective-permute-start | bytes 786440 | tf_op jit(solution)/shard_map/ppermute | solution.py:34
  90.9 14.2 %collective-permute-start.25 = (bf16[512,256]{1,0:T(8,128)(2,1)}, bf16[512,256]{1,0:T(8,128)(2,1)}, u32[]{:S(2)}, u32[]{:S(2)}) collective-permute-start(bf16[512,256]{1,0:T(8,128)(2,1)} %get-tuple-element.45), channel_id=1, source_target_pairs={{0,3},{1,0},{2,1},{3,2},{4,7},{5,4},{6,5},{7,6},{8,11},{9,8},{10,9... | collective-permute-start | bytes 786440 | tf_op jit(solution)/shard_map/ppermute | solution.py:34
  92.3 8.4 %copy-start.3 = (f32[128,8]{0,1:T(8,128)S(1)}, f32[128,8]{0,1:T(8,128)}, u32[]{:S(2)}) copy-start(f32[128,8]{0,1:T(8,128)} %param.19) | copy-start | bytes 12292
  92.3 8.4 %copy-start.4 = (s32[128,8]{0,1:T(8,128)S(1)}, s32[128,8]{0,1:T(8,128)}, u32[]{:S(2)}) copy-start(s32[128,8]{0,1:T(8,128)} %param.18) | copy-start | bytes 12292
  98.8 26.6 %collective-permute-start.20 = (bf16[128,2048]{1,0:T(8,128)(2,1)}, bf16[128,2048]{1,0:T(8,128)(2,1)S(1)}, u32[]{:S(2)}, u32[]{:S(2)}) collective-permute-start(bf16[128,2048]{1,0:T(8,128)(2,1)} %get-tuple-element.39), channel_id=1, source_target_pairs={{0,1},{1,2},{2,3},{3,0},{4,5},{5,6},{6,7},{7,4},{8,9},{9,10},{10,1... | collective-permute-start | bytes 1572872 | tf_op jit(solution)/shard_map/ppermute | solution.py:34
  102.0 27.1 %collective-permute-start.21 = (bf16[128,2048]{1,0:T(8,128)(2,1)}, bf16[128,2048]{1,0:T(8,128)(2,1)S(1)}, u32[]{:S(2)}, u32[]{:S(2)}) collective-permute-start(bf16[128,2048]{1,0:T(8,128)(2,1)} %get-tuple-element.40), channel_id=1, source_target_pairs={{0,2},{1,3},{2,0},{3,1},{4,6},{5,7},{6,4},{7,5},{8,10},{9,11},{10,... | collective-permute-start | bytes 1572872 | tf_op jit(solution)/shard_map/ppermute | solution.py:34
  104.0 25.1 %collective-permute-start.22 = (bf16[128,2048]{1,0:T(8,128)(2,1)}, bf16[128,2048]{1,0:T(8,128)(2,1)}, u32[]{:S(2)}, u32[]{:S(2)}) collective-permute-start(bf16[128,2048]{1,0:T(8,128)(2,1)} %get-tuple-element.41), channel_id=1, source_target_pairs={{0,3},{1,0},{2,1},{3,2},{4,7},{5,4},{6,5},{7,6},{8,11},{9,8},{10,9... | collective-permute-start | bytes 1572872 | tf_op jit(solution)/shard_map/ppermute | solution.py:34
  112.9 24.3 %collective-permute-start.27 = (bf16[128,2048]{1,0:T(8,128)(2,1)}, bf16[128,2048]{1,0:T(8,128)(2,1)S(1)}, u32[]{:S(2)}, u32[]{:S(2)}) collective-permute-start(bf16[128,2048]{1,0:T(8,128)(2,1)} %get-tuple-element.48), channel_id=1, source_target_pairs={{0,4},{1,5},{2,6},{3,7},{4,8},{5,9},{6,10},{7,11},{8,12},{9,13},{1... | collective-permute-start | bytes 1572872 | tf_op jit(solution)/shard_map/ppermute | solution.py:26
  112.9 24.3 %collective-permute-start.28 = (bf16[128,2048]{1,0:T(8,128)(2,1)}, bf16[128,2048]{1,0:T(8,128)(2,1)S(1)}, u32[]{:S(2)}, u32[]{:S(2)}) collective-permute-start(bf16[128,2048]{1,0:T(8,128)(2,1)} %get-tuple-element.49), channel_id=1, source_target_pairs={{0,8},{1,9},{2,10},{3,11},{4,12},{5,13},{6,14},{7,15},{8,0},{9,1},... | collective-permute-start | bytes 1572872 | tf_op jit(solution)/shard_map/ppermute | solution.py:26
  126.2 11.8 %collective-permute-start.29 = (bf16[128,2048]{1,0:T(8,128)(2,1)}, bf16[128,2048]{1,0:T(8,128)(2,1)}, u32[]{:S(2)}, u32[]{:S(2)}) collective-permute-start(bf16[128,2048]{1,0:T(8,128)(2,1)} %get-tuple-element.50), channel_id=1, source_target_pairs={{0,12},{1,13},{2,14},{3,15},{4,0},{5,1},{6,2},{7,3},{8,4},{9,5},{1... | collective-permute-start | bytes 1572872 | tf_op jit(solution)/shard_map/ppermute | solution.py:26
  129.1 8.8 %copy-start.11 = (bf16[128,2048]{1,0:T(8,128)(2,1)}, bf16[128,2048]{1,0:T(8,128)(2,1)S(1)}, u32[]{:S(2)}) copy-start(bf16[128,2048]{1,0:T(8,128)(2,1)S(1)} %collective-permute-done.21.refs_2_) | copy-start | bytes 1572868
  138.1 137.1 %slice-start = ((s8[6291456]{0:T(1024)(128)(4,1)}), s8[2097152]{0:T(1024)(128)(4,1)S(1)}, s32[]{:S(2)}) async-start(s8[6291456]{0:T(1024)(128)(4,1)} %bitcast.32), calls=%async_computation.2 | async-start | bytes 4194304
  148.2 127.0 %slice-start.1 = ((s8[6291456]{0:T(1024)(128)(4,1)}), s8[4194304]{0:T(1024)(128)(4,1)S(1)}, s32[]{:S(2)}) async-start(s8[6291456]{0:T(1024)(128)(4,1)} %bitcast.32), calls=%async_computation.3 | async-start | bytes 8388608
  301.4 125.4 %all-to-all-start.1 = ((bf16[128,8,4608]{2,1,0:T(8,128)(2,1)}), bf16[128,8,4608]{2,1,0:T(8,128)(2,1)}, u32[]{:S(2)}, u32[]{:S(2)}) async-start(bf16[128,8,4608]{2,1,0:T(8,128)(2,1)} %bitcast.34), calls=%async_computation.1 | async-start | bytes 18874368 | tf_op jit(solution)/shard_map/all_to_all | solution.py:577
  (14 other events, 13.8 us)

commit v5 on v4

--- a/solution.py
+++ b/solution.py
@@ -15,6 +15,9 @@
 SLOTS = 8
 SEG = 512
 ROWS = 256
+DISPATCH_COLUMNS = 512
+DOWN_COLUMNS = 512
+COMBINE_COLUMNS = 512
 BLOCK = 512
 NEGATIVE = -1e30
 MIB = 1 << 20
@@ -247,38 +250,42 @@
 
 def projection_kernel(axis, meta, *refs):
     context, weights, outs, held = refs[:4], refs[4:6], refs[6:10], refs[10]
-    me = meta[axis]
+    step, me = pl.program_id(0), meta[axis]
     width = context[0].shape[1]
-    columns = 256
+    columns = weights[0].shape[1]
+    steps = held.shape[1] // (2 * columns)
     for side, weight in enumerate(weights):
-        for start in range(0, weight.shape[1], columns):
-            total = None
-            for number, rows in enumerate(context):
-                part = weight[number * width : (number + 1) * width, start : start + columns]
-                term = dot(rows[...], part)
-                total = term if total is None else total + term
-            held[:, side * weight.shape[1] + start : side * weight.shape[1] + start + columns] = (
-                total.astype(BF16)
-            )
-    for number, out in enumerate(outs):
-        to = lax.rem(me + number, SIDE)
-        out[...] = held[pl.ds(pl.multiple_of(to * TOKENS, TOKENS), TOKENS), :]
+        total = None
+        for number, rows in enumerate(context):
+            term = dot(rows[...], weight[number * width : (number + 1) * width, :])
+            total = term if total is None else total + term
+        start = pl.multiple_of((side * steps + step) * columns, columns)
+        held[:, pl.ds(start, columns)] = total.astype(BF16)
+
+    @pl.when(step == steps - 1)
+    def _():
+        for number, out in enumerate(outs):
+            to = lax.rem(me + number, SIDE)
+            out[...] = held[pl.ds(pl.multiple_of(to * TOKENS, TOKENS), TOKENS), :]
 
 
 def projection(axis, meta, context, weights):
-    columns = 2 * weights[0].shape[1]
-    arrays = (*context, *weights)
+    depth, columns = weights[0].shape
+    part = columns // 4
     return call(
         functools.partial(projection_kernel, axis),
         "projection",
-        [jax.ShapeDtypeStruct((TOKENS, columns), BF16)] * 4,
-        [smem()] + [whole(array) for array in arrays],
-        [pl.BlockSpec((TOKENS, columns), lambda: (0, 0))] * 4,
-        scratch=[pltpu.VMEM((SIDE * TOKENS, columns), BF16)],
+        [jax.ShapeDtypeStruct((TOKENS, 2 * columns), BF16)] * 4,
+        [smem()]
+        + [whole(array) for array in context]
+        + [pl.BlockSpec((depth, part), lambda i: (0, i))] * 2,
+        [pl.BlockSpec((TOKENS, 2 * columns), lambda i: (0, 0))] * 4,
+        grid=(4,),
+        scratch=[pltpu.VMEM((SIDE * TOKENS, 2 * columns), BF16)],
         cost=pl.CostEstimate(
-            flops=2 * 512 * 1024 * columns, bytes_accessed=7 * 10**6, transcendentals=0
+            flops=4 * 512 * 1024 * columns, bytes_accessed=7 * 10**6, transcendentals=0
         ),
-    )(meta, *arrays)
+    )(meta, *context, *weights)
 
 
 def wide_scratch():
@@ -328,15 +335,16 @@
         scale = lax.rsqrt(jnp.mean(value * value, axis=1, keepdims=True) + 1e-06)
         for segment in range(SLOTS):
             columns = slice(segment * SEG, (segment + 1) * SEG)
-            normed[segment] = (state[:, columns] * scale * gain[:, columns]).astype(BF16)
+            normed[:, columns] = (state[:, columns] * scale * gain[:, columns]).astype(BF16)
 
         for segment in range(SLOTS):
-            scatter_rows(wide, segment, dot(late[...], normed[segment]))
+            columns = slice(segment * SEG, (segment + 1) * SEG)
+            scatter_rows(wide, segment, dot(late[...], normed[:, columns]))
         spread[...] = narrow(wide)
 
-    for segment in range(SLOTS):
-        columns = slice(segment * SEG, (segment + 1) * SEG)
-        outgoing[:, columns] = dot(main[...], normed[segment]).astype(BF16)
+    for start in range(0, 2 * half, DISPATCH_COLUMNS):
+        columns = slice(start, start + DISPATCH_COLUMNS)
+        outgoing[:, columns] = dot(main[...], normed[:, columns]).astype(BF16)
     rows = outgoing.shape[0]
     outgoing[:, 2 * half :] = spread[pl.ds(pl.multiple_of(step * rows, rows), rows), :]
 
@@ -360,7 +368,7 @@
         ],
         grid=(rows // ROWS,),
         scratch=[
-            pltpu.VMEM((SLOTS, TOKENS, SEG), BF16),
+            pltpu.VMEM((TOKENS, width), BF16),
             wide_scratch(),
             pltpu.VMEM((rows, SEG), BF16),
         ],
@@ -393,8 +401,8 @@
         spread[...] = narrow(wide)
 
     inner = act(dot(rows_ref[:, :width], up_ref[0]))
-    for segment in range(SLOTS):
-        columns = slice(segment * SEG, (segment + 1) * SEG)
+    for start in range(0, width, DOWN_COLUMNS):
+        columns = slice(start, start + DOWN_COLUMNS)
         out_ref[:, columns] = dot(inner, down_ref[0, :, columns]).astype(BF16)
     mine = pl.ds(pl.multiple_of(step * ROWS, ROWS), ROWS)
     out_ref[:, width:] = spread[mine, :]
@@ -444,7 +452,8 @@
             late_part = both(dot(late[...], gather_rows(wide, segment)))
             total[:, columns] = state[:, columns] + late_part
 
-    for segment, columns in segments:
+    for start in range(0, total.shape[1], COMBINE_COLUMNS):
+        columns = slice(start, start + COMBINE_COLUMNS)
         total[:, columns] += both(dot(main[...], rows_ref[:, columns]))
 
     @pl.when(step == pl.num_programs(0) - 1)
@@ -472,30 +481,56 @@
     )(main, late, returned, returned, state)
 
 
+def routes_kernel(ids, weights, main, late, back_main, back_late):
+    square = (TOKENS, TOKENS)
+    row = lax.broadcasted_iota(jnp.int32, square, 0)
+    column = lax.broadcasted_iota(jnp.int32, square, 1)
+    named, weight = jnp.zeros(square, F32), jnp.zeros(square, F32)
+    for choice in range(ids.shape[1]):
+        chosen = column == ids[:, choice : choice + 1]
+        named = named + jnp.where(chosen, 1.0, 0.0)
+        weight = weight + jnp.where(chosen, weights[:, choice : choice + 1], 0.0)
+    earlier = jnp.where(column < row, 1.0, 0.0).astype(BF16)
+    rank = jnp.where(named > 0.0, dot(earlier, named.astype(BF16)), -1.0)
+    high = weight.astype(BF16)
+    low = (weight - high.astype(F32)).astype(BF16)
+
+    tall = main.shape
+    row = lax.broadcasted_iota(jnp.int32, tall, 0)
+    column = lax.broadcasted_iota(jnp.int32, tall, 1)
+    spread = jnp.where(row // SLOTS == column, 1.0, 0.0).astype(BF16)
+    ranks = dot(spread, rank.T.astype(BF16))
+    main[...] = jnp.where(ranks == (row % SLOTS).astype(F32), 1.0, 0.0).astype(BF16)
+    late[...] = jnp.where(rank.T == SLOTS, 1.0, 0.0).astype(BF16)
+
+    flat = (TOKENS, tall[0])
+    hit = dot_nt(rank.astype(BF16), spread) == (
+        lax.broadcasted_iota(jnp.int32, flat, 1) % SLOTS
+    ).astype(F32)
+    for half, part in enumerate((high, low)):
+        rows = slice(half * TOKENS, (half + 1) * TOKENS)
+        back_main[rows, :] = jnp.where(hit, dot_nt(part, spread), 0.0).astype(BF16)
+        back_late[rows, :] = jnp.where(rank == SLOTS, part.astype(F32), 0.0).astype(BF16)
+
+
 def routes(expert_ids, route_weights, n_experts):
-    tokens = expert_ids.shape[0]
-    chosen = expert_ids.T[:, None, :] == jnp.arange(n_experts, dtype=jnp.int32)[None, :, None]
-    named = jnp.sum(chosen.astype(F32), axis=0)
-    weight = jnp.sum(jnp.where(chosen, route_weights.T[:, None, :], 0.0), axis=0)
-    order = jnp.arange(tokens, dtype=jnp.int32)
-    earlier = (order[:, None] < order[None, :]).astype(BF16)
-    rank = dot(named.astype(BF16), earlier)
-    rank = jnp.where(named > 0, rank, -1.0)
-    slots = jnp.arange(SLOTS, dtype=jnp.int32).astype(F32)
-    hit = rank[:, None, :] == slots[None, :, None]
-    late = rank == SLOTS
-    high = lax.reduce_precision(weight, 8, 7)
-    low = weight - high
-
-    def rows(value):
-        spread = jnp.where(hit, value, 0.0)
-        return spread.astype(BF16).reshape(n_experts * SLOTS, tokens)
-
-    back_main = jnp.concatenate([rows(high[:, None, :]).T, rows(low[:, None, :]).T], axis=0)
-    back_late = jnp.concatenate(
-        [jnp.where(late, value, 0.0).astype(BF16).T for value in (high, low)], axis=0
-    )
-    return rows(1.0), late.astype(BF16), back_main, back_late
+    outs = [
+        jax.ShapeDtypeStruct(shape, BF16)
+        for shape in (
+            (n_experts * SLOTS, TOKENS),
+            (n_experts, TOKENS),
+            (2 * TOKENS, n_experts * SLOTS),
+            (2 * TOKENS, n_experts),
+        )
+    ]
+    return call(
+        routes_kernel,
+        "routes",
+        outs,
+        [whole(expert_ids), whole(route_weights)],
+        [pl.BlockSpec(out.shape, lambda: (0, 0)) for out in outs],
+        cost=pl.CostEstimate(flops=2 * 10**8, bytes_accessed=10**6, transcendentals=0),
+    )(expert_ids, route_weights)
 
 
 def local(
@@ -555,19 +590,20 @@
         far_other,
     ]
 
-    maps = routes(expert_ids, route_weights, n_devices)
+    main, late, back_main, back_late = routes(expert_ids, route_weights, n_devices)
+    queries = after(queries, main)
 
     *far, keys, values, weights_x = attention(meta, queries, pieces, weights_x)
-    other_x = swap_core(weights_x)
+    other_x = swap_core(after(weights_x, *weights_z))
     mine, *parts, weights_z = attention_end(meta, queries, keys, values, far, weights_z)
-    other_z = swap_core(weights_z)
-    context_x = exchange(shift_x, [mine, *far])
-    context_z = exchange(shift_z, parts)
+    mine, *parts, other_x = lax.optimization_barrier((mine, *far, *parts, other_x))
+    context_x = exchange(shift_x, [mine, *parts[:3]])
+    context_z = exchange(shift_z, parts[3:])
+    context_x, context_z = lax.optimization_barrier((context_x, context_z))
+    other_z = swap_core(after(weights_z, *context_x))
     terms_z = projection(6, meta, context_x, [weights_x, other_x])
     terms_x = projection(5, meta, context_z, [weights_z, other_z])
     terms_z, terms_x = exchange(shift_z, terms_z), exchange(shift_x, terms_x)
-    main, late, back_main, back_late = maps
-
     outgoing, state = dispatch(
         meta, terms_z, terms_x, residual, norm_gain[None, :], main, late
     )

time: 441 us -> 429 us (0.973); the launches traced: 436 us -> 431 us
  waiting for transfers between devices: 168 us -> 60.2 us
  blocking collectives: 127 us -> 231 us
  Pallas kernels: 76.9 us -> 91.1 us
  starting transfers between devices: 48.5 us -> 38.9 us
    all_to_all x1 -> x0, waiting for transfers between devices: 116 us -> none  [all_to_all(): lax.all_to_all(blocks, ('dp', 'ctx', 'tp'), split_axis=0, concat_axis=0,...]
    all_to_all x1 -> x2, blocking collectives: 127 us -> 231 us  [all_to_all(): lax.all_to_all(blocks, ('dp', 'ctx', 'tp'), split_axis=0, concat_axis=0,...]
    pallas_call x1, Pallas kernels: 11.4 us -> 20 us  [attention(): call(attention_kernel, 'attention', outs, [smem()] + [whole(array) for ar...]
    ppermute x12, waiting for transfers between devices: 22.2 us -> 29.7 us  [shift_x(): lax.ppermute(value, 'tp', [(x * SIDE + z, (x + step) % SIDE * SIDE + z) f...]
    all_to_all x1 -> x0, starting transfers between devices: 6.88 us -> none  [all_to_all(): lax.all_to_all(blocks, ('dp', 'ctx', 'tp'), split_axis=0, concat_axis=0,...]
  transfers between devices with their start and end apart: 31 -> 30, of which waited for: 13 -> 17; matrix products, arithmetic and copies ran while one was open for 1% -> 1% of each run, Pallas kernels for 7% -> 11%
where the time goes in v5:
time: 429 us; the launch traced here: 431 us
  blocking collectives  231 us (54%)
  Pallas kernels  91.1 us (21%)
  waiting for transfers between devices  60.2 us (14%)
  starting transfers between devices  38.9 us (9%)
  local copies, waits for them, and re-layouts  9.73 us (2%)
    all_to_all x2, blocking collectives, all_to_all(): lax.all_to_all(blocks, ('dp', 'ctx', 'tp'), split_axis=0, concat_axis=0,...  231 us
    ppermute x12, waiting for transfers between devices, shift_x(): lax.ppermute(value, 'tp', [(x * SIDE + z, (x + step) % SIDE * SIDE + z) f...  29.7 us
    ppermute x15, waiting for transfers between devices, shift_z(): lax.ppermute(value, 'tp', [(x * SIDE + z, x * SIDE + (z + step) % SIDE) f...  27.6 us
    pallas_call x1, Pallas kernels, experts(): call(expert_kernel, 'experts', jax.ShapeDtypeStruct((rows, columns), BF16...  26.2 us
    ppermute x15, starting transfers between devices, shift_z(): lax.ppermute(value, 'tp', [(x * SIDE + z, x * SIDE + (z + step) % SIDE) f...  23.6 us
    pallas_call x1, Pallas kernels, attention(): call(attention_kernel, 'attention', outs, [smem()] + [whole(array) for ar...  20 us
    ppermute x12, starting transfers between devices, shift_x(): lax.ppermute(value, 'tp', [(x * SIDE + z, (x + step) % SIDE * SIDE + z) f...  13.5 us
    pallas_call x2, Pallas kernels, projection(): call(functools.partial(projection_kernel, axis), 'projection', [jax.Shape...  13.2 us
  transfers between devices with their start and end apart: 30, of which 17 were waited for; matrix products, arithmetic and copies ran while one was open for 1% of the time, Pallas kernels for 11%

profile of v5, /device:TPU:0, one launch (start us, length us, event | category | flops | bytes accessed | tf_op | source)
XLA Modules:
  0.0 431.5 jit_solution(15921669407237544083)
XLA Ops:
  0.0 0.9 constant_dynamic-slice_fusion.8
  1.0 3.2 collective-permute-start.1
  4.2 1.2 collective-permute-start.2
  5.4 1.0 collective-permute-start
  6.8 1.7 collective-permute-done.2
  8.5 2.4 collective-permute-done
  11.0 1.7 collective-permute-start.3
  12.6 1.9 collective-permute-start.4
  14.5 2.9 collective-permute-done.3.refs_1_
  17.4 4.0 collective-permute-start.7
  21.5 1.3 constant_dynamic-slice_fusion
  22.9 2.5 collective-permute-done.7.refs_5_
  25.4 3.8 collective-permute-start.9
  29.2 1.2 collective-permute-start.12
  30.3 1.0 collective-permute-start.11
  31.8 0.7 copy-done.22
  32.5 1.4 collective-permute-done.9.refs_7_
  35.1 0.7 copy.12.ids
  35.9 0.7 copy.13.weights
  36.6 2.6 routes.1
  39.9 3.1 collective-permute-start.15
  42.9 3.6 collective-permute-done.5.refs_3_
  46.6 2.8 collective-permute-start.14
  50.1 3.4 collective-permute-done.10.refs_9_
  53.5 0.8 copy-done.10
  54.3 20.0 %attention.1 = (bf16[512,256]{1,0:T(8,128)(2,1)}, bf16[512,256]{1,0:T(8,128)(2,1)}, bf16[512,256]{1,0:T(8,128)(2,1)}, bf16[4096,128]{1,0:T(8,128)(2,1)}, bf16[12...) custom-call(s32[8]{0:T(128)} %concatenate.15.meta, bf16[2048,256]{1,0:T(8,128)(2,1)} %q_ref.1, ...), custom_call_target="tpu_custom_call" | custom-call | flops 16000000000 | bytes 7000000 | tf_op jit(solution)/shard_map/attention/pallas_call | solution.py:205
  74.4 0.7 copy-done.13
  75.4 10.2 %attention_end.1 = (bf16[512,256]{1,0:T(8,128)(2,1)}, bf16[512,256]{1,0:T(8,128)(2,1)}, bf16[512,256]{1,0:T(8,128)(2,1)}, bf16[512,256]{1,0:T(8,128)(2,1)}, bf16...) custom-call(s32[8]{0:T(128)} %concatenate.15.meta, bf16[2048,256]{1,0:T(8,128)(2,1)} %q_ref.1, ...), custom_call_target="tpu_custom_call" | custom-call | flops 6000000000 | bytes 7000000 | tf_op jit(solution)/shard_map/attention_end/pallas_call | solution.py:238
  85.7 2.7 collective-permute-start.18
  89.0 2.8 collective-permute-start.20
  91.8 1.3 collective-permute-start.21
  93.1 7.4 %collective-permute-done.17.refs_1_ = bf16[512,256]{1,0:T(8,128)(2,1)S(1)} collective-permute-done((bf16[512,256]{1,0:T(8,128)(2,1)S(1)}, bf16[512,256]{1,0:T(8,128)(2,1)S(1)}, u32[]{:S(2)}, u32[]{:S(2)}) %collective-permute-start.17) | collective-permute-done | bytes 262176 | tf_op jit(solution)/shard_map/ppermute | solution.py:29
  101.1 2.8 collective-permute-done.21.refs_2_
  103.9 3.1 collective-permute-done.22.refs_3_
  107.1 6.6 %projection.2 = (bf16[128,2048]{1,0:T(8,128)(2,1)}, bf16[128,2048]{1,0:T(8,128)(2,1)}, bf16[128,2048]{1,0:T(8,128)(2,1)}, bf16[128,2048]{1,0:T(8,128)(2,1)}) custom-call(s32[8]{0:T(128)} %concatenate.15.meta, bf16[512,256]{1,0:T(8,128)(2,1)} %get-tuple-element.79.refs_0_, bf16[512,256]{1,0:T(8,128)(2,1)} %copy-done.30, bf16[512,256]{1,0:T(8,128)(2,1)} %copy-done.31, ...), custom_call_target="tpu_custom_call" | custom-call | flops 2147483648 | bytes 7000000 | tf_op jit(solution)/shard_map/projection/pallas_call | solution.py:275
  113.8 2.7 collective-permute-start.24
  117.1 1.3 copy-done.7
  118.4 6.6 %projection.3 = (bf16[128,2048]{1,0:T(8,128)(2,1)}, bf16[128,2048]{1,0:T(8,128)(2,1)}, bf16[128,2048]{1,0:T(8,128)(2,1)}, bf16[128,2048]{1,0:T(8,128)(2,1)}) custom-call(s32[8]{0:T(128)} %concatenate.15.meta, bf16[512,256]{1,0:T(8,128)(2,1)} %get-tuple-element.88.refs_0_, bf16[512,256]{1,0:T(8,128)(2,1)} %copy-done.26, bf16[512,256]{1,0:T(8,128)(2,1)} %copy-done.27, ...), custom_call_target="tpu_custom_call" | custom-call | flops 2147483648 | bytes 7000000 | tf_op jit(solution)/shard_map/projection/pallas_call | solution.py:275
  125.0 2.2 collective-permute-start.28
  127.2 13.6 %collective-permute-done.23.refs_1_ = bf16[128,2048]{1,0:T(8,128)(2,1)S(1)} collective-permute-done((bf16[128,2048]{1,0:T(8,128)(2,1)}, bf16[128,2048]{1,0:T(8,128)(2,1)S(1)}, u32[]{:S(2)}, u32[]{:S(2)}) %collective-permute-start.23) | collective-permute-done | bytes 524320 | tf_op jit(solution)/shard_map/ppermute | solution.py:37
  141.4 10.0 %collective-permute-done.27.refs_5_ = bf16[128,2048]{1,0:T(8,128)(2,1)S(1)} collective-permute-done((bf16[128,2048]{1,0:T(8,128)(2,1)}, bf16[128,2048]{1,0:T(8,128)(2,1)S(1)}, u32[]{:S(2)}, u32[]{:S(2)}) %collective-permute-start.27) | collective-permute-done | bytes 524320 | tf_op jit(solution)/shard_map/ppermute | solution.py:29
  151.4 3.1 collective-permute-done.29.refs_7_
  154.5 0.8 copy-done.19
  155.3 10.0 %dispatch.1 = (bf16[1024,4608]{1,0:T(8,128)(2,1)}, f32[128,4096]{1,0:T(8,128)}) custom-call(s32[8]{0:T(128)} %concatenate.15.meta, bf16[128,2048]{1,0:T(8,128)(2,1)} %get-tuple-element.84.refs_0_, bf16[128,2048]{1,0:T(8,128)(2,1)} %copy-done.11, bf16[128,2048]{1,0:T(8,128)(2,1)} %copy-done.12, bf16[128,2048]{1,0:T(8,128)(2,1)} %copy-done.14, ...), custom_call_target="tpu_custom_call" | custom-call | flops 3000000000 | bytes 16000000 | tf_op jit(solution)/shard_map/dispatch/pallas_call | solution.py:355
  165.3 115.6 %all_to_all.10 = bf16[128,8,4608]{2,1,0:T(8,128)(2,1)} all-to-all(bf16[128,8,4608]{2,1,0:T(8,128)(2,1)} %bitcast.18), channel_id=1, replica_groups=mesh['dp'=4,'ctx'=2,'tp'=16] {'dp','ctx','tp'}, dimensions={0} | all-to-all | bytes 18874368 | tf_op jit(solution)/shard_map/all_to_all | solution.py:613
  281.0 26.2 %experts.1 = bf16[1024,4608]{1,0:T(8,128)(2,1)} custom-call(bf16[1024,4608]{1,0:T(8,128)(2,1)} %bitcast.19, bf16[1024,4608]{1,0:T(8,128)(2,1)} %bitcast.20, bf16[1,4096,768]{2,1,0:T(8,128)(2,1)S(1)} %bitcast.15, bf16[1,768,4096]{2,1,0:T(8,128)(2,1)} %down_hbm.1), custom_call_target="tpu_custom_call" | custom-call | flops 14495514624 | bytes 32000000 | tf_op jit(solution)/shard_map/experts/pallas_call | solution.py:414
  307.1 115.4 %all_to_all.11 = bf16[128,8,4608]{2,1,0:T(8,128)(2,1)} all-to-all(bf16[128,8,4608]{2,1,0:T(8,128)(2,1)} %bitcast.21), channel_id=1, replica_groups=mesh['dp'=4,'ctx'=2,'tp'=16] {'dp','ctx','tp'}, dimensions={0} | all-to-all | bytes 18874368 | tf_op jit(solution)/shard_map/all_to_all | solution.py:613
  422.6 8.9 %combine.1 = bf16[128,4096]{1,0:T(8,128)(2,1)} custom-call(bf16[256,1024]{1,0:T(8,128)(2,1)} %get-tuple-element.53.main, bf16[256,128]{1,0:T(8,128)(2,1)} %get-tuple-element.54.late, bf16[1024,4608]{1,0:T(8,128)(2,1)} %bitcast.16, bf16[1024,4608]{1,0:T(8,128)(2,1)} %bitcast.17, f32[128,4096]{1,0:T(8,128)} %get-tuple-element.100.state), custom_call_target="tpu_custom_call" | custom-call | flops 4000000000 | bytes 13000000 | tf_op jit(solution)/shard_map/combine/pallas_call | solution.py:466
  (103 shorter events, 6.7 us)
Async XLA Ops:
  0.0 35.1 %copy-start.3 = (s32[128,8]{0,1:T(8,128)S(1)}, s32[128,8]{0,1:T(8,128)}, u32[]{:S(2)}) copy-start(s32[128,8]{0,1:T(8,128)} %param.18) | copy-start | bytes 12292
  0.0 35.9 %copy-start.4 = (f32[128,8]{0,1:T(8,128)S(1)}, f32[128,8]{0,1:T(8,128)}, u32[]{:S(2)}) copy-start(f32[128,8]{0,1:T(8,128)} %param.19) | copy-start | bytes 12292
  0.9 38.3 %copy-start.5 = (s32[4]{0:T(128)S(1)}, s32[4]{0:T(128)}, u32[]{:S(2)}) copy-start(s32[4]{0:T(128)} %param.14) | copy-start | bytes 52
  1.0 5.8 %collective-permute-start.1 = (bf16[128,256]{1,0:T(8,128)(2,1)S(1)}, bf16[128,256]{1,0:T(8,128)(2,1)S(1)}, u32[]{:S(2)}, u32[]{:S(2)}) collective-permute-start(bf16[128,256]{1,0:T(8,128)(2,1)S(1)} %pad_maximum_fusion.2), channel_id=1, source_target_pairs={{0,8},{1,9},{2,10},{3,11},{4,12},{5,13},{6,14},{7,15},{8,0},{9,1},... | collective-permute-start | bytes 196616 | tf_op jit(solution)/shard_map/ppermute | solution.py:29
  4.2 4.3 %collective-permute-start.2 = (bf16[128,256]{1,0:T(8,128)(2,1)S(1)}, bf16[128,256]{1,0:T(8,128)(2,1)S(1)}, u32[]{:S(2)}, u32[]{:S(2)}) collective-permute-start(bf16[128,256]{1,0:T(8,128)(2,1)S(1)} %pad_maximum_fusion.3), channel_id=1, source_target_pairs={{0,12},{1,13},{2,14},{3,15},{4,0},{5,1},{6,2},{7,3},{8,4},{9,5},{1... | collective-permute-start | bytes 196616 | tf_op jit(solution)/shard_map/ppermute | solution.py:29
  5.4 5.5 %collective-permute-start = (bf16[128,256]{1,0:T(8,128)(2,1)S(1)}, bf16[128,256]{1,0:T(8,128)(2,1)S(1)}, u32[]{:S(2)}, u32[]{:S(2)}) collective-permute-start(bf16[128,256]{1,0:T(8,128)(2,1)S(1)} %pad_maximum_fusion.1), channel_id=1, source_target_pairs={{0,4},{1,5},{2,6},{3,7},{4,8},{5,9},{6,10},{7,11},{8,12},{9,13},{1... | collective-permute-start | bytes 196616 | tf_op jit(solution)/shard_map/ppermute | solution.py:29
  11.0 42.5 %copy-start.2 = (bf16[4,128,256]{2,1,0:T(8,128)(2,1)}, bf16[4,128,256]{2,1,0:T(8,128)(2,1)S(1)}, u32[]{:S(2)}) copy-start(bf16[4,128,256]{2,1,0:T(8,128)(2,1)S(1)} %pad_maximum_fusion.refs_0_) | copy-start | bytes 786436
  11.0 6.5 %collective-permute-start.3 = (bf16[4,128,256]{2,1,0:T(8,128)(2,1)S(1)}, bf16[4,128,256]{2,1,0:T(8,128)(2,1)S(1)}, u32[]{:S(2)}, u32[]{:S(2)}) collective-permute-start(bf16[4,128,256]{2,1,0:T(8,128)(2,1)S(1)} %pad_maximum_fusion.refs_0_), channel_id=1, source_target_pairs={{0,16},{16,0},{1,17},{17,1},{2,18},{18,2},{3,19},{19,3},{4,20},{20... | collective-permute-start | bytes 786440 | tf_op jit(solution)/shard_map/ppermute | solution.py:45
  12.6 10.1 %collective-permute-start.4 = (bf16[4,128,256]{2,1,0:T(8,128)(2,1)S(1)}, bf16[4,128,256]{2,1,0:T(8,128)(2,1)S(1)}, u32[]{:S(2)}, u32[]{:S(2)}) collective-permute-start(bf16[4,128,256]{2,1,0:T(8,128)(2,1)S(1)} %pad_maximum_fusion.refs_0_), channel_id=1, source_target_pairs={{0,1},{1,2},{2,3},{3,0},{4,5},{5,6},{6,7},{7,4},{8,9},{9,10},{10,1... | collective-permute-start | bytes 786440 | tf_op jit(solution)/shard_map/ppermute | solution.py:37
  17.4 36.0 %copy-start.20 = (bf16[4,128,256]{2,1,0:T(8,128)(2,1)}, bf16[4,128,256]{2,1,0:T(8,128)(2,1)S(1)}, u32[]{:S(2)}) copy-start(bf16[4,128,256]{2,1,0:T(8,128)(2,1)S(1)} %collective-permute-done.3.refs_1_) | copy-start | bytes 786436
  17.4 7.9 %collective-permute-start.7 = (bf16[4,128,256]{2,1,0:T(8,128)(2,1)S(1)}, bf16[4,128,256]{2,1,0:T(8,128)(2,1)}, u32[]{:S(2)}, u32[]{:S(2)}) collective-permute-start(bf16[4,128,256]{2,1,0:T(8,128)(2,1)S(1)} %collective-permute-done.3.refs_1_), channel_id=1, source_target_pairs={{0,3},{1,0},{2,1},{3,2},{4,7},{5,4},{6,5},{7,6},{8,11},{9,8},{10,9... | collective-permute-start | bytes 786440 | tf_op jit(solution)/shard_map/ppermute | solution.py:37
  22.7 30.7 %copy-start.1 = (bf16[256,1024]{1,0:T(8,128)(2,1)}, bf16[256,1024]{1,0:T(8,128)(2,1)S(1)}, u32[]{:S(2)}) copy-start(bf16[256,1024]{1,0:T(8,128)(2,1)S(1)} %get-tuple-element.57.refs_8_) | copy-start | bytes 1572868
  22.7 51.5 %copy-start = (bf16[256,1024]{1,0:T(8,128)(2,1)}, bf16[256,1024]{1,0:T(8,128)(2,1)S(1)}, u32[]{:S(2)}) copy-start(bf16[256,1024]{1,0:T(8,128)(2,1)S(1)} %get-tuple-element.63.refs_3_) | copy-start | bytes 1572868
  22.8 30.7 %copy-start.21 = (bf16[4,128,256]{2,1,0:T(8,128)(2,1)}, bf16[4,128,256]{2,1,0:T(8,128)(2,1)S(1)}, u32[]{:S(2)}) copy-start(bf16[4,128,256]{2,1,0:T(8,128)(2,1)S(1)} %collective-permute-done.4.refs_2_) | copy-start | bytes 786436
  22.8 9.0 %collective-permute-start.8 = (bf16[4,128,256]{2,1,0:T(8,128)(2,1)S(1)}, bf16[4,128,256]{2,1,0:T(8,128)(2,1)S(1)}, u32[]{:S(2)}, u32[]{:S(2)}) collective-permute-start(bf16[4,128,256]{2,1,0:T(8,128)(2,1)S(1)} %collective-permute-done.4.refs_2_), channel_id=1, source_target_pairs={{0,1},{1,2},{2,3},{3,0},{4,5},{5,6},{6,7},{7,4},{8,9},{9,10},{10,1... | collective-permute-start | bytes 786440 | tf_op jit(solution)/shard_map/ppermute | solution.py:37
  25.4 8.5 %collective-permute-start.9 = (bf16[4,128,256]{2,1,0:T(8,128)(2,1)}, bf16[4,128,256]{2,1,0:T(8,128)(2,1)S(1)}, u32[]{:S(2)}, u32[]{:S(2)}) collective-permute-start(bf16[4,128,256]{2,1,0:T(8,128)(2,1)} %collective-permute-done.7.refs_5_), channel_id=1, source_target_pairs={{0,3},{1,0},{2,1},{3,2},{4,7},{5,4},{6,5},{7,6},{8,11},{9,8},{10,9... | collective-permute-start | bytes 786440 | tf_op jit(solution)/shard_map/ppermute | solution.py:37
  29.2 20.9 %collective-permute-start.12 = (bf16[256,1024]{1,0:T(8,128)(2,1)S(1)}, bf16[256,1024]{1,0:T(8,128)(2,1)S(1)}, u32[]{:S(2)}, u32[]{:S(2)}) collective-permute-start(bf16[256,1024]{1,0:T(8,128)(2,1)S(1)} %get-tuple-element.57.refs_8_), channel_id=1, source_target_pairs={{0,12},{1,13},{2,14},{3,15},{4,0},{5,1},{6,2},{7,3},{8,4},{9,5},{1... | collective-permute-start | bytes 1572872 | tf_op jit(solution)/shard_map/ppermute | solution.py:29
  30.3 19.7 %collective-permute-start.11 = (bf16[256,1024]{1,0:T(8,128)(2,1)S(1)}, bf16[256,1024]{1,0:T(8,128)(2,1)S(1)}, u32[]{:S(2)}, u32[]{:S(2)}) collective-permute-start(bf16[256,1024]{1,0:T(8,128)(2,1)S(1)} %get-tuple-element.57.refs_8_), channel_id=1, source_target_pairs={{0,8},{1,9},{2,10},{3,11},{4,12},{5,13},{6,14},{7,15},{8,0},{9,1},... | collective-permute-start | bytes 1572872 | tf_op jit(solution)/shard_map/ppermute | solution.py:29
  31.4 22.1 %collective-permute-start.10 = (bf16[256,1024]{1,0:T(8,128)(2,1)S(1)}, bf16[256,1024]{1,0:T(8,128)(2,1)S(1)}, u32[]{:S(2)}, u32[]{:S(2)}) collective-permute-start(bf16[256,1024]{1,0:T(8,128)(2,1)S(1)} %get-tuple-element.57.refs_8_), channel_id=1, source_target_pairs={{0,4},{1,5},{2,6},{3,7},{4,8},{5,9},{6,10},{7,11},{8,12},{9,13},{1... | collective-permute-start | bytes 1572872 | tf_op jit(solution)/shard_map/ppermute | solution.py:29
  31.8 8.1 %collective-permute-start.6 = (bf16[4,128,256]{2,1,0:T(8,128)(2,1)S(1)}, bf16[4,128,256]{2,1,0:T(8,128)(2,1)}, u32[]{:S(2)}, u32[]{:S(2)}) collective-permute-start(bf16[4,128,256]{2,1,0:T(8,128)(2,1)S(1)} %pad_maximum_fusion.refs_0_), channel_id=1, source_target_pairs={{0,3},{1,0},{2,1},{3,2},{4,7},{5,4},{6,5},{7,6},{8,11},{9,8},{10,9... | collective-permute-start | bytes 786440 | tf_op jit(solution)/shard_map/ppermute | solution.py:37
  34.6 12.0 %collective-permute-start.5 = (bf16[4,128,256]{2,1,0:T(8,128)(2,1)S(1)}, bf16[4,128,256]{2,1,0:T(8,128)(2,1)}, u32[]{:S(2)}, u32[]{:S(2)}) collective-permute-start(bf16[4,128,256]{2,1,0:T(8,128)(2,1)S(1)} %collective-permute-done.3.refs_1_), channel_id=1, source_target_pairs={{0,1},{1,2},{2,3},{3,0},{4,5},{5,6},{6,7},{7,4},{8,9},{9,10},{10,1... | collective-permute-start | bytes 786440 | tf_op jit(solution)/shard_map/ppermute | solution.py:37
  39.9 34.3 %collective-permute-start.15 = (bf16[256,1024]{1,0:T(8,128)(2,1)S(1)}, bf16[256,1024]{1,0:T(8,128)(2,1)S(1)}, u32[]{:S(2)}, u32[]{:S(2)}) collective-permute-start(bf16[256,1024]{1,0:T(8,128)(2,1)S(1)} %get-tuple-element.63.refs_3_), channel_id=1, source_target_pairs={{0,3},{1,0},{2,1},{3,2},{4,7},{5,4},{6,5},{7,6},{8,11},{9,8},{10,9... | collective-permute-start | bytes 1572872 | tf_op jit(solution)/shard_map/ppermute | solution.py:37
  46.6 27.7 %collective-permute-start.14 = (bf16[256,1024]{1,0:T(8,128)(2,1)S(1)}, bf16[256,1024]{1,0:T(8,128)(2,1)S(1)}, u32[]{:S(2)}, u32[]{:S(2)}) collective-permute-start(bf16[256,1024]{1,0:T(8,128)(2,1)S(1)} %get-tuple-element.63.refs_3_), channel_id=1, source_target_pairs={{0,2},{1,3},{2,0},{3,1},{4,6},{5,7},{6,4},{7,5},{8,10},{9,11},{10,... | collective-permute-start | bytes 1572872 | tf_op jit(solution)/shard_map/ppermute | solution.py:37
  50.0 24.2 %collective-permute-start.13 = (bf16[256,1024]{1,0:T(8,128)(2,1)S(1)}, bf16[256,1024]{1,0:T(8,128)(2,1)S(1)}, u32[]{:S(2)}, u32[]{:S(2)}) collective-permute-start(bf16[256,1024]{1,0:T(8,128)(2,1)S(1)} %get-tuple-element.63.refs_3_), channel_id=1, source_target_pairs={{0,1},{1,2},{2,3},{3,0},{4,5},{5,6},{6,7},{7,4},{8,9},{9,10},{10,1... | collective-permute-start | bytes 1572872 | tf_op jit(solution)/shard_map/ppermute | solution.py:37
  74.3 11.3 %collective-permute-start.16 = (bf16[1024,1024]{1,0:T(8,128)(2,1)}, bf16[1024,1024]{1,0:T(8,128)(2,1)S(1)}, u32[]{:S(2)}, u32[]{:S(2)}) collective-permute-start(bf16[1024,1024]{1,0:T(8,128)(2,1)} %get-tuple-element.70.refs_4_), channel_id=1, source_target_pairs={{0,32},{32,0},{64,96},{96,64},{1,33},{33,1},{65,97},{97,65},{2,34}... | collective-permute-start | bytes 6291464 | tf_op jit(solution)/shard_map/ppermute | solution.py:49
  75.4 10.2 %copy-start.28 = (bf16[512,256]{1,0:T(8,128)(2,1)S(1)}, bf16[512,256]{1,0:T(8,128)(2,1)}, u32[]{:S(2)}) copy-start(bf16[512,256]{1,0:T(8,128)(2,1)} %get-tuple-element.72.refs_0_) | copy-start | bytes 786436
  75.4 10.3 %copy-start.25 = (bf16[512,256]{1,0:T(8,128)(2,1)S(1)}, bf16[512,256]{1,0:T(8,128)(2,1)}, u32[]{:S(2)}) copy-start(bf16[512,256]{1,0:T(8,128)(2,1)} %get-tuple-element.73.refs_1_) | copy-start | bytes 786436
  75.4 13.0 %copy-start.24 = (bf16[512,256]{1,0:T(8,128)(2,1)S(1)}, bf16[512,256]{1,0:T(8,128)(2,1)}, u32[]{:S(2)}) copy-start(bf16[512,256]{1,0:T(8,128)(2,1)} %get-tuple-element.74.refs_2_) | copy-start | bytes 786436
  85.6 21.5 %copy-start.6 = (bf16[1024,1024]{1,0:T(8,128)(2,1)}, bf16[1024,1024]{1,0:T(8,128)(2,1)S(1)}, u32[]{:S(2)}) copy-start(bf16[1024,1024]{1,0:T(8,128)(2,1)S(1)} %collective-permute-done.16.refs_5_) | copy-start | bytes 6291460
  85.6 14.9 %collective-permute-start.17 = (bf16[512,256]{1,0:T(8,128)(2,1)S(1)}, bf16[512,256]{1,0:T(8,128)(2,1)S(1)}, u32[]{:S(2)}, u32[]{:S(2)}) collective-permute-start(bf16[512,256]{1,0:T(8,128)(2,1)S(1)} %copy-done.28), channel_id=1, source_target_pairs={{0,4},{1,5},{2,6},{3,7},{4,8},{5,9},{6,10},{7,11},{8,12},{9,13},{1... | collective-permute-start | bytes 786440 | tf_op jit(solution)/shard_map/ppermute | solution.py:29
  85.7 14.8 %collective-permute-start.18 = (bf16[512,256]{1,0:T(8,128)(2,1)S(1)}, bf16[512,256]{1,0:T(8,128)(2,1)S(1)}, u32[]{:S(2)}, u32[]{:S(2)}) collective-permute-start(bf16[512,256]{1,0:T(8,128)(2,1)S(1)} %copy-done.25), channel_id=1, source_target_pairs={{0,8},{1,9},{2,10},{3,11},{4,12},{5,13},{6,14},{7,15},{8,0},{9,1},... | collective-permute-start | bytes 786440 | tf_op jit(solution)/shard_map/ppermute | solution.py:29
  88.4 12.7 %collective-permute-start.19 = (bf16[512,256]{1,0:T(8,128)(2,1)S(1)}, bf16[512,256]{1,0:T(8,128)(2,1)S(1)}, u32[]{:S(2)}, u32[]{:S(2)}) collective-permute-start(bf16[512,256]{1,0:T(8,128)(2,1)S(1)} %copy-done.24), channel_id=1, source_target_pairs={{0,12},{1,13},{2,14},{3,15},{4,0},{5,1},{6,2},{7,3},{8,4},{9,5},{1... | collective-permute-start | bytes 786440 | tf_op jit(solution)/shard_map/ppermute | solution.py:29
  89.0 12.1 %collective-permute-start.20 = (bf16[512,256]{1,0:T(8,128)(2,1)}, bf16[512,256]{1,0:T(8,128)(2,1)S(1)}, u32[]{:S(2)}, u32[]{:S(2)}) collective-permute-start(bf16[512,256]{1,0:T(8,128)(2,1)} %get-tuple-element.76), channel_id=1, source_target_pairs={{0,1},{1,2},{2,3},{3,0},{4,5},{5,6},{6,7},{7,4},{8,9},{9,10},{10,1... | collective-permute-start | bytes 786440 | tf_op jit(solution)/shard_map/ppermute | solution.py:37
  91.8 12.1 %collective-permute-start.21 = (bf16[512,256]{1,0:T(8,128)(2,1)}, bf16[512,256]{1,0:T(8,128)(2,1)S(1)}, u32[]{:S(2)}, u32[]{:S(2)}) collective-permute-start(bf16[512,256]{1,0:T(8,128)(2,1)} %get-tuple-element.77), channel_id=1, source_target_pairs={{0,2},{1,3},{2,0},{3,1},{4,6},{5,7},{6,4},{7,5},{8,10},{9,11},{10,... | collective-permute-start | bytes 786440 | tf_op jit(solution)/shard_map/ppermute | solution.py:37
  100.5 6.6 %collective-permute-start.22 = (bf16[512,256]{1,0:T(8,128)(2,1)}, bf16[512,256]{1,0:T(8,128)(2,1)S(1)}, u32[]{:S(2)}, u32[]{:S(2)}) collective-permute-start(bf16[512,256]{1,0:T(8,128)(2,1)} %get-tuple-element.78), channel_id=1, source_target_pairs={{0,3},{1,0},{2,1},{3,2},{4,7},{5,4},{6,5},{7,6},{8,11},{9,8},{10,9... | collective-permute-start | bytes 786440 | tf_op jit(solution)/shard_map/ppermute | solution.py:37
  101.1 12.6 %copy-start.26 = (bf16[512,256]{1,0:T(8,128)(2,1)}, bf16[512,256]{1,0:T(8,128)(2,1)S(1)}, u32[]{:S(2)}) copy-start(bf16[512,256]{1,0:T(8,128)(2,1)S(1)} %collective-permute-done.20.refs_1_) | copy-start | bytes 786436
  107.1 10.0 %collective-permute-start.26 = (bf16[1024,1024]{1,0:T(8,128)(2,1)}, bf16[1024,1024]{1,0:T(8,128)(2,1)S(1)}, u32[]{:S(2)}, u32[]{:S(2)}) collective-permute-start(bf16[1024,1024]{1,0:T(8,128)(2,1)} %get-tuple-element.93.refs_4_), channel_id=1, source_target_pairs={{0,32},{32,0},{64,96},{96,64},{1,33},{33,1},{65,97},{97,65},{2,34}... | collective-permute-start | bytes 6291464 | tf_op jit(solution)/shard_map/ppermute | solution.py:49
  113.8 27.0 %collective-permute-start.23 = (bf16[128,2048]{1,0:T(8,128)(2,1)}, bf16[128,2048]{1,0:T(8,128)(2,1)S(1)}, u32[]{:S(2)}, u32[]{:S(2)}) collective-permute-start(bf16[128,2048]{1,0:T(8,128)(2,1)} %get-tuple-element.85), channel_id=1, source_target_pairs={{0,1},{1,2},{2,3},{3,0},{4,5},{5,6},{6,7},{7,4},{8,9},{9,10},{10,1... | collective-permute-start | bytes 1572872 | tf_op jit(solution)/shard_map/ppermute | solution.py:37
  113.8 26.9 %collective-permute-start.24 = (bf16[128,2048]{1,0:T(8,128)(2,1)}, bf16[128,2048]{1,0:T(8,128)(2,1)S(1)}, u32[]{:S(2)}, u32[]{:S(2)}) collective-permute-start(bf16[128,2048]{1,0:T(8,128)(2,1)} %get-tuple-element.86), channel_id=1, source_target_pairs={{0,2},{1,3},{2,0},{3,1},{4,6},{5,7},{6,4},{7,5},{8,10},{9,11},{10,... | collective-permute-start | bytes 1572872 | tf_op jit(solution)/shard_map/ppermute | solution.py:37
  116.5 24.9 %collective-permute-start.25 = (bf16[128,2048]{1,0:T(8,128)(2,1)}, bf16[128,2048]{1,0:T(8,128)(2,1)S(1)}, u32[]{:S(2)}, u32[]{:S(2)}) collective-permute-start(bf16[128,2048]{1,0:T(8,128)(2,1)} %get-tuple-element.87), channel_id=1, source_target_pairs={{0,3},{1,0},{2,1},{3,2},{4,7},{5,4},{6,5},{7,6},{8,11},{9,8},{10,9... | collective-permute-start | bytes 1572872 | tf_op jit(solution)/shard_map/ppermute | solution.py:37
  125.0 26.4 %collective-permute-start.27 = (bf16[128,2048]{1,0:T(8,128)(2,1)}, bf16[128,2048]{1,0:T(8,128)(2,1)S(1)}, u32[]{:S(2)}, u32[]{:S(2)}) collective-permute-start(bf16[128,2048]{1,0:T(8,128)(2,1)} %get-tuple-element.95), channel_id=1, source_target_pairs={{0,4},{1,5},{2,6},{3,7},{4,8},{5,9},{6,10},{7,11},{8,12},{9,13},{1... | collective-permute-start | bytes 1572872 | tf_op jit(solution)/shard_map/ppermute | solution.py:29
  125.0 26.4 %collective-permute-start.28 = (bf16[128,2048]{1,0:T(8,128)(2,1)}, bf16[128,2048]{1,0:T(8,128)(2,1)S(1)}, u32[]{:S(2)}, u32[]{:S(2)}) collective-permute-start(bf16[128,2048]{1,0:T(8,128)(2,1)} %get-tuple-element.96), channel_id=1, source_target_pairs={{0,8},{1,9},{2,10},{3,11},{4,12},{5,13},{6,14},{7,15},{8,0},{9,1},... | collective-permute-start | bytes 1572872 | tf_op jit(solution)/shard_map/ppermute | solution.py:29
  140.7 13.7 %copy-start.11 = (bf16[128,2048]{1,0:T(8,128)(2,1)}, bf16[128,2048]{1,0:T(8,128)(2,1)S(1)}, u32[]{:S(2)}) copy-start(bf16[128,2048]{1,0:T(8,128)(2,1)S(1)} %collective-permute-done.23.refs_1_) | copy-start | bytes 1572868
  140.8 13.7 %collective-permute-start.29 = (bf16[128,2048]{1,0:T(8,128)(2,1)}, bf16[128,2048]{1,0:T(8,128)(2,1)S(1)}, u32[]{:S(2)}, u32[]{:S(2)}) collective-permute-start(bf16[128,2048]{1,0:T(8,128)(2,1)} %get-tuple-element.97), channel_id=1, source_target_pairs={{0,12},{1,13},{2,14},{3,15},{4,0},{5,1},{6,2},{7,3},{8,4},{9,5},{1... | collective-permute-start | bytes 1572872 | tf_op jit(solution)/shard_map/ppermute | solution.py:29
  140.8 13.7 %copy-start.12 = (bf16[128,2048]{1,0:T(8,128)(2,1)}, bf16[128,2048]{1,0:T(8,128)(2,1)S(1)}, u32[]{:S(2)}) copy-start(bf16[128,2048]{1,0:T(8,128)(2,1)S(1)} %collective-permute-done.24.refs_2_) | copy-start | bytes 1572868
  141.4 13.1 %copy-start.14 = (bf16[128,2048]{1,0:T(8,128)(2,1)}, bf16[128,2048]{1,0:T(8,128)(2,1)S(1)}, u32[]{:S(2)}) copy-start(bf16[128,2048]{1,0:T(8,128)(2,1)S(1)} %collective-permute-done.25.refs_3_) | copy-start | bytes 1572868
  155.3 125.7 %slice-start = ((s8[6291456]{0:T(1024)(128)(4,1)}), s8[2097152]{0:T(1024)(128)(4,1)S(1)}, s32[]{:S(2)}) async-start(s8[6291456]{0:T(1024)(128)(4,1)} %bitcast.14), calls=%async_computation.2 | async-start | bytes 4194304
  165.3 115.7 %slice-start.1 = ((s8[6291456]{0:T(1024)(128)(4,1)}), s8[4194304]{0:T(1024)(128)(4,1)S(1)}, s32[]{:S(2)}) async-start(s8[6291456]{0:T(1024)(128)(4,1)} %bitcast.14), calls=%async_computation.3 | async-start | bytes 8388608
  (17 other events, 56.0 us)

commit v6 on v5

--- a/solution.py
+++ b/solution.py
@@ -169,11 +169,10 @@
 
 
 def attention_kernel(meta, q_ref, *refs):
-    pieces, weights, refs = refs[:8], refs[8:12], refs[12:]
-    outs, keys, values, joined, context, scratch = refs[:3], *refs[3:7], refs[7:]
+    pieces, refs = refs[:8], refs[8:]
+    outs, keys, values, context, scratch = refs[:3], *refs[3:6], refs[6:]
     ctx, x, z = meta[4], meta[5], meta[6]
 
-    join(weights, joined)
     for number, piece in enumerate(pieces):
         part = lax.rem(ctx + number % 2, 2)
         back = (0, 1, 3, 2)[number // 2]
@@ -194,13 +193,12 @@
         out[...] = context[number]
 
 
-def attention(meta, queries, pieces, weights):
+def attention(meta, queries, pieces):
     rows, width = queries.shape
-    arrays = (queries, *pieces, *weights)
+    arrays = (queries, *pieces)
     outs = [jax.ShapeDtypeStruct((BLOCK, width), BF16)] * 3 + [
         jax.ShapeDtypeStruct((2 * rows, HD), BF16),
         jax.ShapeDtypeStruct((HD, 2 * rows), BF16),
-        jax.ShapeDtypeStruct((SIDE * weights[0].shape[0], weights[0].shape[1]), BF16),
     ]
     return call(
         attention_kernel,
@@ -216,10 +214,11 @@
 
 
 def attention_end_kernel(meta, q_ref, keys, values, *refs):
-    others, weights, out, refs = refs[:3], refs[3:7], refs[7], refs[8:]
-    outs_z, joined, scratch = refs[:4], refs[4], refs[5:]
+    others, weights, out, refs = refs[:3], refs[3:11], refs[11], refs[12:]
+    outs_z, joined, scratch = refs[:4], refs[4:6], refs[6:]
     x, z = meta[5], meta[6]
-    join(weights, joined)
+    join(weights[:4], joined[0])
+    join(weights[4:], joined[1])
     out[...] = attend(meta, x, q_ref, keys, values, scratch)
     for number, context in enumerate((out, *others)):
         x_of = lax.rem(x + number, SIDE)
@@ -234,7 +233,7 @@
     width = queries.shape[1]
     arrays = (queries, keys, values, *others, *weights)
     outs = [jax.ShapeDtypeStruct((BLOCK, width), BF16)] * 5
-    outs.append(jax.ShapeDtypeStruct((SIDE * weights[0].shape[0], weights[0].shape[1]), BF16))
+    outs += [jax.ShapeDtypeStruct((SIDE * weights[0].shape[0], weights[0].shape[1]), BF16)] * 2
     return call(
         attention_end_kernel,
         "attention_end",
@@ -312,25 +311,48 @@
         wide[part, rows, :] = value[:, part * HD : (part + 1) * HD]
 
 
+def add_terms(core, terms, residual, state, base):
+    quarter = terms[0].shape[1] // 2
+    for side in range(2):
+        place = base + quarter * lax.rem(core + side, 2)
+        columns = pl.ds(pl.multiple_of(place, quarter), quarter)
+        part = slice(side * quarter, (side + 1) * quarter)
+        total = terms[0][:, part].astype(F32)
+        for term in terms[1:]:
+            total = total + term[:, part].astype(F32)
+        state[:, columns] = residual[:, columns].astype(F32) + total
+
+
+def settle_kernel(meta, *refs):
+    terms, (residual, state) = refs[:4], refs[4:]
+    add_terms(meta[7], terms, residual, state, 0)
+
+
+def settle(meta, terms, residual):
+    half = terms[0].shape[1]
+    return call(
+        settle_kernel,
+        "settle",
+        jax.ShapeDtypeStruct((TOKENS, half), F32),
+        [smem()]
+        + [whole(term) for term in terms]
+        + [pl.BlockSpec((TOKENS, half), lambda i: (0, 0))],
+        pl.BlockSpec((TOKENS, half), lambda i: (0, 0)),
+        grid=(1,),
+        cost=pl.CostEstimate(flops=2 * 10**10, bytes_accessed=4 * 10**6, transcendentals=0),
+    )(meta, *terms, residual)
+
+
 def dispatch_kernel(meta, *refs):
-    terms_z, terms_x, refs = refs[:4], refs[4:8], refs[8:]
-    residual, gain, main, late, outgoing, state, normed, wide, spread = refs
+    terms, refs = refs[:4], refs[4:]
+    first, residual, gain, main, late, outgoing, state, normed, wide, spread = refs
     step = pl.program_id(0)
-    half = terms_z[0].shape[1]
-    quarter = half // 2
-    core = meta[7]
+    half = first.shape[1]
 
     @pl.when(step == 0)
     def _():
-        for base, terms in ((0, terms_z), (half, terms_x)):
-            for side in range(2):
-                place = base + quarter * lax.rem(core + side, 2)
-                columns = pl.ds(pl.multiple_of(place, quarter), quarter)
-                part = slice(side * quarter, (side + 1) * quarter)
-                total = terms[0][:, part].astype(F32)
-                for term in terms[1:]:
-                    total = total + term[:, part].astype(F32)
-                state[:, columns] = residual[:, columns].astype(F32) + total
+        state[:, :half] = first[...]
+        add_terms(meta[7], terms, residual, state, half)
         value = state[...]
         scale = lax.rsqrt(jnp.mean(value * value, axis=1, keepdims=True) + 1e-06)
         for segment in range(SLOTS):
@@ -349,9 +371,9 @@
     outgoing[:, 2 * half :] = spread[pl.ds(pl.multiple_of(step * rows, rows), rows), :]
 
 
-def dispatch(meta, terms_z, terms_x, residual, gain, main, late):
+def dispatch(meta, terms, first, residual, gain, main, late):
     rows, width = main.shape[0], residual.shape[1]
-    arrays = (*terms_z, *terms_x, residual, gain)
+    arrays = (*terms, first, residual, gain)
     return call(
         dispatch_kernel,
         "dispatch",
@@ -593,19 +615,19 @@
     main, late, back_main, back_late = routes(expert_ids, route_weights, n_devices)
     queries = after(queries, main)
 
-    *far, keys, values, weights_x = attention(meta, queries, pieces, weights_x)
-    other_x = swap_core(after(weights_x, *weights_z))
-    mine, *parts, weights_z = attention_end(meta, queries, keys, values, far, weights_z)
-    mine, *parts, other_x = lax.optimization_barrier((mine, *far, *parts, other_x))
-    context_x = exchange(shift_x, [mine, *parts[:3]])
-    context_z = exchange(shift_z, parts[3:])
-    context_x, context_z = lax.optimization_barrier((context_x, context_z))
+    *far, keys, values = attention(meta, queries, pieces)
+    mine, *parts, weights_x, weights_z = attention_end(
+        meta, queries, keys, values, far, [*weights_x, *weights_z]
+    )
+    context_x = exchange(shift_x, [mine, *far])
+    other_x = swap_core(after(weights_x, *context_x[1:]))
+    context_z = exchange(shift_z, [after(part, *context_x) for part in parts])
     other_z = swap_core(after(weights_z, *context_x))
     terms_z = projection(6, meta, context_x, [weights_x, other_x])
-    terms_x = projection(5, meta, context_z, [weights_z, other_z])
+    terms_x = projection(5, meta, context_z, [after(weights_z, terms_z[0]), other_z])
     terms_z, terms_x = exchange(shift_z, terms_z), exchange(shift_x, terms_x)
     outgoing, state = dispatch(
-        meta, terms_z, terms_x, residual, norm_gain[None, :], main, late
+        meta, terms_x, settle(meta, terms_z, residual), residual, norm_gain[None, :], main, late
     )
 
     def all_to_all(rows):

time: 429 us -> 438 us (1.021)
  Pallas kernels: 91.1 us -> 84.7 us
  blocking collectives: 231 us -> 237 us
  starting transfers between devices: 38.9 us -> 44.7 us
    all_to_all x2, blocking collectives: 231 us -> 237 us  [all_to_all(): lax.all_to_all(blocks, ('dp', 'ctx', 'tp'), split_axis=0, concat_axis=0,...]
    ppermute x12, starting transfers between devices: 13.5 us -> 19.5 us  [shift_x(): lax.ppermute(value, 'tp', [(x * SIDE + z, (x + step) % SIDE * SIDE + z) f...]
    ppermute x12, waiting for transfers between devices: 29.7 us -> 23.9 us  [shift_x(): lax.ppermute(value, 'tp', [(x * SIDE + z, (x + step) % SIDE * SIDE + z) f...]
    pallas_call x1, Pallas kernels: 20 us -> 14.3 us  [attention(): call(attention_kernel, 'attention', outs, [smem()] + [whole(array) for ar...]
  transfers between devices with their start and end apart: 30 -> 30, of which waited for: 17 -> 11; matrix products, arithmetic and copies ran while one was open for 1% -> 1% of each run, Pallas kernels for 11% -> 9%
where the time goes in v6:
time: 438 us; the launch traced here: 437 us
  blocking collectives  237 us (54%)
  Pallas kernels  84.7 us (19%)
  waiting for transfers between devices  58.4 us (13%)
  starting transfers between devices  44.7 us (10%)
  local copies, waits for them, and re-layouts  11.6 us (3%)
    all_to_all x2, blocking collectives, all_to_all(): lax.all_to_all(blocks, ('dp', 'ctx', 'tp'), split_axis=0, concat_axis=0,...  237 us
    ppermute x15, waiting for transfers between devices, shift_z(): lax.ppermute(value, 'tp', [(x * SIDE + z, x * SIDE + (z + step) % SIDE) f...  30.7 us
    pallas_call x1, Pallas kernels, experts(): call(expert_kernel, 'experts', jax.ShapeDtypeStruct((rows, columns), BF16...  26.1 us
    ppermute x12, waiting for transfers between devices, shift_x(): lax.ppermute(value, 'tp', [(x * SIDE + z, (x + step) % SIDE * SIDE + z) f...  23.9 us
    ppermute x15, starting transfers between devices, shift_z(): lax.ppermute(value, 'tp', [(x * SIDE + z, x * SIDE + (z + step) % SIDE) f...  23 us
    ppermute x12, starting transfers between devices, shift_x(): lax.ppermute(value, 'tp', [(x * SIDE + z, (x + step) % SIDE * SIDE + z) f...  19.5 us
    pallas_call x1, Pallas kernels, attention(): call(attention_kernel, 'attention', outs, [smem()] + [whole(array) for ar...  14.3 us
    pallas_call x2, Pallas kernels, projection(): call(functools.partial(projection_kernel, axis), 'projection', [jax.Shape...  13.2 us
  transfers between devices with their start and end apart: 30, of which 11 were waited for; matrix products, arithmetic and copies ran while one was open for 1% of the time, Pallas kernels for 9%

profile of v6, /device:TPU:0, one launch (start us, length us, event | category | flops | bytes accessed | tf_op | source)
XLA Modules:
  0.0 436.9 jit_solution(11185456999877348267)
XLA Ops:
  0.0 0.9 constant_dynamic-slice_fusion.8
  1.0 3.2 collective-permute-start.1
  4.2 1.2 collective-permute-start.2
  5.4 1.0 collective-permute-start
  6.8 1.7 collective-permute-done.2
  8.5 2.4 collective-permute-done
  11.0 1.7 collective-permute-start.3
  12.6 1.9 collective-permute-start.4
  14.5 2.9 collective-permute-done.3.refs_1_
  17.4 4.0 collective-permute-start.7
  21.5 1.3 constant_dynamic-slice_fusion
  22.8 1.1 collective-permute-start.12
  23.9 1.8 collective-permute-done.7.refs_5_
  25.7 3.7 collective-permute-start.9
  29.4 2.0 collective-permute-start.5
  31.4 0.7 copy.12.ids
  32.8 2.6 routes.1
  36.1 0.9 collective-permute-start.11
  37.1 0.8 collective-permute-start.10
  37.9 3.5 collective-permute-start.15
  41.3 0.9 collective-permute-start.13
  42.3 14.3 %attention.1 = (bf16[512,256]{1,0:T(8,128)(2,1)}, bf16[512,256]{1,0:T(8,128)(2,1)}, bf16[512,256]{1,0:T(8,128)(2,1)}, bf16[4096,128]{1,0:T(8,128)(2,1)}, bf16[128,4096]{1,0:T(8,128)(2,1)}) custom-call(s32[8]{0:T(128)} %concatenate.15.meta, bf16[2048,256]{1,0:T(8,128)(2,1)} %q_ref.1, bf16[4,128,256]{2,1,0:T(8,128)(2,1)} %copy-done.2, ...), custom_call_target="tpu_custom_call" | custom-call | flops 16000000000 | bytes 7000000 | tf_op jit(solution)/shard_map/attention/pallas_call | solution.py:203
  56.8 1.9 collective-permute-done.10.refs_4_
  58.7 1.3 collective-permute-start.17
  60.0 3.9 collective-permute-start.18
  63.9 0.8 copy-done.13
  64.8 7.1 %attention_end.1 = (bf16[512,256]{1,0:T(8,128)(2,1)}, bf16[512,256]{1,0:T(8,128)(2,1)}, bf16[512,256]{1,0:T(8,128)(2,1)}, bf16[512,256]{1,0:T(8,128)(2,1)}, bf16...) custom-call(s32[8]{0:T(128)} %concatenate.15.meta, bf16[2048,256]{1,0:T(8,128)(2,1)} %q_ref.1, ...), custom_call_target="tpu_custom_call" | custom-call | flops 6000000000 | bytes 7000000 | tf_op jit(solution)/shard_map/attention_end/pallas_call | solution.py:237
  72.9 2.7 collective-permute-start.20
  75.6 0.8 collective-permute-done.22.refs_5_
  76.5 1.3 copy-done.7
  77.8 6.6 %projection.2 = (bf16[128,2048]{1,0:T(8,128)(2,1)}, bf16[128,2048]{1,0:T(8,128)(2,1)}, bf16[128,2048]{1,0:T(8,128)(2,1)}, bf16[128,2048]{1,0:T(8,128)(2,1)}) custom-call(s32[8]{0:T(128)} %concatenate.15.meta, bf16[512,256]{1,0:T(8,128)(2,1)} %get-tuple-element.53.refs_0_, bf16[512,256]{1,0:T(8,128)(2,1)} %copy-done.27, bf16[512,256]{1,0:T(8,128)(2,1)} %copy-done.28, ...), custom_call_target="tpu_custom_call" | custom-call | flops 2147483648 | bytes 7000000 | tf_op jit(solution)/shard_map/projection/pallas_call | solution.py:274
  84.7 2.7 collective-permute-start.28
  87.9 0.9 collective-permute-start.21
  88.8 28.4 %collective-permute-done.21.refs_3_ = bf16[512,256]{1,0:T(8,128)(2,1)S(1)} collective-permute-done((bf16[512,256]{1,0:T(8,128)(2,1)S(1)}, bf16[512,256]{1,0:T(8,128)(2,1)S(1)}, u32[]{:S(2)}, u32[]{:S(2)}) %collective-permute-start.21) | collective-permute-done | bytes 262176 | tf_op jit(solution)/shard_map/ppermute | solution.py:37
  118.0 1.3 copy-done.6
  119.3 6.6 %projection.3 = (bf16[128,2048]{1,0:T(8,128)(2,1)}, bf16[128,2048]{1,0:T(8,128)(2,1)}, bf16[128,2048]{1,0:T(8,128)(2,1)}, bf16[128,2048]{1,0:T(8,128)(2,1)}) custom-call(s32[8]{0:T(128)} %concatenate.15.meta, bf16[512,256]{1,0:T(8,128)(2,1)} %get-tuple-element.54.refs_0_, bf16[512,256]{1,0:T(8,128)(2,1)} %copy-done.30, bf16[512,256]{1,0:T(8,128)(2,1)} %copy-done.31, ...), custom_call_target="tpu_custom_call" | custom-call | flops 2147483648 | bytes 7000000 | tf_op jit(solution)/shard_map/projection/pallas_call | solution.py:274
  125.9 6.1 %collective-permute-start.25 = (bf16[128,2048]{1,0:T(8,128)(2,1)}, bf16[128,2048]{1,0:T(8,128)(2,1)S(1)}, u32[]{:S(2)}, u32[]{:S(2)}) collective-permute-start(bf16[128,2048]{1,0:T(8,128)(2,1)} %get-tuple-element.69), channel_id=1, source_target_pairs={{0,8},{1,9},{2,10},{3,11},{4,12},{5,13},{6,14},{7,15},{8,0},{9,1},... | collective-permute-start | bytes 1572872 | tf_op jit(solution)/shard_map/ppermute | solution.py:29
  132.0 0.8 copy-done.12
  133.0 0.9 copy-done.16
  133.9 3.0 settle.1.refs_4_
  136.9 5.8 %collective-permute-done.24.refs_1_ = bf16[128,2048]{1,0:T(8,128)(2,1)S(1)} collective-permute-done((bf16[128,2048]{1,0:T(8,128)(2,1)}, bf16[128,2048]{1,0:T(8,128)(2,1)S(1)}, u32[]{:S(2)}, u32[]{:S(2)}) %collective-permute-start.24) | collective-permute-done | bytes 524320 | tf_op jit(solution)/shard_map/ppermute | solution.py:29
  142.7 11.6 %collective-permute-done.25.refs_2_ = bf16[128,2048]{1,0:T(8,128)(2,1)S(1)} collective-permute-done((bf16[128,2048]{1,0:T(8,128)(2,1)}, bf16[128,2048]{1,0:T(8,128)(2,1)S(1)}, u32[]{:S(2)}, u32[]{:S(2)}) %collective-permute-start.25) | collective-permute-done | bytes 524320 | tf_op jit(solution)/shard_map/ppermute | solution.py:29
  154.3 0.8 copy-done.18
  155.3 9.4 %dispatch.1 = (bf16[1024,4608]{1,0:T(8,128)(2,1)}, f32[128,4096]{1,0:T(8,128)}) custom-call(s32[8]{0:T(128)} %concatenate.15.meta, bf16[128,2048]{1,0:T(8,128)(2,1)} %get-tuple-element.67.refs_0_, bf16[128,2048]{1,0:T(8,128)(2,1)} %copy-done.17, bf16[128,2048]{1,0:T(8,128)(2,1)} %copy-done.18, bf16[128,2048]{1,0:T(8,128)(2,1)} %copy-done.19, ...), custom_call_target="tpu_custom_call" | custom-call | flops 3000000000 | bytes 16000000 | tf_op jit(solution)/shard_map/dispatch/pallas_call | solution.py:377
  164.7 121.7 %all_to_all.10 = bf16[128,8,4608]{2,1,0:T(8,128)(2,1)} all-to-all(bf16[128,8,4608]{2,1,0:T(8,128)(2,1)} %bitcast.18), channel_id=1, replica_groups=mesh['dp'=4,'ctx'=2,'tp'=16] {'dp','ctx','tp'}, dimensions={0} | all-to-all | bytes 18874368 | tf_op jit(solution)/shard_map/all_to_all | solution.py:635
  286.4 26.1 %experts.1 = bf16[1024,4608]{1,0:T(8,128)(2,1)} custom-call(bf16[1024,4608]{1,0:T(8,128)(2,1)} %bitcast.19, bf16[1024,4608]{1,0:T(8,128)(2,1)} %bitcast.20, bf16[1,4096,768]{2,1,0:T(8,128)(2,1)S(1)} %bitcast.15, bf16[1,768,4096]{2,1,0:T(8,128)(2,1)} %down_hbm.1), custom_call_target="tpu_custom_call" | custom-call | flops 14495514624 | bytes 32000000 | tf_op jit(solution)/shard_map/experts/pallas_call | solution.py:436
  312.5 115.5 %all_to_all.11 = bf16[128,8,4608]{2,1,0:T(8,128)(2,1)} all-to-all(bf16[128,8,4608]{2,1,0:T(8,128)(2,1)} %bitcast.21), channel_id=1, replica_groups=mesh['dp'=4,'ctx'=2,'tp'=16] {'dp','ctx','tp'}, dimensions={0} | all-to-all | bytes 18874368 | tf_op jit(solution)/shard_map/all_to_all | solution.py:635
  428.0 8.9 %combine.1 = bf16[128,4096]{1,0:T(8,128)(2,1)} custom-call(bf16[256,1024]{1,0:T(8,128)(2,1)} %get-tuple-element.41.main, bf16[256,128]{1,0:T(8,128)(2,1)} %get-tuple-element.42.late, bf16[1024,4608]{1,0:T(8,128)(2,1)} %bitcast.16, bf16[1024,4608]{1,0:T(8,128)(2,1)} %bitcast.17, f32[128,4096]{1,0:T(8,128)} %get-tuple-element.76.state), custom_call_target="tpu_custom_call" | custom-call | flops 4000000000 | bytes 13000000 | tf_op jit(solution)/shard_map/combine/pallas_call | solution.py:488
  (104 shorter events, 5.1 us)
Async XLA Ops:
  0.0 31.4 %copy-start.3 = (s32[128,8]{0,1:T(8,128)S(1)}, s32[128,8]{0,1:T(8,128)}, u32[]{:S(2)}) copy-start(s32[128,8]{0,1:T(8,128)} %param.18) | copy-start | bytes 12292
  0.0 32.1 %copy-start.4 = (f32[128,8]{0,1:T(8,128)S(1)}, f32[128,8]{0,1:T(8,128)}, u32[]{:S(2)}) copy-start(f32[128,8]{0,1:T(8,128)} %param.19) | copy-start | bytes 12292
  0.9 34.5 %copy-start.5 = (s32[4]{0:T(128)S(1)}, s32[4]{0:T(128)}, u32[]{:S(2)}) copy-start(s32[4]{0:T(128)} %param.14) | copy-start | bytes 52
  1.0 5.8 %collective-permute-start.1 = (bf16[128,256]{1,0:T(8,128)(2,1)S(1)}, bf16[128,256]{1,0:T(8,128)(2,1)S(1)}, u32[]{:S(2)}, u32[]{:S(2)}) collective-permute-start(bf16[128,256]{1,0:T(8,128)(2,1)S(1)} %pad_maximum_fusion.2), channel_id=1, source_target_pairs={{0,8},{1,9},{2,10},{3,11},{4,12},{5,13},{6,14},{7,15},{8,0},{9,1},... | collective-permute-start | bytes 196616 | tf_op jit(solution)/shard_map/ppermute | solution.py:29
  4.2 4.3 collective-permute-start.2
  5.4 5.5 %collective-permute-start = (bf16[128,256]{1,0:T(8,128)(2,1)S(1)}, bf16[128,256]{1,0:T(8,128)(2,1)S(1)}, u32[]{:S(2)}, u32[]{:S(2)}) collective-permute-start(bf16[128,256]{1,0:T(8,128)(2,1)S(1)} %pad_maximum_fusion.1), channel_id=1, source_target_pairs={{0,4},{1,5},{2,6},{3,7},{4,8},{5,9},{6,10},{7,11},{8,12},{9,13},{1... | collective-permute-start | bytes 196616 | tf_op jit(solution)/shard_map/ppermute | solution.py:29
  11.0 31.3 %copy-start.2 = (bf16[4,128,256]{2,1,0:T(8,128)(2,1)}, bf16[4,128,256]{2,1,0:T(8,128)(2,1)S(1)}, u32[]{:S(2)}) copy-start(bf16[4,128,256]{2,1,0:T(8,128)(2,1)S(1)} %pad_maximum_fusion.refs_0_) | copy-start | bytes 786436
  11.0 6.5 %collective-permute-start.3 = (bf16[4,128,256]{2,1,0:T(8,128)(2,1)S(1)}, bf16[4,128,256]{2,1,0:T(8,128)(2,1)S(1)}, u32[]{:S(2)}, u32[]{:S(2)}) collective-permute-start(bf16[4,128,256]{2,1,0:T(8,128)(2,1)S(1)} %pad_maximum_fusion.refs_0_), channel_id=1, source_target_pairs={{0,16},{16,0},{1,17},{17,1},{2,18},{18,2},{3,19},{19,3},{4,20},{20... | collective-permute-start | bytes 786440 | tf_op jit(solution)/shard_map/ppermute | solution.py:45
  12.6 11.2 %collective-permute-start.4 = (bf16[4,128,256]{2,1,0:T(8,128)(2,1)S(1)}, bf16[4,128,256]{2,1,0:T(8,128)(2,1)S(1)}, u32[]{:S(2)}, u32[]{:S(2)}) collective-permute-start(bf16[4,128,256]{2,1,0:T(8,128)(2,1)S(1)} %pad_maximum_fusion.refs_0_), channel_id=1, source_target_pairs={{0,1},{1,2},{2,3},{3,0},{4,5},{5,6},{6,7},{7,4},{8,9},{9,10},{10,1... | collective-permute-start | bytes 786440 | tf_op jit(solution)/shard_map/ppermute | solution.py:37
  17.4 24.9 %copy-start.20 = (bf16[4,128,256]{2,1,0:T(8,128)(2,1)}, bf16[4,128,256]{2,1,0:T(8,128)(2,1)S(1)}, u32[]{:S(2)}) copy-start(bf16[4,128,256]{2,1,0:T(8,128)(2,1)S(1)} %collective-permute-done.3.refs_1_) | copy-start | bytes 786436
  17.4 8.2 %collective-permute-start.7 = (bf16[4,128,256]{2,1,0:T(8,128)(2,1)S(1)}, bf16[4,128,256]{2,1,0:T(8,128)(2,1)S(1)}, u32[]{:S(2)}, u32[]{:S(2)}) collective-permute-start(bf16[4,128,256]{2,1,0:T(8,128)(2,1)S(1)} %collective-permute-done.3.refs_1_), channel_id=1, source_target_pairs={{0,3},{1,0},{2,1},{3,2},{4,7},{5,4},{6,5},{7,6},{8,11},{9,8},{10,9... | collective-permute-start | bytes 786440 | tf_op jit(solution)/shard_map/ppermute | solution.py:37
  22.7 33.9 %copy-start = (bf16[256,1024]{1,0:T(8,128)(2,1)}, bf16[256,1024]{1,0:T(8,128)(2,1)S(1)}, u32[]{:S(2)}) copy-start(bf16[256,1024]{1,0:T(8,128)(2,1)S(1)} %get-tuple-element.51.refs_7_) | copy-start | bytes 1572868
  22.7 33.9 %copy-start.1 = (bf16[256,1024]{1,0:T(8,128)(2,1)}, bf16[256,1024]{1,0:T(8,128)(2,1)S(1)}, u32[]{:S(2)}) copy-start(bf16[256,1024]{1,0:T(8,128)(2,1)S(1)} %get-tuple-element.50.refs_3_) | copy-start | bytes 1572868
  22.8 18.6 %collective-permute-start.12 = (bf16[256,1024]{1,0:T(8,128)(2,1)S(1)}, bf16[256,1024]{1,0:T(8,128)(2,1)S(1)}, u32[]{:S(2)}, u32[]{:S(2)}) collective-permute-start(bf16[256,1024]{1,0:T(8,128)(2,1)S(1)} %get-tuple-element.50.refs_3_), channel_id=1, source_target_pairs={{0,12},{1,13},{2,14},{3,15},{4,0},{5,1},{6,2},{7,3},{8,4},{9,5},{1... | collective-permute-start | bytes 1572872 | tf_op jit(solution)/shard_map/ppermute | solution.py:29
  23.9 18.4 %copy-start.21 = (bf16[4,128,256]{2,1,0:T(8,128)(2,1)}, bf16[4,128,256]{2,1,0:T(8,128)(2,1)S(1)}, u32[]{:S(2)}) copy-start(bf16[4,128,256]{2,1,0:T(8,128)(2,1)S(1)} %collective-permute-done.4.refs_2_) | copy-start | bytes 786436
  23.9 12.2 %collective-permute-start.8 = (bf16[4,128,256]{2,1,0:T(8,128)(2,1)S(1)}, bf16[4,128,256]{2,1,0:T(8,128)(2,1)S(1)}, u32[]{:S(2)}, u32[]{:S(2)}) collective-permute-start(bf16[4,128,256]{2,1,0:T(8,128)(2,1)S(1)} %collective-permute-done.4.refs_2_), channel_id=1, source_target_pairs={{0,1},{1,2},{2,3},{3,0},{4,5},{5,6},{6,7},{7,4},{8,9},{9,10},{10,1... | collective-permute-start | bytes 786440 | tf_op jit(solution)/shard_map/ppermute | solution.py:37
  25.7 16.6 %copy-start.22 = (bf16[4,128,256]{2,1,0:T(8,128)(2,1)}, bf16[4,128,256]{2,1,0:T(8,128)(2,1)S(1)}, u32[]{:S(2)}) copy-start(bf16[4,128,256]{2,1,0:T(8,128)(2,1)S(1)} %collective-permute-done.7.refs_5_) | copy-start | bytes 786436
  25.7 11.4 %collective-permute-start.9 = (bf16[4,128,256]{2,1,0:T(8,128)(2,1)S(1)}, bf16[4,128,256]{2,1,0:T(8,128)(2,1)S(1)}, u32[]{:S(2)}, u32[]{:S(2)}) collective-permute-start(bf16[4,128,256]{2,1,0:T(8,128)(2,1)S(1)} %collective-permute-done.7.refs_5_), channel_id=1, source_target_pairs={{0,3},{1,0},{2,1},{3,2},{4,7},{5,4},{6,5},{7,6},{8,11},{9,8},{10,9... | collective-permute-start | bytes 786440 | tf_op jit(solution)/shard_map/ppermute | solution.py:37
  29.3 8.5 %collective-permute-start.6 = (bf16[4,128,256]{2,1,0:T(8,128)(2,1)S(1)}, bf16[4,128,256]{2,1,0:T(8,128)(2,1)S(1)}, u32[]{:S(2)}, u32[]{:S(2)}) collective-permute-start(bf16[4,128,256]{2,1,0:T(8,128)(2,1)S(1)} %pad_maximum_fusion.refs_0_), channel_id=1, source_target_pairs={{0,3},{1,0},{2,1},{3,2},{4,7},{5,4},{6,5},{7,6},{8,11},{9,8},{10,9... | collective-permute-start | bytes 786440 | tf_op jit(solution)/shard_map/ppermute | solution.py:37
  29.4 11.9 %collective-permute-start.5 = (bf16[4,128,256]{2,1,0:T(8,128)(2,1)S(1)}, bf16[4,128,256]{2,1,0:T(8,128)(2,1)}, u32[]{:S(2)}, u32[]{:S(2)}) collective-permute-start(bf16[4,128,256]{2,1,0:T(8,128)(2,1)S(1)} %collective-permute-done.3.refs_1_), channel_id=1, source_target_pairs={{0,1},{1,2},{2,3},{3,0},{4,5},{5,6},{6,7},{7,4},{8,9},{9,10},{10,1... | collective-permute-start | bytes 786440 | tf_op jit(solution)/shard_map/ppermute | solution.py:37
  36.1 6.2 %copy-start.23 = (bf16[4,128,256]{2,1,0:T(8,128)(2,1)}, bf16[4,128,256]{2,1,0:T(8,128)(2,1)S(1)}, u32[]{:S(2)}) copy-start(bf16[4,128,256]{2,1,0:T(8,128)(2,1)S(1)} %collective-permute-done.8.refs_6_) | copy-start | bytes 786436
  36.1 20.5 %collective-permute-start.11 = (bf16[256,1024]{1,0:T(8,128)(2,1)S(1)}, bf16[256,1024]{1,0:T(8,128)(2,1)S(1)}, u32[]{:S(2)}, u32[]{:S(2)}) collective-permute-start(bf16[256,1024]{1,0:T(8,128)(2,1)S(1)} %get-tuple-element.50.refs_3_), channel_id=1, source_target_pairs={{0,8},{1,9},{2,10},{3,11},{4,12},{5,13},{6,14},{7,15},{8,0},{9,1},... | collective-permute-start | bytes 1572872 | tf_op jit(solution)/shard_map/ppermute | solution.py:29
  37.1 21.6 %collective-permute-start.10 = (bf16[256,1024]{1,0:T(8,128)(2,1)S(1)}, bf16[256,1024]{1,0:T(8,128)(2,1)S(1)}, u32[]{:S(2)}, u32[]{:S(2)}) collective-permute-start(bf16[256,1024]{1,0:T(8,128)(2,1)S(1)} %get-tuple-element.50.refs_3_), channel_id=1, source_target_pairs={{0,4},{1,5},{2,6},{3,7},{4,8},{5,9},{6,10},{7,11},{8,12},{9,13},{1... | collective-permute-start | bytes 1572872 | tf_op jit(solution)/shard_map/ppermute | solution.py:29
  37.9 22.1 %collective-permute-start.15 = (bf16[256,1024]{1,0:T(8,128)(2,1)S(1)}, bf16[256,1024]{1,0:T(8,128)(2,1)S(1)}, u32[]{:S(2)}, u32[]{:S(2)}) collective-permute-start(bf16[256,1024]{1,0:T(8,128)(2,1)S(1)} %get-tuple-element.51.refs_7_), channel_id=1, source_target_pairs={{0,3},{1,0},{2,1},{3,2},{4,7},{5,4},{6,5},{7,6},{8,11},{9,8},{10,9... | collective-permute-start | bytes 1572872 | tf_op jit(solution)/shard_map/ppermute | solution.py:37
  41.3 22.5 %collective-permute-start.14 = (bf16[256,1024]{1,0:T(8,128)(2,1)S(1)}, bf16[256,1024]{1,0:T(8,128)(2,1)S(1)}, u32[]{:S(2)}, u32[]{:S(2)}) collective-permute-start(bf16[256,1024]{1,0:T(8,128)(2,1)S(1)} %get-tuple-element.51.refs_7_), channel_id=1, source_target_pairs={{0,2},{1,3},{2,0},{3,1},{4,6},{5,7},{6,4},{7,5},{8,10},{9,11},{10,... | collective-permute-start | bytes 1572872 | tf_op jit(solution)/shard_map/ppermute | solution.py:37
  41.3 15.3 %copy-start.8 = (bf16[256,1024]{1,0:T(8,128)(2,1)}, bf16[256,1024]{1,0:T(8,128)(2,1)S(1)}, u32[]{:S(2)}) copy-start(bf16[256,1024]{1,0:T(8,128)(2,1)S(1)} %collective-permute-done.12.refs_6_) | copy-start | bytes 1572868
  41.3 22.5 %collective-permute-start.13 = (bf16[256,1024]{1,0:T(8,128)(2,1)S(1)}, bf16[256,1024]{1,0:T(8,128)(2,1)S(1)}, u32[]{:S(2)}, u32[]{:S(2)}) collective-permute-start(bf16[256,1024]{1,0:T(8,128)(2,1)S(1)} %get-tuple-element.51.refs_7_), channel_id=1, source_target_pairs={{0,1},{1,2},{2,3},{3,0},{4,5},{5,6},{6,7},{7,4},{8,9},{9,10},{10,1... | collective-permute-start | bytes 1572872 | tf_op jit(solution)/shard_map/ppermute | solution.py:37
  56.7 7.2 %copy-start.9 = (bf16[256,1024]{1,0:T(8,128)(2,1)}, bf16[256,1024]{1,0:T(8,128)(2,1)S(1)}, u32[]{:S(2)}) copy-start(bf16[256,1024]{1,0:T(8,128)(2,1)S(1)} %collective-permute-done.11.refs_5_) | copy-start | bytes 1572868
  56.7 15.3 %collective-permute-start.16 = (bf16[512,256]{1,0:T(8,128)(2,1)}, bf16[512,256]{1,0:T(8,128)(2,1)S(1)}, u32[]{:S(2)}, u32[]{:S(2)}) collective-permute-start(bf16[512,256]{1,0:T(8,128)(2,1)} %get-tuple-element.47.refs_0_), channel_id=1, source_target_pairs={{0,4},{1,5},{2,6},{3,7},{4,8},{5,9},{6,10},{7,11},{8,12},{9,13},{1... | collective-permute-start | bytes 786440 | tf_op jit(solution)/shard_map/ppermute | solution.py:29
  58.7 13.3 %collective-permute-start.17 = (bf16[512,256]{1,0:T(8,128)(2,1)}, bf16[512,256]{1,0:T(8,128)(2,1)S(1)}, u32[]{:S(2)}, u32[]{:S(2)}) collective-permute-start(bf16[512,256]{1,0:T(8,128)(2,1)} %get-tuple-element.48.refs_1_), channel_id=1, source_target_pairs={{0,8},{1,9},{2,10},{3,11},{4,12},{5,13},{6,14},{7,15},{8,0},{9,1},... | collective-permute-start | bytes 786440 | tf_op jit(solution)/shard_map/ppermute | solution.py:29
  60.0 12.0 %collective-permute-start.18 = (bf16[512,256]{1,0:T(8,128)(2,1)}, bf16[512,256]{1,0:T(8,128)(2,1)S(1)}, u32[]{:S(2)}, u32[]{:S(2)}) collective-permute-start(bf16[512,256]{1,0:T(8,128)(2,1)} %get-tuple-element.49.refs_2_), channel_id=1, source_target_pairs={{0,12},{1,13},{2,14},{3,15},{4,0},{5,1},{6,2},{7,3},{8,4},{9,5},{1... | collective-permute-start | bytes 786440 | tf_op jit(solution)/shard_map/ppermute | solution.py:29
  72.0 4.5 %collective-permute-start.22 = (bf16[1024,1024]{1,0:T(8,128)(2,1)}, bf16[1024,1024]{1,0:T(8,128)(2,1)S(1)}, u32[]{:S(2)}, u32[]{:S(2)}) collective-permute-start(bf16[1024,1024]{1,0:T(8,128)(2,1)} %get-tuple-element.63.refs_4_), channel_id=1, source_target_pairs={{0,32},{32,0},{64,96},{96,64},{1,33},{33,1},{65,97},{97,65},{2,34}... | collective-permute-start | bytes 6291464 | tf_op jit(solution)/shard_map/ppermute | solution.py:49
  72.1 45.2 %collective-permute-start.23 = (bf16[1024,1024]{1,0:T(8,128)(2,1)}, bf16[1024,1024]{1,0:T(8,128)(2,1)S(1)}, u32[]{:S(2)}, u32[]{:S(2)}) collective-permute-start(bf16[1024,1024]{1,0:T(8,128)(2,1)} %get-tuple-element.66.refs_4_), channel_id=1, source_target_pairs={{0,32},{32,0},{64,96},{96,64},{1,33},{33,1},{65,97},{97,65},{2,34}... | collective-permute-start | bytes 6291464 | tf_op jit(solution)/shard_map/ppermute | solution.py:49
  72.6 15.3 %collective-permute-start.19 = (bf16[512,256]{1,0:T(8,128)(2,1)}, bf16[512,256]{1,0:T(8,128)(2,1)S(1)}, u32[]{:S(2)}, u32[]{:S(2)}) collective-permute-start(bf16[512,256]{1,0:T(8,128)(2,1)} %get-tuple-element.56), channel_id=1, source_target_pairs={{0,1},{1,2},{2,3},{3,0},{4,5},{5,6},{6,7},{7,4},{8,9},{9,10},{10,1... | collective-permute-start | bytes 786440 | tf_op jit(solution)/shard_map/ppermute | solution.py:37
  72.8 15.1 %copy-start.26 = (bf16[512,256]{1,0:T(8,128)(2,1)S(1)}, bf16[512,256]{1,0:T(8,128)(2,1)}, u32[]{:S(2)}) copy-start(bf16[512,256]{1,0:T(8,128)(2,1)} %get-tuple-element.60) | copy-start | bytes 786436
  72.9 15.1 %collective-permute-start.20 = (bf16[512,256]{1,0:T(8,128)(2,1)}, bf16[512,256]{1,0:T(8,128)(2,1)S(1)}, u32[]{:S(2)}, u32[]{:S(2)}) collective-permute-start(bf16[512,256]{1,0:T(8,128)(2,1)} %get-tuple-element.58), channel_id=1, source_target_pairs={{0,2},{1,3},{2,0},{3,1},{4,6},{5,7},{6,4},{7,5},{8,10},{9,11},{10,... | collective-permute-start | bytes 786440 | tf_op jit(solution)/shard_map/ppermute | solution.py:37
  84.4 47.6 %collective-permute-start.27 = (bf16[128,2048]{1,0:T(8,128)(2,1)}, bf16[128,2048]{1,0:T(8,128)(2,1)S(1)}, u32[]{:S(2)}, u32[]{:S(2)}) collective-permute-start(bf16[128,2048]{1,0:T(8,128)(2,1)} %get-tuple-element.71), channel_id=1, source_target_pairs={{0,1},{1,2},{2,3},{3,0},{4,5},{5,6},{6,7},{7,4},{8,9},{9,10},{10,1... | collective-permute-start | bytes 1572872 | tf_op jit(solution)/shard_map/ppermute | solution.py:37
  84.7 47.3 %collective-permute-start.28 = (bf16[128,2048]{1,0:T(8,128)(2,1)}, bf16[128,2048]{1,0:T(8,128)(2,1)S(1)}, u32[]{:S(2)}, u32[]{:S(2)}) collective-permute-start(bf16[128,2048]{1,0:T(8,128)(2,1)} %get-tuple-element.72), channel_id=1, source_target_pairs={{0,2},{1,3},{2,0},{3,1},{4,6},{5,7},{6,4},{7,5},{8,10},{9,11},{10,... | collective-permute-start | bytes 1572872 | tf_op jit(solution)/shard_map/ppermute | solution.py:37
  87.9 29.4 %copy-start.30 = (bf16[512,256]{1,0:T(8,128)(2,1)}, bf16[512,256]{1,0:T(8,128)(2,1)S(1)}, u32[]{:S(2)}) copy-start(bf16[512,256]{1,0:T(8,128)(2,1)S(1)} %collective-permute-done.19.refs_1_) | copy-start | bytes 786436
  87.9 44.1 %collective-permute-start.29 = (bf16[128,2048]{1,0:T(8,128)(2,1)}, bf16[128,2048]{1,0:T(8,128)(2,1)S(1)}, u32[]{:S(2)}, u32[]{:S(2)}) collective-permute-start(bf16[128,2048]{1,0:T(8,128)(2,1)} %get-tuple-element.73), channel_id=1, source_target_pairs={{0,3},{1,0},{2,1},{3,2},{4,7},{5,4},{6,5},{7,6},{8,11},{9,8},{10,9... | collective-permute-start | bytes 1572872 | tf_op jit(solution)/shard_map/ppermute | solution.py:37
  87.9 29.3 %copy-start.31 = (bf16[512,256]{1,0:T(8,128)(2,1)}, bf16[512,256]{1,0:T(8,128)(2,1)S(1)}, u32[]{:S(2)}) copy-start(bf16[512,256]{1,0:T(8,128)(2,1)S(1)} %collective-permute-done.20.refs_2_) | copy-start | bytes 786436
  87.9 29.3 %collective-permute-start.21 = (bf16[512,256]{1,0:T(8,128)(2,1)S(1)}, bf16[512,256]{1,0:T(8,128)(2,1)S(1)}, u32[]{:S(2)}, u32[]{:S(2)}) collective-permute-start(bf16[512,256]{1,0:T(8,128)(2,1)S(1)} %copy-done.26), channel_id=1, source_target_pairs={{0,3},{1,0},{2,1},{3,2},{4,7},{5,4},{6,5},{7,6},{8,11},{9,8},{10,9... | collective-permute-start | bytes 786440 | tf_op jit(solution)/shard_map/ppermute | solution.py:37
  125.9 16.8 %collective-permute-start.24 = (bf16[128,2048]{1,0:T(8,128)(2,1)}, bf16[128,2048]{1,0:T(8,128)(2,1)S(1)}, u32[]{:S(2)}, u32[]{:S(2)}) collective-permute-start(bf16[128,2048]{1,0:T(8,128)(2,1)} %get-tuple-element.68), channel_id=1, source_target_pairs={{0,4},{1,5},{2,6},{3,7},{4,8},{5,9},{6,10},{7,11},{8,12},{9,13},{1... | collective-permute-start | bytes 1572872 | tf_op jit(solution)/shard_map/ppermute | solution.py:29
  125.9 28.4 %collective-permute-start.25 = (bf16[128,2048]{1,0:T(8,128)(2,1)}, bf16[128,2048]{1,0:T(8,128)(2,1)S(1)}, u32[]{:S(2)}, u32[]{:S(2)}) collective-permute-start(bf16[128,2048]{1,0:T(8,128)(2,1)} %get-tuple-element.69), channel_id=1, source_target_pairs={{0,8},{1,9},{2,10},{3,11},{4,12},{5,13},{6,14},{7,15},{8,0},{9,1},... | collective-permute-start | bytes 1572872 | tf_op jit(solution)/shard_map/ppermute | solution.py:29
  132.0 22.3 %collective-permute-start.26 = (bf16[128,2048]{1,0:T(8,128)(2,1)}, bf16[128,2048]{1,0:T(8,128)(2,1)S(1)}, u32[]{:S(2)}, u32[]{:S(2)}) collective-permute-start(bf16[128,2048]{1,0:T(8,128)(2,1)} %get-tuple-element.70), channel_id=1, source_target_pairs={{0,12},{1,13},{2,14},{3,15},{4,0},{5,1},{6,2},{7,3},{8,4},{9,5},{1... | collective-permute-start | bytes 1572872 | tf_op jit(solution)/shard_map/ppermute | solution.py:29
  142.7 11.6 %copy-start.17 = (bf16[128,2048]{1,0:T(8,128)(2,1)}, bf16[128,2048]{1,0:T(8,128)(2,1)S(1)}, u32[]{:S(2)}) copy-start(bf16[128,2048]{1,0:T(8,128)(2,1)S(1)} %collective-permute-done.24.refs_1_) | copy-start | bytes 1572868
  155.3 131.1 %slice-start = ((s8[6291456]{0:T(1024)(128)(4,1)}), s8[2097152]{0:T(1024)(128)(4,1)S(1)}, s32[]{:S(2)}) async-start(s8[6291456]{0:T(1024)(128)(4,1)} %bitcast.14), calls=%async_computation.2 | async-start | bytes 4194304
  164.7 121.7 %slice-start.1 = ((s8[6291456]{0:T(1024)(128)(4,1)}), s8[4194304]{0:T(1024)(128)(4,1)S(1)}, s32[]{:S(2)}) async-start(s8[6291456]{0:T(1024)(128)(4,1)} %bitcast.14), calls=%async_computation.3 | async-start | bytes 8388608
  (17 other events, 41.9 us)

commit v7 on v6

--- a/solution.py
+++ b/solution.py
@@ -622,9 +622,10 @@
     context_x = exchange(shift_x, [mine, *far])
     other_x = swap_core(after(weights_x, *context_x[1:]))
     context_z = exchange(shift_z, [after(part, *context_x) for part in parts])
-    other_z = swap_core(after(weights_z, *context_x))
     terms_z = projection(6, meta, context_x, [weights_x, other_x])
-    terms_x = projection(5, meta, context_z, [after(weights_z, terms_z[0]), other_z])
+    terms_z = [after(term, *context_z[1:]) for term in terms_z]
+    weights_z = after(weights_z, *terms_z)
+    terms_x = projection(5, meta, context_z, [weights_z, swap_core(weights_z)])
     terms_z, terms_x = exchange(shift_z, terms_z), exchange(shift_x, terms_x)
     outgoing, state = dispatch(
         meta, terms_x, settle(meta, terms_z, residual), residual, norm_gain[None, :], main, late

time: 438 us -> 414 us (0.945)
  waiting for transfers between devices: 58.4 us -> 31.2 us
    ppermute x15, waiting for transfers between devices: 30.7 us -> 14.9 us  [shift_z(): lax.ppermute(value, 'tp', [(x * SIDE + z, x * SIDE + (z + step) % SIDE) f...]
    ppermute x12, waiting for transfers between devices: 23.9 us -> 11.6 us  [shift_x(): lax.ppermute(value, 'tp', [(x * SIDE + z, (x + step) % SIDE * SIDE + z) f...]
  transfers between devices with their start and end apart: 30 -> 30, of which waited for: 11 -> 13; matrix products, arithmetic and copies ran while one was open for 1% -> 1% of each run, Pallas kernels for 9% -> 10%
where the time goes in v7:
time: 414 us; the launch traced here: 413 us
  blocking collectives  237 us (57%)
  Pallas kernels  87.6 us (21%)
  starting transfers between devices  45.8 us (11%)
  waiting for transfers between devices  31.2 us (8%)
  local copies, waits for them, and re-layouts  10.6 us (3%)
    all_to_all x2, blocking collectives, all_to_all(): lax.all_to_all(blocks, ('dp', 'ctx', 'tp'), split_axis=0, concat_axis=0,...  237 us
    pallas_call x1, Pallas kernels, experts(): call(expert_kernel, 'experts', jax.ShapeDtypeStruct((rows, columns), BF16...  26.1 us
    ppermute x15, starting transfers between devices, shift_z(): lax.ppermute(value, 'tp', [(x * SIDE + z, x * SIDE + (z + step) % SIDE) f...  22.7 us
    ppermute x12, starting transfers between devices, shift_x(): lax.ppermute(value, 'tp', [(x * SIDE + z, (x + step) % SIDE * SIDE + z) f...  21.3 us
    pallas_call x1, Pallas kernels, attention(): call(attention_kernel, 'attention', outs, [smem()] + [whole(array) for ar...  15.8 us
    ppermute x15, waiting for transfers between devices, shift_z(): lax.ppermute(value, 'tp', [(x * SIDE + z, x * SIDE + (z + step) % SIDE) f...  14.9 us
    pallas_call x2, Pallas kernels, projection(): call(functools.partial(projection_kernel, axis), 'projection', [jax.Shape...  13.2 us
    ppermute x12, waiting for transfers between devices, shift_x(): lax.ppermute(value, 'tp', [(x * SIDE + z, (x + step) % SIDE * SIDE + z) f...  11.6 us
  transfers between devices with their start and end apart: 30, of which 13 were waited for; matrix products, arithmetic and copies ran while one was open for 1% of the time, Pallas kernels for 10%

profile of v7, /device:TPU:0, one launch (start us, length us, event | category | flops | bytes accessed | tf_op | source)
XLA Modules:
  0.0 412.7 jit_solution(6371819620296975798)
XLA Ops:
  0.0 0.9 constant_dynamic-slice_fusion.8
  1.0 3.2 collective-permute-start.1
  4.2 1.2 collective-permute-start.2
  5.4 1.0 collective-permute-start
  6.8 1.7 collective-permute-done.2
  8.5 2.4 collective-permute-done
  11.0 1.7 collective-permute-start.3
  12.6 1.9 collective-permute-start.4
  14.5 2.9 collective-permute-done.3.refs_1_
  17.4 4.0 collective-permute-start.7
  21.5 1.3 constant_dynamic-slice_fusion
  22.8 1.1 collective-permute-start.12
  23.9 1.8 collective-permute-done.7.refs_5_
  25.7 3.7 collective-permute-start.9
  29.4 2.0 collective-permute-start.5
  32.8 2.6 routes.1
  36.1 0.9 collective-permute-start.11
  37.1 0.8 collective-permute-start.10
  37.9 3.5 collective-permute-start.15
  41.3 0.9 collective-permute-start.13
  42.3 15.8 %attention.1 = (bf16[512,256]{1,0:T(8,128)(2,1)}, bf16[512,256]{1,0:T(8,128)(2,1)}, bf16[512,256]{1,0:T(8,128)(2,1)}, bf16[4096,128]{1,0:T(8,128)(2,1)}, bf16[128,4096]{1,0:T(8,128)(2,1)}) custom-call(s32[8]{0:T(128)} %concatenate.15.meta, bf16[2048,256]{1,0:T(8,128)(2,1)} %q_ref.1, bf16[4,128,256]{2,1,0:T(8,128)(2,1)} %copy-done.2, ...), custom_call_target="tpu_custom_call" | custom-call | flops 16000000000 | bytes 7000000 | tf_op jit(solution)/shard_map/attention/pallas_call | solution.py:203
  58.7 1.3 collective-permute-start.17
  60.0 3.9 collective-permute-start.18
  63.9 0.8 copy-done.13
  64.8 8.5 %attention_end.1 = (bf16[512,256]{1,0:T(8,128)(2,1)}, bf16[512,256]{1,0:T(8,128)(2,1)}, bf16[512,256]{1,0:T(8,128)(2,1)}, bf16[512,256]{1,0:T(8,128)(2,1)}, bf16...) custom-call(s32[8]{0:T(128)} %concatenate.15.meta, bf16[2048,256]{1,0:T(8,128)(2,1)} %q_ref.1, ...), custom_call_target="tpu_custom_call" | custom-call | flops 6000000000 | bytes 7000000 | tf_op jit(solution)/shard_map/attention_end/pallas_call | solution.py:237
  74.0 2.6 collective-permute-start.20
  76.8 1.0 collective-permute-done.22.refs_5_
  77.9 1.3 copy-done.8
  79.2 6.6 %projection.2 = (bf16[128,2048]{1,0:T(8,128)(2,1)}, bf16[128,2048]{1,0:T(8,128)(2,1)}, bf16[128,2048]{1,0:T(8,128)(2,1)}, bf16[128,2048]{1,0:T(8,128)(2,1)}) custom-call(s32[8]{0:T(128)} %concatenate.15.meta, bf16[512,256]{1,0:T(8,128)(2,1)} %get-tuple-element.56.refs_0_, bf16[512,256]{1,0:T(8,128)(2,1)} %copy-done.27, bf16[512,256]{1,0:T(8,128)(2,1)} %copy-done.28, ...), custom_call_target="tpu_custom_call" | custom-call | flops 2147483648 | bytes 7000000 | tf_op jit(solution)/shard_map/projection/pallas_call | solution.py:274
  85.8 3.5 collective-permute-done.19.refs_1_
  89.9 2.4 collective-permute-start.29
  92.3 0.9 collective-permute-start.27
  93.2 0.8 collective-permute-done.23.refs_5_
  94.1 1.3 copy-done.7
  95.4 6.6 %projection.3 = (bf16[128,2048]{1,0:T(8,128)(2,1)}, bf16[128,2048]{1,0:T(8,128)(2,1)}, bf16[128,2048]{1,0:T(8,128)(2,1)}, bf16[128,2048]{1,0:T(8,128)(2,1)}) custom-call(s32[8]{0:T(128)} %concatenate.15.meta, bf16[512,256]{1,0:T(8,128)(2,1)} %get-tuple-element.57.refs_0_, bf16[512,256]{1,0:T(8,128)(2,1)} %copy-done.30, bf16[512,256]{1,0:T(8,128)(2,1)} %copy-done.31, ...), custom_call_target="tpu_custom_call" | custom-call | flops 2147483648 | bytes 7000000 | tf_op jit(solution)/shard_map/projection/pallas_call | solution.py:274
  102.0 4.7 %collective-permute-start.25 = (bf16[128,2048]{1,0:T(8,128)(2,1)}, bf16[128,2048]{1,0:T(8,128)(2,1)S(1)}, u32[]{:S(2)}, u32[]{:S(2)}) collective-permute-start(bf16[128,2048]{1,0:T(8,128)(2,1)} %get-tuple-element.78), channel_id=1, source_target_pairs={{0,8},{1,9},{2,10},{3,11},{4,12},{5,13},{6,14},{7,15},{8,0},{9,1},... | collective-permute-start | bytes 1572872 | tf_op jit(solution)/shard_map/ppermute | solution.py:29
  106.7 9.0 %collective-permute-done.29.refs_3_ = bf16[128,2048]{1,0:T(8,128)(2,1)S(1)} collective-permute-done((bf16[128,2048]{1,0:T(8,128)(2,1)}, bf16[128,2048]{1,0:T(8,128)(2,1)S(1)}, u32[]{:S(2)}, u32[]{:S(2)}) %collective-permute-start.29) | collective-permute-done | bytes 524320 | tf_op jit(solution)/shard_map/ppermute | solution.py:37
  115.7 3.2 collective-permute-start.26
  118.9 0.8 copy-done.16
  119.7 0.9 copy-done.18
  120.6 3.0 settle.1.refs_4_
  123.5 6.5 %collective-permute-done.25.refs_2_ = bf16[128,2048]{1,0:T(8,128)(2,1)S(1)} collective-permute-done((bf16[128,2048]{1,0:T(8,128)(2,1)}, bf16[128,2048]{1,0:T(8,128)(2,1)S(1)}, u32[]{:S(2)}, u32[]{:S(2)}) %collective-permute-start.25) | collective-permute-done | bytes 524320 | tf_op jit(solution)/shard_map/ppermute | solution.py:29
  130.1 0.8 copy-done.19
  131.1 9.4 %dispatch.1 = (bf16[1024,4608]{1,0:T(8,128)(2,1)}, f32[128,4096]{1,0:T(8,128)}) custom-call(s32[8]{0:T(128)} %concatenate.15.meta, bf16[128,2048]{1,0:T(8,128)(2,1)} %get-tuple-element.76.refs_0_, bf16[128,2048]{1,0:T(8,128)(2,1)} %copy-done.17, bf16[128,2048]{1,0:T(8,128)(2,1)} %copy-done.19, bf16[128,2048]{1,0:T(8,128)(2,1)} %copy-done.20, ...), custom_call_target="tpu_custom_call" | custom-call | flops 3000000000 | bytes 16000000 | tf_op jit(solution)/shard_map/dispatch/pallas_call | solution.py:377
  140.5 121.6 %all_to_all.10 = bf16[128,8,4608]{2,1,0:T(8,128)(2,1)} all-to-all(bf16[128,8,4608]{2,1,0:T(8,128)(2,1)} %bitcast.18), channel_id=1, replica_groups=mesh['dp'=4,'ctx'=2,'tp'=16] {'dp','ctx','tp'}, dimensions={0} | all-to-all | bytes 18874368 | tf_op jit(solution)/shard_map/all_to_all | solution.py:636
  262.1 26.1 %experts.1 = bf16[1024,4608]{1,0:T(8,128)(2,1)} custom-call(bf16[1024,4608]{1,0:T(8,128)(2,1)} %bitcast.19, bf16[1024,4608]{1,0:T(8,128)(2,1)} %bitcast.20, bf16[1,4096,768]{2,1,0:T(8,128)(2,1)S(1)} %bitcast.15, bf16[1,768,4096]{2,1,0:T(8,128)(2,1)} %down_hbm.1), custom_call_target="tpu_custom_call" | custom-call | flops 14495514624 | bytes 32000000 | tf_op jit(solution)/shard_map/experts/pallas_call | solution.py:436
  288.3 115.5 %all_to_all.11 = bf16[128,8,4608]{2,1,0:T(8,128)(2,1)} all-to-all(bf16[128,8,4608]{2,1,0:T(8,128)(2,1)} %bitcast.21), channel_id=1, replica_groups=mesh['dp'=4,'ctx'=2,'tp'=16] {'dp','ctx','tp'}, dimensions={0} | all-to-all | bytes 18874368 | tf_op jit(solution)/shard_map/all_to_all | solution.py:636
  403.7 8.9 %combine.1 = bf16[128,4096]{1,0:T(8,128)(2,1)} custom-call(bf16[256,1024]{1,0:T(8,128)(2,1)} %get-tuple-element.44.main, bf16[256,128]{1,0:T(8,128)(2,1)} %get-tuple-element.45.late, bf16[1024,4608]{1,0:T(8,128)(2,1)} %bitcast.16, bf16[1024,4608]{1,0:T(8,128)(2,1)} %bitcast.17, f32[128,4096]{1,0:T(8,128)} %get-tuple-element.82.state), custom_call_target="tpu_custom_call" | custom-call | flops 4000000000 | bytes 13000000 | tf_op jit(solution)/shard_map/combine/pallas_call | solution.py:488
  (104 shorter events, 5.3 us)
Async XLA Ops:
  0.0 31.4 %copy-start.3 = (s32[128,8]{0,1:T(8,128)S(1)}, s32[128,8]{0,1:T(8,128)}, u32[]{:S(2)}) copy-start(s32[128,8]{0,1:T(8,128)} %param.18) | copy-start | bytes 12292
  0.0 32.1 %copy-start.4 = (f32[128,8]{0,1:T(8,128)S(1)}, f32[128,8]{0,1:T(8,128)}, u32[]{:S(2)}) copy-start(f32[128,8]{0,1:T(8,128)} %param.19) | copy-start | bytes 12292
  0.9 34.5 %copy-start.5 = (s32[4]{0:T(128)S(1)}, s32[4]{0:T(128)}, u32[]{:S(2)}) copy-start(s32[4]{0:T(128)} %param.14) | copy-start | bytes 52
  1.0 5.8 %collective-permute-start.1 = (bf16[128,256]{1,0:T(8,128)(2,1)S(1)}, bf16[128,256]{1,0:T(8,128)(2,1)S(1)}, u32[]{:S(2)}, u32[]{:S(2)}) collective-permute-start(bf16[128,256]{1,0:T(8,128)(2,1)S(1)} %pad_maximum_fusion.2), channel_id=1, source_target_pairs={{0,8},{1,9},{2,10},{3,11},{4,12},{5,13},{6,14},{7,15},{8,0},{9,1},... | collective-permute-start | bytes 196616 | tf_op jit(solution)/shard_map/ppermute | solution.py:29
  4.2 4.3 %collective-permute-start.2 = (bf16[128,256]{1,0:T(8,128)(2,1)S(1)}, bf16[128,256]{1,0:T(8,128)(2,1)S(1)}, u32[]{:S(2)}, u32[]{:S(2)}) collective-permute-start(bf16[128,256]{1,0:T(8,128)(2,1)S(1)} %pad_maximum_fusion.3), channel_id=1, source_target_pairs={{0,12},{1,13},{2,14},{3,15},{4,0},{5,1},{6,2},{7,3},{8,4},{9,5},{1... | collective-permute-start | bytes 196616 | tf_op jit(solution)/shard_map/ppermute | solution.py:29
  5.4 5.5 %collective-permute-start = (bf16[128,256]{1,0:T(8,128)(2,1)S(1)}, bf16[128,256]{1,0:T(8,128)(2,1)S(1)}, u32[]{:S(2)}, u32[]{:S(2)}) collective-permute-start(bf16[128,256]{1,0:T(8,128)(2,1)S(1)} %pad_maximum_fusion.1), channel_id=1, source_target_pairs={{0,4},{1,5},{2,6},{3,7},{4,8},{5,9},{6,10},{7,11},{8,12},{9,13},{1... | collective-permute-start | bytes 196616 | tf_op jit(solution)/shard_map/ppermute | solution.py:29
  11.0 31.3 %copy-start.2 = (bf16[4,128,256]{2,1,0:T(8,128)(2,1)}, bf16[4,128,256]{2,1,0:T(8,128)(2,1)S(1)}, u32[]{:S(2)}) copy-start(bf16[4,128,256]{2,1,0:T(8,128)(2,1)S(1)} %pad_maximum_fusion.refs_0_) | copy-start | bytes 786436
  11.0 6.5 %collective-permute-start.3 = (bf16[4,128,256]{2,1,0:T(8,128)(2,1)S(1)}, bf16[4,128,256]{2,1,0:T(8,128)(2,1)S(1)}, u32[]{:S(2)}, u32[]{:S(2)}) collective-permute-start(bf16[4,128,256]{2,1,0:T(8,128)(2,1)S(1)} %pad_maximum_fusion.refs_0_), channel_id=1, source_target_pairs={{0,16},{16,0},{1,17},{17,1},{2,18},{18,2},{3,19},{19,3},{4,20},{20... | collective-permute-start | bytes 786440 | tf_op jit(solution)/shard_map/ppermute | solution.py:45
  12.6 11.2 %collective-permute-start.4 = (bf16[4,128,256]{2,1,0:T(8,128)(2,1)S(1)}, bf16[4,128,256]{2,1,0:T(8,128)(2,1)S(1)}, u32[]{:S(2)}, u32[]{:S(2)}) collective-permute-start(bf16[4,128,256]{2,1,0:T(8,128)(2,1)S(1)} %pad_maximum_fusion.refs_0_), channel_id=1, source_target_pairs={{0,1},{1,2},{2,3},{3,0},{4,5},{5,6},{6,7},{7,4},{8,9},{9,10},{10,1... | collective-permute-start | bytes 786440 | tf_op jit(solution)/shard_map/ppermute | solution.py:37
  17.4 24.9 %copy-start.21 = (bf16[4,128,256]{2,1,0:T(8,128)(2,1)}, bf16[4,128,256]{2,1,0:T(8,128)(2,1)S(1)}, u32[]{:S(2)}) copy-start(bf16[4,128,256]{2,1,0:T(8,128)(2,1)S(1)} %collective-permute-done.3.refs_1_) | copy-start | bytes 786436
  17.4 8.2 %collective-permute-start.7 = (bf16[4,128,256]{2,1,0:T(8,128)(2,1)S(1)}, bf16[4,128,256]{2,1,0:T(8,128)(2,1)S(1)}, u32[]{:S(2)}, u32[]{:S(2)}) collective-permute-start(bf16[4,128,256]{2,1,0:T(8,128)(2,1)S(1)} %collective-permute-done.3.refs_1_), channel_id=1, source_target_pairs={{0,3},{1,0},{2,1},{3,2},{4,7},{5,4},{6,5},{7,6},{8,11},{9,8},{10,9... | collective-permute-start | bytes 786440 | tf_op jit(solution)/shard_map/ppermute | solution.py:37
  22.7 35.3 %copy-start = (bf16[256,1024]{1,0:T(8,128)(2,1)}, bf16[256,1024]{1,0:T(8,128)(2,1)S(1)}, u32[]{:S(2)}) copy-start(bf16[256,1024]{1,0:T(8,128)(2,1)S(1)} %get-tuple-element.54.refs_7_) | copy-start | bytes 1572868
  22.7 35.3 %copy-start.1 = (bf16[256,1024]{1,0:T(8,128)(2,1)}, bf16[256,1024]{1,0:T(8,128)(2,1)S(1)}, u32[]{:S(2)}) copy-start(bf16[256,1024]{1,0:T(8,128)(2,1)S(1)} %get-tuple-element.53.refs_3_) | copy-start | bytes 1572868
  22.8 18.6 %collective-permute-start.12 = (bf16[256,1024]{1,0:T(8,128)(2,1)S(1)}, bf16[256,1024]{1,0:T(8,128)(2,1)S(1)}, u32[]{:S(2)}, u32[]{:S(2)}) collective-permute-start(bf16[256,1024]{1,0:T(8,128)(2,1)S(1)} %get-tuple-element.53.refs_3_), channel_id=1, source_target_pairs={{0,12},{1,13},{2,14},{3,15},{4,0},{5,1},{6,2},{7,3},{8,4},{9,5},{1... | collective-permute-start | bytes 1572872 | tf_op jit(solution)/shard_map/ppermute | solution.py:29
  23.9 18.4 %copy-start.22 = (bf16[4,128,256]{2,1,0:T(8,128)(2,1)}, bf16[4,128,256]{2,1,0:T(8,128)(2,1)S(1)}, u32[]{:S(2)}) copy-start(bf16[4,128,256]{2,1,0:T(8,128)(2,1)S(1)} %collective-permute-done.4.refs_2_) | copy-start | bytes 786436
  23.9 12.2 %collective-permute-start.8 = (bf16[4,128,256]{2,1,0:T(8,128)(2,1)S(1)}, bf16[4,128,256]{2,1,0:T(8,128)(2,1)S(1)}, u32[]{:S(2)}, u32[]{:S(2)}) collective-permute-start(bf16[4,128,256]{2,1,0:T(8,128)(2,1)S(1)} %collective-permute-done.4.refs_2_), channel_id=1, source_target_pairs={{0,1},{1,2},{2,3},{3,0},{4,5},{5,6},{6,7},{7,4},{8,9},{9,10},{10,1... | collective-permute-start | bytes 786440 | tf_op jit(solution)/shard_map/ppermute | solution.py:37
  25.7 16.6 %copy-start.23 = (bf16[4,128,256]{2,1,0:T(8,128)(2,1)}, bf16[4,128,256]{2,1,0:T(8,128)(2,1)S(1)}, u32[]{:S(2)}) copy-start(bf16[4,128,256]{2,1,0:T(8,128)(2,1)S(1)} %collective-permute-done.7.refs_5_) | copy-start | bytes 786436
  25.7 11.4 %collective-permute-start.9 = (bf16[4,128,256]{2,1,0:T(8,128)(2,1)S(1)}, bf16[4,128,256]{2,1,0:T(8,128)(2,1)S(1)}, u32[]{:S(2)}, u32[]{:S(2)}) collective-permute-start(bf16[4,128,256]{2,1,0:T(8,128)(2,1)S(1)} %collective-permute-done.7.refs_5_), channel_id=1, source_target_pairs={{0,3},{1,0},{2,1},{3,2},{4,7},{5,4},{6,5},{7,6},{8,11},{9,8},{10,9... | collective-permute-start | bytes 786440 | tf_op jit(solution)/shard_map/ppermute | solution.py:37
  29.3 8.5 %collective-permute-start.6 = (bf16[4,128,256]{2,1,0:T(8,128)(2,1)S(1)}, bf16[4,128,256]{2,1,0:T(8,128)(2,1)S(1)}, u32[]{:S(2)}, u32[]{:S(2)}) collective-permute-start(bf16[4,128,256]{2,1,0:T(8,128)(2,1)S(1)} %pad_maximum_fusion.refs_0_), channel_id=1, source_target_pairs={{0,3},{1,0},{2,1},{3,2},{4,7},{5,4},{6,5},{7,6},{8,11},{9,8},{10,9... | collective-permute-start | bytes 786440 | tf_op jit(solution)/shard_map/ppermute | solution.py:37
  29.4 11.9 %collective-permute-start.5 = (bf16[4,128,256]{2,1,0:T(8,128)(2,1)S(1)}, bf16[4,128,256]{2,1,0:T(8,128)(2,1)}, u32[]{:S(2)}, u32[]{:S(2)}) collective-permute-start(bf16[4,128,256]{2,1,0:T(8,128)(2,1)S(1)} %collective-permute-done.3.refs_1_), channel_id=1, source_target_pairs={{0,1},{1,2},{2,3},{3,0},{4,5},{5,6},{6,7},{7,4},{8,9},{9,10},{10,1... | collective-permute-start | bytes 786440 | tf_op jit(solution)/shard_map/ppermute | solution.py:37
  36.1 6.2 %copy-start.24 = (bf16[4,128,256]{2,1,0:T(8,128)(2,1)}, bf16[4,128,256]{2,1,0:T(8,128)(2,1)S(1)}, u32[]{:S(2)}) copy-start(bf16[4,128,256]{2,1,0:T(8,128)(2,1)S(1)} %collective-permute-done.8.refs_6_) | copy-start | bytes 786436
  36.1 22.0 %collective-permute-start.11 = (bf16[256,1024]{1,0:T(8,128)(2,1)S(1)}, bf16[256,1024]{1,0:T(8,128)(2,1)S(1)}, u32[]{:S(2)}, u32[]{:S(2)}) collective-permute-start(bf16[256,1024]{1,0:T(8,128)(2,1)S(1)} %get-tuple-element.53.refs_3_), channel_id=1, source_target_pairs={{0,8},{1,9},{2,10},{3,11},{4,12},{5,13},{6,14},{7,15},{8,0},{9,1},... | collective-permute-start | bytes 1572872 | tf_op jit(solution)/shard_map/ppermute | solution.py:29
  37.0 5.2 %copy-start.25 = (bf16[4,128,256]{2,1,0:T(8,128)(2,1)}, bf16[4,128,256]{2,1,0:T(8,128)(2,1)S(1)}, u32[]{:S(2)}) copy-start(bf16[4,128,256]{2,1,0:T(8,128)(2,1)S(1)} %collective-permute-done.9.refs_7_) | copy-start | bytes 786436
  37.1 21.6 %collective-permute-start.10 = (bf16[256,1024]{1,0:T(8,128)(2,1)S(1)}, bf16[256,1024]{1,0:T(8,128)(2,1)S(1)}, u32[]{:S(2)}, u32[]{:S(2)}) collective-permute-start(bf16[256,1024]{1,0:T(8,128)(2,1)S(1)} %get-tuple-element.53.refs_3_), channel_id=1, source_target_pairs={{0,4},{1,5},{2,6},{3,7},{4,8},{5,9},{6,10},{7,11},{8,12},{9,13},{1... | collective-permute-start | bytes 1572872 | tf_op jit(solution)/shard_map/ppermute | solution.py:29
  37.9 22.1 %collective-permute-start.15 = (bf16[256,1024]{1,0:T(8,128)(2,1)S(1)}, bf16[256,1024]{1,0:T(8,128)(2,1)S(1)}, u32[]{:S(2)}, u32[]{:S(2)}) collective-permute-start(bf16[256,1024]{1,0:T(8,128)(2,1)S(1)} %get-tuple-element.54.refs_7_), channel_id=1, source_target_pairs={{0,3},{1,0},{2,1},{3,2},{4,7},{5,4},{6,5},{7,6},{8,11},{9,8},{10,9... | collective-permute-start | bytes 1572872 | tf_op jit(solution)/shard_map/ppermute | solution.py:37
  41.3 22.5 %collective-permute-start.14 = (bf16[256,1024]{1,0:T(8,128)(2,1)S(1)}, bf16[256,1024]{1,0:T(8,128)(2,1)S(1)}, u32[]{:S(2)}, u32[]{:S(2)}) collective-permute-start(bf16[256,1024]{1,0:T(8,128)(2,1)S(1)} %get-tuple-element.54.refs_7_), channel_id=1, source_target_pairs={{0,2},{1,3},{2,0},{3,1},{4,6},{5,7},{6,4},{7,5},{8,10},{9,11},{10,... | collective-permute-start | bytes 1572872 | tf_op jit(solution)/shard_map/ppermute | solution.py:37
  41.3 16.8 %copy-start.9 = (bf16[256,1024]{1,0:T(8,128)(2,1)}, bf16[256,1024]{1,0:T(8,128)(2,1)S(1)}, u32[]{:S(2)}) copy-start(bf16[256,1024]{1,0:T(8,128)(2,1)S(1)} %collective-permute-done.12.refs_6_) | copy-start | bytes 1572868
  41.3 22.5 %collective-permute-start.13 = (bf16[256,1024]{1,0:T(8,128)(2,1)S(1)}, bf16[256,1024]{1,0:T(8,128)(2,1)S(1)}, u32[]{:S(2)}, u32[]{:S(2)}) collective-permute-start(bf16[256,1024]{1,0:T(8,128)(2,1)S(1)} %get-tuple-element.54.refs_7_), channel_id=1, source_target_pairs={{0,1},{1,2},{2,3},{3,0},{4,5},{5,6},{6,7},{7,4},{8,9},{9,10},{10,1... | collective-permute-start | bytes 1572872 | tf_op jit(solution)/shard_map/ppermute | solution.py:37
  58.1 5.7 %copy-start.10 = (bf16[256,1024]{1,0:T(8,128)(2,1)}, bf16[256,1024]{1,0:T(8,128)(2,1)S(1)}, u32[]{:S(2)}) copy-start(bf16[256,1024]{1,0:T(8,128)(2,1)S(1)} %collective-permute-done.11.refs_5_) | copy-start | bytes 1572868
  58.1 15.2 %collective-permute-start.16 = (bf16[512,256]{1,0:T(8,128)(2,1)}, bf16[512,256]{1,0:T(8,128)(2,1)S(1)}, u32[]{:S(2)}, u32[]{:S(2)}) collective-permute-start(bf16[512,256]{1,0:T(8,128)(2,1)} %get-tuple-element.50.refs_0_), channel_id=1, source_target_pairs={{0,4},{1,5},{2,6},{3,7},{4,8},{5,9},{6,10},{7,11},{8,12},{9,13},{1... | collective-permute-start | bytes 786440 | tf_op jit(solution)/shard_map/ppermute | solution.py:29
  58.7 5.2 %copy-start.11 = (bf16[256,1024]{1,0:T(8,128)(2,1)}, bf16[256,1024]{1,0:T(8,128)(2,1)S(1)}, u32[]{:S(2)}) copy-start(bf16[256,1024]{1,0:T(8,128)(2,1)S(1)} %collective-permute-done.10.refs_4_) | copy-start | bytes 1572868
  58.7 14.7 %collective-permute-start.17 = (bf16[512,256]{1,0:T(8,128)(2,1)}, bf16[512,256]{1,0:T(8,128)(2,1)S(1)}, u32[]{:S(2)}, u32[]{:S(2)}) collective-permute-start(bf16[512,256]{1,0:T(8,128)(2,1)} %get-tuple-element.51.refs_1_), channel_id=1, source_target_pairs={{0,8},{1,9},{2,10},{3,11},{4,12},{5,13},{6,14},{7,15},{8,0},{9,1},... | collective-permute-start | bytes 786440 | tf_op jit(solution)/shard_map/ppermute | solution.py:29
  60.0 13.4 %collective-permute-start.18 = (bf16[512,256]{1,0:T(8,128)(2,1)}, bf16[512,256]{1,0:T(8,128)(2,1)S(1)}, u32[]{:S(2)}, u32[]{:S(2)}) collective-permute-start(bf16[512,256]{1,0:T(8,128)(2,1)} %get-tuple-element.52.refs_2_), channel_id=1, source_target_pairs={{0,12},{1,13},{2,14},{3,15},{4,0},{5,1},{6,2},{7,3},{8,4},{9,5},{1... | collective-permute-start | bytes 786440 | tf_op jit(solution)/shard_map/ppermute | solution.py:29
  73.4 4.5 %collective-permute-start.22 = (bf16[1024,1024]{1,0:T(8,128)(2,1)}, bf16[1024,1024]{1,0:T(8,128)(2,1)S(1)}, u32[]{:S(2)}, u32[]{:S(2)}) collective-permute-start(bf16[1024,1024]{1,0:T(8,128)(2,1)} %get-tuple-element.66.refs_4_), channel_id=1, source_target_pairs={{0,32},{32,0},{64,96},{96,64},{1,33},{33,1},{65,97},{97,65},{2,34}... | collective-permute-start | bytes 6291464 | tf_op jit(solution)/shard_map/ppermute | solution.py:49
  73.5 16.4 %copy-start.6 = (bf16[1024,1024]{1,0:T(8,128)(2,1)S(1)}, bf16[1024,1024]{1,0:T(8,128)(2,1)}, u32[]{:S(2)}) copy-start(bf16[1024,1024]{1,0:T(8,128)(2,1)} %get-tuple-element.75.refs_4_) | copy-start | bytes 6291460
  73.5 15.8 %collective-permute-start.19 = (bf16[512,256]{1,0:T(8,128)(2,1)}, bf16[512,256]{1,0:T(8,128)(2,1)S(1)}, u32[]{:S(2)}, u32[]{:S(2)}) collective-permute-start(bf16[512,256]{1,0:T(8,128)(2,1)} %get-tuple-element.59), channel_id=1, source_target_pairs={{0,1},{1,2},{2,3},{3,0},{4,5},{5,6},{6,7},{7,4},{8,9},{9,10},{10,1... | collective-permute-start | bytes 786440 | tf_op jit(solution)/shard_map/ppermute | solution.py:37
  74.0 15.3 %collective-permute-start.20 = (bf16[512,256]{1,0:T(8,128)(2,1)}, bf16[512,256]{1,0:T(8,128)(2,1)S(1)}, u32[]{:S(2)}, u32[]{:S(2)}) collective-permute-start(bf16[512,256]{1,0:T(8,128)(2,1)} %get-tuple-element.61), channel_id=1, source_target_pairs={{0,2},{1,3},{2,0},{3,1},{4,6},{5,7},{6,4},{7,5},{8,10},{9,11},{10,... | collective-permute-start | bytes 786440 | tf_op jit(solution)/shard_map/ppermute | solution.py:37
  76.6 13.3 %collective-permute-start.21 = (bf16[512,256]{1,0:T(8,128)(2,1)}, bf16[512,256]{1,0:T(8,128)(2,1)S(1)}, u32[]{:S(2)}, u32[]{:S(2)}) collective-permute-start(bf16[512,256]{1,0:T(8,128)(2,1)} %get-tuple-element.63), channel_id=1, source_target_pairs={{0,3},{1,0},{2,1},{3,2},{4,7},{5,4},{6,5},{7,6},{8,11},{9,8},{10,9... | collective-permute-start | bytes 786440 | tf_op jit(solution)/shard_map/ppermute | solution.py:37
  89.9 4.2 %collective-permute-start.23 = (bf16[1024,1024]{1,0:T(8,128)(2,1)S(1)}, bf16[1024,1024]{1,0:T(8,128)(2,1)S(1)}, u32[]{:S(2)}, u32[]{:S(2)}) collective-permute-start(bf16[1024,1024]{1,0:T(8,128)(2,1)S(1)} %copy-done.6), channel_id=1, source_target_pairs={{0,32},{32,0},{64,96},{96,64},{1,33},{33,1},{65,97},{97,65},{2,34}... | collective-permute-start | bytes 6291464 | tf_op jit(solution)/shard_map/ppermute | solution.py:49
  89.9 25.8 %collective-permute-start.29 = (bf16[128,2048]{1,0:T(8,128)(2,1)}, bf16[128,2048]{1,0:T(8,128)(2,1)S(1)}, u32[]{:S(2)}, u32[]{:S(2)}) collective-permute-start(bf16[128,2048]{1,0:T(8,128)(2,1)} %get-tuple-element.74), channel_id=1, source_target_pairs={{0,3},{1,0},{2,1},{3,2},{4,7},{5,4},{6,5},{7,6},{8,11},{9,8},{10,9... | collective-permute-start | bytes 1572872 | tf_op jit(solution)/shard_map/ppermute | solution.py:37
  92.3 26.6 %collective-permute-start.28 = (bf16[128,2048]{1,0:T(8,128)(2,1)}, bf16[128,2048]{1,0:T(8,128)(2,1)S(1)}, u32[]{:S(2)}, u32[]{:S(2)}) collective-permute-start(bf16[128,2048]{1,0:T(8,128)(2,1)} %get-tuple-element.72), channel_id=1, source_target_pairs={{0,2},{1,3},{2,0},{3,1},{4,6},{5,7},{6,4},{7,5},{8,10},{9,11},{10,... | collective-permute-start | bytes 1572872 | tf_op jit(solution)/shard_map/ppermute | solution.py:37
  92.3 26.6 %collective-permute-start.27 = (bf16[128,2048]{1,0:T(8,128)(2,1)}, bf16[128,2048]{1,0:T(8,128)(2,1)S(1)}, u32[]{:S(2)}, u32[]{:S(2)}) collective-permute-start(bf16[128,2048]{1,0:T(8,128)(2,1)} %get-tuple-element.70), channel_id=1, source_target_pairs={{0,1},{1,2},{2,3},{3,0},{4,5},{5,6},{6,7},{7,4},{8,9},{9,10},{10,1... | collective-permute-start | bytes 1572872 | tf_op jit(solution)/shard_map/ppermute | solution.py:37
  102.0 21.5 %collective-permute-start.24 = (bf16[128,2048]{1,0:T(8,128)(2,1)}, bf16[128,2048]{1,0:T(8,128)(2,1)S(1)}, u32[]{:S(2)}, u32[]{:S(2)}) collective-permute-start(bf16[128,2048]{1,0:T(8,128)(2,1)} %get-tuple-element.77), channel_id=1, source_target_pairs={{0,4},{1,5},{2,6},{3,7},{4,8},{5,9},{6,10},{7,11},{8,12},{9,13},{1... | collective-permute-start | bytes 1572872 | tf_op jit(solution)/shard_map/ppermute | solution.py:29
  102.0 28.0 %collective-permute-start.25 = (bf16[128,2048]{1,0:T(8,128)(2,1)}, bf16[128,2048]{1,0:T(8,128)(2,1)S(1)}, u32[]{:S(2)}, u32[]{:S(2)}) collective-permute-start(bf16[128,2048]{1,0:T(8,128)(2,1)} %get-tuple-element.78), channel_id=1, source_target_pairs={{0,8},{1,9},{2,10},{3,11},{4,12},{5,13},{6,14},{7,15},{8,0},{9,1},... | collective-permute-start | bytes 1572872 | tf_op jit(solution)/shard_map/ppermute | solution.py:29
  115.7 14.4 %collective-permute-start.26 = (bf16[128,2048]{1,0:T(8,128)(2,1)}, bf16[128,2048]{1,0:T(8,128)(2,1)S(1)}, u32[]{:S(2)}, u32[]{:S(2)}) collective-permute-start(bf16[128,2048]{1,0:T(8,128)(2,1)} %get-tuple-element.79), channel_id=1, source_target_pairs={{0,12},{1,13},{2,14},{3,15},{4,0},{5,1},{6,2},{7,3},{8,4},{9,5},{1... | collective-permute-start | bytes 1572872 | tf_op jit(solution)/shard_map/ppermute | solution.py:29
  123.5 6.5 %copy-start.17 = (bf16[128,2048]{1,0:T(8,128)(2,1)}, bf16[128,2048]{1,0:T(8,128)(2,1)S(1)}, u32[]{:S(2)}) copy-start(bf16[128,2048]{1,0:T(8,128)(2,1)S(1)} %collective-permute-done.24.refs_1_) | copy-start | bytes 1572868
  131.1 131.1 %slice-start = ((s8[6291456]{0:T(1024)(128)(4,1)}), s8[2097152]{0:T(1024)(128)(4,1)S(1)}, s32[]{:S(2)}) async-start(s8[6291456]{0:T(1024)(128)(4,1)} %bitcast.14), calls=%async_computation.2 | async-start | bytes 4194304
  140.5 121.6 %slice-start.1 = ((s8[6291456]{0:T(1024)(128)(4,1)}), s8[4194304]{0:T(1024)(128)(4,1)S(1)}, s32[]{:S(2)}) async-start(s8[6291456]{0:T(1024)(128)(4,1)} %bitcast.14), calls=%async_computation.3 | async-start | bytes 8388608
  (17 other events, 46.8 us)

commit v8 on v7

--- a/solution.py
+++ b/solution.py
@@ -15,6 +15,7 @@
 SLOTS = 8
 SEG = 512
 ROWS = 256
+COMBINE_ROWS = 512
 DISPATCH_COLUMNS = 512
 DOWN_COLUMNS = 512
 COMBINE_COLUMNS = 512
@@ -162,12 +163,6 @@
     ] + [pltpu.VMEM((BLOCK, BLOCK), F32)] * 4
 
 
-def join(pieces, joined):
-    rows = pieces[0].shape[0]
-    for number, piece in enumerate(pieces):
-        joined[number * rows : (number + 1) * rows, :] = piece[...]
-
-
 def attention_kernel(meta, q_ref, *refs):
     pieces, refs = refs[:8], refs[8:]
     outs, keys, values, context, scratch = refs[:3], *refs[3:6], refs[6:]
@@ -215,11 +210,28 @@
 
 def attention_end_kernel(meta, q_ref, keys, values, *refs):
     others, weights, out, refs = refs[:3], refs[3:11], refs[11], refs[12:]
-    outs_z, joined, scratch = refs[:4], refs[4:6], refs[6:]
+    outs_z, joined, held, came, went, scratch = refs[:4], refs[4:6], *refs[6:9], refs[9:]
     x, z = meta[5], meta[6]
-    join(weights[:4], joined[0])
-    join(weights[4:], joined[1])
+    depth = weights[0].shape[0]
+    arriving = [
+        pltpu.make_async_copy(
+            piece,
+            held.at[number // SIDE, pl.ds(number % SIDE * depth, depth), :],
+            came.at[number],
+        )
+        for number, piece in enumerate(weights)
+    ]
+    leaving = [
+        pltpu.make_async_copy(held.at[number], whole_of, went.at[number])
+        for number, whole_of in enumerate(joined)
+    ]
+    for copy in arriving:
+        copy.start()
     out[...] = attend(meta, x, q_ref, keys, values, scratch)
+    for copy in arriving:
+        copy.wait()
+    for copy in leaving:
+        copy.start()
     for number, context in enumerate((out, *others)):
         x_of = lax.rem(x + number, SIDE)
         rows = pl.ds(pl.multiple_of(x_of * TOKENS, TOKENS), TOKENS)
@@ -227,24 +239,33 @@
             to_z = lax.rem(z + step_of, SIDE)
             part = pl.ds(pl.multiple_of(to_z * TOKENS, TOKENS), TOKENS)
             outs_z[step_of][rows, :] = context[part, :]
+    for copy in leaving:
+        copy.wait()
 
 
 def attention_end(meta, queries, keys, values, others, weights):
     width = queries.shape[1]
-    arrays = (queries, keys, values, *others, *weights)
+    arrays = (queries, keys, values, *others)
+    depth, columns = weights[0].shape
     outs = [jax.ShapeDtypeStruct((BLOCK, width), BF16)] * 5
-    outs += [jax.ShapeDtypeStruct((SIDE * weights[0].shape[0], weights[0].shape[1]), BF16)] * 2
+    joined = [jax.ShapeDtypeStruct((SIDE * depth, columns), BF16)] * 2
+    anywhere = pl.BlockSpec(memory_space=pl.ANY)
     return call(
         attention_end_kernel,
         "attention_end",
-        outs,
-        [smem()] + [whole(array) for array in arrays],
-        [pl.BlockSpec(out.shape, lambda: (0, 0)) for out in outs],
-        scratch=attend_scratch(),
+        outs + joined,
+        [smem()] + [whole(array) for array in arrays] + [anywhere] * len(weights),
+        [pl.BlockSpec(out.shape, lambda: (0, 0)) for out in outs] + [anywhere] * 2,
+        scratch=[
+            pltpu.VMEM((2, SIDE * depth, columns), BF16),
+            pltpu.SemaphoreType.DMA((2 * SIDE,)),
+            pltpu.SemaphoreType.DMA((2,)),
+            *attend_scratch(),
+        ],
         cost=pl.CostEstimate(
             flops=6 * 10**9, bytes_accessed=7 * 10**6, transcendentals=3 * 10**6
         ),
-    )(meta, *arrays)
+    )(meta, *arrays, *weights)
 
 
 def projection_kernel(axis, meta, *refs):
@@ -398,7 +419,7 @@
     )(meta, *arrays, main, late)
 
 
-def expert_kernel(rows_ref, over_ref, up_ref, down_hbm, out_ref, wide, spread, down_ref, done):
+def expert_kernel(rows_ref, over_ref, up_ref, down_hbm, out_ref, wide, spread, down_ref, mixed, done):
     step = pl.program_id(0)
     width = down_ref.shape[2]
     fetch = pltpu.make_async_copy(down_hbm, down_ref, done)
@@ -406,26 +427,32 @@
     def act(value):
         return (value / (1.0 + jnp.exp(-value))).astype(BF16)
 
-    @pl.when(step == 0)
+    first = step == 0
+
+    @pl.when(first)
     def _():
         fetch.start()
         widen(wide, over_ref)
-        total = None
         for segment in range(SLOTS):
-            part = up_ref[0, segment * SEG : (segment + 1) * SEG, :]
-            term = dot(gather_rows(wide, segment), part)
-            total = term if total is None else total + term
-        inner = act(total)
+            columns = slice(segment * SEG, (segment + 1) * SEG)
+            mixed[:ROWS, columns] = rows_ref[:, columns]
+            mixed[ROWS:, columns] = gather_rows(wide, segment)
+        inner = act(dot(mixed[...], up_ref[0]))
         fetch.wait()
         for segment in range(SLOTS):
-            part = down_ref[0, :, segment * SEG : (segment + 1) * SEG]
-            scatter_rows(wide, segment, dot(inner, part))
+            columns = slice(segment * SEG, (segment + 1) * SEG)
+            made = dot(inner, down_ref[0, :, columns])
+            out_ref[:, columns] = made[:ROWS].astype(BF16)
+            scatter_rows(wide, segment, made[ROWS:])
         spread[...] = narrow(wide)
 
-    inner = act(dot(rows_ref[:, :width], up_ref[0]))
-    for start in range(0, width, DOWN_COLUMNS):
-        columns = slice(start, start + DOWN_COLUMNS)
-        out_ref[:, columns] = dot(inner, down_ref[0, :, columns]).astype(BF16)
+    @pl.when(jnp.logical_not(first))
+    def _():
+        inner = act(dot(rows_ref[:, :width], up_ref[0]))
+        for start in range(0, width, DOWN_COLUMNS):
+            columns = slice(start, start + DOWN_COLUMNS)
+            out_ref[:, columns] = dot(inner, down_ref[0, :, columns]).astype(BF16)
+
     mine = pl.ds(pl.multiple_of(step * ROWS, ROWS), ROWS)
     out_ref[:, width:] = spread[mine, :]
 
@@ -449,6 +476,7 @@
             wide_scratch(),
             pltpu.VMEM((rows, SEG), BF16),
             pltpu.VMEM(down.shape, BF16),
+            pltpu.VMEM((ROWS + TOKENS, down.shape[2]), BF16),
             pltpu.SemaphoreType.DMA,
         ],
         limit=46,
@@ -490,14 +518,14 @@
         "combine",
         jax.ShapeDtypeStruct(state.shape, BF16),
         [
-            pl.BlockSpec((2 * TOKENS, ROWS), lambda i: (0, i)),
+            pl.BlockSpec((2 * TOKENS, COMBINE_ROWS), lambda i: (0, i)),
             whole(late),
-            pl.BlockSpec((ROWS, columns), lambda i: (i, 0)),
+            pl.BlockSpec((COMBINE_ROWS, columns), lambda i: (i, 0)),
             pl.BlockSpec((rows, SEG), lambda i: (0, SLOTS), pipeline_mode=pl.Buffered(1)),
             whole(state),
         ],
         pl.BlockSpec(state.shape, lambda i: (0, 0)),
-        grid=(rows // ROWS,),
+        grid=(rows // COMBINE_ROWS,),
         scratch=[pltpu.VMEM(state.shape, F32), wide_scratch()],
         cost=pl.CostEstimate(flops=4 * 10**9, bytes_accessed=13 * 10**6, transcendentals=0),
     )(main, late, returned, returned, state)
@@ -612,8 +640,6 @@
         far_other,
     ]
 
-    main, late, back_main, back_late = routes(expert_ids, route_weights, n_devices)
-    queries = after(queries, main)
 
     *far, keys, values = attention(meta, queries, pieces)
     mine, *parts, weights_x, weights_z = attention_end(
@@ -626,6 +652,9 @@
     terms_z = [after(term, *context_z[1:]) for term in terms_z]
     weights_z = after(weights_z, *terms_z)
     terms_x = projection(5, meta, context_z, [weights_z, swap_core(weights_z)])
+    main, late, back_main, back_late = routes(
+        after(expert_ids, terms_x[0]), route_weights, n_devices
+    )
     terms_z, terms_x = exchange(shift_z, terms_z), exchange(shift_x, terms_x)
     outgoing, state = dispatch(
         meta, terms_x, settle(meta, terms_z, residual), residual, norm_gain[None, :], main, late

time: 414 us -> 413 us (level)
  Pallas kernels: 87.6 us -> 82.6 us
    ppermute x15, waiting for transfers between devices: 14.9 us -> 19.3 us  [shift_z(): lax.ppermute(value, 'tp', [(x * SIDE + z, x * SIDE + (z + step) % SIDE) f...]
  transfers between devices with their start and end apart: 30 -> 30, of which waited for: 13 -> 11; matrix products, arithmetic and copies ran while one was open for 1% -> 1% of each run, Pallas kernels for 10% -> 10%
where the time goes in v8:
time: 413 us; the launch traced here: 412 us
  blocking collectives  240 us (58%)
  Pallas kernels  82.6 us (20%)
  starting transfers between devices  46.6 us (11%)
  waiting for transfers between devices  32.7 us (8%)
  local copies, waits for them, and re-layouts  9.07 us (2%)
    all_to_all x2, blocking collectives, all_to_all(): lax.all_to_all(blocks, ('dp', 'ctx', 'tp'), split_axis=0, concat_axis=0,...  240 us
    pallas_call x1, Pallas kernels, experts(): call(expert_kernel, 'experts', jax.ShapeDtypeStruct((rows, columns), BF16...  24.4 us
    ppermute x15, starting transfers between devices, shift_z(): lax.ppermute(value, 'tp', [(x * SIDE + z, x * SIDE + (z + step) % SIDE) f...  22.9 us
    ppermute x12, starting transfers between devices, shift_x(): lax.ppermute(value, 'tp', [(x * SIDE + z, (x + step) % SIDE * SIDE + z) f...  21.8 us
    ppermute x15, waiting for transfers between devices, shift_z(): lax.ppermute(value, 'tp', [(x * SIDE + z, x * SIDE + (z + step) % SIDE) f...  19.3 us
    pallas_call x1, Pallas kernels, attention(): call(attention_kernel, 'attention', outs, [smem()] + [whole(array) for ar...  14.4 us
    pallas_call x2, Pallas kernels, projection(): call(functools.partial(projection_kernel, axis), 'projection', [jax.Shape...  13.2 us
    ppermute x12, waiting for transfers between devices, shift_x(): lax.ppermute(value, 'tp', [(x * SIDE + z, (x + step) % SIDE * SIDE + z) f...  10.5 us
  transfers between devices with their start and end apart: 30, of which 11 were waited for; matrix products, arithmetic and copies ran while one was open for 1% of the time, Pallas kernels for 10%

profile of v8, /device:TPU:0, one launch (start us, length us, event | category | flops | bytes accessed | tf_op | source)
XLA Modules:
  0.0 411.5 jit_solution(9045161528696527699)
XLA Ops:
  0.0 0.9 constant_dynamic-slice_fusion.8
  0.9 3.2 collective-permute-start.1
  4.1 1.2 collective-permute-start.2
  5.3 1.0 collective-permute-start
  6.8 1.7 collective-permute-done.2
  8.5 2.4 collective-permute-done
  10.9 1.7 collective-permute-start.3
  12.6 1.9 collective-permute-start.4
  14.5 2.9 collective-permute-done.3.refs_1_
  17.4 4.0 collective-permute-start.7
  21.4 1.3 constant_dynamic-slice_fusion
  22.7 1.1 collective-permute-start.12
  23.8 1.8 collective-permute-done.7.refs_5_
  25.6 3.7 collective-permute-start.9
  29.4 2.0 collective-permute-start.5
  31.3 0.6 concatenate.15.meta
  32.0 2.1 collective-permute-done.8.refs_6_
  35.0 2.7 collective-permute-done.6.refs_4_
  37.7 3.7 collective-permute-start.15
  41.4 3.1 collective-permute-done.12.refs_6_
  44.5 14.4 %attention.1 = (bf16[512,256]{1,0:T(8,128)(2,1)}, bf16[512,256]{1,0:T(8,128)(2,1)}, bf16[512,256]{1,0:T(8,128)(2,1)}, bf16[4096,128]{1,0:T(8,128)(2,1)}, bf16[128,4096]{1,0:T(8,128)(2,1)}) custom-call(s32[8]{0:T(128)} %concatenate.15.meta, bf16[2048,256]{1,0:T(8,128)(2,1)} %q_ref.3, bf16[4,128,256]{2,1,0:T(8,128)(2,1)} %copy-done.2, ...), custom_call_target="tpu_custom_call" | custom-call | flops 16000000000 | bytes 7000000 | tf_op jit(solution)/shard_map/attention/pallas_call | solution.py:198
  59.1 1.7 collective-permute-start.17
  60.8 1.6 collective-permute-start.18
  62.4 0.7 copy-done.12
  63.4 7.5 %attention_end.1 = (bf16[512,256]{1,0:T(8,128)(2,1)}, bf16[512,256]{1,0:T(8,128)(2,1)}, bf16[512,256]{1,0:T(8,128)(2,1)}, bf16[512,256]{1,0:T(8,128)(2,1)}, bf16...) custom-call(s32[8]{0:T(128)} %concatenate.15.meta, bf16[2048,256]{1,0:T(8,128)(2,1)} %q_ref.3, ...), custom_call_target="tpu_custom_call" | custom-call | flops 6000000000 | bytes 7000000 | tf_op jit(solution)/shard_map/attention_end/pallas_call | solution.py:253
  71.4 4.3 %collective-permute-start.20 = (bf16[512,256]{1,0:T(8,128)(2,1)}, bf16[512,256]{1,0:T(8,128)(2,1)S(1)}, u32[]{:S(2)}, u32[]{:S(2)}) collective-permute-start(bf16[512,256]{1,0:T(8,128)(2,1)} %get-tuple-element.57), channel_id=1, source_target_pairs={{0,2},{1,3},{2,0},{3,1},{4,6},{5,7},{6,4},{7,5},{8,10},{9,11},{10,... | collective-permute-start | bytes 786440 | tf_op jit(solution)/shard_map/ppermute | solution.py:38
  75.7 1.3 copy-done.7
  77.1 6.6 %projection.2 = (bf16[128,2048]{1,0:T(8,128)(2,1)}, bf16[128,2048]{1,0:T(8,128)(2,1)}, bf16[128,2048]{1,0:T(8,128)(2,1)}, bf16[128,2048]{1,0:T(8,128)(2,1)}) custom-call(s32[8]{0:T(128)} %concatenate.15.meta, bf16[512,256]{1,0:T(8,128)(2,1)} %get-tuple-element.52.refs_0_, bf16[512,256]{1,0:T(8,128)(2,1)} %copy-done.25, bf16[512,256]{1,0:T(8,128)(2,1)} %copy-done.26, ...), custom_call_target="tpu_custom_call" | custom-call | flops 2147483648 | bytes 7000000 | tf_op jit(solution)/shard_map/projection/pallas_call | solution.py:295
  83.7 4.4 %collective-permute-done.20.refs_2_ = bf16[512,256]{1,0:T(8,128)(2,1)S(1)} collective-permute-done((bf16[512,256]{1,0:T(8,128)(2,1)}, bf16[512,256]{1,0:T(8,128)(2,1)S(1)}, u32[]{:S(2)}, u32[]{:S(2)}) %collective-permute-start.20) | collective-permute-done | bytes 262176 | tf_op jit(solution)/shard_map/ppermute | solution.py:38
  88.8 1.4 collective-permute-start.29
  90.7 1.1 collective-permute-start.27
  91.8 0.7 copy.13.weights
  92.5 6.7 %projection.3 = (bf16[128,2048]{1,0:T(8,128)(2,1)}, bf16[128,2048]{1,0:T(8,128)(2,1)}, bf16[128,2048]{1,0:T(8,128)(2,1)}, bf16[128,2048]{1,0:T(8,128)(2,1)}) custom-call(s32[8]{0:T(128)} %concatenate.15.meta, bf16[512,256]{1,0:T(8,128)(2,1)} %get-tuple-element.53.refs_0_, bf16[512,256]{1,0:T(8,128)(2,1)} %copy-done.28, bf16[512,256]{1,0:T(8,128)(2,1)} %copy-done.29, ...), custom_call_target="tpu_custom_call" | custom-call | flops 2147483648 | bytes 7000000 | tf_op jit(solution)/shard_map/projection/pallas_call | solution.py:295
  99.2 0.9 collective-permute-start.24
  100.1 5.3 %collective-permute-start.25 = (bf16[128,2048]{1,0:T(8,128)(2,1)}, bf16[128,2048]{1,0:T(8,128)(2,1)S(1)}, u32[]{:S(2)}, u32[]{:S(2)}) collective-permute-start(bf16[128,2048]{1,0:T(8,128)(2,1)} %get-tuple-element.77), channel_id=1, source_target_pairs={{0,8},{1,9},{2,10},{3,11},{4,12},{5,13},{6,14},{7,15},{8,0},{9,1},... | collective-permute-start | bytes 1572872 | tf_op jit(solution)/shard_map/ppermute | solution.py:30
  105.4 8.2 %collective-permute-done.29.refs_3_ = bf16[128,2048]{1,0:T(8,128)(2,1)S(1)} collective-permute-done((bf16[128,2048]{1,0:T(8,128)(2,1)}, bf16[128,2048]{1,0:T(8,128)(2,1)S(1)}, u32[]{:S(2)}, u32[]{:S(2)}) %collective-permute-start.29) | collective-permute-done | bytes 524320 | tf_op jit(solution)/shard_map/ppermute | solution.py:38
  113.7 4.8 %collective-permute-start.26 = (bf16[128,2048]{1,0:T(8,128)(2,1)}, bf16[128,2048]{1,0:T(8,128)(2,1)S(1)}, u32[]{:S(2)}, u32[]{:S(2)}) collective-permute-start(bf16[128,2048]{1,0:T(8,128)(2,1)} %get-tuple-element.78), channel_id=1, source_target_pairs={{0,12},{1,13},{2,14},{3,15},{4,0},{5,1},{6,2},{7,3},{8,4},{9,5},{1... | collective-permute-start | bytes 1572872 | tf_op jit(solution)/shard_map/ppermute | solution.py:30
  118.5 0.8 copy-done.17
  119.3 3.0 settle.1.refs_4_
  122.3 0.7 copy.12.ids
  123.0 2.6 routes.1
  125.7 2.8 collective-permute-done.25.refs_2_
  128.5 0.8 copy-done.16
  129.5 9.4 %dispatch.1 = (bf16[1024,4608]{1,0:T(8,128)(2,1)}, f32[128,4096]{1,0:T(8,128)}) custom-call(s32[8]{0:T(128)} %concatenate.15.meta, bf16[128,2048]{1,0:T(8,128)(2,1)} %get-tuple-element.72.refs_0_, bf16[128,2048]{1,0:T(8,128)(2,1)} %copy-done.14, bf16[128,2048]{1,0:T(8,128)(2,1)} %copy-done.16, bf16[128,2048]{1,0:T(8,128)(2,1)} %copy-done.18, ...), custom_call_target="tpu_custom_call" | custom-call | flops 3000000000 | bytes 16000000 | tf_op jit(solution)/shard_map/dispatch/pallas_call | solution.py:398
  138.9 124.7 %all_to_all.10 = bf16[128,8,4608]{2,1,0:T(8,128)(2,1)} all-to-all(bf16[128,8,4608]{2,1,0:T(8,128)(2,1)} %bitcast.18), channel_id=1, replica_groups=mesh['dp'=4,'ctx'=2,'tp'=16] {'dp','ctx','tp'}, dimensions={0} | all-to-all | bytes 18874368 | tf_op jit(solution)/shard_map/all_to_all | solution.py:665
  263.6 24.4 %experts.1 = bf16[1024,4608]{1,0:T(8,128)(2,1)} custom-call(bf16[1024,4608]{1,0:T(8,128)(2,1)} %bitcast.19, bf16[1024,4608]{1,0:T(8,128)(2,1)} %bitcast.20, bf16[1,4096,768]{2,1,0:T(8,128)(2,1)S(1)} %bitcast.15, bf16[1,768,4096]{2,1,0:T(8,128)(2,1)} %down_hbm.1), custom_call_target="tpu_custom_call" | custom-call | flops 14495514624 | bytes 32000000 | tf_op jit(solution)/shard_map/experts/pallas_call | solution.py:463
  288.0 115.5 %all_to_all.11 = bf16[128,8,4608]{2,1,0:T(8,128)(2,1)} all-to-all(bf16[128,8,4608]{2,1,0:T(8,128)(2,1)} %bitcast.21), channel_id=1, replica_groups=mesh['dp'=4,'ctx'=2,'tp'=16] {'dp','ctx','tp'}, dimensions={0} | all-to-all | bytes 18874368 | tf_op jit(solution)/shard_map/all_to_all | solution.py:665
  403.5 8.1 %combine.1 = bf16[128,4096]{1,0:T(8,128)(2,1)} custom-call(bf16[256,1024]{1,0:T(8,128)(2,1)} %get-tuple-element.74.main, bf16[256,128]{1,0:T(8,128)(2,1)} %get-tuple-element.75.late, bf16[1024,4608]{1,0:T(8,128)(2,1)} %bitcast.16, bf16[1024,4608]{1,0:T(8,128)(2,1)} %bitcast.17, f32[128,4096]{1,0:T(8,128)} %get-tuple-element.82.state), custom_call_target="tpu_custom_call" | custom-call | flops 4000000000 | bytes 13000000 | tf_op jit(solution)/shard_map/combine/pallas_call | solution.py:516
  (100 shorter events, 3.7 us)
Async XLA Ops:
  0.0 31.3 %copy-start.5 = (s32[4]{0:T(128)S(1)}, s32[4]{0:T(128)}, u32[]{:S(2)}) copy-start(s32[4]{0:T(128)} %param.14) | copy-start | bytes 52
  0.9 5.8 %collective-permute-start.1 = (bf16[128,256]{1,0:T(8,128)(2,1)S(1)}, bf16[128,256]{1,0:T(8,128)(2,1)S(1)}, u32[]{:S(2)}, u32[]{:S(2)}) collective-permute-start(bf16[128,256]{1,0:T(8,128)(2,1)S(1)} %pad_maximum_fusion.2), channel_id=1, source_target_pairs={{0,8},{1,9},{2,10},{3,11},{4,12},{5,13},{6,14},{7,15},{8,0},{9,1},... | collective-permute-start | bytes 196616 | tf_op jit(solution)/shard_map/ppermute | solution.py:30
  4.1 4.3 %collective-permute-start.2 = (bf16[128,256]{1,0:T(8,128)(2,1)S(1)}, bf16[128,256]{1,0:T(8,128)(2,1)S(1)}, u32[]{:S(2)}, u32[]{:S(2)}) collective-permute-start(bf16[128,256]{1,0:T(8,128)(2,1)S(1)} %pad_maximum_fusion.3), channel_id=1, source_target_pairs={{0,12},{1,13},{2,14},{3,15},{4,0},{5,1},{6,2},{7,3},{8,4},{9,5},{1... | collective-permute-start | bytes 196616 | tf_op jit(solution)/shard_map/ppermute | solution.py:30
  5.3 5.5 %collective-permute-start = (bf16[128,256]{1,0:T(8,128)(2,1)S(1)}, bf16[128,256]{1,0:T(8,128)(2,1)S(1)}, u32[]{:S(2)}, u32[]{:S(2)}) collective-permute-start(bf16[128,256]{1,0:T(8,128)(2,1)S(1)} %pad_maximum_fusion.1), channel_id=1, source_target_pairs={{0,4},{1,5},{2,6},{3,7},{4,8},{5,9},{6,10},{7,11},{8,12},{9,13},{1... | collective-permute-start | bytes 196616 | tf_op jit(solution)/shard_map/ppermute | solution.py:30
  10.9 33.5 %copy-start.2 = (bf16[4,128,256]{2,1,0:T(8,128)(2,1)}, bf16[4,128,256]{2,1,0:T(8,128)(2,1)S(1)}, u32[]{:S(2)}) copy-start(bf16[4,128,256]{2,1,0:T(8,128)(2,1)S(1)} %pad_maximum_fusion.refs_0_) | copy-start | bytes 786436
  10.9 6.5 %collective-permute-start.3 = (bf16[4,128,256]{2,1,0:T(8,128)(2,1)S(1)}, bf16[4,128,256]{2,1,0:T(8,128)(2,1)S(1)}, u32[]{:S(2)}, u32[]{:S(2)}) collective-permute-start(bf16[4,128,256]{2,1,0:T(8,128)(2,1)S(1)} %pad_maximum_fusion.refs_0_), channel_id=1, source_target_pairs={{0,16},{16,0},{1,17},{17,1},{2,18},{18,2},{3,19},{19,3},{4,20},{20... | collective-permute-start | bytes 786440 | tf_op jit(solution)/shard_map/ppermute | solution.py:46
  12.6 11.2 %collective-permute-start.4 = (bf16[4,128,256]{2,1,0:T(8,128)(2,1)S(1)}, bf16[4,128,256]{2,1,0:T(8,128)(2,1)S(1)}, u32[]{:S(2)}, u32[]{:S(2)}) collective-permute-start(bf16[4,128,256]{2,1,0:T(8,128)(2,1)S(1)} %pad_maximum_fusion.refs_0_), channel_id=1, source_target_pairs={{0,1},{1,2},{2,3},{3,0},{4,5},{5,6},{6,7},{7,4},{8,9},{9,10},{10,1... | collective-permute-start | bytes 786440 | tf_op jit(solution)/shard_map/ppermute | solution.py:38
  17.4 27.1 %copy-start.19 = (bf16[4,128,256]{2,1,0:T(8,128)(2,1)}, bf16[4,128,256]{2,1,0:T(8,128)(2,1)S(1)}, u32[]{:S(2)}) copy-start(bf16[4,128,256]{2,1,0:T(8,128)(2,1)S(1)} %collective-permute-done.3.refs_1_) | copy-start | bytes 786436
  17.4 8.2 %collective-permute-start.7 = (bf16[4,128,256]{2,1,0:T(8,128)(2,1)S(1)}, bf16[4,128,256]{2,1,0:T(8,128)(2,1)S(1)}, u32[]{:S(2)}, u32[]{:S(2)}) collective-permute-start(bf16[4,128,256]{2,1,0:T(8,128)(2,1)S(1)} %collective-permute-done.3.refs_1_), channel_id=1, source_target_pairs={{0,3},{1,0},{2,1},{3,2},{4,7},{5,4},{6,5},{7,6},{8,11},{9,8},{10,9... | collective-permute-start | bytes 786440 | tf_op jit(solution)/shard_map/ppermute | solution.py:38
  22.7 36.2 %copy-start = (bf16[256,1024]{1,0:T(8,128)(2,1)}, bf16[256,1024]{1,0:T(8,128)(2,1)S(1)}, u32[]{:S(2)}) copy-start(bf16[256,1024]{1,0:T(8,128)(2,1)S(1)} %get-tuple-element.50.refs_7_) | copy-start | bytes 1572868
  22.7 36.2 %copy-start.1 = (bf16[256,1024]{1,0:T(8,128)(2,1)}, bf16[256,1024]{1,0:T(8,128)(2,1)S(1)}, u32[]{:S(2)}) copy-start(bf16[256,1024]{1,0:T(8,128)(2,1)S(1)} %get-tuple-element.49.refs_3_) | copy-start | bytes 1572868
  22.7 21.7 %collective-permute-start.12 = (bf16[256,1024]{1,0:T(8,128)(2,1)S(1)}, bf16[256,1024]{1,0:T(8,128)(2,1)S(1)}, u32[]{:S(2)}, u32[]{:S(2)}) collective-permute-start(bf16[256,1024]{1,0:T(8,128)(2,1)S(1)} %get-tuple-element.49.refs_3_), channel_id=1, source_target_pairs={{0,12},{1,13},{2,14},{3,15},{4,0},{5,1},{6,2},{7,3},{8,4},{9,5},{1... | collective-permute-start | bytes 1572872 | tf_op jit(solution)/shard_map/ppermute | solution.py:30
  23.8 20.6 %copy-start.20 = (bf16[4,128,256]{2,1,0:T(8,128)(2,1)}, bf16[4,128,256]{2,1,0:T(8,128)(2,1)S(1)}, u32[]{:S(2)}) copy-start(bf16[4,128,256]{2,1,0:T(8,128)(2,1)S(1)} %collective-permute-done.4.refs_2_) | copy-start | bytes 786436
  23.8 10.2 %collective-permute-start.8 = (bf16[4,128,256]{2,1,0:T(8,128)(2,1)S(1)}, bf16[4,128,256]{2,1,0:T(8,128)(2,1)S(1)}, u32[]{:S(2)}, u32[]{:S(2)}) collective-permute-start(bf16[4,128,256]{2,1,0:T(8,128)(2,1)S(1)} %collective-permute-done.4.refs_2_), channel_id=1, source_target_pairs={{0,1},{1,2},{2,3},{3,0},{4,5},{5,6},{6,7},{7,4},{8,9},{9,10},{10,1... | collective-permute-start | bytes 786440 | tf_op jit(solution)/shard_map/ppermute | solution.py:38
  25.6 18.9 %copy-start.21 = (bf16[4,128,256]{2,1,0:T(8,128)(2,1)}, bf16[4,128,256]{2,1,0:T(8,128)(2,1)S(1)}, u32[]{:S(2)}) copy-start(bf16[4,128,256]{2,1,0:T(8,128)(2,1)S(1)} %collective-permute-done.7.refs_5_) | copy-start | bytes 786436
  25.6 8.8 %collective-permute-start.9 = (bf16[4,128,256]{2,1,0:T(8,128)(2,1)S(1)}, bf16[4,128,256]{2,1,0:T(8,128)(2,1)S(1)}, u32[]{:S(2)}, u32[]{:S(2)}) collective-permute-start(bf16[4,128,256]{2,1,0:T(8,128)(2,1)S(1)} %collective-permute-done.7.refs_5_), channel_id=1, source_target_pairs={{0,3},{1,0},{2,1},{3,2},{4,7},{5,4},{6,5},{7,6},{8,11},{9,8},{10,9... | collective-permute-start | bytes 786440 | tf_op jit(solution)/shard_map/ppermute | solution.py:38
  29.3 8.4 %collective-permute-start.6 = (bf16[4,128,256]{2,1,0:T(8,128)(2,1)S(1)}, bf16[4,128,256]{2,1,0:T(8,128)(2,1)S(1)}, u32[]{:S(2)}, u32[]{:S(2)}) collective-permute-start(bf16[4,128,256]{2,1,0:T(8,128)(2,1)S(1)} %pad_maximum_fusion.refs_0_), channel_id=1, source_target_pairs={{0,3},{1,0},{2,1},{3,2},{4,7},{5,4},{6,5},{7,6},{8,11},{9,8},{10,9... | collective-permute-start | bytes 786440 | tf_op jit(solution)/shard_map/ppermute | solution.py:38
  29.4 12.1 %collective-permute-start.5 = (bf16[4,128,256]{2,1,0:T(8,128)(2,1)S(1)}, bf16[4,128,256]{2,1,0:T(8,128)(2,1)}, u32[]{:S(2)}, u32[]{:S(2)}) collective-permute-start(bf16[4,128,256]{2,1,0:T(8,128)(2,1)S(1)} %collective-permute-done.3.refs_1_), channel_id=1, source_target_pairs={{0,1},{1,2},{2,3},{3,0},{4,5},{5,6},{6,7},{7,4},{8,9},{9,10},{10,1... | collective-permute-start | bytes 786440 | tf_op jit(solution)/shard_map/ppermute | solution.py:38
  34.0 10.5 %copy-start.22 = (bf16[4,128,256]{2,1,0:T(8,128)(2,1)}, bf16[4,128,256]{2,1,0:T(8,128)(2,1)S(1)}, u32[]{:S(2)}) copy-start(bf16[4,128,256]{2,1,0:T(8,128)(2,1)S(1)} %collective-permute-done.8.refs_6_) | copy-start | bytes 786436
  34.0 24.9 %collective-permute-start.11 = (bf16[256,1024]{1,0:T(8,128)(2,1)S(1)}, bf16[256,1024]{1,0:T(8,128)(2,1)S(1)}, u32[]{:S(2)}, u32[]{:S(2)}) collective-permute-start(bf16[256,1024]{1,0:T(8,128)(2,1)S(1)} %get-tuple-element.49.refs_3_), channel_id=1, source_target_pairs={{0,8},{1,9},{2,10},{3,11},{4,12},{5,13},{6,14},{7,15},{8,0},{9,1},... | collective-permute-start | bytes 1572872 | tf_op jit(solution)/shard_map/ppermute | solution.py:30
  34.4 10.1 %copy-start.23 = (bf16[4,128,256]{2,1,0:T(8,128)(2,1)}, bf16[4,128,256]{2,1,0:T(8,128)(2,1)S(1)}, u32[]{:S(2)}) copy-start(bf16[4,128,256]{2,1,0:T(8,128)(2,1)S(1)} %collective-permute-done.9.refs_7_) | copy-start | bytes 786436
  34.4 24.7 %collective-permute-start.10 = (bf16[256,1024]{1,0:T(8,128)(2,1)S(1)}, bf16[256,1024]{1,0:T(8,128)(2,1)S(1)}, u32[]{:S(2)}, u32[]{:S(2)}) collective-permute-start(bf16[256,1024]{1,0:T(8,128)(2,1)S(1)} %get-tuple-element.49.refs_3_), channel_id=1, source_target_pairs={{0,4},{1,5},{2,6},{3,7},{4,8},{5,9},{6,10},{7,11},{8,12},{9,13},{1... | collective-permute-start | bytes 1572872 | tf_op jit(solution)/shard_map/ppermute | solution.py:30
  37.7 6.8 %copy-start.24 = (bf16[4,128,256]{2,1,0:T(8,128)(2,1)}, bf16[4,128,256]{2,1,0:T(8,128)(2,1)S(1)}, u32[]{:S(2)}) copy-start(bf16[4,128,256]{2,1,0:T(8,128)(2,1)S(1)} %collective-permute-done.6.refs_4_) | copy-start | bytes 786436
  37.7 23.0 %collective-permute-start.15 = (bf16[256,1024]{1,0:T(8,128)(2,1)S(1)}, bf16[256,1024]{1,0:T(8,128)(2,1)S(1)}, u32[]{:S(2)}, u32[]{:S(2)}) collective-permute-start(bf16[256,1024]{1,0:T(8,128)(2,1)S(1)} %get-tuple-element.50.refs_7_), channel_id=1, source_target_pairs={{0,3},{1,0},{2,1},{3,2},{4,7},{5,4},{6,5},{7,6},{8,11},{9,8},{10,9... | collective-permute-start | bytes 1572872 | tf_op jit(solution)/shard_map/ppermute | solution.py:38
  41.4 21.0 %collective-permute-start.14 = (bf16[256,1024]{1,0:T(8,128)(2,1)S(1)}, bf16[256,1024]{1,0:T(8,128)(2,1)S(1)}, u32[]{:S(2)}, u32[]{:S(2)}) collective-permute-start(bf16[256,1024]{1,0:T(8,128)(2,1)S(1)} %get-tuple-element.50.refs_7_), channel_id=1, source_target_pairs={{0,2},{1,3},{2,0},{3,1},{4,6},{5,7},{6,4},{7,5},{8,10},{9,11},{10,... | collective-permute-start | bytes 1572872 | tf_op jit(solution)/shard_map/ppermute | solution.py:38
  44.5 14.5 %copy-start.8 = (bf16[256,1024]{1,0:T(8,128)(2,1)}, bf16[256,1024]{1,0:T(8,128)(2,1)S(1)}, u32[]{:S(2)}) copy-start(bf16[256,1024]{1,0:T(8,128)(2,1)S(1)} %collective-permute-done.12.refs_6_) | copy-start | bytes 1572868
  44.5 17.9 %collective-permute-start.13 = (bf16[256,1024]{1,0:T(8,128)(2,1)S(1)}, bf16[256,1024]{1,0:T(8,128)(2,1)S(1)}, u32[]{:S(2)}, u32[]{:S(2)}) collective-permute-start(bf16[256,1024]{1,0:T(8,128)(2,1)S(1)} %get-tuple-element.50.refs_7_), channel_id=1, source_target_pairs={{0,1},{1,2},{2,3},{3,0},{4,5},{5,6},{6,7},{7,4},{8,9},{9,10},{10,1... | collective-permute-start | bytes 1572872 | tf_op jit(solution)/shard_map/ppermute | solution.py:38
  59.0 11.9 %collective-permute-start.16 = (bf16[512,256]{1,0:T(8,128)(2,1)}, bf16[512,256]{1,0:T(8,128)(2,1)S(1)}, u32[]{:S(2)}, u32[]{:S(2)}) collective-permute-start(bf16[512,256]{1,0:T(8,128)(2,1)} %get-tuple-element.46.refs_0_), channel_id=1, source_target_pairs={{0,4},{1,5},{2,6},{3,7},{4,8},{5,9},{6,10},{7,11},{8,12},{9,13},{1... | collective-permute-start | bytes 786440 | tf_op jit(solution)/shard_map/ppermute | solution.py:30
  59.1 11.8 %collective-permute-start.17 = (bf16[512,256]{1,0:T(8,128)(2,1)}, bf16[512,256]{1,0:T(8,128)(2,1)S(1)}, u32[]{:S(2)}, u32[]{:S(2)}) collective-permute-start(bf16[512,256]{1,0:T(8,128)(2,1)} %get-tuple-element.47.refs_1_), channel_id=1, source_target_pairs={{0,8},{1,9},{2,10},{3,11},{4,12},{5,13},{6,14},{7,15},{8,0},{9,1},... | collective-permute-start | bytes 786440 | tf_op jit(solution)/shard_map/ppermute | solution.py:30
  60.8 10.2 %collective-permute-start.18 = (bf16[512,256]{1,0:T(8,128)(2,1)}, bf16[512,256]{1,0:T(8,128)(2,1)S(1)}, u32[]{:S(2)}, u32[]{:S(2)}) collective-permute-start(bf16[512,256]{1,0:T(8,128)(2,1)} %get-tuple-element.48.refs_2_), channel_id=1, source_target_pairs={{0,12},{1,13},{2,14},{3,15},{4,0},{5,1},{6,2},{7,3},{8,4},{9,5},{1... | collective-permute-start | bytes 786440 | tf_op jit(solution)/shard_map/ppermute | solution.py:30
  70.9 4.8 %collective-permute-start.22 = (bf16[1024,1024]{1,0:T(8,128)(2,1)}, bf16[1024,1024]{1,0:T(8,128)(2,1)S(1)}, u32[]{:S(2)}, u32[]{:S(2)}) collective-permute-start(bf16[1024,1024]{1,0:T(8,128)(2,1)} %get-tuple-element.62.refs_4_), channel_id=1, source_target_pairs={{0,32},{32,0},{64,96},{96,64},{1,33},{33,1},{65,97},{97,65},{2,34}... | collective-permute-start | bytes 6291464 | tf_op jit(solution)/shard_map/ppermute | solution.py:50
  71.0 17.1 %copy-start.6 = (bf16[1024,1024]{1,0:T(8,128)(2,1)S(1)}, bf16[1024,1024]{1,0:T(8,128)(2,1)}, u32[]{:S(2)}) copy-start(bf16[1024,1024]{1,0:T(8,128)(2,1)} %get-tuple-element.71.refs_4_) | copy-start | bytes 6291460
  71.0 20.7 %copy-start.3 = (f32[128,8]{0,1:T(8,128)S(1)}, f32[128,8]{0,1:T(8,128)}, u32[]{:S(2)}) copy-start(f32[128,8]{0,1:T(8,128)} %param.19) | copy-start | bytes 12292
  71.0 12.6 %collective-permute-start.19 = (bf16[512,256]{1,0:T(8,128)(2,1)}, bf16[512,256]{1,0:T(8,128)(2,1)S(1)}, u32[]{:S(2)}, u32[]{:S(2)}) collective-permute-start(bf16[512,256]{1,0:T(8,128)(2,1)} %get-tuple-element.55), channel_id=1, source_target_pairs={{0,1},{1,2},{2,3},{3,0},{4,5},{5,6},{6,7},{7,4},{8,9},{9,10},{10,1... | collective-permute-start | bytes 786440 | tf_op jit(solution)/shard_map/ppermute | solution.py:38
  71.4 16.7 %collective-permute-start.20 = (bf16[512,256]{1,0:T(8,128)(2,1)}, bf16[512,256]{1,0:T(8,128)(2,1)S(1)}, u32[]{:S(2)}, u32[]{:S(2)}) collective-permute-start(bf16[512,256]{1,0:T(8,128)(2,1)} %get-tuple-element.57), channel_id=1, source_target_pairs={{0,2},{1,3},{2,0},{3,1},{4,6},{5,7},{6,4},{7,5},{8,10},{9,11},{10,... | collective-permute-start | bytes 786440 | tf_op jit(solution)/shard_map/ppermute | solution.py:38
  75.7 12.4 %collective-permute-start.21 = (bf16[512,256]{1,0:T(8,128)(2,1)}, bf16[512,256]{1,0:T(8,128)(2,1)S(1)}, u32[]{:S(2)}, u32[]{:S(2)}) collective-permute-start(bf16[512,256]{1,0:T(8,128)(2,1)} %get-tuple-element.59), channel_id=1, source_target_pairs={{0,3},{1,0},{2,1},{3,2},{4,7},{5,4},{6,5},{7,6},{8,11},{9,8},{10,9... | collective-permute-start | bytes 786440 | tf_op jit(solution)/shard_map/ppermute | solution.py:38
  83.7 8.8 %copy-start.28 = (bf16[512,256]{1,0:T(8,128)(2,1)}, bf16[512,256]{1,0:T(8,128)(2,1)S(1)}, u32[]{:S(2)}) copy-start(bf16[512,256]{1,0:T(8,128)(2,1)S(1)} %collective-permute-done.19.refs_1_) | copy-start | bytes 786436
  88.2 4.4 %collective-permute-start.23 = (bf16[1024,1024]{1,0:T(8,128)(2,1)S(1)}, bf16[1024,1024]{1,0:T(8,128)(2,1)}, u32[]{:S(2)}, u32[]{:S(2)}) collective-permute-start(bf16[1024,1024]{1,0:T(8,128)(2,1)S(1)} %copy-done.6), channel_id=1, source_target_pairs={{0,32},{32,0},{64,96},{96,64},{1,33},{33,1},{65,97},{97,65},{2,34}... | collective-permute-start | bytes 6291464 | tf_op jit(solution)/shard_map/ppermute | solution.py:50
  88.8 24.8 %collective-permute-start.29 = (bf16[128,2048]{1,0:T(8,128)(2,1)}, bf16[128,2048]{1,0:T(8,128)(2,1)S(1)}, u32[]{:S(2)}, u32[]{:S(2)}) collective-permute-start(bf16[128,2048]{1,0:T(8,128)(2,1)} %get-tuple-element.70), channel_id=1, source_target_pairs={{0,3},{1,0},{2,1},{3,2},{4,7},{5,4},{6,5},{7,6},{8,11},{9,8},{10,9... | collective-permute-start | bytes 1572872 | tf_op jit(solution)/shard_map/ppermute | solution.py:38
  90.3 28.2 %collective-permute-start.28 = (bf16[128,2048]{1,0:T(8,128)(2,1)}, bf16[128,2048]{1,0:T(8,128)(2,1)S(1)}, u32[]{:S(2)}, u32[]{:S(2)}) collective-permute-start(bf16[128,2048]{1,0:T(8,128)(2,1)} %get-tuple-element.68), channel_id=1, source_target_pairs={{0,2},{1,3},{2,0},{3,1},{4,6},{5,7},{6,4},{7,5},{8,10},{9,11},{10,... | collective-permute-start | bytes 1572872 | tf_op jit(solution)/shard_map/ppermute | solution.py:38
  90.7 27.8 %collective-permute-start.27 = (bf16[128,2048]{1,0:T(8,128)(2,1)}, bf16[128,2048]{1,0:T(8,128)(2,1)}, u32[]{:S(2)}, u32[]{:S(2)}) collective-permute-start(bf16[128,2048]{1,0:T(8,128)(2,1)} %get-tuple-element.66), channel_id=1, source_target_pairs={{0,1},{1,2},{2,3},{3,0},{4,5},{5,6},{6,7},{7,4},{8,9},{9,10},{10,1... | collective-permute-start | bytes 1572872 | tf_op jit(solution)/shard_map/ppermute | solution.py:38
  99.2 26.5 %collective-permute-start.24 = (bf16[128,2048]{1,0:T(8,128)(2,1)}, bf16[128,2048]{1,0:T(8,128)(2,1)S(1)}, u32[]{:S(2)}, u32[]{:S(2)}) collective-permute-start(bf16[128,2048]{1,0:T(8,128)(2,1)} %get-tuple-element.76), channel_id=1, source_target_pairs={{0,4},{1,5},{2,6},{3,7},{4,8},{5,9},{6,10},{7,11},{8,12},{9,13},{1... | collective-permute-start | bytes 1572872 | tf_op jit(solution)/shard_map/ppermute | solution.py:30
  100.1 28.4 %collective-permute-start.25 = (bf16[128,2048]{1,0:T(8,128)(2,1)}, bf16[128,2048]{1,0:T(8,128)(2,1)S(1)}, u32[]{:S(2)}, u32[]{:S(2)}) collective-permute-start(bf16[128,2048]{1,0:T(8,128)(2,1)} %get-tuple-element.77), channel_id=1, source_target_pairs={{0,8},{1,9},{2,10},{3,11},{4,12},{5,13},{6,14},{7,15},{8,0},{9,1},... | collective-permute-start | bytes 1572872 | tf_op jit(solution)/shard_map/ppermute | solution.py:30
  113.7 4.8 %copy-start.15 = (bf16[128,2048]{1,0:T(8,128)(2,1)}, bf16[128,2048]{1,0:T(8,128)(2,1)S(1)}, u32[]{:S(2)}) copy-start(bf16[128,2048]{1,0:T(8,128)(2,1)S(1)} %collective-permute-done.29.refs_3_) | copy-start | bytes 1572868
  113.7 8.6 %copy-start.4 = (s32[128,8]{0,1:T(8,128)S(1)}, s32[128,8]{0,1:T(8,128)}, u32[]{:S(2)}) copy-start(s32[128,8]{0,1:T(8,128)} %param.18) | copy-start | bytes 12292
  113.7 14.8 %collective-permute-start.26 = (bf16[128,2048]{1,0:T(8,128)(2,1)}, bf16[128,2048]{1,0:T(8,128)(2,1)S(1)}, u32[]{:S(2)}, u32[]{:S(2)}) collective-permute-start(bf16[128,2048]{1,0:T(8,128)(2,1)} %get-tuple-element.78), channel_id=1, source_target_pairs={{0,12},{1,13},{2,14},{3,15},{4,0},{5,1},{6,2},{7,3},{8,4},{9,5},{1... | collective-permute-start | bytes 1572872 | tf_op jit(solution)/shard_map/ppermute | solution.py:30
  129.5 134.1 %slice-start = ((s8[6291456]{0:T(1024)(128)(4,1)}), s8[2097152]{0:T(1024)(128)(4,1)S(1)}, s32[]{:S(2)}) async-start(s8[6291456]{0:T(1024)(128)(4,1)} %bitcast.14), calls=%async_computation.2 | async-start | bytes 4194304
  138.9 124.7 %slice-start.1 = ((s8[6291456]{0:T(1024)(128)(4,1)}), s8[4194304]{0:T(1024)(128)(4,1)S(1)}, s32[]{:S(2)}) async-start(s8[6291456]{0:T(1024)(128)(4,1)} %bitcast.14), calls=%async_computation.3 | async-start | bytes 8388608
  (15 other events, 34.4 us)

commit v9 on v8

--- a/solution.py
+++ b/solution.py
@@ -16,7 +16,6 @@
 SEG = 512
 ROWS = 256
 COMBINE_ROWS = 512
-DISPATCH_COLUMNS = 512
 DOWN_COLUMNS = 512
 COMBINE_COLUMNS = 512
 BLOCK = 512
@@ -210,19 +209,20 @@
 
 def attention_end_kernel(meta, q_ref, keys, values, *refs):
     others, weights, out, refs = refs[:3], refs[3:11], refs[11], refs[12:]
-    outs_z, joined, held, came, went, scratch = refs[:4], refs[4:6], *refs[6:9], refs[9:]
+    outs_z, joined, held, refs = refs[:4], refs[4:6], refs[6:8], refs[8:]
+    came, went, scratch = refs[0], refs[1], refs[2:]
     x, z = meta[5], meta[6]
     depth = weights[0].shape[0]
     arriving = [
         pltpu.make_async_copy(
             piece,
-            held.at[number // SIDE, pl.ds(number % SIDE * depth, depth), :],
+            held[number // SIDE].at[pl.ds(number % SIDE * depth, depth), :],
             came.at[number],
         )
         for number, piece in enumerate(weights)
     ]
     leaving = [
-        pltpu.make_async_copy(held.at[number], whole_of, went.at[number])
+        pltpu.make_async_copy(held[number], whole_of, went.at[number])
         for number, whole_of in enumerate(joined)
     ]
     for copy in arriving:
@@ -246,9 +246,11 @@
 def attention_end(meta, queries, keys, values, others, weights):
     width = queries.shape[1]
     arrays = (queries, keys, values, *others)
-    depth, columns = weights[0].shape
     outs = [jax.ShapeDtypeStruct((BLOCK, width), BF16)] * 5
-    joined = [jax.ShapeDtypeStruct((SIDE * depth, columns), BF16)] * 2
+    joined = [
+        jax.ShapeDtypeStruct((SIDE * piece.shape[0], piece.shape[1]), BF16)
+        for piece in weights[::SIDE]
+    ]
     anywhere = pl.BlockSpec(memory_space=pl.ANY)
     return call(
         attention_end_kernel,
@@ -257,7 +259,7 @@
         [smem()] + [whole(array) for array in arrays] + [anywhere] * len(weights),
         [pl.BlockSpec(out.shape, lambda: (0, 0)) for out in outs] + [anywhere] * 2,
         scratch=[
-            pltpu.VMEM((2, SIDE * depth, columns), BF16),
+            *[pltpu.VMEM(whole_of.shape, BF16) for whole_of in joined],
             pltpu.SemaphoreType.DMA((2 * SIDE,)),
             pltpu.SemaphoreType.DMA((2,)),
             *attend_scratch(),
@@ -291,7 +293,7 @@
 
 def projection(axis, meta, context, weights):
     depth, columns = weights[0].shape
-    part = columns // 4
+    part = 256
     return call(
         functools.partial(projection_kernel, axis),
         "projection",
@@ -300,7 +302,7 @@
         + [whole(array) for array in context]
         + [pl.BlockSpec((depth, part), lambda i: (0, i))] * 2,
         [pl.BlockSpec((TOKENS, 2 * columns), lambda i: (0, 0))] * 4,
-        grid=(4,),
+        grid=(columns // part,),
         scratch=[pltpu.VMEM((SIDE * TOKENS, 2 * columns), BF16)],
         cost=pl.CostEstimate(
             flops=4 * 512 * 1024 * columns, bytes_accessed=7 * 10**6, transcendentals=0
@@ -308,8 +310,8 @@
     )(meta, *context, *weights)
 
 
-def wide_scratch():
-    return pltpu.VMEM((SEG // HD, TOKENS * SLOTS, HD), F32)
+def wide_scratch(rows=TOKENS * SLOTS):
+    return pltpu.VMEM((SEG // HD, rows, HD), F32)
 
 
 def widen(wide, rows_ref):
@@ -322,12 +324,12 @@
 
 
 def gather_rows(wide, segment):
-    rows = pl.ds(segment, TOKENS, stride=SLOTS)
+    rows = pl.ds(segment, wide.shape[1] // SLOTS, stride=SLOTS)
     return jnp.concatenate([wide[part, rows, :] for part in range(SEG // HD)], axis=1).astype(BF16)
 
 
 def scatter_rows(wide, segment, value):
-    rows = pl.ds(segment, TOKENS, stride=SLOTS)
+    rows = pl.ds(segment, value.shape[0], stride=SLOTS)
     for part in range(SEG // HD):
         wide[part, rows, :] = value[:, part * HD : (part + 1) * HD]
 
@@ -366,7 +368,7 @@
 
 def dispatch_kernel(meta, *refs):
     terms, refs = refs[:4], refs[4:]
-    first, residual, gain, main, late, outgoing, state, normed, wide, spread = refs
+    first, residual, gain, main, late, outgoing, state, normed, wide = refs
     step = pl.program_id(0)
     half = first.shape[1]
 
@@ -380,16 +382,14 @@
             columns = slice(segment * SEG, (segment + 1) * SEG)
             normed[:, columns] = (state[:, columns] * scale * gain[:, columns]).astype(BF16)
 
-        for segment in range(SLOTS):
-            columns = slice(segment * SEG, (segment + 1) * SEG)
-            scatter_rows(wide, segment, dot(late[...], normed[:, columns]))
-        spread[...] = narrow(wide)
-
-    for start in range(0, 2 * half, DISPATCH_COLUMNS):
-        columns = slice(start, start + DISPATCH_COLUMNS)
-        outgoing[:, columns] = dot(main[...], normed[:, columns]).astype(BF16)
     rows = outgoing.shape[0]
-    outgoing[:, 2 * half :] = spread[pl.ds(pl.multiple_of(step * rows, rows), rows), :]
+    picks = jnp.concatenate([main[...], late[...]], axis=0)
+    for segment in range(SLOTS):
+        columns = slice(segment * SEG, (segment + 1) * SEG)
+        picked = dot(picks, normed[:, columns])
+        outgoing[:, columns] = picked[:rows].astype(BF16)
+        scatter_rows(wide, segment, picked[rows:])
+    outgoing[:, state.shape[1] :] = narrow(wide)
 
 
 def dispatch(meta, terms, first, residual, gain, main, late):
@@ -404,7 +404,7 @@
         ],
         [smem()]
         + [whole(a) for a in arrays]
-        + [pl.BlockSpec((ROWS, TOKENS), lambda i: (i, 0)), whole(late)],
+        + [pl.BlockSpec((count, TOKENS), lambda i: (i, 0)) for count in (ROWS, ROWS // SLOTS)],
         [
             pl.BlockSpec((ROWS, width + SEG), lambda i: (i, 0)),
             pl.BlockSpec((TOKENS, width), lambda i: (0, 0)),
@@ -412,8 +412,7 @@
         grid=(rows // ROWS,),
         scratch=[
             pltpu.VMEM((TOKENS, width), BF16),
-            wide_scratch(),
-            pltpu.VMEM((rows, SEG), BF16),
+            wide_scratch(ROWS),
         ],
         cost=pl.CostEstimate(flops=3 * 10**9, bytes_accessed=16 * 10**6, transcendentals=0),
     )(meta, *arrays, main, late)
@@ -613,10 +612,11 @@
         )
 
     width = out_proj.shape[1]
-    quarter = width // 4
-
-    def weights_part(base):
-        return lax.dynamic_slice_in_dim(out_proj, base + core * quarter, quarter, 1)
+    columns_z = width // 256 * 5 // 8 * 128
+    columns_x = width // 2 - columns_z
+
+    def weights_part(base, columns):
+        return lax.dynamic_slice_in_dim(out_proj, base + core * columns, columns, 1)
 
     def after(value, *others):
         return lax.optimization_barrier((value, *others))[0]
@@ -627,8 +627,8 @@
     before_other, after_other = shift_z(other, 1), shift_z(other, -1)
     far_own = shift_z(before_own, 1)
     far_other = shift_z(after_other, -1)
-    weights_x = gather_rows_of(shift_x, after(weights_part(0), own))
-    weights_z = gather_rows_of(shift_z, after(weights_part(width // 2), far_own, far_other))
+    weights_x = gather_rows_of(shift_x, after(weights_part(0, columns_z), own))
+    weights_z = gather_rows_of(shift_z, after(weights_part(2 * columns_z, columns_x), far_own, far_other))
     pieces = [
         own,
         other,

time: 413 us -> 414 us (level)
  waiting for transfers between devices: 32.7 us -> 47.3 us
  starting transfers between devices: 46.6 us -> 37.9 us
  blocking collectives: 240 us -> 235 us
    ppermute x15, waiting for transfers between devices: 19.3 us -> 33.2 us  [shift_z(): lax.ppermute(value, 'tp', [(x * SIDE + z, x * SIDE + (z + step) % SIDE) f...]
    ppermute x12, starting transfers between devices: 21.8 us -> 13 us  [shift_x(): lax.ppermute(value, 'tp', [(x * SIDE + z, (x + step) % SIDE * SIDE + z) f...]
    all_to_all x2, blocking collectives: 240 us -> 235 us  [all_to_all(): lax.all_to_all(blocks, ('dp', 'ctx', 'tp'), split_axis=0, concat_axis=0,...]
  transfers between devices with their start and end apart: 30 -> 30, of which waited for: 11 -> 14; matrix products, arithmetic and copies ran while one was open for 1% -> 1% of each run, Pallas kernels for 10% -> 10%
where the time goes in v9:
time: 414 us; the launch traced here: 413 us
  blocking collectives  235 us (57%)
  Pallas kernels  84.7 us (20%)
  waiting for transfers between devices  47.3 us (11%)
  starting transfers between devices  37.9 us (9%)
  local copies, waits for them, and re-layouts  8.47 us (2%)
    all_to_all x2, blocking collectives, all_to_all(): lax.all_to_all(blocks, ('dp', 'ctx', 'tp'), split_axis=0, concat_axis=0,...  235 us
    ppermute x15, waiting for transfers between devices, shift_z(): lax.ppermute(value, 'tp', [(x * SIDE + z, x * SIDE + (z + step) % SIDE) f...  33.2 us
    pallas_call x1, Pallas kernels, experts(): call(expert_kernel, 'experts', jax.ShapeDtypeStruct((rows, columns), BF16...  24.4 us
    ppermute x15, starting transfers between devices, shift_z(): lax.ppermute(value, 'tp', [(x * SIDE + z, x * SIDE + (z + step) % SIDE) f...  23.2 us
    pallas_call x2, Pallas kernels, projection(): call(functools.partial(projection_kernel, axis), 'projection', [jax.Shape...  13.4 us
    ppermute x12, starting transfers between devices, shift_x(): lax.ppermute(value, 'tp', [(x * SIDE + z, (x + step) % SIDE * SIDE + z) f...  13 us
    pallas_call x1, Pallas kernels, attention(): call(attention_kernel, 'attention', outs, [smem()] + [whole(array) for ar...  12.9 us
    pallas_call x1, Pallas kernels, attention_end(): call(attention_end_kernel, 'attention_end', outs + joined, [smem()] + [wh...  10.8 us
  transfers between devices with their start and end apart: 30, of which 14 were waited for; matrix products, arithmetic and copies ran while one was open for 1% of the time, Pallas kernels for 10%

profile of v9, /device:TPU:0, one launch (start us, length us, event | category | flops | bytes accessed | tf_op | source)
XLA Modules:
  0.0 413.4 jit_solution(11306351898326611835)
XLA Ops:
  0.0 1.0 constant_dynamic-slice_fusion.8
  1.1 3.2 collective-permute-start.1
  4.3 1.2 collective-permute-start.2
  5.5 1.0 collective-permute-start
  6.9 1.7 collective-permute-done.2
  8.6 2.4 collective-permute-done
  11.1 1.7 collective-permute-start.3
  12.9 2.0 collective-permute-start.4
  14.9 2.7 collective-permute-done.3.refs_1_
  17.5 4.0 collective-permute-start.7
  22.0 3.4 collective-permute-done.7.refs_5_
  25.5 3.8 collective-permute-start.9
  29.3 2.0 collective-permute-start.5
  31.3 0.7 concatenate.15.meta
  32.0 1.3 collective-permute-start.11
  33.3 0.7 collective-permute-done.9.refs_7_
  34.0 0.8 collective-permute-start.10
  34.8 2.9 collective-permute-done.6.refs_4_
  37.8 3.8 collective-permute-start.15
  41.6 0.9 collective-permute-start.13
  42.4 12.9 %attention.1 = (bf16[512,256]{1,0:T(8,128)(2,1)}, bf16[512,256]{1,0:T(8,128)(2,1)}, bf16[512,256]{1,0:T(8,128)(2,1)}, bf16[4096,128]{1,0:T(8,128)(2,1)}, bf16[128,4096]{1,0:T(8,128)(2,1)}) custom-call(s32[8]{0:T(128)} %concatenate.15.meta, bf16[2048,256]{1,0:T(8,128)(2,1)} %q_ref.3, bf16[4,128,256]{2,1,0:T(8,128)(2,1)} %copy-done.4, ...), custom_call_target="tpu_custom_call" | custom-call | flops 16000000000 | bytes 7000000 | tf_op jit(solution)/shard_map/attention/pallas_call | solution.py:197
  55.4 5.1 %collective-permute-done.10.refs_4_ = bf16[256,1280]{1,0:T(8,128)(2,1)S(1)} collective-permute-done((bf16[256,1280]{1,0:T(8,128)(2,1)S(1)}, bf16[256,1280]{1,0:T(8,128)(2,1)S(1)}, u32[]{:S(2)}, u32[]{:S(2)}) %collective-permute-start.10) | collective-permute-done | bytes 655392 | tf_op jit(solution)/shard_map/ppermute | solution.py:29
  60.5 1.6 collective-permute-start.17
  62.2 3.5 collective-permute-start.18
  65.8 0.7 copy-done.14
  66.6 10.8 %attention_end.1 = (bf16[512,256]{1,0:T(8,128)(2,1)}, bf16[512,256]{1,0:T(8,128)(2,1)}, bf16[512,256]{1,0:T(8,128)(2,1)}, bf16[512,256]{1,0:T(8,128)(2,1)}, bf16...) custom-call(s32[8]{0:T(128)} %concatenate.15.meta, bf16[2048,256]{1,0:T(8,128)(2,1)} %q_ref.3, ...), custom_call_target="tpu_custom_call" | custom-call | flops 6000000000 | bytes 7000000 | tf_op jit(solution)/shard_map/attention_end/pallas_call | solution.py:255
  78.2 2.4 collective-permute-start.20
  81.0 1.7 collective-permute-done.22.refs_5_
  82.7 1.5 copy-done.8
  84.2 7.9 %projection.2 = (bf16[128,2560]{1,0:T(8,128)(2,1)}, bf16[128,2560]{1,0:T(8,128)(2,1)}, bf16[128,2560]{1,0:T(8,128)(2,1)}, bf16[128,2560]{1,0:T(8,128)(2,1)}) custom-call(s32[8]{0:T(128)} %concatenate.15.meta, bf16[512,256]{1,0:T(8,128)(2,1)} %get-tuple-element.52.refs_0_, bf16[512,256]{1,0:T(8,128)(2,1)} %copy-done.21, bf16[512,256]{1,0:T(8,128)(2,1)} %copy-done.22, ...), custom_call_target="tpu_custom_call" | custom-call | flops 2684354560 | bytes 7000000 | tf_op jit(solution)/shard_map/projection/pallas_call | solution.py:297
  92.1 1.3 collective-permute-done.19.refs_1_
  94.0 0.7 copy-done.26
  94.7 2.4 collective-permute-start.29
  97.1 0.9 collective-permute-start.27
  98.0 0.7 copy.13.weights
  98.8 1.2 copy-done.10
  99.9 5.5 %projection.3 = (bf16[128,1536]{1,0:T(8,128)(2,1)}, bf16[128,1536]{1,0:T(8,128)(2,1)}, bf16[128,1536]{1,0:T(8,128)(2,1)}, bf16[128,1536]{1,0:T(8,128)(2,1)}) custom-call(s32[8]{0:T(128)} %concatenate.15.meta, bf16[512,256]{1,0:T(8,128)(2,1)} %get-tuple-element.53.refs_0_, bf16[512,256]{1,0:T(8,128)(2,1)} %copy-done.24, bf16[512,256]{1,0:T(8,128)(2,1)} %copy-done.25, ...), custom_call_target="tpu_custom_call" | custom-call | flops 1610612736 | bytes 7000000 | tf_op jit(solution)/shard_map/projection/pallas_call | solution.py:297
  105.6 20.4 %collective-permute-done.29.refs_3_ = bf16[128,2560]{1,0:T(8,128)(2,1)} collective-permute-done((bf16[128,2560]{1,0:T(8,128)(2,1)}, bf16[128,2560]{1,0:T(8,128)(2,1)}, u32[]{:S(2)}, u32[]{:S(2)}) %collective-permute-start.29) | collective-permute-done | bytes 655392 | tf_op jit(solution)/shard_map/ppermute | solution.py:37
  126.1 3.4 collective-permute-done.27.refs_1_
  129.4 3.4 settle.1.refs_4_
  132.8 0.7 copy.12.ids
  133.5 2.6 routes.1
  136.2 0.7 copy-done.16
  137.2 9.0 %dispatch.1 = (bf16[1024,4608]{1,0:T(8,128)(2,1)}, f32[128,4096]{1,0:T(8,128)}) custom-call(s32[8]{0:T(128)} %concatenate.15.meta, bf16[128,1536]{1,0:T(8,128)(2,1)} %get-tuple-element.72.refs_0_, bf16[128,1536]{1,0:T(8,128)(2,1)} %copy-done.16, bf16[128,1536]{1,0:T(8,128)(2,1)} %copy-done.17, bf16[128,1536]{1,0:T(8,128)(2,1)} %copy-done.18, ...), custom_call_target="tpu_custom_call" | custom-call | flops 3000000000 | bytes 16000000 | tf_op jit(solution)/shard_map/dispatch/pallas_call | solution.py:398
  146.2 119.1 %all_to_all.10 = bf16[128,8,4608]{2,1,0:T(8,128)(2,1)} all-to-all(bf16[128,8,4608]{2,1,0:T(8,128)(2,1)} %bitcast.18), channel_id=1, replica_groups=mesh['dp'=4,'ctx'=2,'tp'=16] {'dp','ctx','tp'}, dimensions={0} | all-to-all | bytes 18874368 | tf_op jit(solution)/shard_map/all_to_all | solution.py:665
  265.4 24.4 %experts.1 = bf16[1024,4608]{1,0:T(8,128)(2,1)} custom-call(bf16[1024,4608]{1,0:T(8,128)(2,1)} %bitcast.19, bf16[1024,4608]{1,0:T(8,128)(2,1)} %bitcast.20, bf16[1,4096,768]{2,1,0:T(8,128)(2,1)S(1)} %bitcast.15, bf16[1,768,4096]{2,1,0:T(8,128)(2,1)} %down_hbm.1), custom_call_target="tpu_custom_call" | custom-call | flops 14495514624 | bytes 32000000 | tf_op jit(solution)/shard_map/experts/pallas_call | solution.py:462
  289.7 115.5 %all_to_all.11 = bf16[128,8,4608]{2,1,0:T(8,128)(2,1)} all-to-all(bf16[128,8,4608]{2,1,0:T(8,128)(2,1)} %bitcast.21), channel_id=1, replica_groups=mesh['dp'=4,'ctx'=2,'tp'=16] {'dp','ctx','tp'}, dimensions={0} | all-to-all | bytes 18874368 | tf_op jit(solution)/shard_map/all_to_all | solution.py:665
  405.2 8.2 %combine.1 = bf16[128,4096]{1,0:T(8,128)(2,1)} custom-call(bf16[256,1024]{1,0:T(8,128)(2,1)} %get-tuple-element.74.main, bf16[256,128]{1,0:T(8,128)(2,1)} %get-tuple-element.75.late, bf16[1024,4608]{1,0:T(8,128)(2,1)} %bitcast.16, bf16[1024,4608]{1,0:T(8,128)(2,1)} %bitcast.17, f32[128,4096]{1,0:T(8,128)} %get-tuple-element.82.state), custom_call_target="tpu_custom_call" | custom-call | flops 4000000000 | bytes 13000000 | tf_op jit(solution)/shard_map/combine/pallas_call | solution.py:515
  (93 shorter events, 3.6 us)
Async XLA Ops:
  0.0 12.7 %copy-start = (bf16[256,4096]{1,0:T(8,128)(2,1)S(1)}, bf16[256,4096]{1,0:T(8,128)(2,1)}, u32[]{:S(2)}) copy-start(bf16[256,4096]{1,0:T(8,128)(2,1)} %param.15) | copy-start | bytes 6291460
  0.0 31.3 %copy-start.7 = (s32[4]{0:T(128)S(1)}, s32[4]{0:T(128)}, u32[]{:S(2)}) copy-start(s32[4]{0:T(128)} %param.14) | copy-start | bytes 52
  1.1 5.8 %collective-permute-start.1 = (bf16[128,256]{1,0:T(8,128)(2,1)S(1)}, bf16[128,256]{1,0:T(8,128)(2,1)S(1)}, u32[]{:S(2)}, u32[]{:S(2)}) collective-permute-start(bf16[128,256]{1,0:T(8,128)(2,1)S(1)} %pad_maximum_fusion.2), channel_id=1, source_target_pairs={{0,8},{1,9},{2,10},{3,11},{4,12},{5,13},{6,14},{7,15},{8,0},{9,1},... | collective-permute-start | bytes 196616 | tf_op jit(solution)/shard_map/ppermute | solution.py:29
  4.3 4.3 %collective-permute-start.2 = (bf16[128,256]{1,0:T(8,128)(2,1)S(1)}, bf16[128,256]{1,0:T(8,128)(2,1)S(1)}, u32[]{:S(2)}, u32[]{:S(2)}) collective-permute-start(bf16[128,256]{1,0:T(8,128)(2,1)S(1)} %pad_maximum_fusion.3), channel_id=1, source_target_pairs={{0,12},{1,13},{2,14},{3,15},{4,0},{5,1},{6,2},{7,3},{8,4},{9,5},{1... | collective-permute-start | bytes 196616 | tf_op jit(solution)/shard_map/ppermute | solution.py:29
  5.5 5.5 %collective-permute-start = (bf16[128,256]{1,0:T(8,128)(2,1)S(1)}, bf16[128,256]{1,0:T(8,128)(2,1)S(1)}, u32[]{:S(2)}, u32[]{:S(2)}) collective-permute-start(bf16[128,256]{1,0:T(8,128)(2,1)S(1)} %pad_maximum_fusion.1), channel_id=1, source_target_pairs={{0,4},{1,5},{2,6},{3,7},{4,8},{5,9},{6,10},{7,11},{8,12},{9,13},{1... | collective-permute-start | bytes 196616 | tf_op jit(solution)/shard_map/ppermute | solution.py:29
  11.1 31.4 %copy-start.4 = (bf16[4,128,256]{2,1,0:T(8,128)(2,1)}, bf16[4,128,256]{2,1,0:T(8,128)(2,1)S(1)}, u32[]{:S(2)}) copy-start(bf16[4,128,256]{2,1,0:T(8,128)(2,1)S(1)} %pad_maximum_fusion.refs_0_) | copy-start | bytes 786436
  11.1 6.5 %collective-permute-start.3 = (bf16[4,128,256]{2,1,0:T(8,128)(2,1)S(1)}, bf16[4,128,256]{2,1,0:T(8,128)(2,1)S(1)}, u32[]{:S(2)}, u32[]{:S(2)}) collective-permute-start(bf16[4,128,256]{2,1,0:T(8,128)(2,1)S(1)} %pad_maximum_fusion.refs_0_), channel_id=1, source_target_pairs={{0,16},{16,0},{1,17},{17,1},{2,18},{18,2},{3,19},{19,3},{4,20},{20... | collective-permute-start | bytes 786440 | tf_op jit(solution)/shard_map/ppermute | solution.py:45
  12.8 42.5 %copy-start.2 = (bf16[256,1280]{1,0:T(8,128)(2,1)}, bf16[256,1280]{1,0:T(8,128)(2,1)S(1)}, u32[]{:S(2)}) copy-start(bf16[256,1280]{1,0:T(8,128)(2,1)S(1)} %constant_dynamic-slice_fusion.1.refs_3_) | copy-start | bytes 1966084
  12.8 28.8 %collective-permute-start.12 = (bf16[256,1280]{1,0:T(8,128)(2,1)S(1)}, bf16[256,1280]{1,0:T(8,128)(2,1)}, u32[]{:S(2)}, u32[]{:S(2)}) collective-permute-start(bf16[256,1280]{1,0:T(8,128)(2,1)S(1)} %constant_dynamic-slice_fusion.1.refs_3_), channel_id=1, source_target_pairs={{0,12},{1,13},{2,14},{3,15},{4,0},{5,1},{6,2},{7,3},{8,4},{9,5},{1... | collective-permute-start | bytes 1966088 | tf_op jit(solution)/shard_map/ppermute | solution.py:29
  12.9 9.1 %collective-permute-start.4 = (bf16[4,128,256]{2,1,0:T(8,128)(2,1)S(1)}, bf16[4,128,256]{2,1,0:T(8,128)(2,1)S(1)}, u32[]{:S(2)}, u32[]{:S(2)}) collective-permute-start(bf16[4,128,256]{2,1,0:T(8,128)(2,1)S(1)} %pad_maximum_fusion.refs_0_), channel_id=1, source_target_pairs={{0,1},{1,2},{2,3},{3,0},{4,5},{5,6},{6,7},{7,4},{8,9},{9,10},{10,1... | collective-permute-start | bytes 786440 | tf_op jit(solution)/shard_map/ppermute | solution.py:37
  17.5 24.9 %copy-start.19 = (bf16[4,128,256]{2,1,0:T(8,128)(2,1)}, bf16[4,128,256]{2,1,0:T(8,128)(2,1)S(1)}, u32[]{:S(2)}) copy-start(bf16[4,128,256]{2,1,0:T(8,128)(2,1)S(1)} %collective-permute-done.3.refs_1_) | copy-start | bytes 786436
  17.5 7.9 %collective-permute-start.7 = (bf16[4,128,256]{2,1,0:T(8,128)(2,1)S(1)}, bf16[4,128,256]{2,1,0:T(8,128)(2,1)}, u32[]{:S(2)}, u32[]{:S(2)}) collective-permute-start(bf16[4,128,256]{2,1,0:T(8,128)(2,1)S(1)} %collective-permute-done.3.refs_1_), channel_id=1, source_target_pairs={{0,3},{1,0},{2,1},{3,2},{4,7},{5,4},{6,5},{7,6},{8,11},{9,8},{10,9... | collective-permute-start | bytes 786440 | tf_op jit(solution)/shard_map/ppermute | solution.py:37
  22.0 20.4 %copy-start.20 = (bf16[4,128,256]{2,1,0:T(8,128)(2,1)}, bf16[4,128,256]{2,1,0:T(8,128)(2,1)S(1)}, u32[]{:S(2)}) copy-start(bf16[4,128,256]{2,1,0:T(8,128)(2,1)S(1)} %collective-permute-done.4.refs_2_) | copy-start | bytes 786436
  22.0 10.0 %collective-permute-start.8 = (bf16[4,128,256]{2,1,0:T(8,128)(2,1)S(1)}, bf16[4,128,256]{2,1,0:T(8,128)(2,1)}, u32[]{:S(2)}, u32[]{:S(2)}) collective-permute-start(bf16[4,128,256]{2,1,0:T(8,128)(2,1)S(1)} %collective-permute-done.4.refs_2_), channel_id=1, source_target_pairs={{0,1},{1,2},{2,3},{3,0},{4,5},{5,6},{6,7},{7,4},{8,9},{9,10},{10,1... | collective-permute-start | bytes 786440 | tf_op jit(solution)/shard_map/ppermute | solution.py:37
  25.5 8.5 %collective-permute-start.9 = (bf16[4,128,256]{2,1,0:T(8,128)(2,1)}, bf16[4,128,256]{2,1,0:T(8,128)(2,1)}, u32[]{:S(2)}, u32[]{:S(2)}) collective-permute-start(bf16[4,128,256]{2,1,0:T(8,128)(2,1)} %collective-permute-done.7.refs_5_), channel_id=1, source_target_pairs={{0,3},{1,0},{2,1},{3,2},{4,7},{5,4},{6,5},{7,6},{8,11},{9,8},{10,9... | collective-permute-start | bytes 786440 | tf_op jit(solution)/shard_map/ppermute | solution.py:37
  29.3 8.5 %collective-permute-start.6 = (bf16[4,128,256]{2,1,0:T(8,128)(2,1)S(1)}, bf16[4,128,256]{2,1,0:T(8,128)(2,1)}, u32[]{:S(2)}, u32[]{:S(2)}) collective-permute-start(bf16[4,128,256]{2,1,0:T(8,128)(2,1)S(1)} %pad_maximum_fusion.refs_0_), channel_id=1, source_target_pairs={{0,3},{1,0},{2,1},{3,2},{4,7},{5,4},{6,5},{7,6},{8,11},{9,8},{10,9... | collective-permute-start | bytes 786440 | tf_op jit(solution)/shard_map/ppermute | solution.py:37
  29.3 12.3 %collective-permute-start.5 = (bf16[4,128,256]{2,1,0:T(8,128)(2,1)S(1)}, bf16[4,128,256]{2,1,0:T(8,128)(2,1)}, u32[]{:S(2)}, u32[]{:S(2)}) collective-permute-start(bf16[4,128,256]{2,1,0:T(8,128)(2,1)S(1)} %collective-permute-done.3.refs_1_), channel_id=1, source_target_pairs={{0,1},{1,2},{2,3},{3,0},{4,5},{5,6},{6,7},{7,4},{8,9},{9,10},{10,1... | collective-permute-start | bytes 786440 | tf_op jit(solution)/shard_map/ppermute | solution.py:37
  32.0 23.3 %copy-start.3 = (bf16[256,768]{1,0:T(8,128)(2,1)}, bf16[256,768]{1,0:T(8,128)(2,1)S(1)}, u32[]{:S(2)}) copy-start(bf16[256,768]{1,0:T(8,128)(2,1)S(1)} %constant_dynamic-slice_fusion.refs_7_) | copy-start | bytes 1179652
  32.0 23.3 %collective-permute-start.11 = (bf16[256,1280]{1,0:T(8,128)(2,1)S(1)}, bf16[256,1280]{1,0:T(8,128)(2,1)S(1)}, u32[]{:S(2)}, u32[]{:S(2)}) collective-permute-start(bf16[256,1280]{1,0:T(8,128)(2,1)S(1)} %constant_dynamic-slice_fusion.1.refs_3_), channel_id=1, source_target_pairs={{0,8},{1,9},{2,10},{3,11},{4,12},{5,13},{6,14},{7,15},{8,0},{9,1},... | collective-permute-start | bytes 1966088 | tf_op jit(solution)/shard_map/ppermute | solution.py:29
  34.0 26.5 %collective-permute-start.10 = (bf16[256,1280]{1,0:T(8,128)(2,1)S(1)}, bf16[256,1280]{1,0:T(8,128)(2,1)S(1)}, u32[]{:S(2)}, u32[]{:S(2)}) collective-permute-start(bf16[256,1280]{1,0:T(8,128)(2,1)S(1)} %constant_dynamic-slice_fusion.1.refs_3_), channel_id=1, source_target_pairs={{0,4},{1,5},{2,6},{3,7},{4,8},{5,9},{6,10},{7,11},{8,12},{9,13},{1... | collective-permute-start | bytes 1966088 | tf_op jit(solution)/shard_map/ppermute | solution.py:29
  37.8 24.4 %collective-permute-start.15 = (bf16[256,768]{1,0:T(8,128)(2,1)S(1)}, bf16[256,768]{1,0:T(8,128)(2,1)S(1)}, u32[]{:S(2)}, u32[]{:S(2)}) collective-permute-start(bf16[256,768]{1,0:T(8,128)(2,1)S(1)} %constant_dynamic-slice_fusion.refs_7_), channel_id=1, source_target_pairs={{0,3},{1,0},{2,1},{3,2},{4,7},{5,4},{6,5},{7,6},{8,11},{9,8},{10,9... | collective-permute-start | bytes 1179656 | tf_op jit(solution)/shard_map/ppermute | solution.py:37
  41.6 24.1 %collective-permute-start.14 = (bf16[256,768]{1,0:T(8,128)(2,1)S(1)}, bf16[256,768]{1,0:T(8,128)(2,1)S(1)}, u32[]{:S(2)}, u32[]{:S(2)}) collective-permute-start(bf16[256,768]{1,0:T(8,128)(2,1)S(1)} %constant_dynamic-slice_fusion.refs_7_), channel_id=1, source_target_pairs={{0,2},{1,3},{2,0},{3,1},{4,6},{5,7},{6,4},{7,5},{8,10},{9,11},{10,... | collective-permute-start | bytes 1179656 | tf_op jit(solution)/shard_map/ppermute | solution.py:37
  41.6 24.1 %collective-permute-start.13 = (bf16[256,768]{1,0:T(8,128)(2,1)S(1)}, bf16[256,768]{1,0:T(8,128)(2,1)S(1)}, u32[]{:S(2)}, u32[]{:S(2)}) collective-permute-start(bf16[256,768]{1,0:T(8,128)(2,1)S(1)} %constant_dynamic-slice_fusion.refs_7_), channel_id=1, source_target_pairs={{0,1},{1,2},{2,3},{3,0},{4,5},{5,6},{6,7},{7,4},{8,9},{9,10},{10,1... | collective-permute-start | bytes 1179656 | tf_op jit(solution)/shard_map/ppermute | solution.py:37
  55.3 10.4 %copy-start.11 = (bf16[256,1280]{1,0:T(8,128)(2,1)}, bf16[256,1280]{1,0:T(8,128)(2,1)S(1)}, u32[]{:S(2)}) copy-start(bf16[256,1280]{1,0:T(8,128)(2,1)S(1)} %collective-permute-done.11.refs_5_) | copy-start | bytes 1966084
  55.3 22.1 %collective-permute-start.16 = (bf16[512,256]{1,0:T(8,128)(2,1)}, bf16[512,256]{1,0:T(8,128)(2,1)S(1)}, u32[]{:S(2)}, u32[]{:S(2)}) collective-permute-start(bf16[512,256]{1,0:T(8,128)(2,1)} %get-tuple-element.46.refs_0_), channel_id=1, source_target_pairs={{0,4},{1,5},{2,6},{3,7},{4,8},{5,9},{6,10},{7,11},{8,12},{9,13},{1... | collective-permute-start | bytes 786440 | tf_op jit(solution)/shard_map/ppermute | solution.py:29
  60.5 16.9 %collective-permute-start.17 = (bf16[512,256]{1,0:T(8,128)(2,1)}, bf16[512,256]{1,0:T(8,128)(2,1)S(1)}, u32[]{:S(2)}, u32[]{:S(2)}) collective-permute-start(bf16[512,256]{1,0:T(8,128)(2,1)} %get-tuple-element.47.refs_1_), channel_id=1, source_target_pairs={{0,8},{1,9},{2,10},{3,11},{4,12},{5,13},{6,14},{7,15},{8,0},{9,1},... | collective-permute-start | bytes 786440 | tf_op jit(solution)/shard_map/ppermute | solution.py:29
  62.2 15.3 %collective-permute-start.18 = (bf16[512,256]{1,0:T(8,128)(2,1)}, bf16[512,256]{1,0:T(8,128)(2,1)S(1)}, u32[]{:S(2)}, u32[]{:S(2)}) collective-permute-start(bf16[512,256]{1,0:T(8,128)(2,1)} %get-tuple-element.48.refs_2_), channel_id=1, source_target_pairs={{0,12},{1,13},{2,14},{3,15},{4,0},{5,1},{6,2},{7,3},{8,4},{9,5},{1... | collective-permute-start | bytes 786440 | tf_op jit(solution)/shard_map/ppermute | solution.py:29
  77.4 5.3 %copy-start.21 = (bf16[512,256]{1,0:T(8,128)(2,1)}, bf16[512,256]{1,0:T(8,128)(2,1)S(1)}, u32[]{:S(2)}) copy-start(bf16[512,256]{1,0:T(8,128)(2,1)S(1)} %collective-permute-done.16.refs_1_) | copy-start | bytes 786436
  77.4 5.2 %copy-start.22 = (bf16[512,256]{1,0:T(8,128)(2,1)}, bf16[512,256]{1,0:T(8,128)(2,1)S(1)}, u32[]{:S(2)}) copy-start(bf16[512,256]{1,0:T(8,128)(2,1)S(1)} %collective-permute-done.17.refs_2_) | copy-start | bytes 786436
  77.5 5.2 %copy-start.23 = (bf16[512,256]{1,0:T(8,128)(2,1)}, bf16[512,256]{1,0:T(8,128)(2,1)S(1)}, u32[]{:S(2)}) copy-start(bf16[512,256]{1,0:T(8,128)(2,1)S(1)} %collective-permute-done.18.refs_3_) | copy-start | bytes 786436
  77.5 5.2 %collective-permute-start.22 = (bf16[1024,1280]{1,0:T(8,128)(2,1)}, bf16[1024,1280]{1,0:T(8,128)(2,1)S(1)}, u32[]{:S(2)}, u32[]{:S(2)}) collective-permute-start(bf16[1024,1280]{1,0:T(8,128)(2,1)} %get-tuple-element.62.refs_4_), channel_id=1, source_target_pairs={{0,32},{32,0},{64,96},{96,64},{1,33},{33,1},{65,97},{97,65},{2,34}... | collective-permute-start | bytes 7864328 | tf_op jit(solution)/shard_map/ppermute | solution.py:49
  77.6 17.1 %copy-start.9 = (bf16[1024,768]{1,0:T(8,128)(2,1)S(1)}, bf16[1024,768]{1,0:T(8,128)(2,1)}, u32[]{:S(2)}) copy-start(bf16[1024,768]{1,0:T(8,128)(2,1)} %get-tuple-element.71.refs_4_) | copy-start | bytes 4718596
  77.6 20.4 %copy-start.5 = (f32[128,8]{0,1:T(8,128)S(1)}, f32[128,8]{0,1:T(8,128)}, u32[]{:S(2)}) copy-start(f32[128,8]{0,1:T(8,128)} %param.19) | copy-start | bytes 12292
  77.6 15.7 %collective-permute-start.19 = (bf16[512,256]{1,0:T(8,128)(2,1)}, bf16[512,256]{1,0:T(8,128)(2,1)S(1)}, u32[]{:S(2)}, u32[]{:S(2)}) collective-permute-start(bf16[512,256]{1,0:T(8,128)(2,1)} %get-tuple-element.55), channel_id=1, source_target_pairs={{0,1},{1,2},{2,3},{3,0},{4,5},{5,6},{6,7},{7,4},{8,9},{9,10},{10,1... | collective-permute-start | bytes 786440 | tf_op jit(solution)/shard_map/ppermute | solution.py:37
  78.2 15.2 %collective-permute-start.20 = (bf16[512,256]{1,0:T(8,128)(2,1)}, bf16[512,256]{1,0:T(8,128)(2,1)S(1)}, u32[]{:S(2)}, u32[]{:S(2)}) collective-permute-start(bf16[512,256]{1,0:T(8,128)(2,1)} %get-tuple-element.57), channel_id=1, source_target_pairs={{0,2},{1,3},{2,0},{3,1},{4,6},{5,7},{6,4},{7,5},{8,10},{9,11},{10,... | collective-permute-start | bytes 786440 | tf_op jit(solution)/shard_map/ppermute | solution.py:37
  80.6 13.3 %collective-permute-start.21 = (bf16[512,256]{1,0:T(8,128)(2,1)}, bf16[512,256]{1,0:T(8,128)(2,1)S(1)}, u32[]{:S(2)}, u32[]{:S(2)}) collective-permute-start(bf16[512,256]{1,0:T(8,128)(2,1)} %get-tuple-element.59), channel_id=1, source_target_pairs={{0,3},{1,0},{2,1},{3,2},{4,7},{5,4},{6,5},{7,6},{8,11},{9,8},{10,9... | collective-permute-start | bytes 786440 | tf_op jit(solution)/shard_map/ppermute | solution.py:37
  93.3 5.4 %copy-start.24 = (bf16[512,256]{1,0:T(8,128)(2,1)}, bf16[512,256]{1,0:T(8,128)(2,1)S(1)}, u32[]{:S(2)}) copy-start(bf16[512,256]{1,0:T(8,128)(2,1)S(1)} %collective-permute-done.19.refs_1_) | copy-start | bytes 786436
  94.7 4.1 collective-permute-start.23
  94.7 31.4 %collective-permute-start.29 = (bf16[128,2560]{1,0:T(8,128)(2,1)}, bf16[128,2560]{1,0:T(8,128)(2,1)}, u32[]{:S(2)}, u32[]{:S(2)}) collective-permute-start(bf16[128,2560]{1,0:T(8,128)(2,1)} %get-tuple-element.70), channel_id=1, source_target_pairs={{0,3},{1,0},{2,1},{3,2},{4,7},{5,4},{6,5},{7,6},{8,11},{9,8},{10,9... | collective-permute-start | bytes 1966088 | tf_op jit(solution)/shard_map/ppermute | solution.py:37
  97.1 29.0 %collective-permute-start.28 = (bf16[128,2560]{1,0:T(8,128)(2,1)}, bf16[128,2560]{1,0:T(8,128)(2,1)}, u32[]{:S(2)}, u32[]{:S(2)}) collective-permute-start(bf16[128,2560]{1,0:T(8,128)(2,1)} %get-tuple-element.68), channel_id=1, source_target_pairs={{0,2},{1,3},{2,0},{3,1},{4,6},{5,7},{6,4},{7,5},{8,10},{9,11},{10,... | collective-permute-start | bytes 1966088 | tf_op jit(solution)/shard_map/ppermute | solution.py:37
  97.1 32.4 %collective-permute-start.27 = (bf16[128,2560]{1,0:T(8,128)(2,1)}, bf16[128,2560]{1,0:T(8,128)(2,1)}, u32[]{:S(2)}, u32[]{:S(2)}) collective-permute-start(bf16[128,2560]{1,0:T(8,128)(2,1)} %get-tuple-element.66), channel_id=1, source_target_pairs={{0,1},{1,2},{2,3},{3,0},{4,5},{5,6},{6,7},{7,4},{8,9},{9,10},{10,1... | collective-permute-start | bytes 1966088 | tf_op jit(solution)/shard_map/ppermute | solution.py:37
  105.4 30.7 %collective-permute-start.24 = (bf16[128,1536]{1,0:T(8,128)(2,1)}, bf16[128,1536]{1,0:T(8,128)(2,1)S(1)}, u32[]{:S(2)}, u32[]{:S(2)}) collective-permute-start(bf16[128,1536]{1,0:T(8,128)(2,1)} %get-tuple-element.76), channel_id=1, source_target_pairs={{0,4},{1,5},{2,6},{3,7},{4,8},{5,9},{6,10},{7,11},{8,12},{9,13},{1... | collective-permute-start | bytes 1179656 | tf_op jit(solution)/shard_map/ppermute | solution.py:29
  105.6 30.6 %collective-permute-start.25 = (bf16[128,1536]{1,0:T(8,128)(2,1)}, bf16[128,1536]{1,0:T(8,128)(2,1)S(1)}, u32[]{:S(2)}, u32[]{:S(2)}) collective-permute-start(bf16[128,1536]{1,0:T(8,128)(2,1)} %get-tuple-element.77), channel_id=1, source_target_pairs={{0,8},{1,9},{2,10},{3,11},{4,12},{5,13},{6,14},{7,15},{8,0},{9,1},... | collective-permute-start | bytes 1179656 | tf_op jit(solution)/shard_map/ppermute | solution.py:29
  126.1 6.8 %copy-start.6 = (s32[128,8]{0,1:T(8,128)S(1)}, s32[128,8]{0,1:T(8,128)}, u32[]{:S(2)}) copy-start(s32[128,8]{0,1:T(8,128)} %param.18) | copy-start | bytes 12292
  126.1 10.1 %collective-permute-start.26 = (bf16[128,1536]{1,0:T(8,128)(2,1)}, bf16[128,1536]{1,0:T(8,128)(2,1)S(1)}, u32[]{:S(2)}, u32[]{:S(2)}) collective-permute-start(bf16[128,1536]{1,0:T(8,128)(2,1)} %get-tuple-element.78), channel_id=1, source_target_pairs={{0,12},{1,13},{2,14},{3,15},{4,0},{5,1},{6,2},{7,3},{8,4},{9,5},{1... | collective-permute-start | bytes 1179656 | tf_op jit(solution)/shard_map/ppermute | solution.py:29
  137.2 128.2 %slice-start = ((s8[6291456]{0:T(1024)(128)(4,1)}), s8[2097152]{0:T(1024)(128)(4,1)S(1)}, s32[]{:S(2)}) async-start(s8[6291456]{0:T(1024)(128)(4,1)} %bitcast.14), calls=%async_computation.2 | async-start | bytes 4194304
  146.2 119.1 %slice-start.1 = ((s8[6291456]{0:T(1024)(128)(4,1)}), s8[4194304]{0:T(1024)(128)(4,1)S(1)}, s32[]{:S(2)}) async-start(s8[6291456]{0:T(1024)(128)(4,1)} %bitcast.14), calls=%async_computation.3 | async-start | bytes 8388608
  405.2 8.2 %copy-start.1 = (bf16[256,4096]{1,0:T(8,128)(2,1)S(1)}, bf16[256,4096]{1,0:T(8,128)(2,1)}, u32[]{:S(2)}) copy-start(bf16[256,4096]{1,0:T(8,128)(2,1)} %param.15) | copy-start | bytes 6291460
  (11 other events, 17.7 us)

commit v10 on v9

--- a/solution.py
+++ b/solution.py
@@ -111,30 +111,45 @@
         for head in range(2):
             held[head][...] = dot_nt(key_block, heads[head])
 
-    def process(number, held, masked):
+    def update(head, scores, value_block, start):
+        peak = peaks[head, :, start:]
+        new_peak = jnp.maximum(peak, jnp.max(scores, axis=0, keepdims=True))
+        weights = jnp.exp2(scores * factor - new_peak * factor)
+        fading = jnp.exp2((peak - new_peak) * factor)
+        peaks[head, :, start:] = new_peak
+        totals[head, :, start:] = totals[head, :, start:] * fading + jnp.sum(
+            weights, axis=0, keepdims=True
+        )
+        sums[head, :, start:] = sums[head, :, start:] * fading + dot(
+            value_block, weights.astype(BF16)
+        )
+
+    def process(number, held):
         value_block = values[:, rows_of(number)]
         for head in range(2):
-            scores = held[head][...]
-            if masked:
-                seen = lax.broadcasted_iota(
-                    jnp.int32, (BLOCK, BLOCK), 0
-                ) <= lax.broadcasted_iota(jnp.int32, (BLOCK, BLOCK), 1)
-                scores = jnp.where(seen, scores, NEGATIVE)
-            peak = peaks[head]
-            new_peak = jnp.maximum(peak, jnp.max(scores, axis=0, keepdims=True))
-            weights = jnp.exp2(scores * factor - new_peak * factor)
-            fading = jnp.exp2((peak - new_peak) * factor)
-            peaks[head] = new_peak
-            totals[head] = totals[head] * fading + jnp.sum(weights, axis=0, keepdims=True)
-            sums[head] = sums[head] * fading + dot(value_block, weights.astype(BF16))
+            update(head, held[head][...], value_block, 0)
+
+    def process_last(number, held):
+        half = BLOCK // 2
+        for part in range(2):
+            start = part * half
+            columns = pl.ds(pl.multiple_of(number * BLOCK + start, half), half)
+            value_block = values[:, columns]
+            shape = (half, BLOCK - start)
+            seen = lax.broadcasted_iota(jnp.int32, shape, 0) <= lax.broadcasted_iota(
+                jnp.int32, shape, 1
+            )
+            for head in range(2):
+                scores = held[head][start : start + half, start:]
+                update(head, jnp.where(seen, scores, NEGATIVE), value_block, start)
 
     score(0, even)
 
     def two(pair, carry):
         score(2 * pair + 1, odd)
-        process(2 * pair, even, False)
+        process(2 * pair, even)
         score(2 * pair + 2, even)
-        process(2 * pair + 1, odd, False)
+        process(2 * pair + 1, odd)
         return carry
 
     lax.fori_loop(0, mine // 2, two, 0)
@@ -142,12 +157,12 @@
     @pl.when(lax.rem(mine, 2) == 1)
     def _():
         score(mine, odd)
-        process(mine - 1, even, False)
-        process(mine, odd, True)
+        process(mine - 1, even)
+        process_last(mine, odd)
 
     @pl.when(lax.rem(mine, 2) == 0)
     def _():
-        process(mine, even, True)
+        process_last(mine, even)
 
     return jnp.concatenate(
         [(sums[head] / totals[head]).T.astype(BF16) for head in range(2)], axis=1
@@ -612,7 +627,7 @@
         )
 
     width = out_proj.shape[1]
-    columns_z = width // 256 * 5 // 8 * 128
+    columns_z = width // 4
     columns_x = width // 2 - columns_z
 
     def weights_part(base, columns):

time: 414 us -> 411 us (level)
  waiting for transfers between devices: 47.3 us -> 40 us
    ppermute x15, waiting for transfers between devices: 33.2 us -> 26.5 us  [shift_z(): lax.ppermute(value, 'tp', [(x * SIDE + z, x * SIDE + (z + step) % SIDE) f...]
    ppermute x12, starting transfers between devices: 13 us -> 17.3 us  [shift_x(): lax.ppermute(value, 'tp', [(x * SIDE + z, (x + step) % SIDE * SIDE + z) f...]
  transfers between devices with their start and end apart: 30 -> 30, of which waited for: 14 -> 13; matrix products, arithmetic and copies ran while one was open for 1% -> 1% of each run, Pallas kernels for 10% -> 11%
where the time goes in v10:
time: 411 us
  blocking collectives  233 us (57%)
  Pallas kernels  86.9 us (21%)
  starting transfers between devices  42 us (10%)
  waiting for transfers between devices  40 us (10%)
  local copies, waits for them, and re-layouts  8.21 us (2%)
    all_to_all x2, blocking collectives, all_to_all(): lax.all_to_all(blocks, ('dp', 'ctx', 'tp'), split_axis=0, concat_axis=0,...  233 us
    ppermute x15, waiting for transfers between devices, shift_z(): lax.ppermute(value, 'tp', [(x * SIDE + z, x * SIDE + (z + step) % SIDE) f...  26.5 us
    pallas_call x1, Pallas kernels, experts(): call(expert_kernel, 'experts', jax.ShapeDtypeStruct((rows, columns), BF16...  24.4 us
    ppermute x15, starting transfers between devices, shift_z(): lax.ppermute(value, 'tp', [(x * SIDE + z, x * SIDE + (z + step) % SIDE) f...  22.9 us
    ppermute x12, starting transfers between devices, shift_x(): lax.ppermute(value, 'tp', [(x * SIDE + z, (x + step) % SIDE * SIDE + z) f...  17.3 us
    pallas_call x1, Pallas kernels, attention(): call(attention_kernel, 'attention', outs, [smem()] + [whole(array) for ar...  15.6 us
    pallas_call x2, Pallas kernels, projection(): call(functools.partial(projection_kernel, axis), 'projection', [jax.Shape...  13.2 us
    pallas_call x1, Pallas kernels, attention_end(): call(attention_end_kernel, 'attention_end', outs + joined, [smem()] + [wh...  10.8 us
  transfers between devices with their start and end apart: 30, of which 13 were waited for; matrix products, arithmetic and copies ran while one was open for 1% of the time, Pallas kernels for 11%

profile of v10, /device:TPU:0, one launch (start us, length us, event | category | flops | bytes accessed | tf_op | source)
XLA Modules:
  0.0 411.1 jit_solution(16628726466135946281)
XLA Ops:
  0.0 0.9 constant_dynamic-slice_fusion.8
  0.9 3.2 collective-permute-start.1
  4.1 1.2 collective-permute-start.2
  5.3 1.0 collective-permute-start
  6.3 0.5 collective-permute-done.1
  6.8 1.7 collective-permute-done.2
  8.5 2.4 collective-permute-done
  10.9 1.7 collective-permute-start.3
  12.6 1.9 collective-permute-start.4
  14.5 2.9 collective-permute-done.3.refs_1_
  17.4 4.0 collective-permute-start.7
  21.4 1.3 constant_dynamic-slice_fusion
  22.7 1.1 collective-permute-start.12
  23.8 1.8 collective-permute-done.7.refs_5_
  25.6 3.7 collective-permute-start.9
  29.4 2.0 collective-permute-start.5
  31.3 0.6 concatenate.15.meta
  32.0 2.1 collective-permute-done.8.refs_6_
  34.4 0.6 collective-permute-start.10
  35.0 2.7 collective-permute-done.6.refs_4_
  37.7 3.7 collective-permute-start.15
  41.4 3.1 collective-permute-done.12.refs_6_
  44.5 15.6 %attention.1 = (bf16[512,256]{1,0:T(8,128)(2,1)}, bf16[512,256]{1,0:T(8,128)(2,1)}, bf16[512,256]{1,0:T(8,128)(2,1)}, bf16[4096,128]{1,0:T(8,128)(2,1)}, bf16[128,4096]{1,0:T(8,128)(2,1)}) custom-call(s32[8]{0:T(128)} %concatenate.15.meta, bf16[2048,256]{1,0:T(8,128)(2,1)} %q_ref.3, bf16[4,128,256]{2,1,0:T(8,128)(2,1)} %copy-done.2, ...), custom_call_target="tpu_custom_call" | custom-call | flops 16000000000 | bytes 7000000 | tf_op jit(solution)/shard_map/attention/pallas_call | solution.py:212
  60.3 7.4 %collective-permute-start.17 = (bf16[512,256]{1,0:T(8,128)(2,1)}, bf16[512,256]{1,0:T(8,128)(2,1)S(1)}, u32[]{:S(2)}, u32[]{:S(2)}) collective-permute-start(bf16[512,256]{1,0:T(8,128)(2,1)} %get-tuple-element.47.refs_1_), channel_id=1, source_target_pairs={{0,8},{1,9},{2,10},{3,11},{4,12},{5,13},{6,14},{7,15},{8,0},{9,1},... | collective-permute-start | bytes 786440 | tf_op jit(solution)/shard_map/ppermute | solution.py:29
  67.7 0.7 copy-done.11
  68.8 10.8 %attention_end.1 = (bf16[512,256]{1,0:T(8,128)(2,1)}, bf16[512,256]{1,0:T(8,128)(2,1)}, bf16[512,256]{1,0:T(8,128)(2,1)}, bf16[512,256]{1,0:T(8,128)(2,1)}, bf16...) custom-call(s32[8]{0:T(128)} %concatenate.15.meta, bf16[2048,256]{1,0:T(8,128)(2,1)} %q_ref.3, ...), custom_call_target="tpu_custom_call" | custom-call | flops 6000000000 | bytes 7000000 | tf_op jit(solution)/shard_map/attention_end/pallas_call | solution.py:270
  80.0 4.5 %collective-permute-start.20 = (bf16[512,256]{1,0:T(8,128)(2,1)}, bf16[512,256]{1,0:T(8,128)(2,1)S(1)}, u32[]{:S(2)}, u32[]{:S(2)}) collective-permute-start(bf16[512,256]{1,0:T(8,128)(2,1)} %get-tuple-element.57), channel_id=1, source_target_pairs={{0,2},{1,3},{2,0},{3,1},{4,6},{5,7},{6,4},{7,5},{8,10},{9,11},{10,... | collective-permute-start | bytes 786440 | tf_op jit(solution)/shard_map/ppermute | solution.py:37
  84.5 1.3 copy-done.7
  85.9 6.6 %projection.2 = (bf16[128,2048]{1,0:T(8,128)(2,1)}, bf16[128,2048]{1,0:T(8,128)(2,1)}, bf16[128,2048]{1,0:T(8,128)(2,1)}, bf16[128,2048]{1,0:T(8,128)(2,1)}) custom-call(s32[8]{0:T(128)} %concatenate.15.meta, bf16[512,256]{1,0:T(8,128)(2,1)} %get-tuple-element.52.refs_0_, bf16[512,256]{1,0:T(8,128)(2,1)} %copy-done.25, bf16[512,256]{1,0:T(8,128)(2,1)} %copy-done.26, ...), custom_call_target="tpu_custom_call" | custom-call | flops 2147483648 | bytes 7000000 | tf_op jit(solution)/shard_map/projection/pallas_call | solution.py:312
  92.5 4.4 %collective-permute-done.20.refs_2_ = bf16[512,256]{1,0:T(8,128)(2,1)S(1)} collective-permute-done((bf16[512,256]{1,0:T(8,128)(2,1)}, bf16[512,256]{1,0:T(8,128)(2,1)S(1)}, u32[]{:S(2)}, u32[]{:S(2)}) %collective-permute-start.20) | collective-permute-done | bytes 262176 | tf_op jit(solution)/shard_map/ppermute | solution.py:37
  97.0 0.6 copy-done.29
  97.6 1.4 collective-permute-start.29
  99.4 1.1 collective-permute-start.27
  100.5 0.7 copy.13.weights
  101.3 6.7 %projection.3 = (bf16[128,2048]{1,0:T(8,128)(2,1)}, bf16[128,2048]{1,0:T(8,128)(2,1)}, bf16[128,2048]{1,0:T(8,128)(2,1)}, bf16[128,2048]{1,0:T(8,128)(2,1)}) custom-call(s32[8]{0:T(128)} %concatenate.15.meta, bf16[512,256]{1,0:T(8,128)(2,1)} %get-tuple-element.53.refs_0_, bf16[512,256]{1,0:T(8,128)(2,1)} %copy-done.28, bf16[512,256]{1,0:T(8,128)(2,1)} %copy-done.29, ...), custom_call_target="tpu_custom_call" | custom-call | flops 2147483648 | bytes 7000000 | tf_op jit(solution)/shard_map/projection/pallas_call | solution.py:312
  107.9 2.4 collective-permute-start.24
  110.4 12.0 %collective-permute-done.29.refs_3_ = bf16[128,2048]{1,0:T(8,128)(2,1)S(1)} collective-permute-done((bf16[128,2048]{1,0:T(8,128)(2,1)}, bf16[128,2048]{1,0:T(8,128)(2,1)S(1)}, u32[]{:S(2)}, u32[]{:S(2)}) %collective-permute-start.29) | collective-permute-done | bytes 524320 | tf_op jit(solution)/shard_map/ppermute | solution.py:37
  122.5 3.5 collective-permute-done.27.refs_1_
  125.9 3.0 settle.1.refs_4_
  128.9 0.7 copy.12.ids
  129.6 2.6 routes.1
  132.2 2.3 collective-permute-done.24.refs_1_
  134.6 0.6 collective-permute-done.26.refs_3_
  136.0 9.2 %dispatch.1 = (bf16[1024,4608]{1,0:T(8,128)(2,1)}, f32[128,4096]{1,0:T(8,128)}) custom-call(s32[8]{0:T(128)} %concatenate.15.meta, bf16[128,2048]{1,0:T(8,128)(2,1)} %get-tuple-element.72.refs_0_, bf16[128,2048]{1,0:T(8,128)(2,1)} %copy-done.14, bf16[128,2048]{1,0:T(8,128)(2,1)} %copy-done.16, bf16[128,2048]{1,0:T(8,128)(2,1)} %copy-done.18, ...), custom_call_target="tpu_custom_call" | custom-call | flops 3000000000 | bytes 16000000 | tf_op jit(solution)/shard_map/dispatch/pallas_call | solution.py:413
  145.2 118.0 %all_to_all.10 = bf16[128,8,4608]{2,1,0:T(8,128)(2,1)} all-to-all(bf16[128,8,4608]{2,1,0:T(8,128)(2,1)} %bitcast.18), channel_id=1, replica_groups=mesh['dp'=4,'ctx'=2,'tp'=16] {'dp','ctx','tp'}, dimensions={0} | all-to-all | bytes 18874368 | tf_op jit(solution)/shard_map/all_to_all | solution.py:680
  263.2 24.4 %experts.1 = bf16[1024,4608]{1,0:T(8,128)(2,1)} custom-call(bf16[1024,4608]{1,0:T(8,128)(2,1)} %bitcast.19, bf16[1024,4608]{1,0:T(8,128)(2,1)} %bitcast.20, bf16[1,4096,768]{2,1,0:T(8,128)(2,1)S(1)} %bitcast.15, bf16[1,768,4096]{2,1,0:T(8,128)(2,1)} %down_hbm.1), custom_call_target="tpu_custom_call" | custom-call | flops 14495514624 | bytes 32000000 | tf_op jit(solution)/shard_map/experts/pallas_call | solution.py:477
  287.5 115.5 %all_to_all.11 = bf16[128,8,4608]{2,1,0:T(8,128)(2,1)} all-to-all(bf16[128,8,4608]{2,1,0:T(8,128)(2,1)} %bitcast.21), channel_id=1, replica_groups=mesh['dp'=4,'ctx'=2,'tp'=16] {'dp','ctx','tp'}, dimensions={0} | all-to-all | bytes 18874368 | tf_op jit(solution)/shard_map/all_to_all | solution.py:680
  403.0 8.1 %combine.1 = bf16[128,4096]{1,0:T(8,128)(2,1)} custom-call(bf16[256,1024]{1,0:T(8,128)(2,1)} %get-tuple-element.74.main, bf16[256,128]{1,0:T(8,128)(2,1)} %get-tuple-element.75.late, bf16[1024,4608]{1,0:T(8,128)(2,1)} %bitcast.16, bf16[1024,4608]{1,0:T(8,128)(2,1)} %bitcast.17, f32[128,4096]{1,0:T(8,128)} %get-tuple-element.82.state), custom_call_target="tpu_custom_call" | custom-call | flops 4000000000 | bytes 13000000 | tf_op jit(solution)/shard_map/combine/pallas_call | solution.py:530
  (100 shorter events, 2.6 us)
Async XLA Ops:
  0.0 31.3 %copy-start.5 = (s32[4]{0:T(128)S(1)}, s32[4]{0:T(128)}, u32[]{:S(2)}) copy-start(s32[4]{0:T(128)} %param.14) | copy-start | bytes 52
  0.9 5.8 %collective-permute-start.1 = (bf16[128,256]{1,0:T(8,128)(2,1)S(1)}, bf16[128,256]{1,0:T(8,128)(2,1)S(1)}, u32[]{:S(2)}, u32[]{:S(2)}) collective-permute-start(bf16[128,256]{1,0:T(8,128)(2,1)S(1)} %pad_maximum_fusion.2), channel_id=1, source_target_pairs={{0,8},{1,9},{2,10},{3,11},{4,12},{5,13},{6,14},{7,15},{8,0},{9,1},... | collective-permute-start | bytes 196616 | tf_op jit(solution)/shard_map/ppermute | solution.py:29
  4.1 4.3 %collective-permute-start.2 = (bf16[128,256]{1,0:T(8,128)(2,1)S(1)}, bf16[128,256]{1,0:T(8,128)(2,1)S(1)}, u32[]{:S(2)}, u32[]{:S(2)}) collective-permute-start(bf16[128,256]{1,0:T(8,128)(2,1)S(1)} %pad_maximum_fusion.3), channel_id=1, source_target_pairs={{0,12},{1,13},{2,14},{3,15},{4,0},{5,1},{6,2},{7,3},{8,4},{9,5},{1... | collective-permute-start | bytes 196616 | tf_op jit(solution)/shard_map/ppermute | solution.py:29
  5.3 5.5 %collective-permute-start = (bf16[128,256]{1,0:T(8,128)(2,1)S(1)}, bf16[128,256]{1,0:T(8,128)(2,1)S(1)}, u32[]{:S(2)}, u32[]{:S(2)}) collective-permute-start(bf16[128,256]{1,0:T(8,128)(2,1)S(1)} %pad_maximum_fusion.1), channel_id=1, source_target_pairs={{0,4},{1,5},{2,6},{3,7},{4,8},{5,9},{6,10},{7,11},{8,12},{9,13},{1... | collective-permute-start | bytes 196616 | tf_op jit(solution)/shard_map/ppermute | solution.py:29
  10.9 33.5 %copy-start.2 = (bf16[4,128,256]{2,1,0:T(8,128)(2,1)}, bf16[4,128,256]{2,1,0:T(8,128)(2,1)S(1)}, u32[]{:S(2)}) copy-start(bf16[4,128,256]{2,1,0:T(8,128)(2,1)S(1)} %pad_maximum_fusion.refs_0_) | copy-start | bytes 786436
  10.9 6.5 %collective-permute-start.3 = (bf16[4,128,256]{2,1,0:T(8,128)(2,1)S(1)}, bf16[4,128,256]{2,1,0:T(8,128)(2,1)S(1)}, u32[]{:S(2)}, u32[]{:S(2)}) collective-permute-start(bf16[4,128,256]{2,1,0:T(8,128)(2,1)S(1)} %pad_maximum_fusion.refs_0_), channel_id=1, source_target_pairs={{0,16},{16,0},{1,17},{17,1},{2,18},{18,2},{3,19},{19,3},{4,20},{20... | collective-permute-start | bytes 786440 | tf_op jit(solution)/shard_map/ppermute | solution.py:45
  12.6 11.2 %collective-permute-start.4 = (bf16[4,128,256]{2,1,0:T(8,128)(2,1)S(1)}, bf16[4,128,256]{2,1,0:T(8,128)(2,1)S(1)}, u32[]{:S(2)}, u32[]{:S(2)}) collective-permute-start(bf16[4,128,256]{2,1,0:T(8,128)(2,1)S(1)} %pad_maximum_fusion.refs_0_), channel_id=1, source_target_pairs={{0,1},{1,2},{2,3},{3,0},{4,5},{5,6},{6,7},{7,4},{8,9},{9,10},{10,1... | collective-permute-start | bytes 786440 | tf_op jit(solution)/shard_map/ppermute | solution.py:37
  17.4 27.1 %copy-start.19 = (bf16[4,128,256]{2,1,0:T(8,128)(2,1)}, bf16[4,128,256]{2,1,0:T(8,128)(2,1)S(1)}, u32[]{:S(2)}) copy-start(bf16[4,128,256]{2,1,0:T(8,128)(2,1)S(1)} %collective-permute-done.3.refs_1_) | copy-start | bytes 786436
  17.4 8.2 %collective-permute-start.7 = (bf16[4,128,256]{2,1,0:T(8,128)(2,1)S(1)}, bf16[4,128,256]{2,1,0:T(8,128)(2,1)S(1)}, u32[]{:S(2)}, u32[]{:S(2)}) collective-permute-start(bf16[4,128,256]{2,1,0:T(8,128)(2,1)S(1)} %collective-permute-done.3.refs_1_), channel_id=1, source_target_pairs={{0,3},{1,0},{2,1},{3,2},{4,7},{5,4},{6,5},{7,6},{8,11},{9,8},{10,9... | collective-permute-start | bytes 786440 | tf_op jit(solution)/shard_map/ppermute | solution.py:37
  22.7 37.4 %copy-start = (bf16[256,1024]{1,0:T(8,128)(2,1)}, bf16[256,1024]{1,0:T(8,128)(2,1)S(1)}, u32[]{:S(2)}) copy-start(bf16[256,1024]{1,0:T(8,128)(2,1)S(1)} %get-tuple-element.50.refs_7_) | copy-start | bytes 1572868
  22.7 37.4 %copy-start.1 = (bf16[256,1024]{1,0:T(8,128)(2,1)}, bf16[256,1024]{1,0:T(8,128)(2,1)S(1)}, u32[]{:S(2)}) copy-start(bf16[256,1024]{1,0:T(8,128)(2,1)S(1)} %get-tuple-element.49.refs_3_) | copy-start | bytes 1572868
  22.7 21.7 %collective-permute-start.12 = (bf16[256,1024]{1,0:T(8,128)(2,1)S(1)}, bf16[256,1024]{1,0:T(8,128)(2,1)S(1)}, u32[]{:S(2)}, u32[]{:S(2)}) collective-permute-start(bf16[256,1024]{1,0:T(8,128)(2,1)S(1)} %get-tuple-element.49.refs_3_), channel_id=1, source_target_pairs={{0,12},{1,13},{2,14},{3,15},{4,0},{5,1},{6,2},{7,3},{8,4},{9,5},{1... | collective-permute-start | bytes 1572872 | tf_op jit(solution)/shard_map/ppermute | solution.py:29
  23.8 20.6 %copy-start.20 = (bf16[4,128,256]{2,1,0:T(8,128)(2,1)}, bf16[4,128,256]{2,1,0:T(8,128)(2,1)S(1)}, u32[]{:S(2)}) copy-start(bf16[4,128,256]{2,1,0:T(8,128)(2,1)S(1)} %collective-permute-done.4.refs_2_) | copy-start | bytes 786436
  23.8 10.2 %collective-permute-start.8 = (bf16[4,128,256]{2,1,0:T(8,128)(2,1)S(1)}, bf16[4,128,256]{2,1,0:T(8,128)(2,1)S(1)}, u32[]{:S(2)}, u32[]{:S(2)}) collective-permute-start(bf16[4,128,256]{2,1,0:T(8,128)(2,1)S(1)} %collective-permute-done.4.refs_2_), channel_id=1, source_target_pairs={{0,1},{1,2},{2,3},{3,0},{4,5},{5,6},{6,7},{7,4},{8,9},{9,10},{10,1... | collective-permute-start | bytes 786440 | tf_op jit(solution)/shard_map/ppermute | solution.py:37
  25.6 18.9 %copy-start.21 = (bf16[4,128,256]{2,1,0:T(8,128)(2,1)}, bf16[4,128,256]{2,1,0:T(8,128)(2,1)S(1)}, u32[]{:S(2)}) copy-start(bf16[4,128,256]{2,1,0:T(8,128)(2,1)S(1)} %collective-permute-done.7.refs_5_) | copy-start | bytes 786436
  25.6 8.8 %collective-permute-start.9 = (bf16[4,128,256]{2,1,0:T(8,128)(2,1)S(1)}, bf16[4,128,256]{2,1,0:T(8,128)(2,1)S(1)}, u32[]{:S(2)}, u32[]{:S(2)}) collective-permute-start(bf16[4,128,256]{2,1,0:T(8,128)(2,1)S(1)} %collective-permute-done.7.refs_5_), channel_id=1, source_target_pairs={{0,3},{1,0},{2,1},{3,2},{4,7},{5,4},{6,5},{7,6},{8,11},{9,8},{10,9... | collective-permute-start | bytes 786440 | tf_op jit(solution)/shard_map/ppermute | solution.py:37
  29.3 8.4 %collective-permute-start.6 = (bf16[4,128,256]{2,1,0:T(8,128)(2,1)S(1)}, bf16[4,128,256]{2,1,0:T(8,128)(2,1)S(1)}, u32[]{:S(2)}, u32[]{:S(2)}) collective-permute-start(bf16[4,128,256]{2,1,0:T(8,128)(2,1)S(1)} %pad_maximum_fusion.refs_0_), channel_id=1, source_target_pairs={{0,3},{1,0},{2,1},{3,2},{4,7},{5,4},{6,5},{7,6},{8,11},{9,8},{10,9... | collective-permute-start | bytes 786440 | tf_op jit(solution)/shard_map/ppermute | solution.py:37
  29.4 12.1 %collective-permute-start.5 = (bf16[4,128,256]{2,1,0:T(8,128)(2,1)S(1)}, bf16[4,128,256]{2,1,0:T(8,128)(2,1)}, u32[]{:S(2)}, u32[]{:S(2)}) collective-permute-start(bf16[4,128,256]{2,1,0:T(8,128)(2,1)S(1)} %collective-permute-done.3.refs_1_), channel_id=1, source_target_pairs={{0,1},{1,2},{2,3},{3,0},{4,5},{5,6},{6,7},{7,4},{8,9},{9,10},{10,1... | collective-permute-start | bytes 786440 | tf_op jit(solution)/shard_map/ppermute | solution.py:37
  34.0 10.5 %copy-start.22 = (bf16[4,128,256]{2,1,0:T(8,128)(2,1)}, bf16[4,128,256]{2,1,0:T(8,128)(2,1)S(1)}, u32[]{:S(2)}) copy-start(bf16[4,128,256]{2,1,0:T(8,128)(2,1)S(1)} %collective-permute-done.8.refs_6_) | copy-start | bytes 786436
  34.0 26.1 %collective-permute-start.11 = (bf16[256,1024]{1,0:T(8,128)(2,1)S(1)}, bf16[256,1024]{1,0:T(8,128)(2,1)S(1)}, u32[]{:S(2)}, u32[]{:S(2)}) collective-permute-start(bf16[256,1024]{1,0:T(8,128)(2,1)S(1)} %get-tuple-element.49.refs_3_), channel_id=1, source_target_pairs={{0,8},{1,9},{2,10},{3,11},{4,12},{5,13},{6,14},{7,15},{8,0},{9,1},... | collective-permute-start | bytes 1572872 | tf_op jit(solution)/shard_map/ppermute | solution.py:29
  34.4 10.1 %copy-start.23 = (bf16[4,128,256]{2,1,0:T(8,128)(2,1)}, bf16[4,128,256]{2,1,0:T(8,128)(2,1)S(1)}, u32[]{:S(2)}) copy-start(bf16[4,128,256]{2,1,0:T(8,128)(2,1)S(1)} %collective-permute-done.9.refs_7_) | copy-start | bytes 786436
  34.4 25.9 %collective-permute-start.10 = (bf16[256,1024]{1,0:T(8,128)(2,1)S(1)}, bf16[256,1024]{1,0:T(8,128)(2,1)S(1)}, u32[]{:S(2)}, u32[]{:S(2)}) collective-permute-start(bf16[256,1024]{1,0:T(8,128)(2,1)S(1)} %get-tuple-element.49.refs_3_), channel_id=1, source_target_pairs={{0,4},{1,5},{2,6},{3,7},{4,8},{5,9},{6,10},{7,11},{8,12},{9,13},{1... | collective-permute-start | bytes 1572872 | tf_op jit(solution)/shard_map/ppermute | solution.py:29
  37.7 6.8 %copy-start.24 = (bf16[4,128,256]{2,1,0:T(8,128)(2,1)}, bf16[4,128,256]{2,1,0:T(8,128)(2,1)S(1)}, u32[]{:S(2)}) copy-start(bf16[4,128,256]{2,1,0:T(8,128)(2,1)S(1)} %collective-permute-done.6.refs_4_) | copy-start | bytes 786436
  37.7 29.9 %collective-permute-start.15 = (bf16[256,1024]{1,0:T(8,128)(2,1)S(1)}, bf16[256,1024]{1,0:T(8,128)(2,1)S(1)}, u32[]{:S(2)}, u32[]{:S(2)}) collective-permute-start(bf16[256,1024]{1,0:T(8,128)(2,1)S(1)} %get-tuple-element.50.refs_7_), channel_id=1, source_target_pairs={{0,3},{1,0},{2,1},{3,2},{4,7},{5,4},{6,5},{7,6},{8,11},{9,8},{10,9... | collective-permute-start | bytes 1572872 | tf_op jit(solution)/shard_map/ppermute | solution.py:37
  41.4 26.2 %collective-permute-start.14 = (bf16[256,1024]{1,0:T(8,128)(2,1)S(1)}, bf16[256,1024]{1,0:T(8,128)(2,1)S(1)}, u32[]{:S(2)}, u32[]{:S(2)}) collective-permute-start(bf16[256,1024]{1,0:T(8,128)(2,1)S(1)} %get-tuple-element.50.refs_7_), channel_id=1, source_target_pairs={{0,2},{1,3},{2,0},{3,1},{4,6},{5,7},{6,4},{7,5},{8,10},{9,11},{10,... | collective-permute-start | bytes 1572872 | tf_op jit(solution)/shard_map/ppermute | solution.py:37
  44.5 15.7 %copy-start.8 = (bf16[256,1024]{1,0:T(8,128)(2,1)}, bf16[256,1024]{1,0:T(8,128)(2,1)S(1)}, u32[]{:S(2)}) copy-start(bf16[256,1024]{1,0:T(8,128)(2,1)S(1)} %collective-permute-done.12.refs_6_) | copy-start | bytes 1572868
  44.5 23.2 %collective-permute-start.13 = (bf16[256,1024]{1,0:T(8,128)(2,1)S(1)}, bf16[256,1024]{1,0:T(8,128)(2,1)S(1)}, u32[]{:S(2)}, u32[]{:S(2)}) collective-permute-start(bf16[256,1024]{1,0:T(8,128)(2,1)S(1)} %get-tuple-element.50.refs_7_), channel_id=1, source_target_pairs={{0,1},{1,2},{2,3},{3,0},{4,5},{5,6},{6,7},{7,4},{8,9},{9,10},{10,1... | collective-permute-start | bytes 1572872 | tf_op jit(solution)/shard_map/ppermute | solution.py:37
  60.1 7.5 %copy-start.9 = (bf16[256,1024]{1,0:T(8,128)(2,1)}, bf16[256,1024]{1,0:T(8,128)(2,1)S(1)}, u32[]{:S(2)}) copy-start(bf16[256,1024]{1,0:T(8,128)(2,1)S(1)} %collective-permute-done.11.refs_5_) | copy-start | bytes 1572868
  60.2 19.5 %collective-permute-start.16 = (bf16[512,256]{1,0:T(8,128)(2,1)}, bf16[512,256]{1,0:T(8,128)(2,1)S(1)}, u32[]{:S(2)}, u32[]{:S(2)}) collective-permute-start(bf16[512,256]{1,0:T(8,128)(2,1)} %get-tuple-element.46.refs_0_), channel_id=1, source_target_pairs={{0,4},{1,5},{2,6},{3,7},{4,8},{5,9},{6,10},{7,11},{8,12},{9,13},{1... | collective-permute-start | bytes 786440 | tf_op jit(solution)/shard_map/ppermute | solution.py:29
  60.3 7.4 %copy-start.10 = (bf16[256,1024]{1,0:T(8,128)(2,1)}, bf16[256,1024]{1,0:T(8,128)(2,1)S(1)}, u32[]{:S(2)}) copy-start(bf16[256,1024]{1,0:T(8,128)(2,1)S(1)} %collective-permute-done.10.refs_4_) | copy-start | bytes 1572868
  60.3 19.4 %collective-permute-start.17 = (bf16[512,256]{1,0:T(8,128)(2,1)}, bf16[512,256]{1,0:T(8,128)(2,1)S(1)}, u32[]{:S(2)}, u32[]{:S(2)}) collective-permute-start(bf16[512,256]{1,0:T(8,128)(2,1)} %get-tuple-element.47.refs_1_), channel_id=1, source_target_pairs={{0,8},{1,9},{2,10},{3,11},{4,12},{5,13},{6,14},{7,15},{8,0},{9,1},... | collective-permute-start | bytes 786440 | tf_op jit(solution)/shard_map/ppermute | solution.py:29
  67.6 12.1 %collective-permute-start.18 = (bf16[512,256]{1,0:T(8,128)(2,1)}, bf16[512,256]{1,0:T(8,128)(2,1)S(1)}, u32[]{:S(2)}, u32[]{:S(2)}) collective-permute-start(bf16[512,256]{1,0:T(8,128)(2,1)} %get-tuple-element.48.refs_2_), channel_id=1, source_target_pairs={{0,12},{1,13},{2,14},{3,15},{4,0},{5,1},{6,2},{7,3},{8,4},{9,5},{1... | collective-permute-start | bytes 786440 | tf_op jit(solution)/shard_map/ppermute | solution.py:29
  79.7 4.7 %collective-permute-start.22 = (bf16[1024,1024]{1,0:T(8,128)(2,1)}, bf16[1024,1024]{1,0:T(8,128)(2,1)S(1)}, u32[]{:S(2)}, u32[]{:S(2)}) collective-permute-start(bf16[1024,1024]{1,0:T(8,128)(2,1)} %get-tuple-element.62.refs_4_), channel_id=1, source_target_pairs={{0,32},{32,0},{64,96},{96,64},{1,33},{33,1},{65,97},{97,65},{2,34}... | collective-permute-start | bytes 6291464 | tf_op jit(solution)/shard_map/ppermute | solution.py:49
  79.8 17.1 %copy-start.6 = (bf16[1024,1024]{1,0:T(8,128)(2,1)S(1)}, bf16[1024,1024]{1,0:T(8,128)(2,1)}, u32[]{:S(2)}) copy-start(bf16[1024,1024]{1,0:T(8,128)(2,1)} %get-tuple-element.71.refs_4_) | copy-start | bytes 6291460
  79.8 20.7 %copy-start.3 = (f32[128,8]{0,1:T(8,128)S(1)}, f32[128,8]{0,1:T(8,128)}, u32[]{:S(2)}) copy-start(f32[128,8]{0,1:T(8,128)} %param.19) | copy-start | bytes 12292
  79.9 12.6 %collective-permute-start.19 = (bf16[512,256]{1,0:T(8,128)(2,1)}, bf16[512,256]{1,0:T(8,128)(2,1)S(1)}, u32[]{:S(2)}, u32[]{:S(2)}) collective-permute-start(bf16[512,256]{1,0:T(8,128)(2,1)} %get-tuple-element.55), channel_id=1, source_target_pairs={{0,1},{1,2},{2,3},{3,0},{4,5},{5,6},{6,7},{7,4},{8,9},{9,10},{10,1... | collective-permute-start | bytes 786440 | tf_op jit(solution)/shard_map/ppermute | solution.py:37
  80.0 17.0 %collective-permute-start.20 = (bf16[512,256]{1,0:T(8,128)(2,1)}, bf16[512,256]{1,0:T(8,128)(2,1)S(1)}, u32[]{:S(2)}, u32[]{:S(2)}) collective-permute-start(bf16[512,256]{1,0:T(8,128)(2,1)} %get-tuple-element.57), channel_id=1, source_target_pairs={{0,2},{1,3},{2,0},{3,1},{4,6},{5,7},{6,4},{7,5},{8,10},{9,11},{10,... | collective-permute-start | bytes 786440 | tf_op jit(solution)/shard_map/ppermute | solution.py:37
  84.5 12.4 %collective-permute-start.21 = (bf16[512,256]{1,0:T(8,128)(2,1)}, bf16[512,256]{1,0:T(8,128)(2,1)S(1)}, u32[]{:S(2)}, u32[]{:S(2)}) collective-permute-start(bf16[512,256]{1,0:T(8,128)(2,1)} %get-tuple-element.59), channel_id=1, source_target_pairs={{0,3},{1,0},{2,1},{3,2},{4,7},{5,4},{6,5},{7,6},{8,11},{9,8},{10,9... | collective-permute-start | bytes 786440 | tf_op jit(solution)/shard_map/ppermute | solution.py:37
  92.5 8.8 %copy-start.28 = (bf16[512,256]{1,0:T(8,128)(2,1)}, bf16[512,256]{1,0:T(8,128)(2,1)S(1)}, u32[]{:S(2)}) copy-start(bf16[512,256]{1,0:T(8,128)(2,1)S(1)} %collective-permute-done.19.refs_1_) | copy-start | bytes 786436
  96.9 4.4 %collective-permute-start.23 = (bf16[1024,1024]{1,0:T(8,128)(2,1)S(1)}, bf16[1024,1024]{1,0:T(8,128)(2,1)}, u32[]{:S(2)}, u32[]{:S(2)}) collective-permute-start(bf16[1024,1024]{1,0:T(8,128)(2,1)S(1)} %copy-done.6), channel_id=1, source_target_pairs={{0,32},{32,0},{64,96},{96,64},{1,33},{33,1},{65,97},{97,65},{2,34}... | collective-permute-start | bytes 6291464 | tf_op jit(solution)/shard_map/ppermute | solution.py:49
  97.6 24.8 %collective-permute-start.29 = (bf16[128,2048]{1,0:T(8,128)(2,1)}, bf16[128,2048]{1,0:T(8,128)(2,1)S(1)}, u32[]{:S(2)}, u32[]{:S(2)}) collective-permute-start(bf16[128,2048]{1,0:T(8,128)(2,1)} %get-tuple-element.70), channel_id=1, source_target_pairs={{0,3},{1,0},{2,1},{3,2},{4,7},{5,4},{6,5},{7,6},{8,11},{9,8},{10,9... | collective-permute-start | bytes 1572872 | tf_op jit(solution)/shard_map/ppermute | solution.py:37
  99.1 23.4 %collective-permute-start.28 = (bf16[128,2048]{1,0:T(8,128)(2,1)}, bf16[128,2048]{1,0:T(8,128)(2,1)S(1)}, u32[]{:S(2)}, u32[]{:S(2)}) collective-permute-start(bf16[128,2048]{1,0:T(8,128)(2,1)} %get-tuple-element.68), channel_id=1, source_target_pairs={{0,2},{1,3},{2,0},{3,1},{4,6},{5,7},{6,4},{7,5},{8,10},{9,11},{10,... | collective-permute-start | bytes 1572872 | tf_op jit(solution)/shard_map/ppermute | solution.py:37
  99.4 26.5 %collective-permute-start.27 = (bf16[128,2048]{1,0:T(8,128)(2,1)}, bf16[128,2048]{1,0:T(8,128)(2,1)}, u32[]{:S(2)}, u32[]{:S(2)}) collective-permute-start(bf16[128,2048]{1,0:T(8,128)(2,1)} %get-tuple-element.66), channel_id=1, source_target_pairs={{0,1},{1,2},{2,3},{3,0},{4,5},{5,6},{6,7},{7,4},{8,9},{9,10},{10,1... | collective-permute-start | bytes 1572872 | tf_op jit(solution)/shard_map/ppermute | solution.py:37
  107.9 26.6 %collective-permute-start.24 = (bf16[128,2048]{1,0:T(8,128)(2,1)}, bf16[128,2048]{1,0:T(8,128)(2,1)S(1)}, u32[]{:S(2)}, u32[]{:S(2)}) collective-permute-start(bf16[128,2048]{1,0:T(8,128)(2,1)} %get-tuple-element.76), channel_id=1, source_target_pairs={{0,4},{1,5},{2,6},{3,7},{4,8},{5,9},{6,10},{7,11},{8,12},{9,13},{1... | collective-permute-start | bytes 1572872 | tf_op jit(solution)/shard_map/ppermute | solution.py:29
  110.4 24.2 %collective-permute-start.25 = (bf16[128,2048]{1,0:T(8,128)(2,1)}, bf16[128,2048]{1,0:T(8,128)(2,1)S(1)}, u32[]{:S(2)}, u32[]{:S(2)}) collective-permute-start(bf16[128,2048]{1,0:T(8,128)(2,1)} %get-tuple-element.77), channel_id=1, source_target_pairs={{0,8},{1,9},{2,10},{3,11},{4,12},{5,13},{6,14},{7,15},{8,0},{9,1},... | collective-permute-start | bytes 1572872 | tf_op jit(solution)/shard_map/ppermute | solution.py:29
  122.4 12.8 %collective-permute-start.26 = (bf16[128,2048]{1,0:T(8,128)(2,1)}, bf16[128,2048]{1,0:T(8,128)(2,1)S(1)}, u32[]{:S(2)}, u32[]{:S(2)}) collective-permute-start(bf16[128,2048]{1,0:T(8,128)(2,1)} %get-tuple-element.78), channel_id=1, source_target_pairs={{0,12},{1,13},{2,14},{3,15},{4,0},{5,1},{6,2},{7,3},{8,4},{9,5},{1... | collective-permute-start | bytes 1572872 | tf_op jit(solution)/shard_map/ppermute | solution.py:29
  136.0 127.2 %slice-start = ((s8[6291456]{0:T(1024)(128)(4,1)}), s8[2097152]{0:T(1024)(128)(4,1)S(1)}, s32[]{:S(2)}) async-start(s8[6291456]{0:T(1024)(128)(4,1)} %bitcast.14), calls=%async_computation.2 | async-start | bytes 4194304
  145.2 118.0 %slice-start.1 = ((s8[6291456]{0:T(1024)(128)(4,1)}), s8[4194304]{0:T(1024)(128)(4,1)S(1)}, s32[]{:S(2)}) async-start(s8[6291456]{0:T(1024)(128)(4,1)} %bitcast.14), calls=%async_computation.3 | async-start | bytes 8388608
  (15 other events, 37.4 us)
